TPU v7x, 32 devices: a whole 2x2x4 slice. The times are simulated.
32 devices in a mesh: fsdp: 2 (over x), seq: 16 (over z, y, core).
Axes of the slice: x: 2, y: 2, z: 4, core: 2. Of those that a mesh axis runs over, the one named last changes fastest.
Arguments:
- activations: bfloat16 [2, 2048, 2048], P('fsdp', 'seq'), may hold values from -6 to 6
- cotangent: bfloat16 [2, 2048, 2048], P('fsdp', 'seq'), may hold values from -6 to 6
- segments: int32 [2, 2048], P('fsdp'), may hold values from 0 to 3, as said below
- routing: int32 [2, 2048, 8], P('fsdp', 'seq'), may hold values from 0 to 15, all different within a row
- attn_gain: bfloat16 [2048], P('fsdp'), may hold values from 0.5 to 1.5
- mlp_gain: bfloat16 [2048], P('fsdp'), may hold values from 0.5 to 1.5
- query_gain: bfloat16 [128], P('fsdp'), may hold values from 0.5 to 1.5
- key_gain: bfloat16 [128], P('fsdp'), may hold values from 0.5 to 1.5
- w_query: bfloat16 [2048, 4096], P('fsdp'), may hold values from -0.125 to 0.125
- key_weight: bfloat16 [2048, 512], P('fsdp'), may hold values from -0.125 to 0.125
- value_weight: bfloat16 [2048, 512], P('fsdp'), may hold values from -0.125 to 0.125
- w_out: bfloat16 [4096, 2048], P('fsdp'), may hold values from -3 to 3
- w_router: bfloat16 [2048, 16], P('fsdp'), may hold values from -0.0625 to 0.0625
- w_gate: bfloat16 [16, 2048, 768], P('seq', 'fsdp'), may hold values from -0.125 to 0.125
- w_up: bfloat16 [16, 2048, 768], P('seq', 'fsdp'), may hold values from -0.125 to 0.125
- w_down: bfloat16 [16, 768, 2048], P('seq', None, 'fsdp'), may hold values from -0.875 to 0.875
Outputs:
- mixed: bfloat16 [2, 2048, 2048], P('fsdp', 'seq')
- input_grad: float32 [2, 2048, 2048], P('fsdp', 'seq')
- attn_gain_grad: float32 [2048], P('fsdp')
- mlp_gain_grad: float32 [2048], P('fsdp')
- query_gain_grad: float32 [128], P('fsdp')
- key_gain_grad: float32 [128], P('fsdp')
- w_query_grad: float32 [2048, 4096], P('fsdp')
- w_key_grad: float32 [2048, 512], P('fsdp')
- w_value_grad: float32 [2048, 512], P('fsdp')
- w_out_grad: float32 [4096, 2048], P('fsdp')
- w_router_grad: float32 [2048, 16], P('fsdp')
- w_gate_grad: float32 [16, 2048, 768], P('seq', 'fsdp')
- w_up_grad: float32 [16, 2048, 768], P('seq', 'fsdp')
- w_down_grad: float32 [16, 768, 2048], P('seq', None, 'fsdp')
Inputs may be any that keep to these rules, and one draw needn't show every extreme that they name: `segments`: in each sequence id 0 marks padding, which fills the last 1 to 63 positions; before it the ids never fall, and the document that starts within the first 64 positions ends within the last 128 positions. `routing`: each token names 8 different experts.
All inputs are finite; a program needn't handle non-finite values.
Results may differ from a plain program's by a relative error of at most 0.024.
Values may be sent and summed in bfloat16 or wider, within the bound.
A program may use at most 320 MiB of HBM per device.

v0:
```python
import math

import jax
import jax.numpy as jnp
import numpy as np
from jax import lax
from jax.sharding import PartitionSpec as P

EPSILON = 1e-06
THETA = 1000000.0
MASKED = -1e30


def as_sent(value):
    return jax.tree.map(lambda a: a.astype(jnp.bfloat16) if a.dtype == jnp.float32 else a, value)


def norm_rows(values, scaling):
    return values * lax.rsqrt(jnp.mean(values * values, axis=-1, keepdims=True) + EPSILON) * scaling


def rotate(values, cosine, sine_table):
    half_width = values.shape[-1] // 2
    first_half = values[..., :half_width]
    second_half = values[..., half_width:]
    return jnp.concatenate(
        [
            first_half * cosine - second_half * sine_table,
            second_half * cosine + first_half * sine_table,
        ],
        axis=-1,
    )


def angles(segment, head_size):
    span_length = segment.shape[0]
    position = jnp.arange(span_length, dtype=jnp.int32)
    starts = jnp.concatenate([jnp.ones((1,), dtype=bool), segment[1:] != segment[:-1]])
    doc_start = lax.cummax(jnp.where(starts, position, jnp.zeros_like(position)), axis=0)
    offset = (position - doc_start).astype(jnp.float32)
    frequency = jnp.exp(
        jnp.arange(head_size // 2, dtype=jnp.float32) * (-2.0 * math.log(THETA) / head_size)
    )
    phases = offset[:, None] * frequency[None, :]
    return (jnp.cos(phases), jnp.sin(phases))


def allowed(segment, first_row, block_rows):
    query_doc = lax.dynamic_slice_in_dim(segment, first_row, block_rows)
    query_pos = first_row + jnp.arange(block_rows, dtype=jnp.int32)
    key_pos = jnp.arange(segment.shape[0], dtype=jnp.int32)
    same_doc = query_doc[:, None] == segment[None, :]
    causal = key_pos[None, :] <= query_pos[:, None]
    live_key = (segment[None, :] > 0) | (key_pos[None, :] == query_pos[:, None])
    return same_doc & causal & live_key


def slot_rank(routes, experts):
    named = jnp.sum(
        (routes[:, :, None] == jnp.arange(experts, dtype=jnp.int32)[None, None, :]).astype(
            jnp.int32
        ),
        axis=1,
        dtype=jnp.int32,
    )
    earlier = jnp.cumsum(named, axis=0, dtype=jnp.int32) - named
    return jnp.take_along_axis(earlier, routes, axis=1)


def per_device(
    activations,
    cotangent,
    segments,
    routing,
    attn_gain,
    mlp_gain,
    query_gain,
    key_gain,
    w_query,
    key_weight,
    value_weight,
    w_out,
    w_router,
    w_gate,
    w_up,
    w_down,
):
    groups = lax.axis_size("seq")
    tokens = activations[0].astype(jnp.float32)
    segment = segments[0]
    routes = routing[0]
    tok_rows = tokens.shape[0]
    model_width = tokens.shape[1]
    span_length = segment.shape[0]
    top_count = routes.shape[1]
    (
        full_attn_gain,
        full_mlp_gain,
        full_query_gain,
        full_key_gain,
        query_proj,
        key_proj,
        value_proj,
        out_proj,
        router_proj,
        gate_proj,
        up_proj,
        down_proj,
    ) = (
        lax.all_gather(attn_gain, "fsdp", axis=0, tiled=True),
        lax.all_gather(mlp_gain, "fsdp", axis=0, tiled=True),
        lax.all_gather(query_gain, "fsdp", axis=0, tiled=True),
        lax.all_gather(key_gain, "fsdp", axis=0, tiled=True),
        lax.all_gather(w_query, "fsdp", axis=0, tiled=True),
        lax.all_gather(key_weight, "fsdp", axis=0, tiled=True),
        lax.all_gather(value_weight, "fsdp", axis=0, tiled=True),
        lax.all_gather(w_out, "fsdp", axis=0, tiled=True),
        lax.all_gather(w_router, "fsdp", axis=0, tiled=True),
        lax.all_gather(w_gate, "fsdp", axis=1, tiled=True),
        lax.all_gather(w_up, "fsdp", axis=1, tiled=True),
        lax.all_gather(w_down, "fsdp", axis=2, tiled=True),
    )
    head_size = full_query_gain.shape[0]
    head_count = query_proj.shape[1] // head_size
    kv_count = key_proj.shape[1] // head_size
    heads_per_group = head_count // groups
    experts = router_proj.shape[1]
    local_experts = gate_proj.shape[0]
    capacity = tok_rows * top_count * 9 // (8 * experts)
    key_head_index = np.arange(groups) * heads_per_group // (head_count // kv_count)
    kv_select = (key_head_index[:, None] == np.arange(kv_count)[None, :]).astype(np.float32)
    attn_scaling = full_attn_gain.astype(jnp.float32)
    mlp_scaling = full_mlp_gain.astype(jnp.float32)
    query_scaling = full_query_gain.astype(jnp.float32)
    key_scaling = full_key_gain.astype(jnp.float32)
    normed_in, in_pullback = jax.vjp(norm_rows, tokens, attn_scaling)
    hidden_input = normed_in.astype(jnp.bfloat16)
    queries = (
        jnp.dot(hidden_input, query_proj, preferred_element_type=jnp.float32)
        .astype(jnp.bfloat16)
        .reshape(tok_rows, head_count, head_size)
    )
    keys_local = (
        jnp.dot(hidden_input, key_proj, preferred_element_type=jnp.float32)
        .astype(jnp.bfloat16)
        .reshape(tok_rows, kv_count, head_size)
    )
    values_local = (
        jnp.dot(hidden_input, value_proj, preferred_element_type=jnp.float32)
        .astype(jnp.bfloat16)
        .reshape(tok_rows, kv_count, head_size)
    )
    keys_wide = keys_local[:, key_head_index]
    values_wide = values_local[:, key_head_index]
    head_query, head_key, head_value = (
        lax.all_to_all(queries, "seq", split_axis=1, concat_axis=0, tiled=True),
        lax.all_to_all(keys_wide, "seq", split_axis=1, concat_axis=0, tiled=True),
        lax.all_to_all(values_wide, "seq", split_axis=1, concat_axis=0, tiled=True),
    )
    cosine, sine_table = angles(segment, head_size)

    def prep_query(raw_values, scaling):
        return rotate(norm_rows(raw_values, scaling), cosine[:, None], sine_table[:, None])

    def prep_key(raw_values, scaling):
        return rotate(norm_rows(raw_values, scaling), cosine, sine_table)

    query_f32, query_pullback = jax.vjp(prep_query, head_query.astype(jnp.float32), query_scaling)
    key_f32, key_pullback = jax.vjp(prep_key, head_key[:, 0].astype(jnp.float32), key_scaling)
    query_ready = query_f32.astype(jnp.bfloat16)
    key_ready = key_f32.astype(jnp.bfloat16)
    value_ready = head_value[:, 0]
    score_scale = head_size ** (-0.5)
    block_rows = min(512, span_length)
    block_count = span_length // block_rows

    def scores_of(first_row):
        query_block = lax.dynamic_slice_in_dim(query_ready, first_row, block_rows, 0)
        raw_scores = (
            jnp.einsum("qph,kh->pqk", query_block, key_ready, preferred_element_type=jnp.float32)
            * score_scale
        )
        return (
            query_block,
            jnp.where(allowed(segment, first_row, block_rows)[None], raw_scores, MASKED),
        )

    def attend(block_index):
        query_block, masked = scores_of(block_index * block_rows)
        row_peak = jnp.max(masked, axis=-1, keepdims=True)
        exponent = jnp.exp(masked - row_peak)
        row_total = jnp.sum(exponent, axis=-1, keepdims=True)
        probability = (exponent / row_total).astype(jnp.bfloat16)
        output = jnp.einsum(
            "pqk,kh->qph", probability, value_ready, preferred_element_type=jnp.float32
        ).astype(jnp.bfloat16)
        return (output, (row_peak + jnp.log(row_total))[..., 0])

    head_out, log_total = lax.map(attend, jnp.arange(block_count, dtype=jnp.int32))
    head_out = head_out.reshape(span_length, heads_per_group, head_size)
    token_out = (
        lax.all_to_all(as_sent(head_out), "seq", split_axis=0, concat_axis=1, tiled=True)
        .astype(head_out.dtype)
        .reshape(tok_rows, head_count * head_size)
    )
    resid = tokens + jnp.dot(token_out, out_proj, preferred_element_type=jnp.float32)
    normed_mid, mid_pullback = jax.vjp(norm_rows, resid, mlp_scaling)
    hidden_mid = normed_mid.astype(jnp.bfloat16)
    logits = jnp.dot(hidden_mid, router_proj, preferred_element_type=jnp.float32)
    gates = jax.nn.softmax(jnp.take_along_axis(logits, routes, axis=1), axis=-1)
    slot_index = slot_rank(routes, experts)
    target = jnp.where(
        slot_index < capacity, routes * capacity + slot_index, experts * capacity
    ).reshape(-1)
    spread = jnp.broadcast_to(hidden_mid[:, None, :], (tok_rows, top_count, model_width)).reshape(
        -1, model_width
    )
    send_rows = (
        jnp.zeros((experts * capacity + 1, model_width), jnp.bfloat16).at[target].add(spread)[:-1]
    )
    send_rows = send_rows.reshape(groups, local_experts, capacity, model_width)
    arrived = lax.all_to_all(send_rows, "seq", split_axis=0, concat_axis=0, tiled=True)
    gate_act = jnp.einsum("secd,edf->secf", arrived, gate_proj, preferred_element_type=jnp.float32)
    up_act = jnp.einsum("secd,edf->secf", arrived, up_proj, preferred_element_type=jnp.float32)
    inner_act = (jax.nn.silu(gate_act) * up_act).astype(jnp.bfloat16)
    result = jnp.einsum(
        "secf,efd->secd", inner_act, down_proj, preferred_element_type=jnp.float32
    ).astype(jnp.bfloat16)
    expert_out, gate_act, up_act, arrived = (result, gate_act, up_act, arrived)
    returned = lax.all_to_all(expert_out, "seq", split_axis=0, concat_axis=0, tiled=True).reshape(
        -1, model_width
    )
    padded_out = jnp.concatenate([returned, jnp.zeros((1, model_width), jnp.bfloat16)], axis=0)
    picked_out = padded_out[target].reshape(tok_rows, top_count, model_width).astype(jnp.float32)
    mixed_out = resid + jnp.sum(gates[:, :, None] * picked_out, axis=1)
    upstream = cotangent[0].astype(jnp.float32)
    gate_grad = jnp.sum(upstream[:, None, :] * picked_out, axis=-1)
    out_grad = (
        (gates[:, :, None] * upstream[:, None, :]).astype(jnp.bfloat16).reshape(-1, model_width)
    )
    send_grad = (
        jnp.zeros((experts * capacity + 1, model_width), jnp.bfloat16).at[target].add(out_grad)[:-1]
    )
    send_grad = send_grad.reshape(groups, local_experts, capacity, model_width)
    arrived_grad = lax.all_to_all(send_grad, "seq", split_axis=0, concat_axis=0, tiled=True)
    silu_gate = jax.nn.silu(gate_act)
    inner_act = (silu_gate * up_act).astype(jnp.bfloat16)
    down_grad = jnp.einsum(
        "secf,secd->efd", inner_act, arrived_grad, preferred_element_type=jnp.float32
    )
    inner_grad = jnp.einsum(
        "secd,efd->secf", arrived_grad, down_proj, preferred_element_type=jnp.float32
    )
    sigmoid_gate = jax.nn.sigmoid(gate_act)
    gate_back = (
        inner_grad * up_act * (sigmoid_gate + gate_act * sigmoid_gate * (1.0 - sigmoid_gate))
    ).astype(jnp.bfloat16)
    up_back = (inner_grad * silu_gate).astype(jnp.bfloat16)
    gate_wgrad = jnp.einsum(
        "secd,secf->edf", arrived, gate_back, preferred_element_type=jnp.float32
    )
    up_wgrad = jnp.einsum("secd,secf->edf", arrived, up_back, preferred_element_type=jnp.float32)
    arrived_back = (
        jnp.einsum("secf,edf->secd", gate_back, gate_proj, preferred_element_type=jnp.float32)
        + jnp.einsum("secf,edf->secd", up_back, up_proj, preferred_element_type=jnp.float32)
    ).astype(jnp.bfloat16)
    row_grad = lax.all_to_all(arrived_back, "seq", split_axis=0, concat_axis=0, tiled=True).reshape(
        -1, model_width
    )
    padded_grad = jnp.concatenate([row_grad, jnp.zeros((1, model_width), jnp.bfloat16)], axis=0)
    mid_from_experts = jnp.sum(
        padded_grad[target].reshape(tok_rows, top_count, model_width).astype(jnp.float32), axis=1
    )
    choice_grad = gates * (gate_grad - jnp.sum(gates * gate_grad, axis=-1, keepdims=True))
    one_hot = (routes[:, :, None] == jnp.arange(experts, dtype=jnp.int32)[None, None, :]).astype(
        jnp.float32
    )
    logit_grad = jnp.einsum("tk,tke->te", choice_grad, one_hot).astype(jnp.bfloat16)
    router_grad = jnp.dot(hidden_mid.T, logit_grad, preferred_element_type=jnp.float32)
    mid_grad = mid_from_experts + jnp.dot(
        logit_grad, router_proj.T, preferred_element_type=jnp.float32
    )
    resid_norm_grad, mid_gain_grad = mid_pullback(mid_grad)
    resid_grad = upstream + resid_norm_grad
    branch_grad = resid_grad.astype(jnp.bfloat16)
    out_wgrad = jnp.dot(token_out.T, branch_grad, preferred_element_type=jnp.float32)
    token_out_grad = (
        jnp.dot(branch_grad, out_proj.T, preferred_element_type=jnp.float32)
        .astype(jnp.bfloat16)
        .reshape(tok_rows, head_count, head_size)
    )
    head_out_grad = lax.all_to_all(token_out_grad, "seq", split_axis=1, concat_axis=0, tiled=True)

    def attend_back(running, block_index):
        key_sum, value_sum = running
        first_row = block_index * block_rows
        query_block, masked = scores_of(first_row)
        probability = jnp.exp(masked - log_total[block_index][..., None])
        grad_block = lax.dynamic_slice_in_dim(head_out_grad, first_row, block_rows, 0)
        prob_grad = jnp.einsum(
            "qph,kh->pqk", grad_block, value_ready, preferred_element_type=jnp.float32
        )
        value_sum = value_sum + jnp.einsum(
            "pqk,qph->kh",
            probability.astype(jnp.bfloat16),
            grad_block,
            preferred_element_type=jnp.float32,
        )
        score_grad = (
            probability * (prob_grad - jnp.sum(probability * prob_grad, axis=-1, keepdims=True))
        ).astype(jnp.bfloat16)
        query_grad = (
            jnp.einsum("pqk,kh->qph", score_grad, key_ready, preferred_element_type=jnp.float32)
            * score_scale
        )
        key_sum = (
            key_sum
            + jnp.einsum("pqk,qph->kh", score_grad, query_block, preferred_element_type=jnp.float32)
            * score_scale
        )
        return ((key_sum, value_sum), query_grad)

    empty_rows = jnp.zeros((span_length, head_size), jnp.float32)
    (key_total, value_total), query_grads = lax.scan(
        attend_back, (empty_rows, empty_rows), jnp.arange(block_count, dtype=jnp.int32)
    )
    head_query_grad, query_gain_grad = query_pullback(
        query_grads.reshape(span_length, heads_per_group, head_size)
    )
    head_key_grad, key_gain_grad = key_pullback(key_total)
    token_query_grad, token_key_grad, token_value_grad = (
        lax.all_to_all(
            head_query_grad.astype(jnp.bfloat16), "seq", split_axis=0, concat_axis=1, tiled=True
        ),
        lax.all_to_all(
            head_key_grad.astype(jnp.bfloat16)[:, None],
            "seq",
            split_axis=0,
            concat_axis=1,
            tiled=True,
        ),
        lax.all_to_all(
            value_total.astype(jnp.bfloat16)[:, None],
            "seq",
            split_axis=0,
            concat_axis=1,
            tiled=True,
        ),
    )
    query_tok_grad = token_query_grad.reshape(tok_rows, head_count * head_size)
    key_tok_grad = (
        jnp.einsum("tsh,sg->tgh", token_key_grad.astype(jnp.float32), kv_select)
        .astype(jnp.bfloat16)
        .reshape(tok_rows, kv_count * head_size)
    )
    value_tok_grad = (
        jnp.einsum("tsh,sg->tgh", token_value_grad.astype(jnp.float32), kv_select)
        .astype(jnp.bfloat16)
        .reshape(tok_rows, kv_count * head_size)
    )
    query_wgrad = jnp.dot(hidden_input.T, query_tok_grad, preferred_element_type=jnp.float32)
    key_wgrad = jnp.dot(hidden_input.T, key_tok_grad, preferred_element_type=jnp.float32)
    value_wgrad = jnp.dot(hidden_input.T, value_tok_grad, preferred_element_type=jnp.float32)
    in_grad = (
        jnp.dot(query_tok_grad, query_proj.T, preferred_element_type=jnp.float32)
        + jnp.dot(key_tok_grad, key_proj.T, preferred_element_type=jnp.float32)
        + jnp.dot(value_tok_grad, value_proj.T, preferred_element_type=jnp.float32)
    )
    token_norm_grad, attn_gain_grad = in_pullback(in_grad)
    input_grad = resid_grad + token_norm_grad
    reduced = (
        lax.psum_scatter(
            attn_gain_grad.astype(jnp.bfloat16), "fsdp", scatter_dimension=0, tiled=True
        ).astype(jnp.float32),
        lax.psum_scatter(
            mid_gain_grad.astype(jnp.bfloat16), "fsdp", scatter_dimension=0, tiled=True
        ).astype(jnp.float32),
        lax.psum_scatter(
            query_gain_grad.astype(jnp.bfloat16), "fsdp", scatter_dimension=0, tiled=True
        ).astype(jnp.float32),
        lax.psum_scatter(
            key_gain_grad.astype(jnp.bfloat16), "fsdp", scatter_dimension=0, tiled=True
        ).astype(jnp.float32),
        lax.psum_scatter(
            query_wgrad.astype(jnp.bfloat16), "fsdp", scatter_dimension=0, tiled=True
        ).astype(jnp.float32),
        lax.psum_scatter(
            key_wgrad.astype(jnp.bfloat16), "fsdp", scatter_dimension=0, tiled=True
        ).astype(jnp.float32),
        lax.psum_scatter(
            value_wgrad.astype(jnp.bfloat16), "fsdp", scatter_dimension=0, tiled=True
        ).astype(jnp.float32),
        lax.psum_scatter(
            out_wgrad.astype(jnp.bfloat16), "fsdp", scatter_dimension=0, tiled=True
        ).astype(jnp.float32),
        lax.psum_scatter(
            router_grad.astype(jnp.bfloat16), "fsdp", scatter_dimension=0, tiled=True
        ).astype(jnp.float32),
        lax.psum_scatter(
            gate_wgrad.astype(jnp.bfloat16), "fsdp", scatter_dimension=1, tiled=True
        ).astype(jnp.float32),
        lax.psum_scatter(
            up_wgrad.astype(jnp.bfloat16), "fsdp", scatter_dimension=1, tiled=True
        ).astype(jnp.float32),
        lax.psum_scatter(
            down_grad.astype(jnp.bfloat16), "fsdp", scatter_dimension=2, tiled=True
        ).astype(jnp.float32),
    )
    shared_part = (
        lax.psum(reduced[0].astype(jnp.bfloat16), "seq").astype(jnp.float32),
        lax.psum(reduced[1].astype(jnp.bfloat16), "seq").astype(jnp.float32),
        lax.psum(reduced[2].astype(jnp.bfloat16), "seq").astype(jnp.float32),
        lax.psum(reduced[3].astype(jnp.bfloat16), "seq").astype(jnp.float32),
        lax.psum(reduced[4].astype(jnp.bfloat16), "seq").astype(jnp.float32),
        lax.psum(reduced[5].astype(jnp.bfloat16), "seq").astype(jnp.float32),
        lax.psum(reduced[6].astype(jnp.bfloat16), "seq").astype(jnp.float32),
        lax.psum(reduced[7].astype(jnp.bfloat16), "seq").astype(jnp.float32),
        lax.psum(reduced[8].astype(jnp.bfloat16), "seq").astype(jnp.float32),
    )
    expert_part = (reduced[9], reduced[10], reduced[11])
    return (
        mixed_out.astype(jnp.bfloat16)[None],
        input_grad[None],
        shared_part[0],
        shared_part[1],
        shared_part[2],
        shared_part[3],
        shared_part[4],
        shared_part[5],
        shared_part[6],
        shared_part[7],
        shared_part[8],
        expert_part[0],
        expert_part[1],
        expert_part[2],
    )


def solution(mesh):
    placed = (
        P("fsdp", "seq", None),
        P("fsdp", "seq", None),
        P("fsdp", None),
        P("fsdp", "seq", None),
        P("fsdp"),
        P("fsdp"),
        P("fsdp"),
        P("fsdp"),
        P("fsdp", None),
        P("fsdp", None),
        P("fsdp", None),
        P("fsdp", None),
        P("fsdp", None),
        P("seq", "fsdp", None),
        P("seq", "fsdp", None),
        P("seq", None, "fsdp"),
    )
    return jax.shard_map(
        per_device,
        mesh=mesh,
        in_specs=placed,
        out_specs=(
            P("fsdp", "seq", None),
            P("fsdp", "seq", None),
            P("fsdp"),
            P("fsdp"),
            P("fsdp"),
            P("fsdp"),
            P("fsdp", None),
            P("fsdp", None),
            P("fsdp", None),
            P("fsdp", None),
            P("fsdp", None),
            P("seq", "fsdp", None),
            P("seq", "fsdp", None),
            P("seq", None, "fsdp"),
        ),
        check_vma=False,
    )
```

profile of v0, /device:TPU:0, one launch (start us, length us, event | category | flops | bytes accessed | tf_op | source)
XLA Modules:
  0.0 2228.1 jit_solution(17550537609963123767)
XLA Ops:
  16.9 28.5 %all-gather.10.cloned.1.call-done = bf16[2048,512]{1,0:T(8,128)(2,1)} async-done(((bf16[1024,512]{1,0:T(8,128)(2,1)}), bf16[2048,512]{1,0:T(8,128)(2,1)}) %all-gather.10.cloned.1.call-update) | async-done | bytes 2097168 | tf_op jit(solution)/shard_map/all_gather | solution.py:115
  61.4 184.5 %all-gather.8.cloned.1.call-done = bf16[2048,4096]{1,0:T(8,128)(2,1)} async-done(((bf16[1024,4096]{1,0:T(8,128)(2,1)}), bf16[2048,4096]{1,0:T(8,128)(2,1)}) %all-gather.8.cloned.1.call-update) | async-done | bytes 16777232 | tf_op jit(solution)/shard_map/all_gather | solution.py:114
  311.2 54.9 %while.27 = (s32[]{:T(128)}, bf16[4,512,2,128]{3,1,0,2:T(8,128)(2,1)}, f32[4,2,512]{2,1,0:T(2,128)}, s32[4]{0:T(128)S(1)}, s32[2048]{0:T(1024)S(1)}, /*index=5*/...) while((s32[]{:T(128)}, ...), condition=%wide.region_8.9_spmd, body=%wide.region_5.8_spmd.sunk | while | flops 1105331712 | bytes 30996692 | solution.py:199
  399.6 82.0 %all-gather.14.cloned.1.call-done = bf16[4096,2048]{1,0:T(8,128)(2,1)} async-done(((bf16[2048,2048]{1,0:T(8,128)(2,1)}), bf16[4096,2048]{1,0:T(8,128)(2,1)}) %all-gather.14.cloned.1.call-update) | async-done | bytes 16777232 | tf_op jit(solution)/shard_map/all_gather | solution.py:117
  548.4 64.8 %all-to-all-done.6 = bf16[16,1,72,2048]{3,2,1,0:T(8,128)(2,1)} async-done(((bf16[16,1,72,2048]{3,2,1,0:T(8,128)(2,1)}), bf16[16,1,72,2048]{3,2,1,0:T(8,128)(2,1)}, u32[]{:S(2)}, u32[]{:S(2)}) %all-to-all-start.6) | async-done | bytes 4718624 | tf_op jit(solution)/shard_map/all_to_all | solution.py:245
  613.2 21.8 all-to-all-start.4
  636.9 45.5 %all-gather.20.cloned.1.call-done = bf16[1,768,2048]{2,1,0:T(8,128)(2,1)} async-done(((bf16[1,768,1024]{2,1,0:T(8,128)(2,1)}), bf16[1,768,2048]{2,1,0:T(8,128)(2,1)}) %all-gather.20.cloned.1.call-update) | async-done | bytes 3145744 | tf_op jit(solution)/shard_map/all_gather | solution.py:121
  691.4 37.4 %all-gather.18.cloned.1.call-done = bf16[1,2048,768]{2,1,0:T(8,128)(2,1)} async-done(((bf16[1,1024,768]{2,1,0:T(8,128)(2,1)}), bf16[1,2048,768]{2,1,0:T(8,128)(2,1)}) %all-gather.18.cloned.1.call-update) | async-done | bytes 3145744 | tf_op jit(solution)/shard_map/all_gather | solution.py:120
  737.7 37.5 %all-gather.16.cloned.1.call-done = bf16[1,2048,768]{2,1,0:T(8,128)(2,1)} async-done(((bf16[1,1024,768]{2,1,0:T(8,128)(2,1)}), bf16[1,2048,768]{2,1,0:T(8,128)(2,1)}) %all-gather.16.cloned.1.call-update) | async-done | bytes 3145744 | tf_op jit(solution)/shard_map/all_gather | solution.py:119
  811.1 78.3 %all-to-all-done.7 = bf16[16,1,72,2048]{3,2,1,0:T(8,128)(2,1)} async-done(((bf16[16,1,72,2048]{3,2,1,0:T(8,128)(2,1)}), bf16[16,1,72,2048]{3,2,1,0:T(8,128)(2,1)}, u32[]{:S(2)}, u32[]{:S(2)}) %all-to-all-start.7) | async-done | bytes 4718624 | tf_op jit(solution)/shard_map/all_to_all | solution.py:267
  889.5 22.0 all-to-all-start.5
  935.0 63.3 %all-to-all-done.5 = bf16[16,1,72,2048]{3,2,1,0:T(8,128)(2,1)} async-done(((bf16[16,1,72,2048]{3,2,1,0:T(8,128)(2,1)}), bf16[16,1,72,2048]{3,2,1,0:T(8,128)(2,1)}, u32[]{:S(2)}, u32[]{:S(2)}) %all-to-all-start.5) | async-done | bytes 4718624 | tf_op jit(solution)/shard_map/all_to_all | solution.py:230
  1037.1 21.7 all-to-all-start.8
  1058.9 22.9 %all-to-all-done.8 = bf16[128,32,128]{2,0,1:T(8,128)(2,1)S(1)} async-done(((bf16[128,32,128]{2,0,1:T(8,128)(2,1)}), bf16[128,32,128]{2,0,1:T(8,128)(2,1)S(1)}, u32[]{:S(2)}, u32[]{:S(2)}) %all-to-all-start.8) | async-done | bytes 1048608 | tf_op jit(solution)/shard_map/all_to_all | solution.py:292
  1082.8 142.3 %while.28 = (s32[]{:T(128)}, f32[2048,128]{1,0:T(8,128)S(1)}, f32[2048,128]{1,0:T(8,128)}, f32[4,512,2,128]{3,1,0,2:T(8,128)}, s32[4]{0:T(128)S(1)}, /*index=5*/...) while((s32[]{:T(128)}, f32[2048,128]{1,0:T(8,128)S(1)}, ...), condition=%wide.region_23.24_spmd.clone, body=%wide.region_21.23_spmd.clone.sunk | while | flops 2723546624 | bytes 124840368 | solution.py:324
  1233.6 21.1 all_to_all.137
  1309.2 28.7 %all_to_all.139 = bf16[2048,2,128]{2,1,0:T(2,128)(2,1)S(1)} all-to-all(bf16[2048,2,128]{2,1,0:T(2,128)(2,1)S(1)} %copy.164), channel_id=1, replica_groups=mesh['fsdp'=2,'seq'=16] {'seq'}, dimensions={0} | all-to-all | bytes 2097152 | tf_op jit(solution)/shard_map/all_to_all | solution.py:332
  1378.1 136.3 %reduce-scatter.15.cloned.1.call-done = bf16[2048,2048]{1,0:T(8,128)(2,1)} async-done(((bf16[4096,2048]{1,0:T(8,128)(2,1)}), bf16[2048,2048]{1,0:T(8,128)(2,1)}) %reduce-scatter.15.cloned.1.call-update) | async-done | bytes 8388624 | tf_op jit(solution)/shard_map/reduce_scatter | solution.py:393
  1514.5 192.1 %reduce-scatter.9.cloned.1.call-done = bf16[1024,4096]{1,0:T(8,128)(2,1)} async-done(((bf16[2048,4096]{1,0:T(8,128)(2,1)}), bf16[1024,4096]{1,0:T(8,128)(2,1)}) %reduce-scatter.9.cloned.1.call-update) | async-done | bytes 8388624 | tf_op jit(solution)/shard_map/reduce_scatter | solution.py:384
  1708.0 44.8 %reduce-scatter.19.cloned.1.call-done = bf16[1,1024,768]{2,1,0:T(8,128)(2,1)} async-done(((bf16[1,2048,768]{2,1,0:T(8,128)(2,1)}), bf16[1,1024,768]{2,1,0:T(8,128)(2,1)}) %reduce-scatter.19.cloned.1.call-update) | async-done | bytes 1572880 | tf_op jit(solution)/shard_map/reduce_scatter | solution.py:399
  1756.0 43.0 %reduce-scatter.21.cloned.1.call-done = bf16[1,1024,768]{2,1,0:T(8,128)(2,1)} async-done(((bf16[1,2048,768]{2,1,0:T(8,128)(2,1)}), bf16[1,1024,768]{2,1,0:T(8,128)(2,1)}) %reduce-scatter.21.cloned.1.call-update) | async-done | bytes 1572880 | tf_op jit(solution)/shard_map/reduce_scatter | solution.py:402
  1802.3 42.2 %reduce-scatter.23.cloned.1.call-done = bf16[1,768,1024]{2,1,0:T(8,128)(2,1)} async-done(((bf16[1,768,2048]{2,1,0:T(8,128)(2,1)}), bf16[1,768,1024]{2,1,0:T(8,128)(2,1)}) %reduce-scatter.23.cloned.1.call-update) | async-done | bytes 1572880 | tf_op jit(solution)/shard_map/reduce_scatter | solution.py:405
  1869.5 63.9 %all-reduce.12 = (bf16[1024]{0:T(1024)(128)(2,1)S(1)}, bf16[1024]{0:T(1024)(128)(2,1)S(1)}, bf16[64]{0:T(256)(128)(2,1)S(1)}, bf16[64]{0:T(256)(128)(2,1)S(1)}, bf16[1024,16]{0,1:T(8,128)(2,1)S(1)}) all-reduce(bf16[1024]{0:T(1024)(128)(2,1)S(1)} %dynamic-slice.3, ...), channel_id=1, replica_groups=mesh['fsdp'=2,'seq'=16] {'seq'}, use_global_device_ids=true, to_apply=%region_29.30 | all-reduce | flops 18560 | bytes 74240 | tf_op jit(solution)/shard_map/psum | solution.py:410
  1937.6 256.6 %all-reduce.18.cloned.1.call-done = (bf16[1024,4096]{1,0:T(8,128)(2,1)}, bf16[1024,512]{1,0:T(8,128)(2,1)}, bf16[1024,512]{1,0:T(8,128)(2,1)}, bf16[2048,2048]{1,0:T(8,128)(2,1)}) async-done(((bf16[1024,4096]{1,0:T(8,128)(2,1)}, bf16[1024,512]{1,0:T(8,128)(2,1)}, bf16[1024,512]{1,0:T(8,128)(2,1)}, bf16[2048,2048]{1,0:T(8,128)(2,1)}), (bf16[1024,4096]{1,0:T(8,128)(2,1)}, bf16[1024,512]{1,0:T(8,128)(2,1)}, ...) | async-done | bytes 18874384 | tf_op jit(solution)/shard_map/psum | solution.py:414
  (472 shorter events, 657.9 us)
Async XLA Ops:
  7.2 38.2 %all-gather.10.cloned.1.call-start = ((), (), s32[]{:S(2)}) async-start(), calls=%async_computation.21 | async-start | bytes 3145728 | tf_op jit(solution)/shard_map/all_gather | solution.py:115
  7.9 237.9 %all-gather.8.cloned.1.call-start = ((), (), s32[]{:S(2)}) async-start(), calls=%async_computation.20 | async-start | bytes 25165824 | tf_op jit(solution)/shard_map/all_gather | solution.py:114
  8.7 271.9 %all-gather.12.cloned.1.call-start = ((), (), s32[]{:S(2)}) async-start(), calls=%async_computation.22 | async-start | bytes 3145728 | tf_op jit(solution)/shard_map/all_gather | solution.py:116
  9.4 472.2 %all-gather.14.cloned.1.call-start = ((), (), s32[]{:S(2)}) async-start(), calls=%async_computation.23 | async-start | bytes 25165824 | tf_op jit(solution)/shard_map/all_gather | solution.py:117
  48.9 206.4 %all-to-all-start.1 = ((bf16[128,16,128]{2,0,1:T(8,128)(2,1)}), bf16[128,16,128]{2,0,1:T(8,128)(2,1)S(1)}, u32[]{:S(2)}, u32[]{:S(2)}) async-start(bf16[128,16,128]{2,0,1:T(8,128)(2,1)} %bitcast.19), calls=%async_computation.1 | async-start | bytes 1048576 | tf_op jit(solution)/shard_map/all_to_all | solution.py:157
  255.4 35.5 %all-to-all-start = ((bf16[128,32,128]{2,0,1:T(8,128)(2,1)}), bf16[128,32,128]{2,0,1:T(8,128)(2,1)S(1)}, u32[]{:S(2)}, u32[]{:S(2)}) async-start(bf16[128,32,128]{2,0,1:T(8,128)(2,1)} %bitcast.554), calls=%async_computation | async-start | bytes 2097152 | tf_op jit(solution)/shard_map/all_to_all | solution.py:156
  370.2 27.3 %all-to-all-start.3 = ((bf16[2048,2,128]{2,1,0:T(2,128)(2,1)}), bf16[2048,2,128]{2,1,0:T(2,128)(2,1)}, u32[]{:S(2)}, u32[]{:S(2)}) async-start(bf16[2048,2,128]{2,1,0:T(2,128)(2,1)} %copy.149), calls=%async_computation.3 | async-start | bytes 2097152 | tf_op jit(solution)/shard_map/all_to_all | solution.py:202
  520.7 92.5 %all-to-all-start.6 = ((bf16[16,1,72,2048]{3,2,1,0:T(8,128)(2,1)}), bf16[16,1,72,2048]{3,2,1,0:T(8,128)(2,1)}, u32[]{:S(2)}, u32[]{:S(2)}) async-start(bf16[16,1,72,2048]{3,2,1,0:T(8,128)(2,1)} %bitcast.536), calls=%async_computation.6 | async-start | bytes 9437184 | tf_op jit(solution)/shard_map/all_to_all | solution.py:245
  613.2 115.6 %all-to-all-start.4 = ((bf16[16,1,72,2048]{3,2,1,0:T(8,128)(2,1)}), bf16[16,1,72,2048]{3,2,1,0:T(8,128)(2,1)}, u32[]{:S(2)}, u32[]{:S(2)}) async-start(bf16[16,1,72,2048]{3,2,1,0:T(8,128)(2,1)} %bitcast.535), calls=%async_computation.4 | async-start | bytes 9437184 | tf_op jit(solution)/shard_map/all_to_all | solution.py:222
  635.0 47.4 %all-gather.20.cloned.1.call-start = ((), (), s32[]{:S(2)}) async-start(), calls=%async_computation.26 | async-start | bytes 4718592 | tf_op jit(solution)/shard_map/all_gather | solution.py:121
  635.6 93.2 %all-gather.18.cloned.1.call-start = ((), (), s32[]{:S(2)}) async-start(), calls=%async_computation.25 | async-start | bytes 4718592 | tf_op jit(solution)/shard_map/all_gather | solution.py:120
  636.2 139.1 %all-gather.16.cloned.1.call-start = ((), (), s32[]{:S(2)}) async-start(), calls=%async_computation.24 | async-start | bytes 4718592 | tf_op jit(solution)/shard_map/all_gather | solution.py:119
  797.0 92.5 %all-to-all-start.7 = ((bf16[16,1,72,2048]{3,2,1,0:T(8,128)(2,1)}), bf16[16,1,72,2048]{3,2,1,0:T(8,128)(2,1)}, u32[]{:S(2)}, u32[]{:S(2)}) async-start(bf16[16,1,72,2048]{3,2,1,0:T(8,128)(2,1)} %fusion.55), calls=%async_computation.7 | async-start | bytes 9437184 | tf_op jit(solution)/shard_map/all_to_all | solution.py:267
  889.5 108.8 %all-to-all-start.5 = ((bf16[16,1,72,2048]{3,2,1,0:T(8,128)(2,1)}), bf16[16,1,72,2048]{3,2,1,0:T(8,128)(2,1)}, u32[]{:S(2)}, u32[]{:S(2)}) async-start(bf16[16,1,72,2048]{3,2,1,0:T(8,128)(2,1)} %convert_bitcast_fusion), calls=%async_computation.5 | async-start | bytes 9437184 | tf_op jit(solution)/shard_map/all_to_all | solution.py:230
  1037.1 44.7 %all-to-all-start.8 = ((bf16[128,32,128]{2,0,1:T(8,128)(2,1)}), bf16[128,32,128]{2,0,1:T(8,128)(2,1)S(1)}, u32[]{:S(2)}, u32[]{:S(2)}) async-start(bf16[128,32,128]{2,0,1:T(8,128)(2,1)} %bitcast.478), calls=%async_computation.8 | async-start | bytes 2097152 | tf_op jit(solution)/shard_map/all_to_all | solution.py:292
  1058.8 319.3 %reduce-scatter.11.cloned.1.call-start = ((), (), s32[]{:S(2)}) async-start(), calls=%async_computation.28 | async-start | bytes 3145728 | tf_op jit(solution)/shard_map/reduce_scatter | solution.py:387
  1257.9 120.2 %reduce-scatter.13.cloned.1.call-start = ((), (), s32[]{:S(2)}) async-start(), calls=%async_computation.29 | async-start | bytes 3145728 | tf_op jit(solution)/shard_map/reduce_scatter | solution.py:390
  1283.3 231.2 %reduce-scatter.15.cloned.1.call-start = ((), (), s32[]{:S(2)}) async-start(), calls=%async_computation.30 | async-start | bytes 25165824 | tf_op jit(solution)/shard_map/reduce_scatter | solution.py:393
  1291.9 414.8 %reduce-scatter.9.cloned.1.call-start = ((), (), s32[]{:S(2)}) async-start(), calls=%async_computation.27 | async-start | bytes 25165824 | tf_op jit(solution)/shard_map/reduce_scatter | solution.py:384
  1349.4 403.4 %reduce-scatter.19.cloned.1.call-start = ((), (), s32[]{:S(2)}) async-start(), calls=%async_computation.32 | async-start | bytes 4718592 | tf_op jit(solution)/shard_map/reduce_scatter | solution.py:399
  1358.8 440.2 %reduce-scatter.21.cloned.1.call-start = ((), (), s32[]{:S(2)}) async-start(), calls=%async_computation.33 | async-start | bytes 4718592 | tf_op jit(solution)/shard_map/reduce_scatter | solution.py:402
  1367.8 476.7 %reduce-scatter.23.cloned.1.call-start = ((), (), s32[]{:S(2)}) async-start(), calls=%async_computation.34 | async-start | bytes 4718592 | tf_op jit(solution)/shard_map/reduce_scatter | solution.py:405
  1377.1 492.5 %reduce-scatter.17.cloned.1.call-start = ((), (), s32[]{:S(2)}) async-start(), calls=%async_computation.31 | async-start | bytes 98304 | tf_op jit(solution)/shard_map/reduce_scatter | solution.py:396
  1378.0 816.1 %all-reduce.18.cloned.1.call-start = ((), (), s32[]{:S(2)}) async-start(), calls=%async_computation.35 | async-start | bytes 37748736 | tf_op jit(solution)/shard_map/psum | solution.py:414
  (88 other events, 2545.0 us)
Sparse Core Ops, SparseCore 0:
  9.6 35.7 all-gather.9
  46.9 198.8 all-gather.7
  247.4 33.1 all-gather.11
  281.9 199.5 all-gather.13
  637.1 45.2 all-gather.19
  683.8 44.9 all-gather.17
  730.3 44.9 all-gather.15
  1258.0 30.2 reduce-scatter.10
  1290.7 31.8 reduce-scatter.12
  1325.3 189.1 reduce-scatter.14
  1517.5 189.1 reduce-scatter.8
  1709.3 43.3 reduce-scatter.18
  1755.6 43.3 reduce-scatter.20
  1801.1 43.3 reduce-scatter.22
  1847.2 9.8 reduce-scatter.16
  1862.1 331.9 all-reduce.17
where the time goes:
time: 2240 us; the launch traced here: 2230 us
  waiting for transfers between devices  1400 us (62%)
  matrix products  265 us (12%)
  other arithmetic  173 us (8%)
  blocking collectives  158 us (7%)
  local copies, waits for them, and re-layouts  104 us (5%)
  starting transfers between devices  99.6 us (4%)
    psum x1, waiting for transfers between devices, per_device(): lax.psum(reduced[4].astype(jnp.bfloat16), 'seq').astype(jnp.float32)  257 us
    reduce_scatter x1, waiting for transfers between devices, per_device(): lax.psum_scatter(query_wgrad.astype(jnp.bfloat16), 'fsdp', scatter_dimens...  192 us
    all_gather x1, waiting for transfers between devices, per_device(): lax.all_gather(w_query, 'fsdp', axis=0, tiled=True)  184 us
    reduce_scatter x1, waiting for transfers between devices, per_device(): lax.psum_scatter(out_wgrad.astype(jnp.bfloat16), 'fsdp', scatter_dimensio...  136 us
    all_gather x1, waiting for transfers between devices, per_device(): lax.all_gather(w_out, 'fsdp', axis=0, tiled=True)  82 us
    all_to_all x1, waiting for transfers between devices, per_device(): lax.all_to_all(arrived_back, 'seq', split_axis=0, concat_axis=0, tiled=True)  78.3 us
    all_to_all x1, waiting for transfers between devices, per_device(): lax.all_to_all(send_grad, 'seq', split_axis=0, concat_axis=0, tiled=True)  64.8 us
    psum x1, blocking collectives, per_device(): lax.psum(reduced[0].astype(jnp.bfloat16), 'seq').astype(jnp.float32)  63.9 us
  transfers between devices with their start and end apart: 25, of which 19 were waited for; matrix products, arithmetic and copies ran while one was open for 12% of the time, Pallas kernels for 0%

commit v1 on v0

v1 whole, which is shorter than its diff:
```python
import functools
import math

import jax
import jax.numpy as jnp
from jax import lax
from jax.experimental import pallas as pl
from jax.experimental.pallas import tpu as pltpu
from jax.sharding import PartitionSpec as P

EPSILON = 1e-06
THETA = 1000000.0
BF16 = jnp.bfloat16
F32 = jnp.float32
MESH = pl.DeviceIdType.MESH
MIB = 1 << 20
LOG2E = math.log2(math.e)


def ring_of(chip, chips):
    return (chip % 2) * (chips - 1 - chip // 2) + (1 - chip % 2) * (chip // 2)


def chip_of(position, chips):
    upper = position // (chips // 2)
    return (1 - upper) * (2 * position) + upper * (2 * (chips - 1 - position) + 1)


def places(count):
    me = lax.axis_index("seq")
    chips = count // 2
    lane = me % 2
    position = ring_of(me // 2, chips)
    step = 1 - 2 * lane
    following = chip_of((position + step + chips) % chips, chips) * 2 + lane
    previous = chip_of((position - step + chips) % chips, chips) * 2 + lane
    sibling = me + 1 - 2 * lane
    return me, chips, lane, position, step, following, previous, sibling


def greet(senders):
    barrier = pltpu.get_barrier_semaphore()
    for device in senders:
        pl.semaphore_signal(barrier, inc=1, device_id={"seq": device}, device_id_type=MESH)
    pl.semaphore_wait(barrier, len(senders))


def gather_kernel(count, cuts, x_ref, o_ref, own_sem, ring_out, ring_in, side_out, side_in):
    me, chips, lane, position, step, following, previous, sibling = places(count)
    rows = x_ref.shape[0] // cuts
    greet((previous, sibling))

    def hop(src, owner, s, c, device, out_sem, in_sem):
        return pltpu.make_async_remote_copy(
            src_ref=src,
            dst_ref=o_ref.at[owner, pl.ds(c * rows, rows)],
            send_sem=out_sem.at[s, c],
            recv_sem=in_sem.at[s, c],
            device_id={"seq": device},
            device_id_type=MESH,
        )

    def ring(src, owner, s, c):
        return hop(src, owner, s, c, following, ring_out, ring_in)

    def side(src, owner, s, c):
        return hop(src, owner, s, c, sibling, side_out, side_in)

    own = pltpu.make_async_copy(x_ref, o_ref.at[me], own_sem)
    own.start()
    for c in range(cuts):
        src = x_ref.at[pl.ds(c * rows, rows)]
        ring(src, me, 0, c).start()
        side(src, me, 0, c).start()
    for s in range(1, chips):
        owner = chip_of((position - s * step + chips) % chips, chips) * 2 + lane
        for c in range(cuts):
            src = o_ref.at[owner, pl.ds(c * rows, rows)]
            ring(src, owner, s - 1, c).wait_recv()
            if s < chips - 1:
                ring(src, owner, s, c).start()
            side(src, owner, s, c).start()
    for s in range(chips):
        for c in range(cuts):
            src = x_ref.at[pl.ds(c * rows, rows)]
            side(src, me, s, c).wait()
            if s < chips - 1:
                ring(src, me, s, c).wait_send()
    own.wait()


def gather_seq(x, count, call, cuts=4):
    chips = count // 2
    return pl.pallas_call(
        functools.partial(gather_kernel, count, cuts),
        out_shape=jax.ShapeDtypeStruct((count,) + x.shape, x.dtype),
        in_specs=[pl.BlockSpec(memory_space=pl.ANY)],
        out_specs=pl.BlockSpec(memory_space=pl.ANY),
        scratch_shapes=[pltpu.SemaphoreType.DMA]
        + [pltpu.SemaphoreType.DMA((chips, cuts))] * 4,
        compiler_params=pltpu.CompilerParams(collective_id=call, has_side_effects=True),
    )(x)


def scatter_kernel(
    count, cuts, p_ref, o_ref, own, sent, came, given, own_sem, ring_out, ring_in, side_out, side_in
):
    me, chips, lane, position, step, following, previous, sibling = places(count)
    rows = p_ref.shape[1] // cuts
    greet((previous, sibling))

    def my_block(k):
        return chip_of((position - (k + 1) * step + 2 * chips) % chips, chips) * 2 + lane

    def sibling_block(k):
        return chip_of((position + (k + 1) * step + 2 * chips) % chips, chips) * 2 + 1 - lane

    def ring(k, c):
        return pltpu.make_async_remote_copy(
            src_ref=sent.at[k, pl.ds(c * rows, rows)],
            dst_ref=came.at[k, pl.ds(c * rows, rows)],
            send_sem=ring_out.at[k, c],
            recv_sem=ring_in.at[k, c],
            device_id={"seq": following},
            device_id_type=MESH,
        )

    def side(k):
        return pltpu.make_async_remote_copy(
            src_ref=p_ref.at[sibling_block(k)],
            dst_ref=given.at[k],
            send_sem=side_out.at[k],
            recv_sem=side_in.at[k],
            device_id={"seq": sibling},
            device_id_type=MESH,
        )

    def load(k):
        return pltpu.make_async_copy(p_ref.at[my_block(k)], own.at[k], own_sem.at[k])

    for k in range(chips):
        side(k).start()
        load(k).start()
    for k in range(chips):
        load(k).wait()
        side(k).wait_recv()
        for c in range(cuts):
            part = pl.ds(c * rows, rows)
            total = own[k, part].astype(F32) + given[k, part].astype(F32)
            if k > 0:
                ring(k - 1, c).wait_recv()
                total = total + came[k - 1, part].astype(F32)
            if k < chips - 1:
                sent[k, part] = total.astype(BF16)
                ring(k, c).start()
            else:
                o_ref[part] = total
    for k in range(chips):
        side(k).wait_send()
        if k < chips - 1:
            for c in range(cuts):
                ring(k, c).wait_send()


def scatter_seq(p, count, call, cuts=2):
    chips = count // 2
    _, rows, columns = p.shape
    return pl.pallas_call(
        functools.partial(scatter_kernel, count, cuts),
        out_shape=jax.ShapeDtypeStruct((rows, columns), F32),
        in_specs=[pl.BlockSpec(memory_space=pl.ANY)],
        out_specs=pl.BlockSpec(memory_space=pltpu.VMEM),
        scratch_shapes=[
            pltpu.VMEM((chips, rows, columns), BF16),
            pltpu.VMEM((chips - 1, rows, columns), BF16),
            pltpu.VMEM((chips - 1, rows, columns), BF16),
            pltpu.VMEM((chips, rows, columns), BF16),
            pltpu.SemaphoreType.DMA((chips,)),
            pltpu.SemaphoreType.DMA((chips, cuts)),
            pltpu.SemaphoreType.DMA((chips, cuts)),
            pltpu.SemaphoreType.DMA((chips,)),
            pltpu.SemaphoreType.DMA((chips,)),
        ],
        compiler_params=pltpu.CompilerParams(
            collective_id=call, has_side_effects=True, vmem_limit_bytes=48 * MIB
        ),
    )(p)


NT = (((1,), (1,)), ((), ()))
TN = (((0,), (0,)), ((), ()))


def attend_kernel(heads, tile, q_ref, k_ref, v_ref, start_ref, o_ref, total_ref):
    span = q_ref.shape[0]
    width = k_ref.shape[1]
    for i in range(span // tile):
        rows = pl.ds(i * tile, tile)
        start = start_ref[rows, :]
        row = i * tile + lax.broadcasted_iota(jnp.int32, (tile, tile), 0)
        for h in range(heads):
            cols = pl.ds(h * width, width)
            q = q_ref[rows, cols]
            total = jnp.zeros((tile, 2 * width), F32)
            for j in range(i + 1):
                keys = pl.ds(j * tile, tile)
                s = lax.dot_general(q, k_ref[keys, :], NT, preferred_element_type=F32)
                col = j * tile + lax.broadcasted_iota(jnp.int32, (tile, tile), 1)
                keep = col >= start
                if i == j:
                    keep = keep & (col <= row)
                p = jnp.where(keep, jnp.exp2(s), 0.0).astype(BF16)
                total = total + jnp.dot(p, v_ref[keys, :], preferred_element_type=F32)
            weight = total[:, width:]
            o_ref[rows, cols] = (total[:, :width] / weight).astype(BF16)
            total_ref[rows, cols] = jnp.log2(weight)


def attend(q, k, v, start, tile=512):
    span, width = k.shape
    heads = q.shape[1] // width
    vx = jnp.concatenate([v, jnp.ones_like(v)], axis=1)
    return pl.pallas_call(
        functools.partial(attend_kernel, heads, min(tile, span)),
        out_shape=(
            jax.ShapeDtypeStruct((span, heads * width), BF16),
            jax.ShapeDtypeStruct((span, heads * width), F32),
        ),
        in_specs=[pl.BlockSpec(memory_space=pltpu.VMEM)] * 4,
        out_specs=[pl.BlockSpec(memory_space=pltpu.VMEM)] * 2,
        compiler_params=pltpu.CompilerParams(vmem_limit_bytes=48 * MIB),
    )(q, k, vx, start[:, None])


def attend_back_kernel(
    heads, tile, q_ref, k_ref, v_ref, g_ref, start_ref, dq_ref, dk_ref, dv_ref
):
    span = q_ref.shape[0]
    width = k_ref.shape[1] // 2
    dq_ref[...] = jnp.zeros_like(dq_ref)
    for j in range(span // tile):
        keys = pl.ds(j * tile, tile)
        kx = k_ref[keys, :]
        vx = v_ref[keys, :]
        dk = jnp.zeros((tile, width), F32)
        dv = jnp.zeros((tile, width), F32)
        key = j * tile + lax.broadcasted_iota(jnp.int32, (tile, tile), 0)
        for i in range(j, span // tile):
            rows = pl.ds(i * tile, tile)
            keep = key >= start_ref[:, rows]
            if i == j:
                row = i * tile + lax.broadcasted_iota(jnp.int32, (tile, tile), 1)
                keep = keep & (key <= row)
            for h in range(heads):
                qx = q_ref[rows, pl.ds(2 * h * width, 2 * width)]
                gx = g_ref[rows, pl.ds(2 * h * width, 2 * width)]
                s = lax.dot_general(kx, qx, NT, preferred_element_type=F32)
                p = jnp.where(keep, jnp.exp2(s), 0.0)
                dp = lax.dot_general(vx, gx, NT, preferred_element_type=F32)
                ds = (p * dp).astype(BF16)
                dv = dv + jnp.dot(p.astype(BF16), gx[:, :width], preferred_element_type=F32)
                dk = dk + jnp.dot(ds, qx[:, :width], preferred_element_type=F32)
                dq_ref[rows, pl.ds(h * width, width)] += lax.dot_general(
                    ds, kx[:, :width], TN, preferred_element_type=F32
                )
        dk_ref[keys, :] = dk
        dv_ref[keys, :] = dv


def attend_back(qx, kx, vx, gx, start, tile=512):
    span = qx.shape[0]
    width = kx.shape[1] // 2
    heads = qx.shape[1] // (2 * width)
    return pl.pallas_call(
        functools.partial(attend_back_kernel, heads, min(tile, span)),
        out_shape=(
            jax.ShapeDtypeStruct((span, heads * width), F32),
            jax.ShapeDtypeStruct((span, width), F32),
            jax.ShapeDtypeStruct((span, width), F32),
        ),
        in_specs=[pl.BlockSpec(memory_space=pltpu.VMEM)] * 5,
        out_specs=[pl.BlockSpec(memory_space=pltpu.VMEM)] * 3,
        compiler_params=pltpu.CompilerParams(vmem_limit_bytes=56 * MIB),
    )(qx, kx, vx, gx, start[None, :])


def split3(x):
    first = x.astype(BF16)
    rest = x - first.astype(F32)
    second = rest.astype(BF16)
    return first, second, (rest - second.astype(F32)).astype(BF16)


def norm_rows(values, scaling):
    return values * lax.rsqrt(jnp.mean(values * values, axis=-1, keepdims=True) + EPSILON) * scaling


def rotate(values, cosine, sine):
    half = values.shape[-1] // 2
    first = values[..., :half]
    second = values[..., half:]
    return jnp.concatenate([first * cosine - second * sine, second * cosine + first * sine], axis=-1)


def run_starts(segment):
    position = jnp.arange(segment.shape[0], dtype=jnp.int32)
    fresh = jnp.concatenate([jnp.ones((1,), dtype=bool), segment[1:] != segment[:-1]])
    return position, lax.cummax(jnp.where(fresh, position, jnp.zeros_like(position)), axis=0)


def angles(offset, head_size):
    frequency = jnp.exp(
        jnp.arange(head_size // 2, dtype=F32) * (-2.0 * math.log(THETA) / head_size)
    )
    phases = offset[:, None] * frequency[None, :]
    return jnp.cos(phases), jnp.sin(phases)


def dot(a, b, dims=(((1,), (0,)), ((), ()))):
    return lax.dot_general(a, b, dims, preferred_element_type=F32)


def per_device(
    activations,
    cotangent,
    segments,
    routing,
    attn_gain,
    mlp_gain,
    query_gain,
    key_gain,
    w_query,
    key_weight,
    value_weight,
    w_out,
    w_router,
    w_gate,
    w_up,
    w_down,
):
    count = lax.axis_size("seq")
    shards = lax.axis_size("fsdp")
    me = lax.axis_index("seq")
    chips = count // 2
    x = activations[0].astype(F32)
    dy = cotangent[0]
    segment = segments[0]
    routes = routing[0]
    tok, dim = x.shape
    span = segment.shape[0]
    top = routes.shape[1]
    hd = query_gain.shape[0] * shards
    heads = w_query.shape[1] // hd
    kv_heads = key_weight.shape[1] // hd
    share = heads // count
    experts = w_router.shape[1]
    local_rows = w_out.shape[0]
    capacity = tok * top * 9 // (8 * experts)
    group = (me % 2) * chips + me // 2
    gcols = share * hd
    kv_head = group * share // (heads // kv_heads)

    small = jnp.concatenate(
        [attn_gain, mlp_gain, query_gain, key_gain, w_router.reshape(-1)], axis=0
    )
    small = lax.all_gather(small, "fsdp", axis=0, tiled=False)
    local_dim = attn_gain.shape[0]
    local_hd = query_gain.shape[0]
    cut = [local_dim, 2 * local_dim, 2 * local_dim + local_hd, 2 * local_dim + 2 * local_hd]
    g_attn, g_mlp, g_query, g_key, router = jnp.split(small, cut, axis=1)
    g_attn = g_attn.reshape(-1).astype(F32)
    g_mlp = g_mlp.reshape(-1).astype(F32)
    g_query = g_query.reshape(-1).astype(F32)
    g_key = g_key.reshape(-1).astype(F32)
    router = router.reshape(dim, experts)
    qkv_local = jnp.concatenate(
        [
            lax.dynamic_slice_in_dim(w_query, group * gcols, gcols, 1),
            lax.dynamic_slice_in_dim(key_weight, kv_head * hd, hd, 1),
            lax.dynamic_slice_in_dim(value_weight, kv_head * hd, hd, 1),
        ],
        axis=1,
    )
    w_qkv = lax.all_gather(qkv_local, "fsdp", axis=0, tiled=True)
    first_row = group * gcols
    out_owner = first_row // local_rows
    out_local = lax.dynamic_slice_in_dim(w_out, first_row % local_rows, gcols, 0)
    w_o = lax.dynamic_index_in_dim(
        lax.all_gather(out_local, "fsdp", axis=0, tiled=False), out_owner, 0, keepdims=False
    )
    wg = lax.all_gather(w_gate[0], "fsdp", axis=0, tiled=True)
    wu = lax.all_gather(w_up[0], "fsdp", axis=0, tiled=True)
    wd = lax.all_gather(w_down[0], "fsdp", axis=1, tiled=True)
    routes_all = lax.all_gather(routes, "seq", axis=0, tiled=False)

    r1 = lax.rsqrt(jnp.mean(x * x, axis=-1, keepdims=True) + EPSILON)
    h1 = (x * r1 * g_attn).astype(BF16)
    h1_all = gather_seq(h1, count, 1).reshape(span, dim)
    qkv = dot(h1_all, w_qkv).astype(BF16)
    position, doc_start = run_starts(segment)
    cosine, sine = angles((position - doc_start).astype(F32), hd)
    start = jnp.where(segment > 0, doc_start, position)

    def prep_query(raw, scaling):
        return rotate(norm_rows(raw, scaling), cosine[:, None], sine[:, None])

    def prep_key(raw, scaling):
        return rotate(norm_rows(raw, scaling), cosine, sine)

    q_raw = qkv[:, :gcols].reshape(span, share, hd).astype(F32)
    k_raw = qkv[:, gcols : gcols + hd].astype(F32)
    v = qkv[:, gcols + hd :]
    q_rot, query_pullback = jax.vjp(prep_query, q_raw, g_query)
    k_rot, key_pullback = jax.vjp(prep_key, k_raw, g_key)
    scale = hd**-0.5
    qs = (q_rot * (scale * LOG2E)).astype(BF16)
    kn = k_rot.astype(BF16)
    o, weight = attend(qs.reshape(span, gcols), kn, v, start)
    x2_parts = dot(o, w_o).astype(BF16).reshape(count, tok, dim)
    x2 = x + scatter_seq(x2_parts, count, 2)

    r2 = lax.rsqrt(jnp.mean(x2 * x2, axis=-1, keepdims=True) + EPSILON)
    h2 = (x2 * r2 * g_mlp).astype(BF16)
    h2_all = gather_seq(h2, count, 3)
    dy_all = gather_seq(dy, count, 4)

    def gates_of(hidden, chosen):
        logits = dot(hidden, router)
        return jax.nn.softmax(jnp.where(chosen, logits, -1e30), axis=-1) * chosen

    def chosen_of(named):
        names = jnp.arange(experts, dtype=jnp.int32)
        return jnp.any(named[..., :, None] == names, axis=-2)

    hit = jnp.any(routes_all == me, axis=-1)
    rank = jnp.cumsum(hit.astype(jnp.int32), axis=1) - hit
    slots = jnp.arange(capacity, dtype=jnp.int32)
    pick = hit[:, None, :] & (rank[:, None, :] == slots[None, :, None])
    one_hot = pick.astype(BF16)
    gates_all = gates_of(h2_all.reshape(span, dim), chosen_of(routes_all.reshape(span, top)))
    gate_tok = lax.dynamic_index_in_dim(gates_all, me, 1, keepdims=False).reshape(count, tok)
    gate_slot = jnp.sum(jnp.where(pick, gate_tok[:, None, :], 0.0), axis=-1).reshape(-1, 1)

    def to_slots(rows):
        return (
            jnp.einsum("bri,bid->brd", one_hot, rows, preferred_element_type=F32)
            .astype(BF16)
            .reshape(count * capacity, dim)
        )

    def to_tokens(rows):
        return jnp.einsum(
            "bri,brd->bid",
            one_hot,
            rows.reshape(count, capacity, dim),
            preferred_element_type=F32,
        )

    xs = to_slots(h2_all)
    dys = to_slots(dy_all)
    gate_act = dot(xs, wg)
    up_act = dot(xs, wu)
    sig = jax.nn.sigmoid(gate_act)
    silu = gate_act * sig
    inner = (silu * up_act).astype(BF16)
    e_out = dot(inner, wd)
    mixed_parts = to_tokens((gate_slot * e_out).astype(BF16)).astype(BF16)
    mixed = x2 + scatter_seq(mixed_parts, count, 5)

    dgate_slot = jnp.sum(dys.astype(F32) * e_out, axis=-1).reshape(count, capacity)
    dgate_tok = jnp.sum(jnp.where(pick, dgate_slot[:, :, None], 0.0), axis=1)
    de = (gate_slot * dys.astype(F32)).astype(BF16)
    dinner = dot(de, wd, NT)
    dg = (dinner * up_act * (sig + silu * (1.0 - sig))).astype(BF16)
    du = (dinner * silu).astype(BF16)
    w_down_part = dot(inner, de, TN)
    w_gate_part = dot(xs, dg, TN)
    w_up_part = dot(xs, du, TN)
    dxs = (dot(dg, wg, NT) + dot(du, wu, NT)).astype(BF16)
    own_lane = (jnp.arange(128, dtype=jnp.int32) == me)[None, None, :]
    dgate_hi, dgate_lo, _ = split3(dgate_tok[:, :, None])
    zero = jnp.zeros((), BF16)
    lanes = jnp.where(own_lane, dgate_hi, zero) + jnp.where(
        jnp.roll(own_lane, 64, axis=-1), dgate_lo, zero
    )
    dh2_parts = jnp.concatenate([to_tokens(dxs).astype(BF16), lanes], axis=2)
    dh2_wide = scatter_seq(dh2_parts, count, 6)
    dgate = dh2_wide[:, dim : dim + experts] + dh2_wide[:, dim + 64 : dim + 64 + experts]
    gates = gates_of(h2, chosen_of(routes))
    dlogits = (gates * (dgate - jnp.sum(gates * dgate, axis=-1, keepdims=True))).astype(BF16)
    dh2 = dh2_wide[:, :dim] + dot(dlogits, router, NT)
    router_part = dot(h2, dlogits, TN)
    xh = x2 * r2
    mlp_gain_part = jnp.sum(dh2 * xh, axis=0)
    dn = dh2 * g_mlp
    dx2 = dy.astype(F32) + r2 * (dn - xh * jnp.mean(dn * xh, axis=-1, keepdims=True))

    da_all = gather_seq(dx2.astype(BF16), count, 7).reshape(span, dim)
    do = dot(da_all, w_o, NT).astype(BF16)
    w_out_part = dot(o, da_all, TN).astype(BF16)
    do_h = do.reshape(span, share, hd)
    inner_sum = jnp.sum(
        do_h.astype(F32) * o.reshape(span, share, hd).astype(F32), axis=-1, keepdims=True
    )

    def widen(values, extra):
        cols = list(split3(extra))
        pad = jnp.zeros(values.shape[:-1] + (hd - len(cols),), BF16)
        return jnp.concatenate([values] + cols + [pad], axis=-1)

    qx = widen(qs, -weight.reshape(span, share, hd)[:, :, :1]).reshape(span, 2 * gcols)
    gx = widen(do_h, -inner_sum).reshape(span, 2 * gcols)
    ones = jnp.ones_like(kn)
    dq_rot, dk_rot, dv = attend_back(
        qx, jnp.concatenate([kn, ones], axis=1), jnp.concatenate([v, ones], axis=1), gx, start
    )
    dq, query_gain_part = query_pullback(dq_rot.reshape(span, share, hd) * scale)
    dk, key_gain_part = key_pullback(dk_rot * (1.0 / LOG2E))
    dqkv = jnp.concatenate(
        [dq.reshape(span, gcols).astype(BF16), dk.astype(BF16), dv.astype(BF16)], axis=1
    )
    qkv_part = dot(h1_all, dqkv, TN).astype(BF16)
    dh1 = scatter_seq(dot(dqkv, w_qkv, NT).astype(BF16).reshape(count, tok, dim), count, 8)
    xh1 = x * r1
    dn1 = dh1 * g_attn
    input_grad = dx2 + r1 * (dn1 - xh1 * jnp.mean(dn1 * xh1, axis=-1, keepdims=True))

    def sum_fsdp(part, axis):
        return lax.psum_scatter(part.astype(BF16), "fsdp", scatter_dimension=axis, tiled=True)

    w_gate_grad = sum_fsdp(w_gate_part, 0).astype(F32)
    w_up_grad = sum_fsdp(w_up_part, 0).astype(F32)
    w_down_grad = sum_fsdp(w_down_part, 1).astype(F32)

    small_part = jnp.concatenate(
        [
            router_part.reshape(shards, -1),
            mlp_gain_part.reshape(shards, -1),
            query_gain_part.reshape(shards, -1),
            key_gain_part.reshape(shards, -1),
        ],
        axis=1,
    )
    small_sum = lax.psum(sum_fsdp(small_part, 0), "seq").astype(F32)[0]
    router_grad, mlp_gain_grad, query_gain_grad, key_gain_grad = jnp.split(
        small_sum,
        [local_dim * experts, local_dim * (experts + 1), local_dim * (experts + 1) + local_hd],
    )
    router_grad = router_grad.reshape(local_dim, experts)

    out_sum = jnp.sum(
        lax.all_gather(w_out_part, "fsdp", axis=0, tiled=False).astype(F32), axis=0
    ).astype(BF16)
    pair = lax.all_gather(
        out_sum,
        "seq",
        axis=0,
        tiled=False,
        axis_index_groups=[[2 * c, 2 * c + 1] for c in range(chips)],
    )
    w_out_grad = out_rows(pair, out_sum, count, shards, tok)

    qkv_sum = sum_fsdp(qkv_part, 0)
    qkv_all = gather_seq(qkv_sum, count, 10)
    order = [(g % chips) * 2 + g // chips for g in range(count)]
    qkv_groups = qkv_all[jnp.array(order)].astype(F32)
    w_query_grad = jnp.swapaxes(qkv_groups[:, :, :gcols], 0, 1).reshape(local_dim, heads * hd)
    kv_groups = qkv_groups[:, :, gcols:].reshape(kv_heads, count // kv_heads, local_dim, 2 * hd)
    kv_groups = jnp.swapaxes(jnp.sum(kv_groups, axis=1), 0, 1)
    w_key_grad = kv_groups[:, :, :hd].reshape(local_dim, kv_heads * hd)
    w_value_grad = kv_groups[:, :, hd:].reshape(local_dim, kv_heads * hd)
    attn_gain_grad = (
        jnp.sum(w_query.astype(F32) * w_query_grad, axis=1)
        + jnp.sum(key_weight.astype(F32) * w_key_grad, axis=1)
        + jnp.sum(value_weight.astype(F32) * w_value_grad, axis=1)
    ) / attn_gain.astype(F32)
    return (
        mixed.astype(BF16)[None],
        input_grad[None],
        attn_gain_grad,
        mlp_gain_grad,
        query_gain_grad,
        key_gain_grad,
        w_query_grad,
        w_key_grad,
        w_value_grad,
        w_out_grad,
        router_grad,
        w_gate_grad[None],
        w_up_grad[None],
        w_down_grad[None],
    )


def out_rows(pair, out_sum, count, shards, tok):
    chips = count // 2
    gcols, dim = out_sum.shape
    me = lax.axis_index("seq")
    mine = lax.axis_index("fsdp")
    if shards == 2:
        half = lax.dynamic_slice(
            pair, (mine, (me % 2) * (gcols // 2), 0), (1, gcols // 2, dim)
        )[0]
        return gather_seq(half, count, 9).reshape(chips * gcols, dim).astype(F32)
    groups = count // shards
    first = mine * groups
    group = (me % 2) * chips + me // 2
    place = jnp.clip(group - first, 0, groups - 1)
    keep = (group >= first) & (group < first + groups)
    rows = jnp.where(keep, out_sum, jnp.zeros_like(out_sum))
    blank = jnp.zeros((groups * gcols, dim), BF16)
    return lax.psum(lax.dynamic_update_slice(blank, rows, (place * gcols, 0)), "seq").astype(F32)


def solution(mesh):
    tokens = P("fsdp", "seq", None)
    rows = P("fsdp", None)
    vector = P("fsdp")
    expert_rows = P("seq", "fsdp", None)
    expert_columns = P("seq", None, "fsdp")
    return jax.shard_map(
        per_device,
        mesh=mesh,
        in_specs=(tokens, tokens, rows, tokens)
        + (vector,) * 4
        + (rows,) * 5
        + (expert_rows, expert_rows, expert_columns),
        out_specs=(tokens, tokens)
        + (vector,) * 4
        + (rows,) * 5
        + (expert_rows, expert_rows, expert_columns),
        check_vma=False,
    )
```

time: 2240 us -> 1170 us (0.52)
  waiting for transfers between devices: 1400 us -> 14.8 us
  Pallas kernels: 0 us -> 524 us
  matrix products: 265 us -> 153 us
  starting transfers between devices: 99.6 us -> 0.7 us
  local copies, waits for them, and re-layouts: 104 us -> 194 us
  blocking collectives: 158 us -> 88.9 us
    pallas_call x0 -> x12, Pallas kernels: none -> 524 us  [the longest x6 314 us: gather_seq(): pl.pallas_call(functools.partial(gather_kernel, count, cuts), out_shape=j...]
    reduce_scatter x8 -> x4, waiting for transfers between devices: 458 us -> 0.01 us  [sum_fsdp(): lax.psum_scatter(part.astype(BF16), 'fsdp', scatter_dimension=axis, tiled...]
    all_gather x7, waiting for transfers between devices: 435 us -> 12.8 us  [the longest x1 12.8 us: per_device(): lax.all_gather(w_out_part, 'fsdp', axis=0, tiled=False).astype(F32)]
    psum x1 -> x0, waiting for transfers between devices: 257 us -> none  [per_device(): lax.psum(reduced[4].astype(jnp.bfloat16), 'seq').astype(jnp.float32)]
    all_to_all x9 -> x0, waiting for transfers between devices: 244 us -> none  [the longest x1 78.3 us: per_device(): lax.all_to_all(arrived_back, 'seq', split_axis=0, concat_axis=0, tiled=True)]
    dot_general x55 -> x23, matrix products: 265 us -> 153 us  [the longest x19 130 us: dot(): return lax.dot_general(a, b, dims, preferred_element_type=F32)]
    all_to_all x9 -> x0, starting transfers between devices: 98.3 us -> none  [the longest x1 22 us: per_device(): lax.all_to_all(expert_out, 'seq', split_axis=0, concat_axis=0, tiled=True)]
    all_to_all x3 -> x0, blocking collectives: 68.2 us -> none  [the longest x1 28.7 us: per_device(): lax.all_to_all(head_query_grad.astype(jnp.bfloat16), 'seq', split_axis=0,...]
  transfers between devices with their start and end apart: 25 -> 12, of which waited for: 19 -> 1; matrix products, arithmetic and copies ran while one was open for 12% -> 30% of each run, Pallas kernels for 0% -> 36%
where the time goes in v1:
time: 1170 us; the launch traced here: 1160 us
  Pallas kernels  524 us (45%)
  local copies, waits for them, and re-layouts  194 us (17%)
  other arithmetic  164 us (14%)
  matrix products  153 us (13%)
  blocking collectives  88.9 us (8%)
  between operations  15.8 us (1%)
  waiting for transfers between devices  14.8 us (1%)
    pallas_call x6, Pallas kernels, gather_seq(): pl.pallas_call(functools.partial(gather_kernel, count, cuts), out_shape=j...  314 us
    pallas_call x4, Pallas kernels, scatter_seq(): pl.pallas_call(functools.partial(scatter_kernel, count, cuts), out_shape=...  183 us
    dot_general x19, matrix products, dot(): return lax.dot_general(a, b, dims, preferred_element_type=F32)  130 us
    psum x1, blocking collectives, per_device(): small_sum = lax.psum(sum_fsdp(small_part, 0), 'seq').astype(F32)[0]  61 us
    unnamed x154, local copies, waits for them, and re-layouts  58.4 us
    concatenate x2, local copies, waits for them, and re-layouts, widen(): return jnp.concatenate([values] + cols + [pad], axis=-1)  39.7 us
    transpose x2, local copies, waits for them, and re-layouts, per_device(): jnp.swapaxes(qkv_groups[:, :, :gcols], 0, 1).reshape(local_dim, heads * hd)  29.2 us
  transfers between devices with their start and end apart: 12, of which 1 were waited for; matrix products, arithmetic and copies ran while one was open for 30% of the time, Pallas kernels for 36%

profile of v1, /device:TPU:0, one launch (start us, length us, event | category | flops | bytes accessed | tf_op | source)
XLA Modules:
  0.0 1155.6 jit_solution(3769053457468450943)
XLA Ops:
  23.1 45.7 %shard_map.272 = bf16[16,128,2048]{2,1,0:T(8,128)(2,1)} custom-call(bf16[128,2048]{1,0:T(8,128)(2,1)} %fusion.30.x_ref), custom_call_target="tpu_custom_call" | custom-call | tf_op jit(solution)/shard_map/pallas_call | solution.py:94
  70.6 46.1 %shard_map.277 = bf16[16,128,2048]{2,1,0:T(8,128)(2,1)} custom-call(bf16[128,2048]{1,0:T(8,128)(2,1)} %bitcast.203), custom_call_target="tpu_custom_call" | custom-call | tf_op jit(solution)/shard_map/pallas_call | solution.py:94
  116.7 22.0 %all_gather.44 = s32[16,128,8]{1,2,0:T(8,128)S(1)} all-gather(s32[1,128,8]{1,2,0:T(8,128)S(1)} %copy-done.44), channel_id=1, replica_groups=mesh['fsdp'=2,'seq'=16] {'seq'}, dimensions={0}, use_global_device_ids=true | all-gather | bytes 69632 | tf_op jit(solution)/shard_map/all_gather | solution.py:394
  211.3 19.9 %concatenate.54 = bf16[2048,2,256]{2,1,0:T(2,128)(2,1)} concatenate(bf16[2048,2,128]{2,1,0:T(2,128)(2,1)S(1)} %copy-done.16, bf16[2048,2,1]{2,1,0:T(2,128)(2,1)} %copy.159, bf16[2048,2,1]{2,1,0:T(2,128)(2,1)} %copy.160, bf16[2048,2,1]{2,1,0:T(2,128)(2,1)} %copy.161, bf16[2048,2,125]{2,1,0:T(2,128)(2,1)S(1)} %broadcast.211), dimensions={2} | concatenate | bytes 4194304 | tf_op jit(solution)/shard_map/concatenate | solution.py:509
  243.8 44.6 %shard_map.274 = f32[128,2048]{1,0:T(8,128)S(1)} custom-call(bf16[16,128,2048]{2,1,0:T(8,128)(2,1)} %bitcast.182), custom_call_target="tpu_custom_call" | custom-call | tf_op jit(solution)/shard_map/pallas_call | solution.py:168
  289.6 45.7 %shard_map.275 = bf16[16,128,2048]{2,1,0:T(8,128)(2,1)} custom-call(bf16[128,2048]{1,0:T(8,128)(2,1)} %multiply_convert_fusion.4.x_ref), custom_call_target="tpu_custom_call" | custom-call | tf_op jit(solution)/shard_map/pallas_call | solution.py:94
  377.8 11.7 %fusion = (bf16[1152,2048]{1,0:T(8,128)(2,1)}, bf16[1152,2048]{1,0:T(8,128)(2,1)}) fusion(bf16[16,72,2048]{2,1,0:T(8,128)(2,1)} %convolution_convert_fusion.4, f32[1152]{0:T(1024)S(1)} %mul.456, f32[1152,2048]{1,0:T(8,128)} %get-tuple-element.158), kind=kLoop, calls=%fused_computation.6 | loop fusion | flops 11796480 | bytes 23597568 | tf_op jit(solution)/shard_map/convert_element_type | solution.py:472
  389.5 11.6 %multiply_convert_fusion.1 = (bf16[1152,768]{1,0:T(8,128)(2,1)}, bf16[1152,768]{1,0:T(8,128)(2,1)S(1)}) fusion(f32[1152,768]{1,0:T(8,128)} %fusion.11, f32[1152,768]{1,0:T(8,128)} %get-tuple-element.156, bf16[1152,2048]{1,0:T(8,128)(2,1)} %get-tuple-element.151, bf16[1,768,2048]{2,1,0:T(8,128)(2,1)} %all-gather.24.cloned.1.call-done), kind=kOutput, calls=%fused_computation.18 | convolution fusion | flops 3634495488 | bytes 18481152 | tf_op jit(solution)/shard_map/dot_general | solution.py:320
  425.3 47.5 %shard_map.278 = f32[128,2176]{1,0:T(8,128)S(1)} custom-call(bf16[16,128,2176]{2,1,0:T(8,128)(2,1)} %pad_maximum_fusion.p_ref), custom_call_target="tpu_custom_call" | custom-call | tf_op jit(solution)/shard_map/pallas_call | solution.py:168
  475.0 45.7 %shard_map.279 = bf16[16,128,2048]{2,1,0:T(8,128)(2,1)} custom-call(bf16[128,2048]{1,0:T(8,128)(2,1)} %fusion.76.x_ref), custom_call_target="tpu_custom_call" | custom-call | tf_op jit(solution)/shard_map/pallas_call | solution.py:94
  550.8 19.8 %concatenate.56 = bf16[2048,2,256]{2,1,0:T(2,128)(2,1)} concatenate(bf16[2048,2,128]{2,1,0:T(2,128)(2,1)S(1)} %copy.164, bf16[2048,2,1]{2,1,0:T(2,128)(2,1)} %copy.165, bf16[2048,2,1]{2,1,0:T(2,128)(2,1)} %copy.166, bf16[2048,2,1]{2,1,0:T(2,128)(2,1)} %copy.167, bf16[2048,2,125]{2,1,0:T(2,128)(2,1)S(1)} %copy-done.14), dimensions={2} | concatenate | bytes 4194304 | tf_op jit(solution)/shard_map/concatenate | solution.py:509
  573.9 19.5 %shard_map.280 = (f32[2048,256]{1,0:T(8,128)}, f32[2048,128]{1,0:T(8,128)}, f32[2048,128]{1,0:T(8,128)}) custom-call(bf16[2048,512]{1,0:T(8,128)(2,1)} %bitcast.199, bf16[2048,256]{1,0:T(8,128)(2,1)} %concatenate.55.k_ref, bf16[2048,256]{1,0:T(8,128)(2,1)} %copy-done, bf16[2048,512]{1,0:T(8,128)(2,1)} %bitcast.200, s32[1,2048]{1,0:T(1,128)} %compare_select_fusion.start_ref), custom_call_target="tpu_custom_call" | custom-call | tf_op jit(solution)/shard_map/pallas_call | solution.py:274
  649.1 12.8 %all-gather.26.cloned.1.call-done = bf16[512,2048]{1,0:T(8,128)(2,1)} async-done(((bf16[256,2048]{1,0:T(8,128)(2,1)}), bf16[512,2048]{1,0:T(8,128)(2,1)}) %all-gather.26.cloned.1.call-update) | async-done | bytes 2097168 | tf_op jit(solution)/shard_map/all_gather | solution.py:552
  685.5 12.2 %copy.170 = bf16[1024,4096]{0,1:T(8,128)(2,1)} copy(bf16[1024,4096]{1,0:T(8,128)(2,1)} %param.25) | data formatting | bytes 16777216 | tf_op args[8]
  710.0 46.1 %shard_map.281 = f32[128,2048]{1,0:T(8,128)S(1)} custom-call(bf16[16,128,2048]{2,1,0:T(8,128)(2,1)} %bitcast.196), custom_call_target="tpu_custom_call" | custom-call | tf_op jit(solution)/shard_map/pallas_call | solution.py:168
  761.9 45.0 %shard_map.276 = f32[128,2048]{1,0:T(8,128)S(1)} custom-call(bf16[16,128,2048]{2,1,0:T(8,128)(2,1)} %convolution_convert_fusion.3.p_ref), custom_call_target="tpu_custom_call" | custom-call | tf_op jit(solution)/shard_map/pallas_call | solution.py:168
  816.5 61.0 %psum.7 = bf16[1,17536]{1,0:T(2,128)(2,1)S(1)} all-reduce(bf16[1,17536]{1,0:T(2,128)(2,1)S(1)} %constant_dynamic-slice_fusion.4), channel_id=1, replica_groups=mesh['fsdp'=2,'seq'=16] {'seq'}, use_global_device_ids=true, to_apply=%region_32.33 | all-reduce | flops 17536 | bytes 70144 | tf_op jit(solution)/shard_map/psum | solution.py:544
  880.0 85.2 %shard_map.282 = bf16[16,1024,512]{2,1,0:T(8,128)(2,1)} custom-call(bf16[1024,512]{1,0:T(8,128)(2,1)} %reduce-scatter.5.cloned.1.call-done.x_ref), custom_call_target="tpu_custom_call" | custom-call | tf_op jit(solution)/shard_map/pallas_call | solution.py:94
  965.2 13.1 %gather_fusion = bf16[16,1024,512]{2,1,0:T(8,128)(2,1)} fusion(bf16[16,1024,512]{2,1,0:T(8,128)(2,1)} %shard_map.282, s32[1024]{0:T(1024)S(1)} %pad_clamp_fusion), kind=kCustom, calls=%fused_computation | custom fusion | bytes 33554496 | tf_op jit(solution)/shard_map/gather | solution.py:566
  978.3 18.8 %convert_element_type.392 = f32[16,1024,512]{2,1,0:T(8,128)} convert(bf16[16,1024,512]{2,1,0:T(8,128)(2,1)} %gather_fusion) | non-fusion elementwise | flops 8388608 | bytes 50331648 | tf_op jit(solution)/shard_map/convert_element_type | solution.py:566
  1024.7 17.6 %copy.171 = f32[1024,16,256]{0,2,1:T(8,128)} copy(f32[1024,16,256]{2,0,1:T(8,128)} %slice_bitcast_fusion) | data formatting | bytes 33554432 | tf_op jit(solution)/shard_map/transpose | solution.py:567
  1045.2 17.4 %copy.177 = f32[1024,4096]{1,0:T(8,128)} copy(f32[1024,4096]{0,1:T(8,128)} %bitcast.179) | data formatting | bytes 33554432
  1069.2 45.7 %shard_map.283 = bf16[16,128,2048]{2,1,0:T(8,128)(2,1)} custom-call(bf16[128,2048]{1,0:T(8,128)(2,1)} %dynamic-slice_bitcast_fusion.x_ref), custom_call_target="tpu_custom_call" | custom-call | tf_op jit(solution)/shard_map/pallas_call | solution.py:94
  1126.8 11.7 %bitcast_convert_fusion = f32[2048,2048]{1,0:T(8,128)} fusion(bf16[16,128,2048]{2,1,0:T(8,128)(2,1)} %shard_map.283), kind=kLoop, calls=%fused_computation.11 | loop fusion | flops 4194304 | bytes 25165824 | tf_op jit(solution)/shard_map/convert_element_type | solution.py:604
  (345 shorter events, 373.4 us)
Async XLA Ops:
  7.2 141.1 %all-gather.16.cloned.1.call-start = ((), (), s32[]{:S(2)}) async-start(), calls=%async_computation.4 | async-start | bytes 3145728 | tf_op jit(solution)/shard_map/all_gather | solution.py:384
  10.5 226.3 %all-gather.18.cloned.1.call-start = ((), (), s32[]{:S(2)}) async-start(), calls=%async_computation.9 | async-start | bytes 3145728 | tf_op jit(solution)/shard_map/all_gather | solution.py:389
  13.0 332.4 %all-gather.20.cloned.1.call-start = ((), (), s32[]{:S(2)}) async-start(), calls=%async_computation.10 | async-start | bytes 4718592 | tf_op jit(solution)/shard_map/all_gather | solution.py:391
  13.8 341.1 %all-gather.22.cloned.1.call-start = ((), (), s32[]{:S(2)}) async-start(), calls=%async_computation.11 | async-start | bytes 4718592 | tf_op jit(solution)/shard_map/all_gather | solution.py:392
  14.3 351.3 %all-gather.24.cloned.1.call-start = ((), (), s32[]{:S(2)}) async-start(), calls=%async_computation.12 | async-start | bytes 4718592 | tf_op jit(solution)/shard_map/all_gather | solution.py:393
  14.9 647.0 %all-gather.26.cloned.1.call-start = ((), (), s32[]{:S(2)}) async-start(), calls=%async_computation.13 | async-start | bytes 3145728 | tf_op jit(solution)/shard_map/all_gather | solution.py:552
  21.6 152.9 %copy-start.52 = (f32[64]{0:T(128)}, f32[64]{0:T(128)S(1)}, u32[]{:S(2)}) copy-start(f32[64]{0:T(128)S(1)} %multiply_exponential_fusion) | copy-start | bytes 772
  22.1 46.8 %copy-start.47 = (f32[128]{0:T(128)}, f32[128]{0:T(128)S(1)}, u32[]{:S(2)}) copy-start(f32[128]{0:T(128)S(1)} %add_rsqrt_fusion.1) | copy-start | bytes 1540
  22.1 46.8 %copy-start.34 = (f32[2048]{0:T(1024)}, f32[2048]{0:T(1024)S(1)}, u32[]{:S(2)}) copy-start(f32[2048]{0:T(1024)S(1)} %get-tuple-element.167) | copy-start | bytes 24580
  69.0 105.2 %copy-start.49 = (f32[128]{0:T(128)}, f32[128]{0:T(128)S(1)}, u32[]{:S(2)}) copy-start(f32[128]{0:T(128)S(1)} %reshape.481) | copy-start | bytes 1540
  69.7 104.9 %copy-start.39 = (f32[2048]{0:T(1024)}, f32[2048]{0:T(1024)S(1)}, u32[]{:S(2)}) copy-start(f32[2048]{0:T(1024)S(1)} %get-tuple-element.122) | copy-start | bytes 24580
  70.6 46.1 %copy-start.44 = (s32[1,128,8]{1,2,0:T(8,128)S(1)}, s32[1,128,8]{1,2,0:T(8,128)}, u32[]{:S(2)}) copy-start(s32[1,128,8]{1,2,0:T(8,128)} %param.20) | copy-start | bytes 12292
  425.3 47.9 %copy-start.20 = (bf16[2048,16]{1,0:T(8,128)(2,1)S(1)}, bf16[2048,16]{1,0:T(8,128)(2,1)}, u32[]{:S(2)}) copy-start(bf16[2048,16]{1,0:T(8,128)(2,1)} %reshape.458) | copy-start | bytes 196612
  473.7 47.0 %copy-start.11 = (f32[128,2048]{1,0:T(8,128)}, f32[128,2048]{1,0:T(8,128)S(1)}, u32[]{:S(2)}) copy-start(f32[128,2048]{1,0:T(8,128)S(1)} %get-tuple-element.163) | copy-start | bytes 3145732
  628.7 186.2 %all-reduce.9.cloned.1.call-start = ((), (), s32[]{:S(2)}) async-start(), calls=%async_computation.15 | async-start | bytes 140288
  638.9 241.0 %reduce-scatter.5.cloned.1.call-start = ((), (), s32[]{:S(2)}) async-start(), calls=%async_computation.5 | async-start | bytes 3145728 | tf_op jit(solution)/shard_map/reduce_scatter | solution.py:529
  649.0 418.3 %all-gather.28.cloned.1.call-start = ((), (), s32[]{:S(2)}) async-start(), calls=%async_computation.14 | async-start | bytes 3145728 | tf_op jit(solution)/shard_map/all_gather | solution.py:554
  665.2 473.2 %reduce-scatter.7.cloned.1.call-start = ((), (), s32[]{:S(2)}) async-start(), calls=%async_computation.6 | async-start | bytes 4718592 | tf_op jit(solution)/shard_map/reduce_scatter | solution.py:529
  673.4 468.4 %reduce-scatter.9.cloned.1.call-start = ((), (), s32[]{:S(2)}) async-start(), calls=%async_computation.7 | async-start | bytes 4718592 | tf_op jit(solution)/shard_map/reduce_scatter | solution.py:529
  683.0 462.1 %reduce-scatter.11.cloned.1.call-start = ((), (), s32[]{:S(2)}) async-start(), calls=%async_computation.8 | async-start | bytes 4718592 | tf_op jit(solution)/shard_map/reduce_scatter | solution.py:529
  710.0 46.1 %slice-start = ((s8[4718592]{0:T(1024)(128)(4,1)}), s8[4194304]{0:T(1024)(128)(4,1)S(1)}, s32[]{:S(2)}) async-start(s8[4718592]{0:T(1024)(128)(4,1)} %bitcast.183), calls=%async_computation.16 | async-start | bytes 8388608
  710.0 46.1 %slice-start.1 = ((s8[4718592]{0:T(1024)(128)(4,1)}), s8[524288]{0:T(1024)(128)(4,1)S(1)}, s32[]{:S(2)}) async-start(s8[4718592]{0:T(1024)(128)(4,1)} %bitcast.183), calls=%async_computation.17 | async-start | bytes 1048576
  756.1 53.0 %slice-start.3 = ((s8[4718592]{0:T(1024)(128)(4,1)}), s8[524288]{0:T(1024)(128)(4,1)S(1)}, s32[]{:S(2)}) async-start(s8[4718592]{0:T(1024)(128)(4,1)} %bitcast.204), calls=%async_computation.19 | async-start | bytes 1048576
  761.9 47.2 %slice-start.4 = ((s8[4718592]{0:T(1024)(128)(4,1)}), s8[4194304]{0:T(1024)(128)(4,1)S(1)}, s32[]{:S(2)}) async-start(s8[4718592]{0:T(1024)(128)(4,1)} %bitcast.204), calls=%async_computation.20 | async-start | bytes 8388608
  (57 other events, 702.8 us)
Sparse Core Ops, SparseCore 0:
  10.7 35.8 all-gather.15
  48.0 33.1 all-gather.17
  82.8 44.9 all-gather.19
  129.1 44.9 all-gather.21
  175.5 44.9 all-gather.23
  628.8 33.0 all-gather.25
  664.1 20.1 all-reduce.8
  687.2 32.5 reduce-scatter.4
  721.4 10.5 all-gather.27
  734.7 44.5 reduce-scatter.6
  782.1 43.3 reduce-scatter.8
  827.7 43.3 reduce-scatter.10

commit v2 on v1

--- a/solution.py
+++ b/solution.py
@@ -45,61 +45,78 @@
     pl.semaphore_wait(barrier, len(senders))
 
 
-def gather_kernel(count, cuts, x_ref, o_ref, own_sem, ring_out, ring_in, side_out, side_in):
+def row_parts(rows, cuts):
+    if cuts == 1:
+        return [pl.ds(0, rows)]
+    size = rows // cuts // 16 * 16
+    return [pl.ds(c * size, size) for c in range(cuts - 1)] + [
+        pl.ds((cuts - 1) * size, rows - (cuts - 1) * size)
+    ]
+
+
+def gather_kernel(count, cuts, *refs):
+    arrays = len(cuts)
+    x_refs, o_refs = refs[:arrays], refs[arrays : 2 * arrays]
+    own_sem, ring_out, ring_in, side_out, side_in = refs[2 * arrays :]
     me, chips, lane, position, step, following, previous, sibling = places(count)
-    rows = x_ref.shape[0] // cuts
     greet((previous, sibling))
-
-    def hop(src, owner, s, c, device, out_sem, in_sem):
+    pieces = []
+    for a in range(arrays):
+        pieces += [(x_refs[a], o_refs[a], part) for part in row_parts(x_refs[a].shape[0], cuts[a])]
+
+    def hop(c, owner, s, device, out_sem, in_sem, first):
+        x_ref, o_ref, part = pieces[c]
         return pltpu.make_async_remote_copy(
-            src_ref=src,
-            dst_ref=o_ref.at[owner, pl.ds(c * rows, rows)],
+            src_ref=x_ref.at[part] if first else o_ref.at[owner, part],
+            dst_ref=o_ref.at[owner, part],
             send_sem=out_sem.at[s, c],
             recv_sem=in_sem.at[s, c],
             device_id={"seq": device},
             device_id_type=MESH,
         )
 
-    def ring(src, owner, s, c):
-        return hop(src, owner, s, c, following, ring_out, ring_in)
-
-    def side(src, owner, s, c):
-        return hop(src, owner, s, c, sibling, side_out, side_in)
-
-    own = pltpu.make_async_copy(x_ref, o_ref.at[me], own_sem)
-    own.start()
-    for c in range(cuts):
-        src = x_ref.at[pl.ds(c * rows, rows)]
-        ring(src, me, 0, c).start()
-        side(src, me, 0, c).start()
+    def ring(c, owner, s, first=False):
+        return hop(c, owner, s, following, ring_out, ring_in, first)
+
+    def side(c, owner, s, first=False):
+        return hop(c, owner, s, sibling, side_out, side_in, first)
+
+    own = [
+        pltpu.make_async_copy(x_refs[a], o_refs[a].at[me], own_sem.at[a]) for a in range(arrays)
+    ]
+    for copy in own:
+        copy.start()
+    for c in range(len(pieces)):
+        ring(c, me, 0, True).start()
+        side(c, me, 0, True).start()
     for s in range(1, chips):
         owner = chip_of((position - s * step + chips) % chips, chips) * 2 + lane
-        for c in range(cuts):
-            src = o_ref.at[owner, pl.ds(c * rows, rows)]
-            ring(src, owner, s - 1, c).wait_recv()
+        for c in range(len(pieces)):
+            ring(c, owner, s - 1).wait_recv()
             if s < chips - 1:
-                ring(src, owner, s, c).start()
-            side(src, owner, s, c).start()
+                ring(c, owner, s).start()
+            side(c, owner, s).start()
     for s in range(chips):
-        for c in range(cuts):
-            src = x_ref.at[pl.ds(c * rows, rows)]
-            side(src, me, s, c).wait()
+        for c in range(len(pieces)):
+            side(c, me, s).wait()
             if s < chips - 1:
-                ring(src, me, s, c).wait_send()
-    own.wait()
-
-
-def gather_seq(x, count, call, cuts=4):
+                ring(c, me, s).wait_send()
+    for copy in own:
+        copy.wait()
+
+
+def gather_seq(arrays, count, call, cuts):
     chips = count // 2
+    anywhere = pl.BlockSpec(memory_space=pl.ANY)
     return pl.pallas_call(
         functools.partial(gather_kernel, count, cuts),
-        out_shape=jax.ShapeDtypeStruct((count,) + x.shape, x.dtype),
-        in_specs=[pl.BlockSpec(memory_space=pl.ANY)],
-        out_specs=pl.BlockSpec(memory_space=pl.ANY),
-        scratch_shapes=[pltpu.SemaphoreType.DMA]
-        + [pltpu.SemaphoreType.DMA((chips, cuts))] * 4,
+        out_shape=[jax.ShapeDtypeStruct((count,) + x.shape, x.dtype) for x in arrays],
+        in_specs=[anywhere] * len(arrays),
+        out_specs=[anywhere] * len(arrays),
+        scratch_shapes=[pltpu.SemaphoreType.DMA((len(arrays),))]
+        + [pltpu.SemaphoreType.DMA((chips, sum(cuts)))] * 4,
         compiler_params=pltpu.CompilerParams(collective_id=call, has_side_effects=True),
-    )(x)
+    )(*arrays)
 
 
 def scatter_kernel(
@@ -191,57 +208,139 @@
 TN = (((0,), (0,)), ((), ()))
 
 
-def attend_kernel(heads, tile, q_ref, k_ref, v_ref, start_ref, o_ref, total_ref):
-    span = q_ref.shape[0]
-    width = k_ref.shape[1]
+def split3(x):
+    first = x.astype(BF16)
+    rest = x - first.astype(F32)
+    second = rest.astype(BF16)
+    return first, second, (rest - second.astype(F32)).astype(BF16)
+
+
+def in_lanes(x):
+    lane = lax.broadcasted_iota(jnp.int32, x.shape, 1)
+    first = x.astype(BF16).astype(F32)
+    second = (x - first).astype(BF16).astype(F32)
+    third = x - first - second
+    spread = jnp.where(lane == 0, first, jnp.where(lane == 1, second, third))
+    return jnp.where(lane < 3, spread, 0.0).astype(BF16)
+
+
+def swap_halves(x):
+    half = x.shape[1] // 2
+    return jnp.concatenate([x[:, half:], x[:, :half]], axis=1)
+
+
+def unit_rows(u):
+    r = lax.rsqrt(jnp.mean(u * u, axis=1, keepdims=True) + EPSILON)
+    return r, u * r
+
+
+def attend_kernel(
+    heads, tile, qkv_ref, gq_ref, gk_ref, cos_ref, sin_ref, start_ref, o_ref, qx_ref, kn_ref, vx_ref
+):
+    span = qkv_ref.shape[0]
+    width = kn_ref.shape[1]
+    scale = width**-0.5 * LOG2E
+    for i in range(span // tile):
+        rows = pl.ds(i * tile, tile)
+        cos, sin = cos_ref[rows, :], sin_ref[rows, :]
+        for h in range(heads + 1):
+            _, unit = unit_rows(qkv_ref[rows, pl.ds(h * width, width)].astype(F32))
+            u = unit * (gk_ref[...] if h == heads else gq_ref[...])
+            u = u * cos + swap_halves(u) * sin
+            if h == heads:
+                kn_ref[rows, :] = u.astype(BF16)
+            else:
+                qx_ref[rows, pl.ds(2 * h * width, width)] = (u * scale).astype(BF16)
+        vx_ref[rows, :width] = qkv_ref[rows, pl.ds((heads + 1) * width, width)]
+        vx_ref[rows, width:] = jnp.ones((tile, width), BF16)
     for i in range(span // tile):
         rows = pl.ds(i * tile, tile)
         start = start_ref[rows, :]
         row = i * tile + lax.broadcasted_iota(jnp.int32, (tile, tile), 0)
         for h in range(heads):
-            cols = pl.ds(h * width, width)
-            q = q_ref[rows, cols]
+            q = qx_ref[rows, pl.ds(2 * h * width, width)]
             total = jnp.zeros((tile, 2 * width), F32)
             for j in range(i + 1):
                 keys = pl.ds(j * tile, tile)
-                s = lax.dot_general(q, k_ref[keys, :], NT, preferred_element_type=F32)
+                s = lax.dot_general(q, kn_ref[keys, :], NT, preferred_element_type=F32)
                 col = j * tile + lax.broadcasted_iota(jnp.int32, (tile, tile), 1)
                 keep = col >= start
                 if i == j:
                     keep = keep & (col <= row)
                 p = jnp.where(keep, jnp.exp2(s), 0.0).astype(BF16)
-                total = total + jnp.dot(p, v_ref[keys, :], preferred_element_type=F32)
+                total = total + jnp.dot(p, vx_ref[keys, :], preferred_element_type=F32)
             weight = total[:, width:]
-            o_ref[rows, cols] = (total[:, :width] / weight).astype(BF16)
-            total_ref[rows, cols] = jnp.log2(weight)
-
-
-def attend(q, k, v, start, tile=512):
-    span, width = k.shape
-    heads = q.shape[1] // width
-    vx = jnp.concatenate([v, jnp.ones_like(v)], axis=1)
+            o_ref[rows, pl.ds(h * width, width)] = (total[:, :width] / weight).astype(BF16)
+            qx_ref[rows, pl.ds((2 * h + 1) * width, width)] = in_lanes(-jnp.log2(weight))
+
+
+def attend(qkv, gq, gk, cos, sin, start, tile=512):
+    span = qkv.shape[0]
+    width = gq.shape[0]
+    heads = qkv.shape[1] // width - 2
+    vmem = pl.BlockSpec(memory_space=pltpu.VMEM)
     return pl.pallas_call(
         functools.partial(attend_kernel, heads, min(tile, span)),
         out_shape=(
             jax.ShapeDtypeStruct((span, heads * width), BF16),
-            jax.ShapeDtypeStruct((span, heads * width), F32),
+            jax.ShapeDtypeStruct((span, 2 * heads * width), BF16),
+            jax.ShapeDtypeStruct((span, width), BF16),
         ),
-        in_specs=[pl.BlockSpec(memory_space=pltpu.VMEM)] * 4,
-        out_specs=[pl.BlockSpec(memory_space=pltpu.VMEM)] * 2,
+        in_specs=[vmem] * 6,
+        out_specs=[vmem] * 3,
+        scratch_shapes=[pltpu.VMEM((span, 2 * width), BF16)],
         compiler_params=pltpu.CompilerParams(vmem_limit_bytes=48 * MIB),
-    )(q, k, vx, start[:, None])
+    )(qkv, gq[None, :], gk[None, :], cos, sin, start[:, None])
 
 
 def attend_back_kernel(
-    heads, tile, q_ref, k_ref, v_ref, g_ref, start_ref, dq_ref, dk_ref, dv_ref
+    heads,
+    tile,
+    qx_ref,
+    kn_ref,
+    qkv_ref,
+    o_ref,
+    do_ref,
+    gq_ref,
+    gk_ref,
+    cos_ref,
+    sin_ref,
+    start_ref,
+    dqkv_ref,
+    gains_ref,
+    gx_ref,
+    dq_ref,
 ):
-    span = q_ref.shape[0]
-    width = k_ref.shape[1] // 2
+    span = qx_ref.shape[0]
+    width = kn_ref.shape[1]
+    scale = width**-0.5
+    ones = jnp.ones((tile, width), BF16)
+
+    def to_raw(d, h, rows, gain):
+        r, unit = unit_rows(qkv_ref[rows, pl.ds(h * width, width)].astype(F32))
+        d = d * cos_ref[rows, :] + swap_halves(d * sin_ref[rows, :])
+        dg = d * gain
+        raw = r * (dg - unit * jnp.mean(dg * unit, axis=1, keepdims=True))
+        dqkv_ref[rows, pl.ds(h * width, width)] = raw.astype(BF16)
+        return jnp.sum(d * unit, axis=0, keepdims=True)
+
+    for i in range(span // tile):
+        rows = pl.ds(i * tile, tile)
+        for h in range(heads):
+            cols = pl.ds(h * width, width)
+            do = do_ref[rows, cols]
+            inner = jnp.sum(do.astype(F32) * o_ref[rows, cols].astype(F32), axis=1, keepdims=True)
+            gx_ref[rows, pl.ds(2 * h * width, width)] = do
+            gx_ref[rows, pl.ds((2 * h + 1) * width, width)] = in_lanes(
+                jnp.broadcast_to(-inner, (tile, width))
+            )
     dq_ref[...] = jnp.zeros_like(dq_ref)
+    key_gain = jnp.zeros((1, width), F32)
     for j in range(span // tile):
         keys = pl.ds(j * tile, tile)
-        kx = k_ref[keys, :]
-        vx = v_ref[keys, :]
+        kn = kn_ref[keys, :]
+        kx = jnp.concatenate([kn, ones], axis=1)
+        vx = jnp.concatenate([qkv_ref[keys, pl.ds((heads + 1) * width, width)], ones], axis=1)
         dk = jnp.zeros((tile, width), F32)
         dv = jnp.zeros((tile, width), F32)
         key = j * tile + lax.broadcasted_iota(jnp.int32, (tile, tile), 0)
@@ -252,8 +351,8 @@
                 row = i * tile + lax.broadcasted_iota(jnp.int32, (tile, tile), 1)
                 keep = keep & (key <= row)
             for h in range(heads):
-                qx = q_ref[rows, pl.ds(2 * h * width, 2 * width)]
-                gx = g_ref[rows, pl.ds(2 * h * width, 2 * width)]
+                qx = qx_ref[rows, pl.ds(2 * h * width, 2 * width)]
+                gx = gx_ref[rows, pl.ds(2 * h * width, 2 * width)]
                 s = lax.dot_general(kx, qx, NT, preferred_element_type=F32)
                 p = jnp.where(keep, jnp.exp2(s), 0.0)
                 dp = lax.dot_general(vx, gx, NT, preferred_element_type=F32)
@@ -261,45 +360,207 @@
                 dv = dv + jnp.dot(p.astype(BF16), gx[:, :width], preferred_element_type=F32)
                 dk = dk + jnp.dot(ds, qx[:, :width], preferred_element_type=F32)
                 dq_ref[rows, pl.ds(h * width, width)] += lax.dot_general(
-                    ds, kx[:, :width], TN, preferred_element_type=F32
+                    ds, kn, TN, preferred_element_type=F32
                 )
-        dk_ref[keys, :] = dk
-        dv_ref[keys, :] = dv
-
-
-def attend_back(qx, kx, vx, gx, start, tile=512):
-    span = qx.shape[0]
-    width = kx.shape[1] // 2
-    heads = qx.shape[1] // (2 * width)
+        dqkv_ref[keys, pl.ds((heads + 1) * width, width)] = dv.astype(BF16)
+        key_gain = key_gain + to_raw(dk * (1.0 / LOG2E), heads, keys, gk_ref[...])
+    query_gain = jnp.zeros((1, width), F32)
+    for i in range(span // tile):
+        rows = pl.ds(i * tile, tile)
+        for h in range(heads):
+            dq = dq_ref[rows, pl.ds(h * width, width)] * scale
+            query_gain = query_gain + to_raw(dq, h, rows, gq_ref[...])
+    gains_ref[0:1, :] = query_gain
+    gains_ref[1:2, :] = key_gain
+
+
+def attend_back(qx, kn, qkv, o, do, gq, gk, cos, sin, start, tile=512):
+    span, width = kn.shape
+    heads = o.shape[1] // width
+    vmem = pl.BlockSpec(memory_space=pltpu.VMEM)
     return pl.pallas_call(
         functools.partial(attend_back_kernel, heads, min(tile, span)),
         out_shape=(
-            jax.ShapeDtypeStruct((span, heads * width), F32),
-            jax.ShapeDtypeStruct((span, width), F32),
-            jax.ShapeDtypeStruct((span, width), F32),
+            jax.ShapeDtypeStruct(qkv.shape, BF16),
+            jax.ShapeDtypeStruct((2, width), F32),
         ),
-        in_specs=[pl.BlockSpec(memory_space=pltpu.VMEM)] * 5,
-        out_specs=[pl.BlockSpec(memory_space=pltpu.VMEM)] * 3,
+        in_specs=[vmem] * 10,
+        out_specs=[vmem] * 2,
+        scratch_shapes=[
+            pltpu.VMEM((span, 2 * heads * width), BF16),
+            pltpu.VMEM((span, heads * width), F32),
+        ],
         compiler_params=pltpu.CompilerParams(vmem_limit_bytes=56 * MIB),
-    )(qx, kx, vx, gx, start[None, :])
-
-
-def split3(x):
-    first = x.astype(BF16)
-    rest = x - first.astype(F32)
-    second = rest.astype(BF16)
-    return first, second, (rest - second.astype(F32)).astype(BF16)
-
-
-def norm_rows(values, scaling):
-    return values * lax.rsqrt(jnp.mean(values * values, axis=-1, keepdims=True) + EPSILON) * scaling
-
-
-def rotate(values, cosine, sine):
-    half = values.shape[-1] // 2
-    first = values[..., :half]
-    second = values[..., half:]
-    return jnp.concatenate([first * cosine - second * sine, second * cosine + first * sine], axis=-1)
+    )(qx, kn, qkv, o, do, gq[None, :], gk[None, :], cos, sin, start[None, :])
+
+
+def last_gather_kernel(
+    count, members, cuts, q_ref, kv_ref, q_all, kv_all, heap, kv_sum, sems, own_sem, mo, mi, ro, ri, so, si
+):
+    me, chips, lane, position, step, following, previous, sibling = places(count)
+    chip = me // 2
+    place = chip % members
+    first = chip - place
+    rows = kv_sum.shape[0]
+
+    def member(i):
+        return (first + (place + i) % members) * 2 + lane
+
+    greet([previous, sibling] + [member(i) for i in range(1, members)])
+
+    def give(i):
+        target = (place + i) % members
+        return pltpu.make_async_remote_copy(
+            src_ref=kv_ref.at[pl.ds(target * rows, rows)],
+            dst_ref=heap.at[i - 1],
+            send_sem=mo.at[i - 1],
+            recv_sem=mi.at[i - 1],
+            device_id={"seq": member(i)},
+            device_id_type=MESH,
+        )
+
+    pieces = [(q_ref, q_all, part) for part in row_parts(q_ref.shape[0], cuts)]
+    pieces.append((kv_sum, kv_all, pl.ds(0, rows)))
+
+    def hop(c, owner, s, device, out_sem, in_sem, first_hop):
+        x_ref, o_ref, part = pieces[c]
+        return pltpu.make_async_remote_copy(
+            src_ref=x_ref.at[part] if first_hop else o_ref.at[owner, part],
+            dst_ref=o_ref.at[owner, part],
+            send_sem=out_sem.at[s, c],
+            recv_sem=in_sem.at[s, c],
+            device_id={"seq": device},
+            device_id_type=MESH,
+        )
+
+    def ring(c, owner, s, first_hop=False):
+        return hop(c, owner, s, following, ro, ri, first_hop)
+
+    def side(c, owner, s, first_hop=False):
+        return hop(c, owner, s, sibling, so, si, first_hop)
+
+    for i in range(1, members):
+        give(i).start()
+    mine = pltpu.make_async_copy(kv_ref.at[pl.ds(place * rows, rows)], kv_sum, own_sem.at[0])
+    mine.start()
+    own_q = pltpu.make_async_copy(q_ref, q_all.at[me], own_sem.at[1])
+    own_q.start()
+    for c in range(cuts):
+        ring(c, me, 0, True).start()
+        side(c, me, 0, True).start()
+    mine.wait()
+    total = kv_sum[...].astype(F32)
+    for i in range(1, members):
+        give(i).wait_recv()
+        total = total + heap[i - 1].astype(F32)
+    kv_sum[...] = total.astype(BF16)
+    own_kv = pltpu.make_async_copy(kv_sum, kv_all.at[me], own_sem.at[2])
+    own_kv.start()
+    ring(cuts, me, 0, True).start()
+    side(cuts, me, 0, True).start()
+    for s in range(1, chips):
+        owner = chip_of((position - s * step + chips) % chips, chips) * 2 + lane
+        for c in range(cuts + 1):
+            ring(c, owner, s - 1).wait_recv()
+            if s < chips - 1:
+                ring(c, owner, s).start()
+            side(c, owner, s).start()
+    for i in range(1, members):
+        give(i).wait_send()
+    for s in range(chips):
+        for c in range(cuts + 1):
+            side(c, me, s).wait()
+            if s < chips - 1:
+                ring(c, me, s).wait_send()
+    own_q.wait()
+    own_kv.wait()
+
+
+def last_gather(q, kv, count, members, call, cuts=4):
+    chips = count // 2
+    rows = kv.shape[0] // members
+    anywhere = pl.BlockSpec(memory_space=pl.ANY)
+    dma = pltpu.SemaphoreType.DMA
+    return pl.pallas_call(
+        functools.partial(last_gather_kernel, count, members, cuts),
+        out_shape=(
+            jax.ShapeDtypeStruct((count,) + q.shape, BF16),
+            jax.ShapeDtypeStruct((count, rows, kv.shape[1]), BF16),
+        ),
+        in_specs=[anywhere] * 2,
+        out_specs=[anywhere] * 2,
+        scratch_shapes=[
+            pltpu.VMEM((members - 1, rows, kv.shape[1]), BF16),
+            pltpu.VMEM((rows, kv.shape[1]), BF16),
+            dma,
+            dma((3,)),
+            dma((members - 1,)),
+            dma((members - 1,)),
+        ]
+        + [dma((chips, cuts + 1))] * 4,
+        compiler_params=pltpu.CompilerParams(collective_id=call, has_side_effects=True),
+    )(q, kv)
+
+
+def finish_kernel(
+    count, kv_heads, tile, q_ref, kv_ref, wq_ref, wk_ref, wv_ref, gain_ref, dq_ref, dk_ref, dv_ref, dg_ref
+):
+    chips = count // 2
+    members = count // kv_heads
+    width = q_ref.shape[2]
+    hd = kv_ref.shape[2] // 2
+    member = pl.program_id(0) * members // pl.num_programs(0)
+
+    def place(group):
+        return (group % chips) * 2 + group // chips
+
+    total = jnp.zeros((tile, 1), F32)
+    for g in range(count):
+        cols = pl.ds(g * width, width)
+        grad = q_ref[place(g)].astype(F32)
+        dq_ref[:, cols] = grad
+        total += jnp.sum(grad * wq_ref[:, cols].astype(F32), axis=1, keepdims=True)
+    for j in range(kv_heads):
+        cols = pl.ds(j * hd, hd)
+        pair = kv_ref[place(j * members + member)].astype(F32)
+        dk_ref[:, cols] = pair[:, :hd]
+        dv_ref[:, cols] = pair[:, hd:]
+        total += jnp.sum(pair[:, :hd] * wk_ref[:, cols].astype(F32), axis=1, keepdims=True)
+        total += jnp.sum(pair[:, hd:] * wv_ref[:, cols].astype(F32), axis=1, keepdims=True)
+    dg_ref[...] = total / gain_ref[...].astype(F32)
+
+
+def finish(q_all, kv_all, w_query, key_weight, value_weight, gain, kv_heads):
+    count = q_all.shape[0]
+    local, columns = w_query.shape
+    rows = kv_all.shape[1]
+    tile = min(128, rows)
+    per = rows // tile
+    kv_columns = key_weight.shape[1]
+
+    def row_block(n):
+        return pl.BlockSpec((tile, n), lambda r: (r, 0))
+
+    return pl.pallas_call(
+        functools.partial(finish_kernel, count, kv_heads, tile),
+        grid=(local // tile,),
+        out_shape=(
+            jax.ShapeDtypeStruct((local, columns), F32),
+            jax.ShapeDtypeStruct((local, kv_columns), F32),
+            jax.ShapeDtypeStruct((local, kv_columns), F32),
+            jax.ShapeDtypeStruct((local, 1), F32),
+        ),
+        in_specs=[
+            pl.BlockSpec((count, tile, q_all.shape[2]), lambda r: (0, r, 0)),
+            pl.BlockSpec((count, tile, kv_all.shape[2]), lambda r: (0, r % per, 0)),
+            row_block(columns),
+            row_block(kv_columns),
+            row_block(kv_columns),
+            row_block(1),
+        ],
+        out_specs=[row_block(columns), row_block(kv_columns), row_block(kv_columns), row_block(1)],
+        compiler_params=pltpu.CompilerParams(vmem_limit_bytes=48 * MIB),
+    )(q_all, kv_all, w_query, key_weight, value_weight, gain[:, None])
 
 
 def run_starts(segment):
@@ -391,38 +652,25 @@
     wg = lax.all_gather(w_gate[0], "fsdp", axis=0, tiled=True)
     wu = lax.all_gather(w_up[0], "fsdp", axis=0, tiled=True)
     wd = lax.all_gather(w_down[0], "fsdp", axis=1, tiled=True)
-    routes_all = lax.all_gather(routes, "seq", axis=0, tiled=False)
 
     r1 = lax.rsqrt(jnp.mean(x * x, axis=-1, keepdims=True) + EPSILON)
     h1 = (x * r1 * g_attn).astype(BF16)
-    h1_all = gather_seq(h1, count, 1).reshape(span, dim)
+    h1_all = gather_seq([h1], count, 1, (4,))[0].reshape(span, dim)
     qkv = dot(h1_all, w_qkv).astype(BF16)
     position, doc_start = run_starts(segment)
     cosine, sine = angles((position - doc_start).astype(F32), hd)
     start = jnp.where(segment > 0, doc_start, position)
 
-    def prep_query(raw, scaling):
-        return rotate(norm_rows(raw, scaling), cosine[:, None], sine[:, None])
-
-    def prep_key(raw, scaling):
-        return rotate(norm_rows(raw, scaling), cosine, sine)
-
-    q_raw = qkv[:, :gcols].reshape(span, share, hd).astype(F32)
-    k_raw = qkv[:, gcols : gcols + hd].astype(F32)
-    v = qkv[:, gcols + hd :]
-    q_rot, query_pullback = jax.vjp(prep_query, q_raw, g_query)
-    k_rot, key_pullback = jax.vjp(prep_key, k_raw, g_key)
-    scale = hd**-0.5
-    qs = (q_rot * (scale * LOG2E)).astype(BF16)
-    kn = k_rot.astype(BF16)
-    o, weight = attend(qs.reshape(span, gcols), kn, v, start)
+    cos_full = jnp.concatenate([cosine, cosine], axis=1)
+    sin_full = jnp.concatenate([-sine, sine], axis=1)
+    o, qx, kn = attend(qkv, g_query, g_key, cos_full, sin_full, start)
     x2_parts = dot(o, w_o).astype(BF16).reshape(count, tok, dim)
     x2 = x + scatter_seq(x2_parts, count, 2)
 
     r2 = lax.rsqrt(jnp.mean(x2 * x2, axis=-1, keepdims=True) + EPSILON)
     h2 = (x2 * r2 * g_mlp).astype(BF16)
-    h2_all = gather_seq(h2, count, 3)
-    dy_all = gather_seq(dy, count, 4)
+    h2_all = gather_seq([h2], count, 3, (4,))[0]
+    dy_all, routes_all = gather_seq([dy, routes], count, 4, (4, 1))
 
     def gates_of(hidden, chosen):
         logits = dot(hidden, router)
@@ -495,29 +743,11 @@
     dn = dh2 * g_mlp
     dx2 = dy.astype(F32) + r2 * (dn - xh * jnp.mean(dn * xh, axis=-1, keepdims=True))
 
-    da_all = gather_seq(dx2.astype(BF16), count, 7).reshape(span, dim)
+    da_all = gather_seq([dx2.astype(BF16)], count, 7, (4,))[0].reshape(span, dim)
     do = dot(da_all, w_o, NT).astype(BF16)
     w_out_part = dot(o, da_all, TN).astype(BF16)
-    do_h = do.reshape(span, share, hd)
-    inner_sum = jnp.sum(
-        do_h.astype(F32) * o.reshape(span, share, hd).astype(F32), axis=-1, keepdims=True
-    )
-
-    def widen(values, extra):
-        cols = list(split3(extra))
-        pad = jnp.zeros(values.shape[:-1] + (hd - len(cols),), BF16)
-        return jnp.concatenate([values] + cols + [pad], axis=-1)
-
-    qx = widen(qs, -weight.reshape(span, share, hd)[:, :, :1]).reshape(span, 2 * gcols)
-    gx = widen(do_h, -inner_sum).reshape(span, 2 * gcols)
-    ones = jnp.ones_like(kn)
-    dq_rot, dk_rot, dv = attend_back(
-        qx, jnp.concatenate([kn, ones], axis=1), jnp.concatenate([v, ones], axis=1), gx, start
-    )
-    dq, query_gain_part = query_pullback(dq_rot.reshape(span, share, hd) * scale)
-    dk, key_gain_part = key_pullback(dk_rot * (1.0 / LOG2E))
-    dqkv = jnp.concatenate(
-        [dq.reshape(span, gcols).astype(BF16), dk.astype(BF16), dv.astype(BF16)], axis=1
+    dqkv, head_gains = attend_back(
+        qx, kn, qkv, o, do, g_query, g_key, cos_full, sin_full, start
     )
     qkv_part = dot(h1_all, dqkv, TN).astype(BF16)
     dh1 = scatter_seq(dot(dqkv, w_qkv, NT).astype(BF16).reshape(count, tok, dim), count, 8)
@@ -533,20 +763,11 @@
     w_down_grad = sum_fsdp(w_down_part, 1).astype(F32)
 
     small_part = jnp.concatenate(
-        [
-            router_part.reshape(shards, -1),
-            mlp_gain_part.reshape(shards, -1),
-            query_gain_part.reshape(shards, -1),
-            key_gain_part.reshape(shards, -1),
-        ],
-        axis=1,
-    )
-    small_sum = lax.psum(sum_fsdp(small_part, 0), "seq").astype(F32)[0]
-    router_grad, mlp_gain_grad, query_gain_grad, key_gain_grad = jnp.split(
-        small_sum,
-        [local_dim * experts, local_dim * (experts + 1), local_dim * (experts + 1) + local_hd],
-    )
-    router_grad = router_grad.reshape(local_dim, experts)
+        [router_part.reshape(shards, -1), mlp_gain_part.reshape(shards, -1)], axis=1
+    )
+    small_rows = -(-small_part.shape[1] // dim // 16) * 16
+    small_part = jnp.pad(small_part, ((0, 0), (0, small_rows * dim - small_part.shape[1])))
+    small_sum = sum_fsdp(small_part, 0).reshape(small_rows, dim)
 
     out_sum = jnp.sum(
         lax.all_gather(w_out_part, "fsdp", axis=0, tiled=False).astype(F32), axis=0
@@ -558,22 +779,32 @@
         tiled=False,
         axis_index_groups=[[2 * c, 2 * c + 1] for c in range(chips)],
     )
-    w_out_grad = out_rows(pair, out_sum, count, shards, tok)
-
+    w_out_grad, small_all = out_rows(pair, out_sum, small_sum, count, shards)
+    small_total = jnp.sum(small_all.astype(F32), axis=0).reshape(-1)
+    router_grad = small_total[: local_dim * experts].reshape(local_dim, experts)
+    mlp_gain_grad = small_total[local_dim * experts : local_dim * (experts + 1)]
+
+    gains_part = jnp.concatenate(
+        [head_gains[0].reshape(shards, 1, local_hd), head_gains[1].reshape(shards, 1, local_hd)],
+        axis=2,
+    ).astype(BF16)
+    gains_part = jnp.pad(
+        gains_part, ((0, 0), (0, 15), (0, qkv_part.shape[1] - 2 * local_hd))
+    )
+    qkv_part = jnp.concatenate(
+        [qkv_part.reshape(shards, local_dim, -1), gains_part], axis=1
+    ).reshape(shards * (local_dim + 16), -1)
     qkv_sum = sum_fsdp(qkv_part, 0)
-    qkv_all = gather_seq(qkv_sum, count, 10)
-    order = [(g % chips) * 2 + g // chips for g in range(count)]
-    qkv_groups = qkv_all[jnp.array(order)].astype(F32)
-    w_query_grad = jnp.swapaxes(qkv_groups[:, :, :gcols], 0, 1).reshape(local_dim, heads * hd)
-    kv_groups = qkv_groups[:, :, gcols:].reshape(kv_heads, count // kv_heads, local_dim, 2 * hd)
-    kv_groups = jnp.swapaxes(jnp.sum(kv_groups, axis=1), 0, 1)
-    w_key_grad = kv_groups[:, :, :hd].reshape(local_dim, kv_heads * hd)
-    w_value_grad = kv_groups[:, :, hd:].reshape(local_dim, kv_heads * hd)
-    attn_gain_grad = (
-        jnp.sum(w_query.astype(F32) * w_query_grad, axis=1)
-        + jnp.sum(key_weight.astype(F32) * w_key_grad, axis=1)
-        + jnp.sum(value_weight.astype(F32) * w_value_grad, axis=1)
-    ) / attn_gain.astype(F32)
+    q_all, kv_all = last_gather(
+        qkv_sum[:, :gcols], qkv_sum[:local_dim, gcols:], count, count // kv_heads, 10
+    )
+    w_query_grad, w_key_grad, w_value_grad, attn_gain_grad = finish(
+        q_all, kv_all, w_query, key_weight, value_weight, attn_gain, kv_heads
+    )
+    attn_gain_grad = attn_gain_grad[:, 0]
+    head_gain_grads = jnp.sum(q_all[:, local_dim, : 2 * local_hd].astype(F32), axis=0)
+    query_gain_grad = head_gain_grads[:local_hd]
+    key_gain_grad = head_gain_grads[local_hd:]
     return (
         mixed.astype(BF16)[None],
         input_grad[None],
@@ -592,16 +823,16 @@
     )
 
 
-def out_rows(pair, out_sum, count, shards, tok):
+def out_rows(pair, out_sum, small_sum, count, shards):
     chips = count // 2
     gcols, dim = out_sum.shape
     me = lax.axis_index("seq")
     mine = lax.axis_index("fsdp")
     if shards == 2:
-        half = lax.dynamic_slice(
-            pair, (mine, (me % 2) * (gcols // 2), 0), (1, gcols // 2, dim)
-        )[0]
-        return gather_seq(half, count, 9).reshape(chips * gcols, dim).astype(F32)
+        half = lax.dynamic_slice(pair, (mine, (me % 2) * (gcols // 2), 0), (1, gcols // 2, dim))[0]
+        halves, small_all = gather_seq([half, small_sum], count, 9, (4, 1))
+        return halves.reshape(chips * gcols, dim).astype(F32), small_all
+    small_all = gather_seq([small_sum], count, 9, (1,))[0]
     groups = count // shards
     first = mine * groups
     group = (me % 2) * chips + me // 2
@@ -609,7 +840,8 @@
     keep = (group >= first) & (group < first + groups)
     rows = jnp.where(keep, out_sum, jnp.zeros_like(out_sum))
     blank = jnp.zeros((groups * gcols, dim), BF16)
-    return lax.psum(lax.dynamic_update_slice(blank, rows, (place * gcols, 0)), "seq").astype(F32)
+    total = lax.psum(lax.dynamic_update_slice(blank, rows, (place * gcols, 0)), "seq")
+    return total.astype(F32), small_all
 
 
 def solution(mesh):

time: 1170 us -> 828 us (0.71)
  local copies, waits for them, and re-layouts: 194 us -> 26.9 us
  other arithmetic: 164 us -> 69.1 us
  blocking collectives: 88.9 us -> 5.93 us
  Pallas kernels: 524 us -> 537 us
  waiting for transfers between devices: 14.8 us -> 2.1 us
    psum x1 -> x0, blocking collectives: 61 us -> none  [per_device(): small_sum = lax.psum(sum_fsdp(small_part, 0), 'seq').astype(F32)[0]]
    unnamed x154 -> x83, local copies, waits for them, and re-layouts: 58.4 us -> 7.05 us
    concatenate x5 -> x2, local copies, waits for them, and re-layouts: 41.8 us -> 0.17 us  [per_device(): jnp.concatenate([head_gains[0].reshape(shards, 1, local_hd), head_gains[1...]
    convert_element_type x12 -> x2, other arithmetic: 51.8 us -> 14 us  [the longest x1 11.8 us: out_rows(): return (halves.reshape(chips * gcols, dim).astype(F32), small_all)]
    reduce_sum x9 -> x2, other arithmetic: 39.6 us -> 2.17 us  [the longest x1 1.38 us: per_device(): small_total = jnp.sum(small_all.astype(F32), axis=0).reshape(-1)]
    transpose x2 -> x0, local copies, waits for them, and re-layouts: 29.2 us -> none  [per_device(): jnp.swapaxes(qkv_groups[:, :, :gcols], 0, 1).reshape(local_dim, heads * hd)]
    all_gather x1 -> x0, blocking collectives: 22 us -> none  [per_device(): routes_all = lax.all_gather(routes, 'seq', axis=0, tiled=False)]
    convert_element_type x8 -> x0, local copies, waits for them, and re-layouts: 18.3 us -> none  [the longest x2 4.16 us: split3(): first = x.astype(BF16)]
  transfers between devices with their start and end apart: 12 -> 12, of which waited for: 1 -> 1; matrix products, arithmetic and copies ran while one was open for 30% -> 21% of each run, Pallas kernels for 36% -> 54%
where the time goes in v2:
time: 828 us; the launch traced here: 818 us
  Pallas kernels  537 us (65%)
  matrix products  160 us (19%)
  other arithmetic  69.1 us (8%)
  local copies, waits for them, and re-layouts  26.9 us (3%)
  between operations  15.3 us (2%)
    pallas_call x5, Pallas kernels, gather_seq(): pl.pallas_call(functools.partial(gather_kernel, count, cuts), out_shape=[...  239 us
    pallas_call x4, Pallas kernels, scatter_seq(): pl.pallas_call(functools.partial(scatter_kernel, count, cuts), out_shape=...  186 us
    dot_general x19, matrix products, dot(): return lax.dot_general(a, b, dims, preferred_element_type=F32)  135 us
    pallas_call x1, Pallas kernels, last_gather(): pl.pallas_call(functools.partial(last_gather_kernel, count, members, cuts...  62 us
    pallas_call x1, Pallas kernels, attend_back(): pl.pallas_call(functools.partial(attend_back_kernel, heads, min(tile, spa...  22 us
  transfers between devices with their start and end apart: 12, of which 1 were waited for; matrix products, arithmetic and copies ran while one was open for 21% of the time, Pallas kernels for 54%

profile of v2, /device:TPU:0, one launch (start us, length us, event | category | flops | bytes accessed | tf_op | source)
XLA Modules:
  0.0 817.9 jit_solution(3303166264140035386)
XLA Ops:
  27.5 45.7 %shard_map.263 = bf16[16,128,2048]{2,1,0:T(8,128)(2,1)} custom-call(bf16[128,2048]{1,0:T(8,128)(2,1)} %fusion.19.refs_0_), custom_call_target="tpu_custom_call" | custom-call | tf_op jit(solution)/shard_map/pallas_call | solution.py:111
  73.2 51.2 %shard_map.266 = (bf16[16,128,2048]{2,1,0:T(8,128)(2,1)}, s32[16,128,8]{2,1,0:T(8,128)}) custom-call(bf16[128,2048]{1,0:T(8,128)(2,1)} %bitcast.155, s32[128,8]{1,0:T(8,128)} %bitcast.165), custom_call_target="tpu_custom_call" | custom-call | tf_op jit(solution)/shard_map/pallas_call | solution.py:111
  140.9 10.7 %convolution_convert_fusion.10.qkv_ref = bf16[2048,512]{1,0:T(8,128)(2,1)} fusion(bf16[2048,2048]{1,0:T(8,128)(2,1)} %bitcast.152, bf16[2048,512]{1,0:T(8,128)(2,1)} %all-gather.16.cloned.1.call-done), kind=kOutput, calls=%fused_computation.35 | convolution fusion | flops 4296015872 | bytes 12582912 | tf_op jit(solution)/shard_map/dot_general | solution.py:581
  151.7 12.4 %shard_map.264 = (bf16[2048,256]{1,0:T(8,128)(2,1)S(1)}, bf16[2048,512]{1,0:T(8,128)(2,1)}, bf16[2048,128]{1,0:T(8,128)(2,1)S(1)}) custom-call(bf16[2048,512]{1,0:T(8,128)(2,1)} %convolution_convert_fusion.10.qkv_ref, f32[1,128]{1,0:T(1,128)S(1)} %reshape.351.gq_ref, f32[1,128]{1,0:T(1,128)S(1)} %reshape.352.gk_ref, ...), custom_call_target="tpu_custom_call" | custom-call | tf_op jit(solution)/shard_map/pallas_call | solution.py:282
  172.4 47.2 %shard_map.265 = f32[128,2048]{1,0:T(8,128)S(1)} custom-call(bf16[16,128,2048]{2,1,0:T(8,128)(2,1)} %bitcast.144), custom_call_target="tpu_custom_call" | custom-call | tf_op jit(solution)/shard_map/pallas_call | solution.py:185
  220.8 45.7 %shard_map.267 = bf16[16,128,2048]{2,1,0:T(8,128)(2,1)} custom-call(bf16[128,2048]{1,0:T(8,128)(2,1)} %multiply_convert_fusion.4.refs_0_), custom_call_target="tpu_custom_call" | custom-call | tf_op jit(solution)/shard_map/pallas_call | solution.py:111
  276.6 9.0 %fusion.12 = f32[1152,768]{1,0:T(8,128)} fusion(bf16[1152,2048]{1,0:T(8,128)(2,1)} %bitcast.146, bf16[1,2048,768]{2,1,0:T(8,128)(2,1)} %all-gather.20.cloned.1.call-done), kind=kOutput, calls=%fused_computation.32 | convolution fusion | flops 3623878656 | bytes 11403264 | tf_op jit(solution)/shard_map/dot_general | solution.py:581
  285.5 11.3 %multiply_convert_fusion.3 = (bf16[1152,768]{1,0:T(8,128)(2,1)}, f32[1152,768]{1,0:T(8,128)}) fusion(f32[1152,768]{1,0:T(8,128)} %fusion.12, bf16[1152,2048]{1,0:T(8,128)(2,1)} %bitcast.147, bf16[1,2048,768]{2,1,0:T(8,128)(2,1)} %all-gather.22.cloned.1.call-done), kind=kOutput, calls=%fused_computation.18 | convolution fusion | flops 3629187072 | bytes 16711680 | tf_op jit(solution)/shard_map/dot_general | solution.py:581
  296.8 11.4 %fusion.1 = (f32[1152]{0:T(1024)S(1)}, f32[1152,2048]{1,0:T(8,128)}) fusion(bf16[16,72,2048]{2,1,0:T(8,128)(2,1)} %convolution_convert_fusion.4, bf16[1152,768]{1,0:T(8,128)(2,1)} %get-tuple-element.131, bf16[1,768,2048]{2,1,0:T(8,128)(2,1)} %all-gather.24.cloned.1.call-done), kind=kOutput, calls=%fused_computation.3 | convolution fusion | flops 3630955520 | bytes 19075584 | tf_op jit(solution)/shard_map/dot_general | solution.py:581
  309.0 11.8 %fusion = (bf16[1152,2048]{1,0:T(8,128)(2,1)}, bf16[1152,2048]{1,0:T(8,128)(2,1)}) fusion(bf16[16,72,2048]{2,1,0:T(8,128)(2,1)} %convolution_convert_fusion.4, f32[1152]{0:T(1024)S(1)} %mul.204, f32[1152,2048]{1,0:T(8,128)} %get-tuple-element.134), kind=kLoop, calls=%fused_computation.2 | loop fusion | flops 11796480 | bytes 23597568 | tf_op jit(solution)/shard_map/convert_element_type | solution.py:720
  320.8 11.6 %multiply_convert_fusion.1 = (bf16[1152,768]{1,0:T(8,128)(2,1)}, bf16[1152,768]{1,0:T(8,128)(2,1)S(1)}) fusion(f32[1152,768]{1,0:T(8,128)} %fusion.12, f32[1152,768]{1,0:T(8,128)} %get-tuple-element.132, bf16[1152,2048]{1,0:T(8,128)(2,1)} %get-tuple-element.125, bf16[1,768,2048]{2,1,0:T(8,128)(2,1)} %all-gather.24.cloned.1.call-done), kind=kOutput, calls=%fused_computation.16 | convolution fusion | flops 3634495488 | bytes 18481152 | tf_op jit(solution)/shard_map/dot_general | solution.py:581
  356.6 48.2 %shard_map.269 = f32[128,2176]{1,0:T(8,128)S(1)} custom-call(bf16[16,128,2176]{2,1,0:T(8,128)(2,1)} %pad_maximum_fusion.p_ref), custom_call_target="tpu_custom_call" | custom-call | tf_op jit(solution)/shard_map/pallas_call | solution.py:185
  410.8 45.7 %shard_map.270 = bf16[16,128,2048]{2,1,0:T(8,128)(2,1)} custom-call(bf16[128,2048]{1,0:T(8,128)(2,1)} %fusion.54.refs_0_), custom_call_target="tpu_custom_call" | custom-call | tf_op jit(solution)/shard_map/pallas_call | solution.py:111
  471.7 22.0 %shard_map.271 = (bf16[2048,512]{1,0:T(8,128)(2,1)}, f32[2,128]{1,0:T(2,128)}) custom-call(bf16[2048,512]{1,0:T(8,128)(2,1)} %get-tuple-element.32.qx_ref, bf16[2048,128]{1,0:T(8,128)(2,1)} %copy-done.7, bf16[2048,512]{1,0:T(8,128)(2,1)} %convolution_convert_fusion.10.qkv_ref, bf16[2048,256]{1,0:T(8,128)(2,1)} %copy-done, ...), custom_call_target="tpu_custom_call" | custom-call | tf_op jit(solution)/shard_map/pallas_call | solution.py:381
  498.2 8.5 %convolution_convert_fusion.9 = bf16[2048,512]{1,0:T(8,128)(2,1)S(1)} fusion(bf16[2048,2048]{1,0:T(8,128)(2,1)} %bitcast.153, bf16[2048,512]{1,0:T(8,128)(2,1)} %get-tuple-element.34), kind=kOutput, calls=%fused_computation.34 | convolution fusion | flops 4296015872 | bytes 12582912 | tf_op jit(solution)/shard_map/dot_general | solution.py:581
  508.5 8.8 %convolution_convert_fusion.6 = bf16[768,2048]{1,0:T(8,128)(2,1)} fusion(bf16[1152,768]{1,0:T(8,128)(2,1)} %get-tuple-element.131, bf16[1152,2048]{1,0:T(8,128)(2,1)} %get-tuple-element.125), kind=kOutput, calls=%fused_computation.20 | convolution fusion | flops 3625451520 | bytes 9633792 | tf_op jit(solution)/shard_map/dot_general | solution.py:581
  517.4 8.9 %convolution_convert_fusion.7 = bf16[2048,768]{1,0:T(8,128)(2,1)} fusion(bf16[1152,2048]{1,0:T(8,128)(2,1)} %bitcast.148, bf16[1152,768]{1,0:T(8,128)(2,1)} %get-tuple-element.114), kind=kOutput, calls=%fused_computation.21 | convolution fusion | flops 3625451520 | bytes 9633792 | tf_op jit(solution)/shard_map/dot_general | solution.py:581
  526.8 9.6 %convolution_convert_fusion.8 = bf16[2048,768]{1,0:T(8,128)(2,1)} fusion(bf16[1152,2048]{1,0:T(8,128)(2,1)} %bitcast.149, bf16[1152,768]{1,0:T(8,128)(2,1)} %copy-done.36), kind=kOutput, calls=%fused_computation.22 | convolution fusion | flops 3625451520 | bytes 9633792 | tf_op jit(solution)/shard_map/dot_general | solution.py:581
  545.5 46.0 %shard_map.268 = f32[128,2048]{1,0:T(8,128)S(1)} custom-call(bf16[16,128,2048]{2,1,0:T(8,128)(2,1)} %convolution_convert_fusion.3.p_ref), custom_call_target="tpu_custom_call" | custom-call | tf_op jit(solution)/shard_map/pallas_call | solution.py:185
  598.5 45.0 %shard_map.272 = f32[128,2048]{1,0:T(8,128)S(1)} custom-call(bf16[16,128,2048]{2,1,0:T(8,128)(2,1)} %bitcast.151), custom_call_target="tpu_custom_call" | custom-call | tf_op jit(solution)/shard_map/pallas_call | solution.py:185
  650.0 50.8 %shard_map.275 = (bf16[16,128,2048]{2,1,0:T(8,128)(2,1)}, bf16[16,16,2048]{2,1,0:T(8,128)(2,1)}) custom-call(bf16[128,2048]{1,0:T(8,128)(2,1)} %dynamic-slice_bitcast_fusion.refs_0_, bf16[16,2048]{1,0:T(8,128)(2,1)} %reshape.346.refs_1_), custom_call_target="tpu_custom_call" | custom-call | tf_op jit(solution)/shard_map/pallas_call | solution.py:111
  703.8 11.8 %bitcast_convert_fusion = f32[2048,2048]{1,0:T(8,128)} fusion(bf16[16,128,2048]{2,1,0:T(8,128)(2,1)} %get-tuple-element.43), kind=kLoop, calls=%fused_computation.7 | loop fusion | flops 4194304 | bytes 25165824 | tf_op jit(solution)/shard_map/convert_element_type | solution.py:834
  719.5 62.0 %shard_map.273 = (bf16[16,1040,256]{2,1,0:T(8,128)(2,1)}, bf16[16,256,256]{2,1,0:T(8,128)(2,1)}) custom-call(bf16[1040,256]{1,0:T(8,128)(2,1)} %slice.82.q_ref, bf16[1024,256]{1,0:T(8,128)(2,1)} %slice.83.kv_ref), custom_call_target="tpu_custom_call" | custom-call | tf_op jit(solution)/shard_map/pallas_call | solution.py:484
  783.1 15.5 %shard_map.274 = (f32[1024,4096]{1,0:T(8,128)}, f32[1024,512]{1,0:T(8,128)}, f32[1024,512]{1,0:T(8,128)}, f32[1024,1]{1,0:T(8,128)S(1)}) custom-call(bf16[16,1040,256]{2,1,0:T(8,128)(2,1)} %get-tuple-element.36.q_ref, bf16[16,256,256]{2,1,0:T(8,128)(2,1)S(1)} %copy-done.4, bf16[1024,4096]{1,0:T(8,128)(2,1)} %wq_ref.1, bf16[1024,512]{1,0:T(8,128)(2,1)S(1)} %copy-done.6, ...), custom_call_target="tpu_custom_call" | custom-call | tf_op jit(solution)/shard_map/pallas_call | solution.py:544
  (222 shorter events, 151.8 us)
Async XLA Ops:
  7.2 133.7 %all-gather.16.cloned.1.call-start = ((), (), s32[]{:S(2)}) async-start(), calls=%async_computation.4 | async-start | bytes 3145728 | tf_op jit(solution)/shard_map/all_gather | solution.py:645
  10.5 154.3 %all-gather.18.cloned.1.call-start = ((), (), s32[]{:S(2)}) async-start(), calls=%async_computation.9 | async-start | bytes 3145728 | tf_op jit(solution)/shard_map/all_gather | solution.py:650
  13.0 263.5 %all-gather.20.cloned.1.call-start = ((), (), s32[]{:S(2)}) async-start(), calls=%async_computation.10 | async-start | bytes 4718592 | tf_op jit(solution)/shard_map/all_gather | solution.py:652
  13.8 271.8 %all-gather.22.cloned.1.call-start = ((), (), s32[]{:S(2)}) async-start(), calls=%async_computation.11 | async-start | bytes 4718592 | tf_op jit(solution)/shard_map/all_gather | solution.py:653
  14.3 282.5 %all-gather.24.cloned.1.call-start = ((), (), s32[]{:S(2)}) async-start(), calls=%async_computation.12 | async-start | bytes 4718592 | tf_op jit(solution)/shard_map/all_gather | solution.py:654
  14.9 479.8 %all-gather.26.cloned.1.call-start = ((), (), s32[]{:S(2)}) async-start(), calls=%async_computation.13 | async-start | bytes 3145728 | tf_op jit(solution)/shard_map/all_gather | solution.py:773
  22.1 51.2 %copy-start.26 = (f32[128]{0:T(128)}, f32[128]{0:T(128)S(1)}, u32[]{:S(2)}) copy-start(f32[128]{0:T(128)S(1)} %add_rsqrt_fusion.1) | copy-start | bytes 1540
  24.9 126.8 %copy-start.8 = (f32[1,128]{1,0:T(1,128)}, f32[1,128]{1,0:T(1,128)S(1)}, u32[]{:S(2)}) copy-start(f32[1,128]{1,0:T(1,128)S(1)} %reshape.352.gk_ref) | copy-start | bytes 1540
  24.9 126.7 %copy-start.9 = (f32[1,128]{1,0:T(1,128)}, f32[1,128]{1,0:T(1,128)S(1)}, u32[]{:S(2)}) copy-start(f32[1,128]{1,0:T(1,128)S(1)} %reshape.351.gq_ref) | copy-start | bytes 1540
  26.5 46.8 %copy-start.19 = (f32[2048]{0:T(1024)}, f32[2048]{0:T(1024)S(1)}, u32[]{:S(2)}) copy-start(f32[2048]{0:T(1024)S(1)} %get-tuple-element.141) | copy-start | bytes 24580
  164.8 291.6 %copy-start = (bf16[2048,256]{1,0:T(8,128)(2,1)}, bf16[2048,256]{1,0:T(8,128)(2,1)S(1)}, u32[]{:S(2)}) copy-start(bf16[2048,256]{1,0:T(8,128)(2,1)S(1)} %get-tuple-element.29.o_ref) | copy-start | bytes 3145732
  172.4 47.2 %copy-start.12 = (bf16[1,128,2048]{2,1,0:T(8,128)(2,1)S(1)}, bf16[1,128,2048]{2,1,0:T(8,128)(2,1)}, u32[]{:S(2)}) copy-start(bf16[1,128,2048]{2,1,0:T(8,128)(2,1)} %param.16) | copy-start | bytes 1572868
  220.8 45.7 %copy-start.16 = (bf16[128,2048]{1,0:T(8,128)(2,1)S(1)}, bf16[128,2048]{1,0:T(8,128)(2,1)}, u32[]{:S(2)}) copy-start(bf16[128,2048]{1,0:T(8,128)(2,1)} %multiply_convert_fusion.4.refs_0_) | copy-start | bytes 1572868
  356.6 48.5 %copy-start.15 = (bf16[2048,16]{1,0:T(8,128)(2,1)S(1)}, bf16[2048,16]{1,0:T(8,128)(2,1)}, u32[]{:S(2)}) copy-start(bf16[2048,16]{1,0:T(8,128)(2,1)} %reshape.336) | copy-start | bytes 196612
  463.2 182.3 %all-reduce.5.cloned.1.call-start = ((), (), s32[]{:S(2)}) async-start(), calls=%async_computation.15 | async-start | bytes 262144
  464.0 184.1 %all-gather.28.cloned.1.call-start = ((), (), s32[]{:S(2)}) async-start(), calls=%async_computation.14 | async-start | bytes 3145728 | tf_op jit(solution)/shard_map/all_gather | solution.py:775
  498.1 217.6 %reduce-scatter.5.cloned.1.call-start = ((), (), s32[]{:S(2)}) async-start(), calls=%async_computation.5 | async-start | bytes 3194880 | tf_op jit(solution)/shard_map/reduce_scatter | solution.py:759
  508.2 292.5 %reduce-scatter.11.cloned.1.call-start = ((), (), s32[]{:S(2)}) async-start(), calls=%async_computation.8 | async-start | bytes 4718592 | tf_op jit(solution)/shard_map/reduce_scatter | solution.py:759
  517.3 286.9 %reduce-scatter.9.cloned.1.call-start = ((), (), s32[]{:S(2)}) async-start(), calls=%async_computation.7 | async-start | bytes 4718592 | tf_op jit(solution)/shard_map/reduce_scatter | solution.py:759
  526.4 281.2 %reduce-scatter.7.cloned.1.call-start = ((), (), s32[]{:S(2)}) async-start(), calls=%async_computation.6 | async-start | bytes 4718592 | tf_op jit(solution)/shard_map/reduce_scatter | solution.py:759
  545.5 46.0 %copy-start.33 = (bf16[2048,512]{1,0:T(8,128)(2,1)S(1)}, bf16[2048,512]{1,0:T(8,128)(2,1)}, u32[]{:S(2)}) copy-start(bf16[2048,512]{1,0:T(8,128)(2,1)} %all-gather.16.cloned.1.call-done) | copy-start | bytes 6291460
  545.5 46.0 %copy-start.34 = (bf16[2048,512]{1,0:T(8,128)(2,1)S(1)}, bf16[2048,512]{1,0:T(8,128)(2,1)}, u32[]{:S(2)}) copy-start(bf16[2048,512]{1,0:T(8,128)(2,1)} %get-tuple-element.34) | copy-start | bytes 6291460
  715.6 65.9 %copy-start.5 = (bf16[1024,512]{1,0:T(8,128)(2,1)S(1)}, bf16[1024,512]{1,0:T(8,128)(2,1)}, u32[]{:S(2)}) copy-start(bf16[1024,512]{1,0:T(8,128)(2,1)} %wv_ref.1) | copy-start | bytes 3145732
  715.6 65.9 %copy-start.6 = (bf16[1024,512]{1,0:T(8,128)(2,1)S(1)}, bf16[1024,512]{1,0:T(8,128)(2,1)}, u32[]{:S(2)}) copy-start(bf16[1024,512]{1,0:T(8,128)(2,1)} %wk_ref.1) | copy-start | bytes 3145732
  (25 other events, 345.4 us)
Sparse Core Ops, SparseCore 0:
  10.7 35.8 all-gather.15
  48.6 33.0 all-gather.17
  83.3 44.9 all-gather.19
  129.7 44.9 all-gather.21
  176.1 44.9 all-gather.23
  463.3 31.3 all-gather.25
  497.0 21.4 all-reduce.4
  520.6 10.5 all-gather.27
  534.0 33.3 reduce-scatter.4
  570.1 43.3 reduce-scatter.10
  616.4 43.3 reduce-scatter.8
  662.4 43.3 reduce-scatter.6

commit v3 on v2

--- a/solution.py
+++ b/solution.py
@@ -119,23 +119,98 @@
     )(*arrays)
 
 
-def scatter_kernel(
-    count, cuts, p_ref, o_ref, own, sent, came, given, own_sem, ring_out, ring_in, side_out, side_in
-):
+NT = (((1,), (1,)), ((), ()))
+TN = (((0,), (0,)), ((), ()))
+NN = (((1,), (0,)), ((), ()))
+
+
+def mm(a, b, dims=NN):
+    return lax.dot_general(a, b, dims, preferred_element_type=F32)
+
+
+def gather_steps(count, cuts, x_ref, land, sems, use):
     me, chips, lane, position, step, following, previous, sibling = places(count)
-    rows = p_ref.shape[1] // cuts
+    ring_out, ring_in, side_out, side_in = sems
+    block = x_ref.shape[0]
+    rows = block // cuts
     greet((previous, sibling))
 
-    def my_block(k):
-        return chip_of((position - (k + 1) * step + 2 * chips) % chips, chips) * 2 + lane
-
-    def sibling_block(k):
-        return chip_of((position + (k + 1) * step + 2 * chips) % chips, chips) * 2 + 1 - lane
+    def ring(s, c):
+        part = pl.ds(c * rows, rows)
+        return pltpu.make_async_remote_copy(
+            src_ref=land.at[s, part],
+            dst_ref=land.at[s + 1, part],
+            send_sem=ring_out.at[s, c],
+            recv_sem=ring_in.at[s, c],
+            device_id={"seq": following},
+            device_id_type=MESH,
+        )
+
+    def side(s, c):
+        return pltpu.make_async_remote_copy(
+            src_ref=land.at[s, pl.ds(c * rows, rows)],
+            dst_ref=land.at[s, pl.ds(block + c * rows, rows)],
+            send_sem=side_out.at[s, c],
+            recv_sem=side_in.at[s, c],
+            device_id={"seq": sibling},
+            device_id_type=MESH,
+        )
+
+    land[0, :block] = x_ref[...]
+
+    def one(s, carry):
+        for c in range(cuts):
+
+            @pl.when(s > 0)
+            def _():
+                ring(s - 1, c).wait_recv()
+
+            @pl.when(s < chips - 1)
+            def _():
+                ring(s, c).start()
+
+            side(s, c).start()
+        for c in range(cuts):
+            side(s, c).wait_recv()
+        first = chip_of((position - s * step + chips) % chips, chips) * 2 + lane
+        second = chip_of((position + s * step + chips) % chips, chips) * 2 + 1 - lane
+        use(s, first, second)
+        return carry
+
+    lax.fori_loop(0, chips, one, 0)
+
+    def close(s, carry):
+        for c in range(cuts):
+            side(s, c).wait_send()
+
+            @pl.when(s < chips - 1)
+            def _():
+                ring(s, c).wait_send()
+
+        return carry
+
+    lax.fori_loop(0, chips, close, 0)
+
+
+def gather_scratch(count, cuts, block, columns):
+    chips = count // 2
+    return [pltpu.VMEM((chips, 2 * block, columns), BF16)] + [
+        pltpu.SemaphoreType.DMA((chips, cuts))
+    ] * 4
+
+
+def scatter_steps(count, cuts, o_ref, bufs, sems, produce, extra=None):
+    me, chips, lane, position, step, following, previous, sibling = places(count)
+    own, sent, came, give, given = bufs
+    ring_out, ring_in, side_out, side_in = sems
+    rows = own.shape[0] // cuts
+    greet((previous, sibling))
 
     def ring(k, c):
+        part = pl.ds(c * rows, rows)
         return pltpu.make_async_remote_copy(
-            src_ref=sent.at[k, pl.ds(c * rows, rows)],
-            dst_ref=came.at[k, pl.ds(c * rows, rows)],
+            src_ref=sent.at[k, part],
+            dst_ref=came.at[k, part],
             send_sem=ring_out.at[k, c],
             recv_sem=ring_in.at[k, c],
             device_id={"seq": following},
@@ -144,7 +219,7 @@
 
     def side(k):
         return pltpu.make_async_remote_copy(
-            src_ref=p_ref.at[sibling_block(k)],
+            src_ref=give.at[k],
             dst_ref=given.at[k],
             send_sem=side_out.at[k],
             recv_sem=side_in.at[k],
@@ -152,60 +227,434 @@
             device_id_type=MESH,
         )
 
-    def load(k):
-        return pltpu.make_async_copy(p_ref.at[my_block(k)], own.at[k], own_sem.at[k])
-
-    for k in range(chips):
+    def one(k, carry):
+        first = chip_of((position - (k + 1) * step + chips) % chips, chips) * 2 + lane
+        second = chip_of((position + (k + 1) * step + chips) % chips, chips) * 2 + 1 - lane
+        mine, theirs = produce(k, first, second)
+        give[k] = theirs.astype(BF16)
         side(k).start()
-        load(k).start()
-    for k in range(chips):
-        load(k).wait()
+        own[...] = mine
         side(k).wait_recv()
         for c in range(cuts):
             part = pl.ds(c * rows, rows)
-            total = own[k, part].astype(F32) + given[k, part].astype(F32)
-            if k > 0:
+
+            @pl.when(k > 0)
+            def _():
                 ring(k - 1, c).wait_recv()
-                total = total + came[k - 1, part].astype(F32)
-            if k < chips - 1:
+                own[part] += came[k - 1, part].astype(F32)
+
+            total = own[part] + given[k, part].astype(F32)
+
+            @pl.when(k < chips - 1)
+            def _():
                 sent[k, part] = total.astype(BF16)
                 ring(k, c).start()
-            else:
+
+            @pl.when(k == chips - 1)
+            def _():
                 o_ref[part] = total
-    for k in range(chips):
+
+        if extra is not None:
+            extra(k)
+        return carry
+
+    lax.fori_loop(0, chips, one, 0)
+
+    def close(k, carry):
         side(k).wait_send()
-        if k < chips - 1:
+
+        @pl.when(k < chips - 1)
+        def _():
             for c in range(cuts):
                 ring(k, c).wait_send()
 
-
-def scatter_seq(p, count, call, cuts=2):
+        return carry
+
+    lax.fori_loop(0, chips, close, 0)
+
+
+def scatter_scratch(count, cuts, rows, columns):
     chips = count // 2
-    _, rows, columns = p.shape
+    dma = pltpu.SemaphoreType.DMA
+    return [
+        pltpu.VMEM((rows, columns), F32),
+        pltpu.VMEM((chips - 1, rows, columns), BF16),
+        pltpu.VMEM((chips - 1, rows, columns), BF16),
+        pltpu.VMEM((chips, rows, columns), BF16),
+        pltpu.VMEM((chips, rows, columns), BF16),
+        dma((chips, cuts)),
+        dma((chips, cuts)),
+        dma((chips,)),
+        dma((chips,)),
+    ]
+
+
+def remote_params(call, mib):
+    return pltpu.CompilerParams(
+        collective_id=call, has_side_effects=True, vmem_limit_bytes=mib * MIB
+    )
+
+
+VMEM = pl.BlockSpec(memory_space=pltpu.VMEM)
+ANY = pl.BlockSpec(memory_space=pl.ANY)
+
+
+def project_kernel(count, cuts, h_ref, w_ref, all_ref, y_ref, land, *rest):
+    sems, out_sem = rest[:4], rest[4]
+    block = h_ref.shape[0]
+
+    def out(s, owner, half):
+        return pltpu.make_async_copy(
+            land.at[s, pl.ds(half * block, block)],
+            all_ref.at[pl.ds(pl.multiple_of(owner * block, block), block)],
+            out_sem.at[half],
+        )
+
+    def use(s, first, second):
+        out(s, first, 0).start()
+        out(s, second, 1).start()
+        y = mm(land[s], w_ref[...]).astype(BF16)
+        y_ref[pl.ds(pl.multiple_of(first * block, block), block), :] = y[:block]
+        y_ref[pl.ds(pl.multiple_of(second * block, block), block), :] = y[block:]
+
+    gather_steps(count, cuts, h_ref, land, sems, use)
+    half_rows = all_ref.shape[0] // 2
+    for half in range(2):
+        pltpu.make_async_copy(
+            all_ref.at[pl.ds(0, half_rows)], all_ref.at[pl.ds(0, half_rows)], out_sem.at[half]
+        ).wait()
+
+
+def project_gathered(h, w, count, call, cuts=4):
+    block, dim = h.shape
     return pl.pallas_call(
-        functools.partial(scatter_kernel, count, cuts),
-        out_shape=jax.ShapeDtypeStruct((rows, columns), F32),
-        in_specs=[pl.BlockSpec(memory_space=pl.ANY)],
-        out_specs=pl.BlockSpec(memory_space=pltpu.VMEM),
-        scratch_shapes=[
-            pltpu.VMEM((chips, rows, columns), BF16),
-            pltpu.VMEM((chips - 1, rows, columns), BF16),
-            pltpu.VMEM((chips - 1, rows, columns), BF16),
-            pltpu.VMEM((chips, rows, columns), BF16),
-            pltpu.SemaphoreType.DMA((chips,)),
-            pltpu.SemaphoreType.DMA((chips, cuts)),
-            pltpu.SemaphoreType.DMA((chips, cuts)),
-            pltpu.SemaphoreType.DMA((chips,)),
-            pltpu.SemaphoreType.DMA((chips,)),
-        ],
-        compiler_params=pltpu.CompilerParams(
-            collective_id=call, has_side_effects=True, vmem_limit_bytes=48 * MIB
+        functools.partial(project_kernel, count, cuts),
+        out_shape=(
+            jax.ShapeDtypeStruct((count * block, dim), BF16),
+            jax.ShapeDtypeStruct((count * block, w.shape[1]), BF16),
         ),
-    )(p)
-
-
-NT = (((1,), (1,)), ((), ()))
-TN = (((0,), (0,)), ((), ()))
+        in_specs=[VMEM, VMEM],
+        out_specs=[ANY, VMEM],
+        scratch_shapes=gather_scratch(count, cuts, block, dim) + [pltpu.SemaphoreType.DMA((2,))],
+        compiler_params=remote_params(call, 48),
+    )(h, w)
+
+
+def out_back_kernel(count, cuts, da_ref, w_ref, o_ref, do_ref, part_ref, land, *rest):
+    sems, total = rest[:4], rest[4]
+    block = da_ref.shape[0]
+    total[...] = jnp.zeros_like(total)
+
+    def use(s, first, second):
+        pair = land[s]
+        a = pl.ds(pl.multiple_of(first * block, block), block)
+        b = pl.ds(pl.multiple_of(second * block, block), block)
+        do = mm(pair, w_ref[...], NT).astype(BF16)
+        do_ref[a, :] = do[:block]
+        do_ref[b, :] = do[block:]
+        total[...] += mm(jnp.concatenate([o_ref[a, :], o_ref[b, :]], axis=0), pair, TN)
+
+    gather_steps(count, cuts, da_ref, land, sems, use)
+    part_ref[...] = total[...].astype(BF16)
+
+
+def out_back(da, w, o, count, call, cuts=4):
+    block, dim = da.shape
+    return pl.pallas_call(
+        functools.partial(out_back_kernel, count, cuts),
+        out_shape=(jax.ShapeDtypeStruct(o.shape, BF16), jax.ShapeDtypeStruct(w.shape, BF16)),
+        in_specs=[VMEM] * 3,
+        out_specs=[VMEM] * 2,
+        scratch_shapes=gather_scratch(count, cuts, block, dim) + [pltpu.VMEM(w.shape, F32)],
+        compiler_params=remote_params(call, 48),
+    )(da, w, o)
+
+
+def product_kernel(count, cuts, dims, y_ref, w_ref, o_ref, *rest):
+    block = o_ref.shape[0]
+
+    def produce(k, first, second):
+        a = y_ref[pl.ds(pl.multiple_of(first * block, block), block), :]
+        b = y_ref[pl.ds(pl.multiple_of(second * block, block), block), :]
+        both = mm(jnp.concatenate([a, b], axis=0), w_ref[...], dims)
+        return both[:block], both[block:]
+
+    scatter_steps(count, cuts, o_ref, rest[:5], rest[5:], produce)
+
+
+def product_scattered(y, w, dims, count, call, cuts=2):
+    block = y.shape[0] // count
+    columns = w.shape[1 - dims[0][1][0]]
+    return pl.pallas_call(
+        functools.partial(product_kernel, count, cuts, dims),
+        out_shape=jax.ShapeDtypeStruct((block, columns), F32),
+        in_specs=[VMEM, VMEM],
+        out_specs=VMEM,
+        scratch_shapes=scatter_scratch(count, cuts, block, columns),
+        compiler_params=remote_params(call, 48),
+    )(y, w)
+
+
+def one_hot_of(slot_ref, first, second, capacity):
+    a = slot_ref[pl.ds(first, 1), :]
+    b = slot_ref[pl.ds(second, 1), :]
+    wanted = jnp.concatenate([a, jnp.where(b >= 0, b + capacity, -1)], axis=1)
+    row = lax.broadcasted_iota(jnp.int32, (2 * capacity, wanted.shape[1]), 0)
+    return jnp.where(row == wanted, 1.0, 0.0).astype(BF16)
+
+
+def expert_kernel(
+    count,
+    cuts,
+    capacity,
+    h_ref,
+    slot_ref,
+    chosen_ref,
+    router_ref,
+    dy_ref,
+    wg_ref,
+    wu_ref,
+    wd_ref,
+    xs_out,
+    de_out,
+    dx_out,
+    ce_out,
+    hid_out,
+    dgu_out,
+    land,
+    ring_out,
+    ring_in,
+    side_out,
+    side_in,
+    wg,
+    wu,
+    wd,
+    dyb,
+    xs,
+    de,
+    dx,
+    ce,
+    hid,
+    dgu,
+    w_sem,
+    dy_sem,
+    out_sem,
+):
+    block, dim = h_ref.shape
+    ffe = wg.shape[1]
+    me, chips, lane, position, step, _, _, _ = places(count)
+    weights = [
+        pltpu.make_async_copy(src, dst, w_sem.at[i])
+        for i, (src, dst) in enumerate(((wg_ref, wg), (wu_ref, wu), (wd_ref, wd)))
+    ]
+    staged = ((xs, xs_out), (de, de_out), (dx, dx_out), (ce, ce_out), (hid, hid_out), (dgu, dgu_out))
+
+    def dy_copies(s):
+        first = chip_of((position - s * step + chips) % chips, chips) * 2 + lane
+        second = chip_of((position + s * step + chips) % chips, chips) * 2 + 1 - lane
+        return [
+            pltpu.make_async_copy(
+                dy_ref.at[owner], dyb.at[s % 2, pl.ds(half * block, block)], dy_sem.at[s % 2, half]
+            )
+            for half, owner in ((0, first), (1, second))
+        ]
+
+    for copy in weights + dy_copies(0):
+        copy.start()
+
+    def use(s, first, second):
+        @pl.when(s == 0)
+        def _():
+            for copy in weights:
+                copy.wait()
+
+        @pl.when(s < chips - 1)
+        def _():
+            for copy in dy_copies(s + 1):
+                copy.start()
+
+        for copy in dy_copies(s):
+            copy.wait()
+        rows = pl.ds(pl.multiple_of(s * 2 * capacity, 16), 2 * capacity)
+        pick = one_hot_of(slot_ref, first, second, capacity)
+        x = mm(pick, land[s]).astype(BF16)
+        xs[rows, :] = x
+        chosen = mm(
+            pick,
+            jnp.concatenate(
+                [
+                    chosen_ref[pl.ds(pl.multiple_of(first * block, block), block), :],
+                    chosen_ref[pl.ds(pl.multiple_of(second * block, block), block), :],
+                ],
+                axis=0,
+            ),
+        )
+        logits = jnp.where(chosen > 0.5, mm(x, router_ref[...]), -1e30)
+        weight = jnp.exp(logits - jnp.max(logits, axis=1, keepdims=True)) * chosen
+        mass = jnp.sum(weight, axis=1, keepdims=True)
+        expert_lane = lax.broadcasted_iota(jnp.int32, weight.shape, 1)
+        gate = jnp.sum(jnp.where(expert_lane == me, weight, 0.0), axis=1, keepdims=True)
+        gate = gate / jnp.where(mass > 0.0, mass, 1.0)
+        g = mm(x, wg[...])
+        u = mm(x, wu[...])
+        sig = jax.nn.sigmoid(g)
+        silu = g * sig
+        h = (silu * u).astype(BF16)
+        hid[rows, :] = h
+        e = mm(h, wd[...])
+        ce[rows, :] = (gate * e).astype(BF16)
+        dys = mm(pick, dyb[s % 2])
+        dgate = jnp.sum(dys * e, axis=1, keepdims=True)
+        d = (gate * dys).astype(BF16)
+        de[rows, :] = d
+        dh = mm(d, wd[...], NT)
+        dg = (dh * u * (sig + silu * (1.0 - sig))).astype(BF16)
+        du = (dh * silu).astype(BF16)
+        dgu[rows, :ffe] = dg
+        dgu[rows, ffe:] = du
+        dx[rows, :dim] = (mm(dg, wg[...], NT) + mm(du, wu[...], NT)).astype(BF16)
+        high = dgate.astype(BF16).astype(F32)
+        dx[rows, dim:] = jnp.where(
+            expert_lane == me, high, jnp.where(expert_lane == me + 64, dgate - high, 0.0)
+        ).astype(BF16)
+        for i, (src, dst) in enumerate(staged):
+            pltpu.make_async_copy(src.at[rows], dst.at[rows], out_sem.at[i]).start()
+
+    gather_steps(count, cuts, h_ref, land, (ring_out, ring_in, side_out, side_in), use)
+    for i, (src, dst) in enumerate(staged):
+        pltpu.make_async_copy(src, dst, out_sem.at[i]).wait()
+
+
+def expert_gathered(h2, slot, chosen, router, dy_all, wg, wu, wd, capacity, count, call, cuts=4):
+    block, dim = h2.shape
+    ffe = wg.shape[1]
+    total = count * capacity
+    widths = (dim, dim, dim + 128, dim, ffe, 2 * ffe)
+    dma = pltpu.SemaphoreType.DMA
+    return pl.pallas_call(
+        functools.partial(expert_kernel, count, cuts, capacity),
+        out_shape=[jax.ShapeDtypeStruct((total, n), BF16) for n in widths],
+        in_specs=[VMEM] * 4 + [ANY] * 4,
+        out_specs=[ANY] * 6,
+        scratch_shapes=gather_scratch(count, cuts, block, dim)
+        + [
+            pltpu.VMEM(wg.shape, BF16),
+            pltpu.VMEM(wu.shape, BF16),
+            pltpu.VMEM(wd.shape, BF16),
+            pltpu.VMEM((2, 2 * block, dim), BF16),
+        ]
+        + [pltpu.VMEM((total, n), BF16) for n in widths]
+        + [dma((3,)), dma((2, 2)), dma((6,))],
+        compiler_params=remote_params(call, 60),
+    )(h2, slot, chosen, router, dy_all, wg, wu, wd)
+
+
+def slots_kernel(count, cuts, capacity, slot_ref, rows_ref, o_ref, *rest):
+    bufs, sems, held, held_sem = rest[:5], rest[5:9], rest[9], rest[10]
+    chips = count // 2
+    block = o_ref.shape[0]
+    load = pltpu.make_async_copy(rows_ref, held, held_sem)
+    load.start()
+
+    def produce(k, first, second):
+        @pl.when(k == 0)
+        def _():
+            load.wait()
+
+        pair = pl.multiple_of((k + 1) % chips * 2 * capacity, 16)
+        pick = one_hot_of(slot_ref, first, second, capacity)
+        both = mm(pick, held[pl.ds(pair, 2 * capacity), :], TN)
+        return both[:block], both[block:]
+
+    scatter_steps(count, cuts, o_ref, bufs, sems, produce)
+
+
+def slots_scattered(rows, slot, capacity, count, call, cuts=2):
+    block = slot.shape[1]
+    columns = rows.shape[1]
+    return pl.pallas_call(
+        functools.partial(slots_kernel, count, cuts, capacity),
+        out_shape=jax.ShapeDtypeStruct((block, columns), F32),
+        in_specs=[VMEM, ANY],
+        out_specs=VMEM,
+        scratch_shapes=scatter_scratch(count, cuts, block, columns)
+        + [pltpu.VMEM(rows.shape, BF16), pltpu.SemaphoreType.DMA],
+        compiler_params=remote_params(call, 48),
+    )(slot, rows)
+
+
+def slots_back_kernel(
+    count, cuts, capacity, slot_ref, dx_ref, xs_ref, de_ref, hid_ref, dgu_ref, o_ref, gu_out, down_out, *rest
+):
+    bufs, sems = rest[:5], rest[5:9]
+    dx, xs, de, hid, dgu, gu, down, sem, gu_sem, down_sem = rest[9:]
+    chips = count // 2
+    block = o_ref.shape[0]
+    loads = [
+        pltpu.make_async_copy(src, dst, sem.at[i])
+        for i, (src, dst) in enumerate(
+            ((dx_ref, dx), (xs_ref, xs), (dgu_ref, dgu), (hid_ref, hid), (de_ref, de))
+        )
+    ]
+    for load in loads:
+        load.start()
+    part = xs.shape[1] // chips
+    down_part = 256
+    downs = hid.shape[1] // down_part
+
+    def produce(k, first, second):
+        @pl.when(k == 0)
+        def _():
+            loads[0].wait()
+
+        pair = pl.multiple_of((k + 1) % chips * 2 * capacity, 16)
+        pick = one_hot_of(slot_ref, first, second, capacity)
+        both = mm(pick, dx[pl.ds(pair, 2 * capacity), :], TN)
+        return both[:block], both[block:]
+
+    def extra(k):
+        @pl.when(k == 0)
+        def _():
+            for load in loads[1:]:
+                load.wait()
+
+        columns = pl.ds(pl.multiple_of(k * part, 128), part)
+        rows = pl.ds(pl.multiple_of(k * part, 16), part)
+        gu[rows, :] = mm(xs[:, columns], dgu[...], TN).astype(BF16)
+        pltpu.make_async_copy(gu.at[rows], gu_out.at[rows], gu_sem).start()
+
+        @pl.when((k % 2 == 0) & (k // 2 < downs))
+        def _():
+            start = pl.multiple_of(k // 2 * down_part, 128)
+            down_rows = pl.ds(start, down_part)
+            down[down_rows, :] = mm(hid[:, down_rows], de[...], TN).astype(BF16)
+            pltpu.make_async_copy(down.at[down_rows], down_out.at[down_rows], down_sem).start()
+
+    scatter_steps(count, cuts, o_ref, bufs, sems, produce, extra)
+    pltpu.make_async_copy(gu, gu_out, gu_sem).wait()
+    pltpu.make_async_copy(down, down_out, down_sem).wait()
+
+
+def slots_back(slot, dx, xs, de, hid, dgu, capacity, count, call, cuts=2):
+    block = slot.shape[1]
+    columns = dx.shape[1]
+    dim, ffe = xs.shape[1], hid.shape[1]
+    dma = pltpu.SemaphoreType.DMA
+    return pl.pallas_call(
+        functools.partial(slots_back_kernel, count, cuts, capacity),
+        out_shape=(
+            jax.ShapeDtypeStruct((block, columns), F32),
+            jax.ShapeDtypeStruct((dim, 2 * ffe), BF16),
+            jax.ShapeDtypeStruct((ffe, dim), BF16),
+        ),
+        in_specs=[VMEM] + [ANY] * 5,
+        out_specs=[VMEM, ANY, ANY],
+        scratch_shapes=scatter_scratch(count, cuts, block, columns)
+        + [pltpu.VMEM(a.shape, BF16) for a in (dx, xs, de, hid, dgu)]
+        + [pltpu.VMEM((dim, 2 * ffe), BF16), pltpu.VMEM((ffe, dim), BF16)]
+        + [dma((5,)), dma, dma],
+        compiler_params=remote_params(call, 60),
+    )(slot, dx, xs, de, hid, dgu)
 
 
 def split3(x):
@@ -577,10 +1026,6 @@
     return jnp.cos(phases), jnp.sin(phases)
 
 
-def dot(a, b, dims=(((1,), (0,)), ((), ()))):
-    return lax.dot_general(a, b, dims, preferred_element_type=F32)
-
-
 def per_device(
     activations,
     cotangent,
@@ -655,8 +1100,9 @@
 
     r1 = lax.rsqrt(jnp.mean(x * x, axis=-1, keepdims=True) + EPSILON)
     h1 = (x * r1 * g_attn).astype(BF16)
-    h1_all = gather_seq([h1], count, 1, (4,))[0].reshape(span, dim)
-    qkv = dot(h1_all, w_qkv).astype(BF16)
+    dy_all, routes_all = gather_seq([dy, routes], count, 4, (4, 1))
+    h1, dy_all = lax.optimization_barrier((h1, dy_all))
+    h1_all, qkv = project_gathered(h1, w_qkv, count, 1)
     position, doc_start = run_starts(segment)
     cosine, sine = angles((position - doc_start).astype(F32), hd)
     start = jnp.where(segment > 0, doc_start, position)
@@ -664,16 +1110,12 @@
     cos_full = jnp.concatenate([cosine, cosine], axis=1)
     sin_full = jnp.concatenate([-sine, sine], axis=1)
     o, qx, kn = attend(qkv, g_query, g_key, cos_full, sin_full, start)
-    x2_parts = dot(o, w_o).astype(BF16).reshape(count, tok, dim)
-    x2 = x + scatter_seq(x2_parts, count, 2)
+    x2 = x + product_scattered(o, w_o, NN, count, 2)
 
     r2 = lax.rsqrt(jnp.mean(x2 * x2, axis=-1, keepdims=True) + EPSILON)
     h2 = (x2 * r2 * g_mlp).astype(BF16)
-    h2_all = gather_seq([h2], count, 3, (4,))[0]
-    dy_all, routes_all = gather_seq([dy, routes], count, 4, (4, 1))
-
     def gates_of(hidden, chosen):
-        logits = dot(hidden, router)
+        logits = mm(hidden, router)
         return jax.nn.softmax(jnp.where(chosen, logits, -1e30), axis=-1) * chosen
 
     def chosen_of(named):
@@ -682,75 +1124,33 @@
 
     hit = jnp.any(routes_all == me, axis=-1)
     rank = jnp.cumsum(hit.astype(jnp.int32), axis=1) - hit
-    slots = jnp.arange(capacity, dtype=jnp.int32)
-    pick = hit[:, None, :] & (rank[:, None, :] == slots[None, :, None])
-    one_hot = pick.astype(BF16)
-    gates_all = gates_of(h2_all.reshape(span, dim), chosen_of(routes_all.reshape(span, top)))
-    gate_tok = lax.dynamic_index_in_dim(gates_all, me, 1, keepdims=False).reshape(count, tok)
-    gate_slot = jnp.sum(jnp.where(pick, gate_tok[:, None, :], 0.0), axis=-1).reshape(-1, 1)
-
-    def to_slots(rows):
-        return (
-            jnp.einsum("bri,bid->brd", one_hot, rows, preferred_element_type=F32)
-            .astype(BF16)
-            .reshape(count * capacity, dim)
-        )
-
-    def to_tokens(rows):
-        return jnp.einsum(
-            "bri,brd->bid",
-            one_hot,
-            rows.reshape(count, capacity, dim),
-            preferred_element_type=F32,
-        )
-
-    xs = to_slots(h2_all)
-    dys = to_slots(dy_all)
-    gate_act = dot(xs, wg)
-    up_act = dot(xs, wu)
-    sig = jax.nn.sigmoid(gate_act)
-    silu = gate_act * sig
-    inner = (silu * up_act).astype(BF16)
-    e_out = dot(inner, wd)
-    mixed_parts = to_tokens((gate_slot * e_out).astype(BF16)).astype(BF16)
-    mixed = x2 + scatter_seq(mixed_parts, count, 5)
-
-    dgate_slot = jnp.sum(dys.astype(F32) * e_out, axis=-1).reshape(count, capacity)
-    dgate_tok = jnp.sum(jnp.where(pick, dgate_slot[:, :, None], 0.0), axis=1)
-    de = (gate_slot * dys.astype(F32)).astype(BF16)
-    dinner = dot(de, wd, NT)
-    dg = (dinner * up_act * (sig + silu * (1.0 - sig))).astype(BF16)
-    du = (dinner * silu).astype(BF16)
-    w_down_part = dot(inner, de, TN)
-    w_gate_part = dot(xs, dg, TN)
-    w_up_part = dot(xs, du, TN)
-    dxs = (dot(dg, wg, NT) + dot(du, wu, NT)).astype(BF16)
-    own_lane = (jnp.arange(128, dtype=jnp.int32) == me)[None, None, :]
-    dgate_hi, dgate_lo, _ = split3(dgate_tok[:, :, None])
-    zero = jnp.zeros((), BF16)
-    lanes = jnp.where(own_lane, dgate_hi, zero) + jnp.where(
-        jnp.roll(own_lane, 64, axis=-1), dgate_lo, zero
-    )
-    dh2_parts = jnp.concatenate([to_tokens(dxs).astype(BF16), lanes], axis=2)
-    dh2_wide = scatter_seq(dh2_parts, count, 6)
+    slot = jnp.where(hit & (rank < capacity), rank, -1)
+    chosen_all = chosen_of(routes_all.reshape(span, top)).astype(BF16)
+    chosen_all = jnp.pad(chosen_all, ((0, 0), (0, 128 - experts)))
+    router_wide = jnp.pad(router, ((0, 0), (0, 128 - experts)))
+    xs, de, dxs, ce, hid, dgu = expert_gathered(
+        h2, slot, chosen_all, router_wide, dy_all, wg, wu, wd, capacity, count, 3
+    )
+    dh2_wide, w_gate_up_part, w_down_part = slots_back(
+        slot, dxs, xs, de, hid, dgu, capacity, count, 6
+    )
+    mixed = x2 + slots_scattered(ce, slot, capacity, count, 5)
     dgate = dh2_wide[:, dim : dim + experts] + dh2_wide[:, dim + 64 : dim + 64 + experts]
     gates = gates_of(h2, chosen_of(routes))
     dlogits = (gates * (dgate - jnp.sum(gates * dgate, axis=-1, keepdims=True))).astype(BF16)
-    dh2 = dh2_wide[:, :dim] + dot(dlogits, router, NT)
-    router_part = dot(h2, dlogits, TN)
+    dh2 = dh2_wide[:, :dim] + mm(dlogits, router, NT)
+    router_part = mm(h2, dlogits, TN)
     xh = x2 * r2
     mlp_gain_part = jnp.sum(dh2 * xh, axis=0)
     dn = dh2 * g_mlp
     dx2 = dy.astype(F32) + r2 * (dn - xh * jnp.mean(dn * xh, axis=-1, keepdims=True))
 
-    da_all = gather_seq([dx2.astype(BF16)], count, 7, (4,))[0].reshape(span, dim)
-    do = dot(da_all, w_o, NT).astype(BF16)
-    w_out_part = dot(o, da_all, TN).astype(BF16)
+    do, w_out_part = out_back(dx2.astype(BF16), w_o, o, count, 7)
     dqkv, head_gains = attend_back(
         qx, kn, qkv, o, do, g_query, g_key, cos_full, sin_full, start
     )
-    qkv_part = dot(h1_all, dqkv, TN).astype(BF16)
-    dh1 = scatter_seq(dot(dqkv, w_qkv, NT).astype(BF16).reshape(count, tok, dim), count, 8)
+    qkv_part = mm(h1_all, dqkv, TN).astype(BF16)
+    dh1 = product_scattered(dqkv, w_qkv, NT, count, 8)
     xh1 = x * r1
     dn1 = dh1 * g_attn
     input_grad = dx2 + r1 * (dn1 - xh1 * jnp.mean(dn1 * xh1, axis=-1, keepdims=True))
@@ -758,8 +1158,9 @@
     def sum_fsdp(part, axis):
         return lax.psum_scatter(part.astype(BF16), "fsdp", scatter_dimension=axis, tiled=True)
 
-    w_gate_grad = sum_fsdp(w_gate_part, 0).astype(F32)
-    w_up_grad = sum_fsdp(w_up_part, 0).astype(F32)
+    w_gate_up_grad = sum_fsdp(w_gate_up_part, 0).astype(F32)
+    w_gate_grad = w_gate_up_grad[:, : wg.shape[1]]
+    w_up_grad = w_gate_up_grad[:, wg.shape[1] :]
     w_down_grad = sum_fsdp(w_down_part, 1).astype(F32)
 
     small_part = jnp.concatenate(

time: 828 us -> 722 us (0.87)
  matrix products: 160 us -> 10.8 us
  Pallas kernels: 537 us -> 572 us
  other arithmetic: 69.1 us -> 43.2 us
  waiting for transfers between devices: 2.1 us -> 26.7 us
  local copies, waits for them, and re-layouts: 26.9 us -> 38.6 us
    pallas_call x4 -> x7, Pallas kernels: 186 us -> 358 us  [the longest x2 94 us: product_scattered(): pl.pallas_call(functools.partial(product_kernel, count, cuts, dims), out_...]
    dot_general x23 -> x4, matrix products: 160 us -> 10.8 us  [mm(): return lax.dot_general(a, b, dims, preferred_element_type=F32)]
    pallas_call x5 -> x2, Pallas kernels: 239 us -> 102 us  [gather_seq(): pl.pallas_call(functools.partial(gather_kernel, count, cuts), out_shape=[...]
    all_gather x1, waiting for transfers between devices: 0.01 us -> 18.7 us  [per_device(): wd = lax.all_gather(w_down[0], 'fsdp', axis=1, tiled=True)]
    convert_element_type x3 -> x2, other arithmetic: 14 us -> 3.1 us  [the longest x1 2.75 us: per_device(): w_gate_up_grad = sum_fsdp(w_gate_up_part, 0).astype(F32)]
    unnamed x83 -> x89, local copies, waits for them, and re-layouts: 7.05 us -> 15.5 us
  transfers between devices with their start and end apart: 12 -> 11, of which waited for: 1 -> 2; matrix products, arithmetic and copies ran while one was open for 21% -> 9% of each run, Pallas kernels for 54% -> 56%
where the time goes in v3:
time: 722 us; the launch traced here: 714 us
  Pallas kernels  572 us (79%)
  other arithmetic  43.2 us (6%)
  local copies, waits for them, and re-layouts  38.6 us (5%)
  waiting for transfers between devices  26.7 us (4%)
  between operations  15.1 us (2%)
  matrix products  10.8 us (1%)
    pallas_call x2, Pallas kernels, gather_seq(): pl.pallas_call(functools.partial(gather_kernel, count, cuts), out_shape=[...  102 us
    pallas_call x2, Pallas kernels, product_scattered(): pl.pallas_call(functools.partial(product_kernel, count, cuts, dims), out_...  94 us
    pallas_call x1, Pallas kernels, expert_gathered(): pl.pallas_call(functools.partial(expert_kernel, count, cuts, capacity), o...  65.2 us
    pallas_call x1, Pallas kernels, last_gather(): pl.pallas_call(functools.partial(last_gather_kernel, count, members, cuts...  61.8 us
    pallas_call x1, Pallas kernels, slots_back(): pl.pallas_call(functools.partial(slots_back_kernel, count, cuts, capacity...  59.1 us
    pallas_call x1, Pallas kernels, slots_scattered(): pl.pallas_call(functools.partial(slots_kernel, count, cuts, capacity), ou...  47 us
    pallas_call x1, Pallas kernels, project_gathered(): pl.pallas_call(functools.partial(project_kernel, count, cuts), out_shape=...  46.6 us
    pallas_call x1, Pallas kernels, out_back(): pl.pallas_call(functools.partial(out_back_kernel, count, cuts), out_shape...  46.3 us
  transfers between devices with their start and end apart: 11, of which 2 were waited for; matrix products, arithmetic and copies ran while one was open for 9% of the time, Pallas kernels for 56%

profile of v3, /device:TPU:0, one launch (start us, length us, event | category | flops | bytes accessed | tf_op | source)
XLA Modules:
  0.0 713.8 jit_solution(18130807231656298731)
XLA Ops:
  15.5 5.9 all-gather.7
  23.0 51.0 %shard_map.263 = (bf16[16,128,2048]{2,1,0:T(8,128)(2,1)}, s32[16,128,8]{2,1,0:T(8,128)}) custom-call(bf16[128,2048]{1,0:T(8,128)(2,1)} %bitcast.80, s32[128,8]{1,0:T(8,128)} %bitcast.92), custom_call_target="tpu_custom_call" | custom-call | tf_op jit(solution)/shard_map/pallas_call | solution.py:111
  81.2 3.7 fusion.14
  89.0 46.6 %shard_map.264 = (bf16[2048,2048]{1,0:T(8,128)(2,1)}, bf16[2048,512]{1,0:T(8,128)(2,1)S(1)}) custom-call(bf16[128,2048]{1,0:T(8,128)(2,1)S(1)} %fusion.5.h_ref, bf16[2048,512]{1,0:T(8,128)(2,1)S(1)} %copy-done.3), custom_call_target="tpu_custom_call" | custom-call | tf_op jit(solution)/shard_map/pallas_call | solution.py:330
  136.9 12.6 %shard_map.265 = (bf16[2048,256]{1,0:T(8,128)(2,1)S(1)}, bf16[2048,512]{1,0:T(8,128)(2,1)}, bf16[2048,128]{1,0:T(8,128)(2,1)S(1)}) custom-call(bf16[2048,512]{1,0:T(8,128)(2,1)} %copy-done.5, f32[1,128]{1,0:T(1,128)S(1)} %reshape.276.gq_ref, f32[1,128]{1,0:T(1,128)S(1)} %reshape.277.gk_ref, f32[2048,128]{1,0:T(8,128)S(1)} %get-tuple-element.156.cos_ref, ...), custom_call_target="tpu_custom_call" | custom-call | tf_op jit(solution)/shard_map/pallas_call | solution.py:731
  152.0 48.2 %shard_map.266 = f32[128,2048]{1,0:T(8,128)S(1)} custom-call(bf16[2048,256]{1,0:T(8,128)(2,1)S(1)} %get-tuple-element.47.y_ref.o_ref, bf16[256,2048]{1,0:T(8,128)(2,1)S(1)} %dynamic-slice_bitcast_fusion.w_ref), custom_call_target="tpu_custom_call" | custom-call | tf_op jit(solution)/shard_map/pallas_call | solution.py:388
  202.3 18.7 %all-gather.24.cloned.1.call-done = bf16[1,768,2048]{2,1,0:T(8,128)(2,1)} async-done(((bf16[1,768,1024]{2,1,0:T(8,128)(2,1)}), bf16[1,768,2048]{2,1,0:T(8,128)(2,1)}) %all-gather.24.cloned.1.call-update) | async-done | bytes 3145744 | tf_op jit(solution)/shard_map/all_gather | solution.py:1099
  221.0 65.2 %shard_map.267 = (bf16[1152,2048]{1,0:T(8,128)(2,1)}, bf16[1152,2048]{1,0:T(8,128)(2,1)}, bf16[1152,2176]{1,0:T(8,128)(2,1)}, bf16[1152,2048]{1,0:T(8,128)(2,1)}...) custom-call(bf16[128,2048]{1,0:T(8,128)(2,1)} %copy-done.25, s32[16,128]{1,0:T(8,128)} %and_select_fusion.slot_ref, ...), custom_call_target="tpu_custom_call" | custom-call | tf_op jit(solution)/shard_map/pallas_call | solution.py:534
  286.2 59.1 %shard_map.269 = (f32[128,2176]{1,0:T(8,128)}, bf16[2048,1536]{1,0:T(8,128)(2,1)}, bf16[768,2048]{1,0:T(8,128)(2,1)}) custom-call(s32[16,128]{1,0:T(8,128)} %and_select_fusion.slot_ref, bf16[1152,2176]{1,0:T(8,128)(2,1)} %get-tuple-element.51.dx_ref, bf16[1152,2048]{1,0:T(8,128)(2,1)} %get-tuple-element.52.xs_ref, ...), custom_call_target="tpu_custom_call" | custom-call | tf_op jit(solution)/shard_map/pallas_call | solution.py:643
  350.7 46.3 %shard_map.270 = (bf16[2048,256]{1,0:T(8,128)(2,1)S(1)}, bf16[256,2048]{1,0:T(8,128)(2,1)}) custom-call(bf16[128,2048]{1,0:T(8,128)(2,1)S(1)} %fusion.21.da_ref, bf16[256,2048]{1,0:T(8,128)(2,1)S(1)} %dynamic-slice_bitcast_fusion.w_ref, bf16[2048,256]{1,0:T(8,128)(2,1)S(1)} %get-tuple-element.47.y_ref.o_ref), custom_call_target="tpu_custom_call" | custom-call | tf_op jit(solution)/shard_map/pallas_call | solution.py:363
  400.5 22.6 %shard_map.271 = (bf16[2048,512]{1,0:T(8,128)(2,1)}, f32[2,128]{1,0:T(2,128)}) custom-call(bf16[2048,512]{1,0:T(8,128)(2,1)} %get-tuple-element.57.qx_ref, bf16[2048,128]{1,0:T(8,128)(2,1)} %copy-done.13, bf16[2048,512]{1,0:T(8,128)(2,1)} %copy-done.5, bf16[2048,256]{1,0:T(8,128)(2,1)} %copy-done, bf16[2048,256]{1,0:T(8,128)(2,1)} %copy-done.12, ...), custom_call_target="tpu_custom_call" | custom-call | tf_op jit(solution)/shard_map/pallas_call | solution.py:830
  424.2 5.2 all-gather.26.cloned.1.call-done
  429.4 3.3 reduce_sum.99
  432.9 8.4 %convolution_convert_fusion = bf16[2048,512]{1,0:T(8,128)(2,1)S(1)} fusion(bf16[2048,2048]{1,0:T(8,128)(2,1)} %get-tuple-element.61, bf16[2048,512]{1,0:T(8,128)(2,1)S(1)} %copy-done.8), kind=kOutput, calls=%fused_computation.5 | convolution fusion | flops 4296015872 | bytes 12582912 | tf_op jit(solution)/shard_map/dot_general | solution.py:128
  445.0 2.4 copy-done.6
  447.3 47.0 %shard_map.268 = f32[128,2048]{1,0:T(8,128)S(1)} custom-call(s32[16,128]{1,0:T(8,128)S(1)} %copy-done.14, bf16[1152,2048]{1,0:T(8,128)(2,1)S(1)} %copy-done.6), custom_call_target="tpu_custom_call" | custom-call | tf_op jit(solution)/shard_map/pallas_call | solution.py:575
  494.4 45.8 %shard_map.272 = f32[128,2048]{1,0:T(8,128)S(1)} custom-call(bf16[2048,512]{1,0:T(8,128)(2,1)S(1)} %copy-done.8, bf16[2048,512]{1,0:T(8,128)(2,1)S(1)} %copy-done.4), custom_call_target="tpu_custom_call" | custom-call | tf_op jit(solution)/shard_map/pallas_call | solution.py:388
  546.7 50.8 %shard_map.275 = (bf16[16,128,2048]{2,1,0:T(8,128)(2,1)}, bf16[16,16,2048]{2,1,0:T(8,128)(2,1)}) custom-call(bf16[128,2048]{1,0:T(8,128)(2,1)} %dynamic-slice_bitcast_fusion.1.refs_0_, bf16[16,2048]{1,0:T(8,128)(2,1)} %reshape.271.refs_1_), custom_call_target="tpu_custom_call" | custom-call | tf_op jit(solution)/shard_map/pallas_call | solution.py:111
  600.6 11.8 %bitcast_convert_fusion = f32[2048,2048]{1,0:T(8,128)} fusion(bf16[16,128,2048]{2,1,0:T(8,128)(2,1)} %get-tuple-element.71), kind=kLoop, calls=%fused_computation | loop fusion | flops 4194304 | bytes 25165824 | tf_op jit(solution)/shard_map/convert_element_type | solution.py:1235
  616.3 61.8 %shard_map.273 = (bf16[16,1040,256]{2,1,0:T(8,128)(2,1)}, bf16[16,256,256]{2,1,0:T(8,128)(2,1)}) custom-call(bf16[1040,256]{1,0:T(8,128)(2,1)} %slice.80.q_ref, bf16[1024,256]{1,0:T(8,128)(2,1)} %slice.81.kv_ref), custom_call_target="tpu_custom_call" | custom-call | tf_op jit(solution)/shard_map/pallas_call | solution.py:933
  679.7 15.5 %shard_map.274 = (f32[1024,4096]{1,0:T(8,128)}, f32[1024,512]{1,0:T(8,128)}, f32[1024,512]{1,0:T(8,128)}, f32[1024,1]{1,0:T(8,128)S(1)}) custom-call(bf16[16,1040,256]{2,1,0:T(8,128)(2,1)} %get-tuple-element.63.q_ref, bf16[16,256,256]{2,1,0:T(8,128)(2,1)S(1)} %copy-done.9, bf16[1024,4096]{1,0:T(8,128)(2,1)} %wq_ref.1, bf16[1024,512]{1,0:T(8,128)(2,1)S(1)} %copy-done.11, ...), custom_call_target="tpu_custom_call" | custom-call | tf_op jit(solution)/shard_map/pallas_call | solution.py:993
  697.4 3.5 bitcast_convert_fusion.1
  700.8 2.8 convert_element_type.145
  703.6 3.2 slice_bitcast_fusion
  (196 shorter events, 57.2 us)
Async XLA Ops:
  7.2 80.2 %all-gather.16.cloned.1.call-start = ((), (), s32[]{:S(2)}) async-start(), calls=%async_computation.3 | async-start | bytes 3145728 | tf_op jit(solution)/shard_map/all_gather | solution.py:1090
  10.5 139.8 %all-gather.18.cloned.1.call-start = ((), (), s32[]{:S(2)}) async-start(), calls=%async_computation.7 | async-start | bytes 3145728 | tf_op jit(solution)/shard_map/all_gather | solution.py:1095
  13.0 189.3 %all-gather.20.cloned.1.call-start = ((), (), s32[]{:S(2)}) async-start(), calls=%async_computation.8 | async-start | bytes 4718592 | tf_op jit(solution)/shard_map/all_gather | solution.py:1097
  13.8 188.6 %all-gather.22.cloned.1.call-start = ((), (), s32[]{:S(2)}) async-start(), calls=%async_computation.9 | async-start | bytes 4718592 | tf_op jit(solution)/shard_map/all_gather | solution.py:1098
  14.4 206.7 %all-gather.24.cloned.1.call-start = ((), (), s32[]{:S(2)}) async-start(), calls=%async_computation.10 | async-start | bytes 4718592 | tf_op jit(solution)/shard_map/all_gather | solution.py:1099
  14.9 414.5 %all-gather.26.cloned.1.call-start = ((), (), s32[]{:S(2)}) async-start(), calls=%async_computation.11 | async-start | bytes 3145728 | tf_op jit(solution)/shard_map/all_gather | solution.py:1174
  74.1 62.8 %copy-start.15 = (f32[1,128]{1,0:T(1,128)}, f32[1,128]{1,0:T(1,128)S(1)}, u32[]{:S(2)}) copy-start(f32[1,128]{1,0:T(1,128)S(1)} %reshape.276.gq_ref) | copy-start | bytes 1540
  74.2 62.7 %copy-start.16 = (f32[1,128]{1,0:T(1,128)}, f32[1,128]{1,0:T(1,128)S(1)}, u32[]{:S(2)}) copy-start(f32[1,128]{1,0:T(1,128)S(1)} %reshape.277.gk_ref) | copy-start | bytes 1540
  86.1 50.8 %copy-start.1 = (f32[2048,128]{1,0:T(8,128)}, f32[2048,128]{1,0:T(8,128)S(1)}, u32[]{:S(2)}) copy-start(f32[2048,128]{1,0:T(8,128)S(1)} %get-tuple-element.156.cos_ref) | copy-start | bytes 3145732
  86.1 50.8 %copy-start.2 = (f32[2048,128]{1,0:T(8,128)}, f32[2048,128]{1,0:T(8,128)S(1)}, u32[]{:S(2)}) copy-start(f32[2048,128]{1,0:T(8,128)S(1)} %get-tuple-element.157.sin_ref) | copy-start | bytes 3145732
  89.0 48.0 %copy-start.7 = (s32[2048,1]{1,0:T(8,128)S(1)}, s32[2048,1]{1,0:T(8,128)}, u32[]{:S(2)}) copy-start(s32[2048,1]{1,0:T(8,128)} %iota_select_fusion.start_ref) | copy-start | bytes 24580
  150.3 200.4 %copy-start = (bf16[2048,256]{1,0:T(8,128)(2,1)}, bf16[2048,256]{1,0:T(8,128)(2,1)S(1)}, u32[]{:S(2)}) copy-start(bf16[2048,256]{1,0:T(8,128)(2,1)S(1)} %get-tuple-element.47.y_ref.o_ref) | copy-start | bytes 3145732
  150.3 49.9 %copy-start.18 = (bf16[1,128,2048]{2,1,0:T(8,128)(2,1)S(1)}, bf16[1,128,2048]{2,1,0:T(8,128)(2,1)}, u32[]{:S(2)}) copy-start(bf16[1,128,2048]{2,1,0:T(8,128)(2,1)} %param.16) | copy-start | bytes 1572868
  286.2 61.3 %copy-start.24 = (bf16[2048,16]{1,0:T(8,128)(2,1)S(1)}, bf16[2048,16]{1,0:T(8,128)(2,1)}, u32[]{:S(2)}) copy-start(bf16[2048,16]{1,0:T(8,128)(2,1)} %copy-done.22) | copy-start | bytes 196612
  398.0 144.2 %all-reduce.7.cloned.1.call-start = ((), (), s32[]{:S(2)}) async-start(), calls=%async_computation.13 | async-start | bytes 262144
  399.7 145.1 %all-gather.28.cloned.1.call-start = ((), (), s32[]{:S(2)}) async-start(), calls=%async_computation.12 | async-start | bytes 3145728 | tf_op jit(solution)/shard_map/all_gather | solution.py:1176
  432.7 179.7 %reduce-scatter.4.cloned.1.call-start = ((), (), s32[]{:S(2)}) async-start(), calls=%async_computation.4 | async-start | bytes 3194880 | tf_op jit(solution)/shard_map/reduce_scatter | solution.py:1159
  442.8 254.6 %reduce-scatter.8.cloned.1.call-start = ((), (), s32[]{:S(2)}) async-start(), calls=%async_computation.6 | async-start | bytes 4718592 | tf_op jit(solution)/shard_map/reduce_scatter | solution.py:1159
  443.4 257.4 %reduce-scatter.6.cloned.1.call-start = ((), (), s32[]{:S(2)}) async-start(), calls=%async_computation.5 | async-start | bytes 9437184 | tf_op jit(solution)/shard_map/reduce_scatter | solution.py:1159
  447.3 47.0 %copy-start.4 = (bf16[2048,512]{1,0:T(8,128)(2,1)S(1)}, bf16[2048,512]{1,0:T(8,128)(2,1)}, u32[]{:S(2)}) copy-start(bf16[2048,512]{1,0:T(8,128)(2,1)} %all-gather.16.cloned.1.call-done.w_ref) | copy-start | bytes 6291460
  494.4 46.1 %copy-start.21 = (f32[128,2048]{1,0:T(8,128)S(1)}, f32[128,2048]{1,0:T(8,128)}, u32[]{:S(2)}) copy-start(f32[128,2048]{1,0:T(8,128)} %copy-done.20) | copy-start | bytes 3145732
  494.4 46.1 %copy-start.28 = (bf16[1,128,2048]{2,1,0:T(8,128)(2,1)S(1)}, bf16[1,128,2048]{2,1,0:T(8,128)(2,1)}, u32[]{:S(2)}) copy-start(bf16[1,128,2048]{2,1,0:T(8,128)(2,1)} %param.17) | copy-start | bytes 1572868
  612.4 65.7 %copy-start.10 = (bf16[1024,512]{1,0:T(8,128)(2,1)S(1)}, bf16[1024,512]{1,0:T(8,128)(2,1)}, u32[]{:S(2)}) copy-start(bf16[1024,512]{1,0:T(8,128)(2,1)} %wv_ref.1) | copy-start | bytes 3145732
  612.4 65.7 %copy-start.11 = (bf16[1024,512]{1,0:T(8,128)(2,1)S(1)}, bf16[1024,512]{1,0:T(8,128)(2,1)}, u32[]{:S(2)}) copy-start(bf16[1024,512]{1,0:T(8,128)(2,1)} %wk_ref.1) | copy-start | bytes 3145732
  (26 other events, 117.6 us)
Sparse Core Ops, SparseCore 0:
  10.7 35.8 all-gather.15
  48.6 33.1 all-gather.17
  83.3 44.9 all-gather.19
  129.7 44.9 all-gather.21
  176.1 44.9 all-gather.23
  398.2 31.1 all-gather.25
  431.7 21.4 all-reduce.6
  455.2 10.5 all-gather.27
  468.7 33.6 reduce-scatter.3
  504.5 43.3 reduce-scatter.7
  550.4 77.0 reduce-scatter.5

commit v4 on v3

--- a/solution.py
+++ b/solution.py
@@ -38,11 +38,79 @@
     return me, chips, lane, position, step, following, previous, sibling
 
 
-def greet(senders):
+def greet(places_over_seq, shards=1):
     barrier = pltpu.get_barrier_semaphore()
-    for device in senders:
+    for device in places_over_seq:
         pl.semaphore_signal(barrier, inc=1, device_id={"seq": device}, device_id_type=MESH)
-    pl.semaphore_wait(barrier, len(senders))
+    for i in range(1, shards):
+        peer = (lax.axis_index("fsdp") + i) % shards
+        pl.semaphore_signal(barrier, inc=1, device_id={"fsdp": peer}, device_id_type=MESH)
+    pl.semaphore_wait(barrier, len(places_over_seq) + shards - 1)
+
+
+def crossing(shards, items, out_sems, in_sems, own_sems=None):
+    mine = lax.axis_index("fsdp")
+
+    def place(src, dst, axis):
+        if axis is None:
+            return dst.at[mine]
+        size = src.shape[axis]
+        part = pl.ds(pl.multiple_of(mine * size, 128 if axis else 16), size)
+        return dst.at[:, part] if axis else dst.at[part]
+
+    def own(n):
+        src, dst, axis = items[n]
+        return pltpu.make_async_copy(src, place(src, dst, axis), own_sems.at[n])
+
+    def send(n, i):
+        src, dst, axis = items[n]
+        return pltpu.make_async_remote_copy(
+            src_ref=src,
+            dst_ref=place(src, dst, axis),
+            send_sem=out_sems.at[n, i - 1],
+            recv_sem=in_sems.at[n, i - 1],
+            device_id={"fsdp": (mine + i) % shards},
+            device_id_type=MESH,
+        )
+
+    def start(n):
+        for i in range(1, shards):
+            send(n, i).start()
+        if own_sems is not None:
+            own(n).start()
+
+    def wait(n):
+        for i in range(1, shards):
+            send(n, i).wait()
+        if own_sems is not None:
+            own(n).wait()
+
+    return start, wait
+
+
+def crossing_scratch(shards, items):
+    dma = pltpu.SemaphoreType.DMA
+    return [dma((items, max(1, shards - 1))), dma((items, max(1, shards - 1)))]
+
+
+def spread_units(units, steps):
+    total = sum(weight for weight, _ in units)
+    plan = [[] for _ in range(steps)]
+    done = 0.0
+    for weight, run in units:
+        plan[min(steps - 1, int((done + weight / 2) * steps / total))].append(run)
+        done += weight
+    return plan
+
+
+def run_units(plan, k):
+    for step, units in enumerate(plan):
+        if units:
+
+            @pl.when(k == step)
+            def _(units=units):
+                for run in units:
+                    run()
 
 
 def row_parts(rows, cuts):
@@ -111,7 +179,7 @@
     return pl.pallas_call(
         functools.partial(gather_kernel, count, cuts),
         out_shape=[jax.ShapeDtypeStruct((count,) + x.shape, x.dtype) for x in arrays],
-        in_specs=[anywhere] * len(arrays),
+        in_specs=[pl.BlockSpec(memory_space=pltpu.VMEM)] * len(arrays),
         out_specs=[anywhere] * len(arrays),
         scratch_shapes=[pltpu.SemaphoreType.DMA((len(arrays),))]
         + [pltpu.SemaphoreType.DMA((chips, sum(cuts)))] * 4,
@@ -128,18 +196,19 @@
     return lax.dot_general(a, b, dims, preferred_element_type=F32)
 
 
-def gather_steps(count, cuts, x_ref, land, sems, use):
+def gather_steps(count, cuts, x_ref, land, sems, use, shards=1, begin=None, tag=None):
     me, chips, lane, position, step, following, previous, sibling = places(count)
     ring_out, ring_in, side_out, side_in = sems
     block = x_ref.shape[0]
     rows = block // cuts
-    greet((previous, sibling))
+    pieces = cuts + (tag is not None)
+    greet((previous, sibling), shards)
 
     def ring(s, c):
         part = pl.ds(c * rows, rows)
         return pltpu.make_async_remote_copy(
-            src_ref=land.at[s, part],
-            dst_ref=land.at[s + 1, part],
+            src_ref=tag.at[s, 0] if c == cuts else land.at[s, part],
+            dst_ref=tag.at[s + 1, 0] if c == cuts else land.at[s + 1, part],
             send_sem=ring_out.at[s, c],
             recv_sem=ring_in.at[s, c],
             device_id={"seq": following},
@@ -148,39 +217,43 @@
 
     def side(s, c):
         return pltpu.make_async_remote_copy(
-            src_ref=land.at[s, pl.ds(c * rows, rows)],
-            dst_ref=land.at[s, pl.ds(block + c * rows, rows)],
+            src_ref=tag.at[s, 0] if c == cuts else land.at[s, pl.ds(c * rows, rows)],
+            dst_ref=tag.at[s, 1] if c == cuts else land.at[s, pl.ds(block + c * rows, rows)],
             send_sem=side_out.at[s, c],
             recv_sem=side_in.at[s, c],
             device_id={"seq": sibling},
             device_id_type=MESH,
         )
 
+    def forward(s, c):
+        @pl.when(s < chips - 1)
+        def _():
+            ring(s, c).start()
+
+        side(s, c).start()
+
     land[0, :block] = x_ref[...]
+    for c in range(pieces):
+        forward(0, c)
+    if begin is not None:
+        begin()
 
     def one(s, carry):
-        for c in range(cuts):
-
-            @pl.when(s > 0)
-            def _():
-                ring(s - 1, c).wait_recv()
-
+        def pump(c):
             @pl.when(s < chips - 1)
             def _():
-                ring(s, c).start()
-
-            side(s, c).start()
-        for c in range(cuts):
+                ring(s, c).wait_recv()
+                forward(s + 1, c)
+
+        for c in range(pieces):
             side(s, c).wait_recv()
-        first = chip_of((position - s * step + chips) % chips, chips) * 2 + lane
-        second = chip_of((position + s * step + chips) % chips, chips) * 2 + 1 - lane
-        use(s, first, second)
+        use(s, *pair_owners(count, s), pump)
         return carry
 
     lax.fori_loop(0, chips, one, 0)
 
     def close(s, carry):
-        for c in range(cuts):
+        for c in range(pieces):
             side(s, c).wait_send()
 
             @pl.when(s < chips - 1)
@@ -192,19 +265,32 @@
     lax.fori_loop(0, chips, close, 0)
 
 
-def gather_scratch(count, cuts, block, columns):
+def pair_owners(count, s):
+    _, chips, lane, position, step, _, _, _ = places(count)
+    first = chip_of((position - s * step + chips) % chips, chips) * 2 + lane
+    second = chip_of((position + s * step + chips) % chips, chips) * 2 + 1 - lane
+    return first, second
+
+
+def at_block(owner, block):
+    return pl.ds(pl.multiple_of(owner * block, block), block)
+
+
+def gather_scratch(count, pieces, block, columns):
     chips = count // 2
     return [pltpu.VMEM((chips, 2 * block, columns), BF16)] + [
-        pltpu.SemaphoreType.DMA((chips, cuts))
+        pltpu.SemaphoreType.DMA((chips, pieces))
     ] * 4
 
 
-def scatter_steps(count, cuts, o_ref, bufs, sems, produce, extra=None):
+def scatter_steps(count, cuts, o_ref, bufs, sems, produce, extra=None, shards=1, begin=None):
     me, chips, lane, position, step, following, previous, sibling = places(count)
     own, sent, came, give, given = bufs
     ring_out, ring_in, side_out, side_in = sems
     rows = own.shape[0] // cuts
-    greet((previous, sibling))
+    greet((previous, sibling), shards)
+    if begin is not None:
+        begin()
 
     def ring(k, c):
         part = pl.ds(c * rows, rows)
@@ -227,13 +313,15 @@
             device_id_type=MESH,
         )
 
-    def one(k, carry):
-        first = chip_of((position - (k + 1) * step + chips) % chips, chips) * 2 + lane
-        second = chip_of((position + (k + 1) * step + chips) % chips, chips) * 2 + 1 - lane
-        mine, theirs = produce(k, first, second)
+    def make(k):
+        mine, theirs = produce(k, *pair_owners(count, (k + 1) % chips))
         give[k] = theirs.astype(BF16)
         side(k).start()
         own[...] = mine
+
+    make(0)
+
+    def one(k, carry):
         side(k).wait_recv()
         for c in range(cuts):
             part = pl.ds(c * rows, rows)
@@ -253,6 +341,10 @@
             @pl.when(k == chips - 1)
             def _():
                 o_ref[part] = total
+
+        @pl.when(k < chips - 1)
+        def _():
+            make(k + 1)
 
         if extra is not None:
             extra(k)
@@ -299,100 +391,304 @@
 ANY = pl.BlockSpec(memory_space=pl.ANY)
 
 
-def project_kernel(count, cuts, h_ref, w_ref, all_ref, y_ref, land, *rest):
-    sems, out_sem = rest[:4], rest[4]
-    block = h_ref.shape[0]
-
-    def out(s, owner, half):
+def front_kernel(
+    count,
+    shards,
+    cuts,
+    widths,
+    x_ref,
+    small_ref,
+    wq_ref,
+    wk_ref,
+    wv_ref,
+    wo_ref,
+    wd_ref,
+    h_all,
+    qkv_ref,
+    w_ref,
+    wo_all,
+    small_all,
+    wd_all,
+    land,
+    ring_out,
+    ring_in,
+    side_out,
+    side_in,
+    x_out,
+    x_in,
+    x_own,
+    d_out,
+    d_in,
+    h1,
+    gain,
+    h_sem,
+    o_out,
+    o_in,
+    o_own,
+):
+    block, dim = x_ref.shape
+    chips = count // 2
+    gcols, hd, members = widths
+    local = wq_ref.shape[0]
+    me = lax.axis_index("seq")
+    mine = lax.axis_index("fsdp")
+    group = (me % 2) * chips + me // 2
+    kv_cols = pl.ds(pl.multiple_of(group // members * hd, 128), hd)
+    q_cols = pl.ds(pl.multiple_of(group * gcols, 128), gcols)
+    items = [
+        (small_ref, small_all, None),
+        (wq_ref.at[:, q_cols], w_ref.at[:, pl.ds(0, gcols)], 0),
+        (wk_ref.at[:, kv_cols], w_ref.at[:, pl.ds(gcols, hd)], 0),
+        (wv_ref.at[:, kv_cols], w_ref.at[:, pl.ds(gcols + hd, hd)], 0),
+    ]
+    start, wait = crossing(shards, items, x_out, x_in, x_own)
+    start_down, wait_down = crossing(shards, [(wd_ref, wd_all, 1)], d_out, d_in)
+    owner = group * gcols // wo_ref.shape[0]
+    wo_src = wo_ref.at[pl.ds(pl.multiple_of(group * gcols % wo_ref.shape[0], 16), gcols)]
+    wo_own = pltpu.make_async_copy(wo_src, wo_all, o_own)
+
+    def wo_send(i):
+        return pltpu.make_async_remote_copy(
+            src_ref=wo_src,
+            dst_ref=wo_all,
+            send_sem=o_out.at[i - 1],
+            recv_sem=o_in,
+            device_id={"fsdp": (mine + i) % shards},
+            device_id_type=MESH,
+        )
+
+    def begin():
+        for n in range(len(items)):
+            start(n)
+
+        @pl.when(mine == owner)
+        def _():
+            wo_own.start()
+            for i in range(1, shards):
+                wo_send(i).start()
+
+        start_down(0)
+
+    def h_copy(s, holder, half):
         return pltpu.make_async_copy(
-            land.at[s, pl.ds(half * block, block)],
-            all_ref.at[pl.ds(pl.multiple_of(owner * block, block), block)],
-            out_sem.at[half],
+            h1.at[s, pl.ds(half * block, block)], h_all.at[at_block(holder, block)], h_sem.at[half]
         )
 
-    def use(s, first, second):
-        out(s, first, 0).start()
-        out(s, second, 1).start()
-        y = mm(land[s], w_ref[...]).astype(BF16)
-        y_ref[pl.ds(pl.multiple_of(first * block, block), block), :] = y[:block]
-        y_ref[pl.ds(pl.multiple_of(second * block, block), block), :] = y[block:]
-
-    gather_steps(count, cuts, h_ref, land, sems, use)
-    half_rows = all_ref.shape[0] // 2
+    def multiply(p):
+        first, second = pair_owners(count, p)
+        y = mm(h1[p], w_ref[...]).astype(BF16)
+        qkv_ref[at_block(first, block), :] = y[:block]
+        qkv_ref[at_block(second, block), :] = y[block:]
+
+    def use(s, first, second, pump):
+        @pl.when(s == 0)
+        def _():
+            wait(0)
+            for f in range(shards):
+                for r in range(local // 128):
+                    gain[:, pl.ds(f * local + r * 128, 128)] = small_all[f, r : r + 1, :].astype(F32)
+
+        x = land[s].astype(F32)
+        r1 = lax.rsqrt(jnp.mean(x * x, axis=1, keepdims=True) + EPSILON)
+        h1[s] = (x * r1 * gain[...]).astype(BF16)
+        h_copy(s, first, 0).start()
+        h_copy(s, second, 1).start()
+        pump(0)
+
+        @pl.when(s == chips // 2)
+        def _():
+            for n in range(1, len(items)):
+                wait(n)
+
+        @pl.when(s >= chips // 2)
+        def _():
+            multiply(2 * s - chips)
+            pump(1)
+            multiply(2 * s - chips + 1)
+
+        @pl.when(s < chips // 2)
+        def _():
+            pump(1)
+
+        for c in range(2, cuts):
+            pump(c)
+
+    gather_steps(
+        count, cuts, x_ref, land, (ring_out, ring_in, side_out, side_in), use, shards, begin
+    )
+
+    @pl.when(mine == owner)
+    def _():
+        wo_own.wait()
+        for i in range(1, shards):
+            wo_send(i).wait_send()
+
+    @pl.when(mine != owner)
+    def _():
+        wo_send(1).wait_recv()
+
+    wait_down(0)
+    half_rows = count * block // 2
     for half in range(2):
         pltpu.make_async_copy(
-            all_ref.at[pl.ds(0, half_rows)], all_ref.at[pl.ds(0, half_rows)], out_sem.at[half]
+            h_all.at[pl.ds(0, half_rows)], h_all.at[pl.ds(0, half_rows)], h_sem.at[half]
         ).wait()
 
 
-def project_gathered(h, w, count, call, cuts=4):
-    block, dim = h.shape
+def front(
+    x, small, w_query, key_weight, value_weight, w_out, w_down, hd, count, shards, call, cuts=4
+):
+    block, dim = x.shape
+    gcols = w_query.shape[1] // count
+    members = count * hd // key_weight.shape[1]
+    columns = gcols + 2 * hd
+    chips = count // 2
+    dma = pltpu.SemaphoreType.DMA
     return pl.pallas_call(
-        functools.partial(project_kernel, count, cuts),
+        functools.partial(front_kernel, count, shards, cuts, (gcols, hd, members)),
         out_shape=(
             jax.ShapeDtypeStruct((count * block, dim), BF16),
-            jax.ShapeDtypeStruct((count * block, w.shape[1]), BF16),
+            jax.ShapeDtypeStruct((count * block, columns), BF16),
+            jax.ShapeDtypeStruct((dim, columns), BF16),
+            jax.ShapeDtypeStruct((gcols, w_out.shape[1]), BF16),
+            jax.ShapeDtypeStruct((shards,) + small.shape, BF16),
+            whole_of(w_down, 1, shards),
         ),
-        in_specs=[VMEM, VMEM],
-        out_specs=[ANY, VMEM],
-        scratch_shapes=gather_scratch(count, cuts, block, dim) + [pltpu.SemaphoreType.DMA((2,))],
+        in_specs=[VMEM, VMEM] + [ANY] * 5,
+        out_specs=[ANY, VMEM, VMEM, VMEM, VMEM, ANY],
+        scratch_shapes=gather_scratch(count, cuts, block, dim)
+        + crossing_scratch(shards, 4)
+        + [
+            dma((4,)),
+        ]
+        + crossing_scratch(shards, 1)
+        + [
+            pltpu.VMEM((chips, 2 * block, dim), BF16),
+            pltpu.VMEM((1, dim), F32),
+            dma((2,)),
+            dma((max(1, shards - 1),)),
+            dma,
+            dma,
+        ],
         compiler_params=remote_params(call, 48),
-    )(h, w)
-
-
-def out_back_kernel(count, cuts, da_ref, w_ref, o_ref, do_ref, part_ref, land, *rest):
-    sems, total = rest[:4], rest[4]
+    )(x, small, w_query, key_weight, value_weight, w_out, w_down)
+
+
+def out_back_kernel(
+    count, cuts, da_ref, w_ref, o_ref, hid_ref, de_ref, do_ref, part_ref, down_ref, land, *rest
+):
+    sems = rest[:4]
+    total, hid, de, hid_sem, de_sem = rest[4:]
     block = da_ref.shape[0]
+    columns = de.shape[2]
     total[...] = jnp.zeros_like(total)
-
-    def use(s, first, second):
+    load_hid = pltpu.make_async_copy(hid_ref, hid, hid_sem)
+
+    def load_de(s):
+        part = pl.ds(pl.multiple_of(s * columns, 128), columns)
+        return pltpu.make_async_copy(de_ref.at[:, part], de.at[s % 2], de_sem.at[s % 2])
+
+    def begin():
+        load_hid.start()
+        load_de(0).start()
+
+    def use(s, first, second, pump):
+        @pl.when(s == 0)
+        def _():
+            load_hid.wait()
+
+        @pl.when(s < count // 2 - 1)
+        def _():
+            load_de(s + 1).start()
+
         pair = land[s]
-        a = pl.ds(pl.multiple_of(first * block, block), block)
-        b = pl.ds(pl.multiple_of(second * block, block), block)
+        a = at_block(first, block)
+        b = at_block(second, block)
         do = mm(pair, w_ref[...], NT).astype(BF16)
         do_ref[a, :] = do[:block]
         do_ref[b, :] = do[block:]
+        pump(0)
         total[...] += mm(jnp.concatenate([o_ref[a, :], o_ref[b, :]], axis=0), pair, TN)
-
-    gather_steps(count, cuts, da_ref, land, sems, use)
+        pump(1)
+        load_de(s).wait()
+        part = pl.ds(pl.multiple_of(s * columns, 128), columns)
+        down_ref[:, part] = mm(hid[...], de[s % 2], TN).astype(BF16)
+        for c in range(2, cuts):
+            pump(c)
+
+    gather_steps(count, cuts, da_ref, land, sems, use, 1, begin)
     part_ref[...] = total[...].astype(BF16)
 
 
-def out_back(da, w, o, count, call, cuts=4):
+def out_back(da, w, o, hid, de, count, call, cuts=4):
     block, dim = da.shape
+    chips = count // 2
+    dma = pltpu.SemaphoreType.DMA
     return pl.pallas_call(
         functools.partial(out_back_kernel, count, cuts),
-        out_shape=(jax.ShapeDtypeStruct(o.shape, BF16), jax.ShapeDtypeStruct(w.shape, BF16)),
-        in_specs=[VMEM] * 3,
-        out_specs=[VMEM] * 2,
-        scratch_shapes=gather_scratch(count, cuts, block, dim) + [pltpu.VMEM(w.shape, F32)],
+        out_shape=(
+            jax.ShapeDtypeStruct(o.shape, BF16),
+            jax.ShapeDtypeStruct(w.shape, BF16),
+            jax.ShapeDtypeStruct((hid.shape[1], dim), BF16),
+        ),
+        in_specs=[VMEM] * 3 + [ANY] * 2,
+        out_specs=[VMEM] * 3,
+        scratch_shapes=gather_scratch(count, cuts, block, dim)
+        + [
+            pltpu.VMEM(w.shape, F32),
+            pltpu.VMEM(hid.shape, BF16),
+            pltpu.VMEM((2, de.shape[0], dim // chips), BF16),
+            dma,
+            dma((2,)),
+        ],
         compiler_params=remote_params(call, 48),
-    )(da, w, o)
-
-
-def product_kernel(count, cuts, dims, y_ref, w_ref, o_ref, *rest):
+    )(da, w, o, hid, de)
+
+
+def product_kernel(count, shards, cuts, dims, axes, y_ref, w_ref, *refs):
+    cargo = len(axes)
+    srcs, o_ref, dsts = refs[:cargo], refs[cargo], refs[cargo + 1 : 2 * cargo + 1]
+    rest = refs[2 * cargo + 1 :]
     block = o_ref.shape[0]
+    if cargo:
+        start, wait = crossing(shards, list(zip(srcs, dsts, axes)), *rest[9:])
+
+    def begin():
+        for n in range(cargo):
+            start(n)
 
     def produce(k, first, second):
-        a = y_ref[pl.ds(pl.multiple_of(first * block, block), block), :]
-        b = y_ref[pl.ds(pl.multiple_of(second * block, block), block), :]
+        a = y_ref[at_block(first, block), :]
+        b = y_ref[at_block(second, block), :]
         both = mm(jnp.concatenate([a, b], axis=0), w_ref[...], dims)
         return both[:block], both[block:]
 
-    scatter_steps(count, cuts, o_ref, rest[:5], rest[5:], produce)
-
-
-def product_scattered(y, w, dims, count, call, cuts=2):
+    scatter_steps(
+        count, cuts, o_ref, rest[:5], rest[5:9], produce, None, shards if cargo else 1, begin
+    )
+    for n in range(cargo):
+        wait(n)
+
+
+def whole_of(part, axis, shards):
+    shape = list(part.shape)
+    shape[axis] *= shards
+    return jax.ShapeDtypeStruct(tuple(shape), part.dtype)
+
+
+def product_scattered(y, w, dims, cargo, axes, count, shards, call, cuts=2):
     block = y.shape[0] // count
     columns = w.shape[1 - dims[0][1][0]]
     return pl.pallas_call(
-        functools.partial(product_kernel, count, cuts, dims),
-        out_shape=jax.ShapeDtypeStruct((block, columns), F32),
-        in_specs=[VMEM, VMEM],
-        out_specs=VMEM,
-        scratch_shapes=scatter_scratch(count, cuts, block, columns),
+        functools.partial(product_kernel, count, shards, cuts, dims, axes),
+        out_shape=[jax.ShapeDtypeStruct((block, columns), F32)]
+        + [whole_of(part, axis, shards) for part, axis in zip(cargo, axes)],
+        in_specs=[VMEM, VMEM] + [ANY] * len(cargo),
+        out_specs=[VMEM] + [ANY] * len(cargo),
+        scratch_shapes=scatter_scratch(count, cuts, block, columns)
+        + (crossing_scratch(shards, len(cargo)) if cargo else []),
         compiler_params=remote_params(call, 48),
-    )(y, w)
+    )(y, w, *cargo)
 
 
 def one_hot_of(slot_ref, first, second, capacity):
@@ -403,8 +699,33 @@
     return jnp.where(row == wanted, 1.0, 0.0).astype(BF16)
 
 
+def parts_of_own(i, shards, size, unit):
+    place = (lax.axis_index("fsdp") + i) % shards
+    return pl.ds(pl.multiple_of(place * (size // shards), unit), size // shards)
+
+
+def gate_up_parts(i, shards, whole, own, wgu):
+    rows = parts_of_own(i, shards, wgu.shape[0], 16)
+    ffe = wgu.shape[1] // 2
+    return [
+        (whole[n].at[rows] if i else own[n], wgu.at[rows, pl.ds(n * ffe, ffe)]) for n in range(2)
+    ]
+
+
+def down_parts(i, shards, pieces, own, wd):
+    columns = parts_of_own(i, shards, wd.shape[1], 128)
+    parts = []
+    first = 0
+    for piece in pieces:
+        rows = pl.ds(first, piece.shape[0])
+        first += piece.shape[0]
+        parts.append((piece.at[:, columns] if i else own.at[rows], wd.at[rows, columns]))
+    return parts
+
+
 def expert_kernel(
     count,
+    shards,
     cuts,
     capacity,
     h_ref,
@@ -414,10 +735,15 @@
     dy_ref,
     wg_ref,
     wu_ref,
-    wd_ref,
+    wd1_ref,
+    wd2_ref,
+    wd3_ref,
+    wg_own,
+    wu_own,
+    wd_own,
     xs_out,
     de_out,
-    dx_out,
+    dl_out,
     ce_out,
     hid_out,
     dgu_out,
@@ -426,13 +752,12 @@
     ring_in,
     side_out,
     side_in,
-    wg,
-    wu,
+    wgu,
     wd,
     dyb,
     xs,
     de,
-    dx,
+    dl,
     ce,
     hid,
     dgu,
@@ -441,20 +766,25 @@
     out_sem,
 ):
     block, dim = h_ref.shape
-    ffe = wg.shape[1]
-    me, chips, lane, position, step, _, _, _ = places(count)
+    ffe = wd.shape[0]
+    wd_refs = (wd1_ref, wd2_ref, wd3_ref)
+    me = lax.axis_index("seq")
+    chips = count // 2
     weights = [
-        pltpu.make_async_copy(src, dst, w_sem.at[i])
-        for i, (src, dst) in enumerate(((wg_ref, wg), (wu_ref, wu), (wd_ref, wd)))
+        pltpu.make_async_copy(src, dst, w_sem.at[i, n])
+        for i in range(shards)
+        for n, (src, dst) in enumerate(
+            gate_up_parts(i, shards, (wg_ref, wu_ref), (wg_own, wu_own), wgu)
+            + down_parts(i, shards, wd_refs, wd_own, wd)
+        )
     ]
-    staged = ((xs, xs_out), (de, de_out), (dx, dx_out), (ce, ce_out), (hid, hid_out), (dgu, dgu_out))
+    staged = ((xs, xs_out), (de, de_out), (dl, dl_out), (ce, ce_out), (hid, hid_out), (dgu, dgu_out))
 
     def dy_copies(s):
-        first = chip_of((position - s * step + chips) % chips, chips) * 2 + lane
-        second = chip_of((position + s * step + chips) % chips, chips) * 2 + 1 - lane
+        first, second = pair_owners(count, s)
         return [
             pltpu.make_async_copy(
-                dy_ref.at[owner], dyb.at[s % 2, pl.ds(half * block, block)], dy_sem.at[s % 2, half]
+                dy_ref.at[at_block(owner, block)], dyb.at[s % 2, pl.ds(half * block, block)], dy_sem.at[s % 2, half]
             )
             for half, owner in ((0, first), (1, second))
         ]
@@ -462,19 +792,12 @@
     for copy in weights + dy_copies(0):
         copy.start()
 
-    def use(s, first, second):
-        @pl.when(s == 0)
-        def _():
-            for copy in weights:
-                copy.wait()
-
+    def use(s, first, second, pump):
         @pl.when(s < chips - 1)
         def _():
             for copy in dy_copies(s + 1):
                 copy.start()
 
-        for copy in dy_copies(s):
-            copy.wait()
         rows = pl.ds(pl.multiple_of(s * 2 * capacity, 16), 2 * capacity)
         pick = one_hot_of(slot_ref, first, second, capacity)
         x = mm(pick, land[s]).astype(BF16)
@@ -495,26 +818,38 @@
         expert_lane = lax.broadcasted_iota(jnp.int32, weight.shape, 1)
         gate = jnp.sum(jnp.where(expert_lane == me, weight, 0.0), axis=1, keepdims=True)
         gate = gate / jnp.where(mass > 0.0, mass, 1.0)
-        g = mm(x, wg[...])
-        u = mm(x, wu[...])
+
+        @pl.when(s == 0)
+        def _():
+            for copy in weights:
+                copy.wait()
+
+        gu = mm(x, wgu[...])
+        pump(0)
+        g, u = gu[:, :ffe], gu[:, ffe:]
         sig = jax.nn.sigmoid(g)
         silu = g * sig
         h = (silu * u).astype(BF16)
         hid[rows, :] = h
         e = mm(h, wd[...])
         ce[rows, :] = (gate * e).astype(BF16)
+        pump(1)
+        for copy in dy_copies(s):
+            copy.wait()
         dys = mm(pick, dyb[s % 2])
         dgate = jnp.sum(dys * e, axis=1, keepdims=True)
         d = (gate * dys).astype(BF16)
         de[rows, :] = d
+        pump(2)
         dh = mm(d, wd[...], NT)
+        for c in range(3, cuts):
+            pump(c)
         dg = (dh * u * (sig + silu * (1.0 - sig))).astype(BF16)
         du = (dh * silu).astype(BF16)
         dgu[rows, :ffe] = dg
         dgu[rows, ffe:] = du
-        dx[rows, :dim] = (mm(dg, wg[...], NT) + mm(du, wu[...], NT)).astype(BF16)
         high = dgate.astype(BF16).astype(F32)
-        dx[rows, dim:] = jnp.where(
+        dl[rows, :] = jnp.where(
             expert_lane == me, high, jnp.where(expert_lane == me + 64, dgate - high, 0.0)
         ).astype(BF16)
         for i, (src, dst) in enumerate(staged):
@@ -525,91 +860,77 @@
         pltpu.make_async_copy(src, dst, out_sem.at[i]).wait()
 
 
-def expert_gathered(h2, slot, chosen, router, dy_all, wg, wu, wd, capacity, count, call, cuts=4):
+def expert_gathered(h2, slot, chosen, router, dy_all, weights, capacity, count, shards, call, cuts=4):
     block, dim = h2.shape
-    ffe = wg.shape[1]
+    ffe = weights[0].shape[1]
     total = count * capacity
-    widths = (dim, dim, dim + 128, dim, ffe, 2 * ffe)
+    widths = (dim, dim, 128, dim, ffe, 2 * ffe)
     dma = pltpu.SemaphoreType.DMA
     return pl.pallas_call(
-        functools.partial(expert_kernel, count, cuts, capacity),
+        functools.partial(expert_kernel, count, shards, cuts, capacity),
         out_shape=[jax.ShapeDtypeStruct((total, n), BF16) for n in widths],
-        in_specs=[VMEM] * 4 + [ANY] * 4,
+        in_specs=[VMEM] * 4 + [ANY] * 9,
         out_specs=[ANY] * 6,
         scratch_shapes=gather_scratch(count, cuts, block, dim)
         + [
-            pltpu.VMEM(wg.shape, BF16),
-            pltpu.VMEM(wu.shape, BF16),
-            pltpu.VMEM(wd.shape, BF16),
+            pltpu.VMEM((dim, 2 * ffe), BF16),
+            pltpu.VMEM((ffe, dim), BF16),
             pltpu.VMEM((2, 2 * block, dim), BF16),
         ]
         + [pltpu.VMEM((total, n), BF16) for n in widths]
-        + [dma((3,)), dma((2, 2)), dma((6,))],
+        + [dma((shards, 5)), dma((2, 2)), dma((6,))],
         compiler_params=remote_params(call, 60),
-    )(h2, slot, chosen, router, dy_all, wg, wu, wd)
-
-
-def slots_kernel(count, cuts, capacity, slot_ref, rows_ref, o_ref, *rest):
-    bufs, sems, held, held_sem = rest[:5], rest[5:9], rest[9], rest[10]
+    )(h2, slot, chosen, router, dy_all, *weights)
+
+
+def slots_back_kernel(
+    count,
+    shards,
+    cuts,
+    capacity,
+    slot_ref,
+    dl,
+    xs_ref,
+    dgu_ref,
+    wg_ref,
+    wu_ref,
+    wg_own,
+    wu_own,
+    o_ref,
+    gu_out,
+    *rest,
+):
+    bufs, sems = rest[:5], rest[5:9]
+    xs, dgu, wgu, gu, sem, w_sem, gu_sem = rest[9:]
     chips = count // 2
     block = o_ref.shape[0]
-    load = pltpu.make_async_copy(rows_ref, held, held_sem)
-    load.start()
+    dim = xs.shape[1]
+    loads = [
+        pltpu.make_async_copy(src, dst, sem.at[i])
+        for i, (src, dst) in enumerate(((dgu_ref, dgu), (xs_ref, xs)))
+    ]
+    weights = [
+        pltpu.make_async_copy(src, dst, w_sem.at[i, n])
+        for i in range(shards)
+        for n, (src, dst) in enumerate(
+            gate_up_parts(i, shards, (wg_ref, wu_ref), (wg_own, wu_own), wgu)
+        )
+    ]
+    for load in loads[:1] + weights + loads[1:]:
+        load.start()
+    part = xs.shape[1] // chips
 
     def produce(k, first, second):
         @pl.when(k == 0)
         def _():
-            load.wait()
+            for load in loads[:1] + weights:
+                load.wait()
 
         pair = pl.multiple_of((k + 1) % chips * 2 * capacity, 16)
+        rows = pl.ds(pair, 2 * capacity)
         pick = one_hot_of(slot_ref, first, second, capacity)
-        both = mm(pick, held[pl.ds(pair, 2 * capacity), :], TN)
-        return both[:block], both[block:]
-
-    scatter_steps(count, cuts, o_ref, bufs, sems, produce)
-
-
-def slots_scattered(rows, slot, capacity, count, call, cuts=2):
-    block = slot.shape[1]
-    columns = rows.shape[1]
-    return pl.pallas_call(
-        functools.partial(slots_kernel, count, cuts, capacity),
-        out_shape=jax.ShapeDtypeStruct((block, columns), F32),
-        in_specs=[VMEM, ANY],
-        out_specs=VMEM,
-        scratch_shapes=scatter_scratch(count, cuts, block, columns)
-        + [pltpu.VMEM(rows.shape, BF16), pltpu.SemaphoreType.DMA],
-        compiler_params=remote_params(call, 48),
-    )(slot, rows)
-
-
-def slots_back_kernel(
-    count, cuts, capacity, slot_ref, dx_ref, xs_ref, de_ref, hid_ref, dgu_ref, o_ref, gu_out, down_out, *rest
-):
-    bufs, sems = rest[:5], rest[5:9]
-    dx, xs, de, hid, dgu, gu, down, sem, gu_sem, down_sem = rest[9:]
-    chips = count // 2
-    block = o_ref.shape[0]
-    loads = [
-        pltpu.make_async_copy(src, dst, sem.at[i])
-        for i, (src, dst) in enumerate(
-            ((dx_ref, dx), (xs_ref, xs), (dgu_ref, dgu), (hid_ref, hid), (de_ref, de))
-        )
-    ]
-    for load in loads:
-        load.start()
-    part = xs.shape[1] // chips
-    down_part = 256
-    downs = hid.shape[1] // down_part
-
-    def produce(k, first, second):
-        @pl.when(k == 0)
-        def _():
-            loads[0].wait()
-
-        pair = pl.multiple_of((k + 1) % chips * 2 * capacity, 16)
-        pick = one_hot_of(slot_ref, first, second, capacity)
-        both = mm(pick, dx[pl.ds(pair, 2 * capacity), :], TN)
+        dx = mm(dgu[rows, :], wgu[...], NT).astype(BF16)
+        both = jnp.concatenate([mm(pick, dx, TN), mm(pick, dl[rows, :], TN)], axis=1)
         return both[:block], both[block:]
 
     def extra(k):
@@ -623,38 +944,29 @@
         gu[rows, :] = mm(xs[:, columns], dgu[...], TN).astype(BF16)
         pltpu.make_async_copy(gu.at[rows], gu_out.at[rows], gu_sem).start()
 
-        @pl.when((k % 2 == 0) & (k // 2 < downs))
-        def _():
-            start = pl.multiple_of(k // 2 * down_part, 128)
-            down_rows = pl.ds(start, down_part)
-            down[down_rows, :] = mm(hid[:, down_rows], de[...], TN).astype(BF16)
-            pltpu.make_async_copy(down.at[down_rows], down_out.at[down_rows], down_sem).start()
-
     scatter_steps(count, cuts, o_ref, bufs, sems, produce, extra)
     pltpu.make_async_copy(gu, gu_out, gu_sem).wait()
-    pltpu.make_async_copy(down, down_out, down_sem).wait()
-
-
-def slots_back(slot, dx, xs, de, hid, dgu, capacity, count, call, cuts=2):
+
+
+def slots_back(slot, dl, xs, dgu, weights, capacity, count, shards, call, cuts=2):
     block = slot.shape[1]
-    columns = dx.shape[1]
-    dim, ffe = xs.shape[1], hid.shape[1]
+    dim, ffe = xs.shape[1], dgu.shape[1] // 2
+    columns = dim + dl.shape[1]
     dma = pltpu.SemaphoreType.DMA
     return pl.pallas_call(
-        functools.partial(slots_back_kernel, count, cuts, capacity),
+        functools.partial(slots_back_kernel, count, shards, cuts, capacity),
         out_shape=(
             jax.ShapeDtypeStruct((block, columns), F32),
             jax.ShapeDtypeStruct((dim, 2 * ffe), BF16),
-            jax.ShapeDtypeStruct((ffe, dim), BF16),
         ),
-        in_specs=[VMEM] + [ANY] * 5,
-        out_specs=[VMEM, ANY, ANY],
+        in_specs=[VMEM] * 2 + [ANY] * 6,
+        out_specs=[VMEM, ANY],
         scratch_shapes=scatter_scratch(count, cuts, block, columns)
-        + [pltpu.VMEM(a.shape, BF16) for a in (dx, xs, de, hid, dgu)]
-        + [pltpu.VMEM((dim, 2 * ffe), BF16), pltpu.VMEM((ffe, dim), BF16)]
-        + [dma((5,)), dma, dma],
+        + [pltpu.VMEM(a.shape, BF16) for a in (xs, dgu)]
+        + [pltpu.VMEM((dim, 2 * ffe), BF16)] * 2
+        + [dma((2,)), dma((shards, 2)), dma],
         compiler_params=remote_params(call, 60),
-    )(slot, dx, xs, de, hid, dgu)
+    )(slot, dl, xs, dgu, *weights)
 
 
 def split3(x):
@@ -684,12 +996,47 @@
 
 
 def attend_kernel(
-    heads, tile, qkv_ref, gq_ref, gk_ref, cos_ref, sin_ref, start_ref, o_ref, qx_ref, kn_ref, vx_ref
+    count,
+    shards,
+    cuts,
+    heads,
+    tile,
+    dy_ref,
+    routes_ref,
+    qkv_ref,
+    gq_ref,
+    gk_ref,
+    cos_ref,
+    sin_ref,
+    start_ref,
+    wg_ref,
+    wd_ref,
+    dy_all,
+    routes_all,
+    o_ref,
+    qx_ref,
+    kn_ref,
+    wg_all,
+    wd_all,
+    land,
+    ring_out,
+    ring_in,
+    side_out,
+    side_in,
+    x_out,
+    x_in,
+    tag,
+    vx_ref,
+    dy_sem,
 ):
     span = qkv_ref.shape[0]
     width = kn_ref.shape[1]
+    block = dy_ref.shape[0]
     scale = width**-0.5 * LOG2E
-    for i in range(span // tile):
+    items = [(wg_ref, wg_all, 0), (wd_ref, wd_all, 1)]
+    start_item, wait_item = crossing(shards, items, x_out, x_in)
+
+    def prepare(i):
         rows = pl.ds(i * tile, tile)
         cos, sin = cos_ref[rows, :], sin_ref[rows, :]
         for h in range(heads + 1):
@@ -702,47 +1049,96 @@
                 qx_ref[rows, pl.ds(2 * h * width, width)] = (u * scale).astype(BF16)
         vx_ref[rows, :width] = qkv_ref[rows, pl.ds((heads + 1) * width, width)]
         vx_ref[rows, width:] = jnp.ones((tile, width), BF16)
-    for i in range(span // tile):
+
+    def attend_rows(i, h):
         rows = pl.ds(i * tile, tile)
         start = start_ref[rows, :]
         row = i * tile + lax.broadcasted_iota(jnp.int32, (tile, tile), 0)
-        for h in range(heads):
-            q = qx_ref[rows, pl.ds(2 * h * width, width)]
-            total = jnp.zeros((tile, 2 * width), F32)
-            for j in range(i + 1):
-                keys = pl.ds(j * tile, tile)
-                s = lax.dot_general(q, kn_ref[keys, :], NT, preferred_element_type=F32)
-                col = j * tile + lax.broadcasted_iota(jnp.int32, (tile, tile), 1)
-                keep = col >= start
-                if i == j:
-                    keep = keep & (col <= row)
-                p = jnp.where(keep, jnp.exp2(s), 0.0).astype(BF16)
-                total = total + jnp.dot(p, vx_ref[keys, :], preferred_element_type=F32)
-            weight = total[:, width:]
-            o_ref[rows, pl.ds(h * width, width)] = (total[:, :width] / weight).astype(BF16)
-            qx_ref[rows, pl.ds((2 * h + 1) * width, width)] = in_lanes(-jnp.log2(weight))
-
-
-def attend(qkv, gq, gk, cos, sin, start, tile=512):
+        q = qx_ref[rows, pl.ds(2 * h * width, width)]
+        total = jnp.zeros((tile, 2 * width), F32)
+        for j in range(i + 1):
+            keys = pl.ds(j * tile, tile)
+            s = mm(q, kn_ref[keys, :], NT)
+            col = j * tile + lax.broadcasted_iota(jnp.int32, (tile, tile), 1)
+            keep = col >= start
+            if i == j:
+                keep = keep & (col <= row)
+            p = jnp.where(keep, jnp.exp2(s), 0.0).astype(BF16)
+            total = total + mm(p, vx_ref[keys, :])
+        weight = total[:, width:]
+        o_ref[rows, pl.ds(h * width, width)] = (total[:, :width] / weight).astype(BF16)
+        qx_ref[rows, pl.ds((2 * h + 1) * width, width)] = in_lanes(-jnp.log2(weight))
+
+    units = []
+    for i in range(span // tile):
+        units.append((1.0, functools.partial(prepare, i)))
+        units += [(0.7 * (i + 1), functools.partial(attend_rows, i, h)) for h in range(heads)]
+    plan = spread_units(units, count // 2 - 1)
+
+    def begin():
+        for n in range(len(items)):
+            start_item(n)
+
+    tag[0, 0] = routes_ref[...]
+
+    def use(s, first, second, pump):
+        for half, owner in ((0, first), (1, second)):
+            pltpu.make_async_copy(
+                land.at[s, pl.ds(half * block, block)],
+                dy_all.at[at_block(owner, block)],
+                dy_sem.at[half],
+            ).start()
+            routes_all[owner] = tag[s, half]
+        run_units(plan, s)
+        for c in range(cuts + 1):
+            pump(c)
+
+    gather_steps(
+        count, cuts, dy_ref, land, (ring_out, ring_in, side_out, side_in), use, shards, begin, tag
+    )
+    for n in range(len(items)):
+        wait_item(n)
+    half_rows = count * block // 2
+    for half in range(2):
+        pltpu.make_async_copy(
+            dy_all.at[pl.ds(0, half_rows)], dy_all.at[pl.ds(0, half_rows)], dy_sem.at[half]
+        ).wait()
+
+
+def attend(dy, routes, qkv, gq, gk, cos, sin, start, w_gate, w_down, count, shards, call, tile=512, cuts=4):
     span = qkv.shape[0]
     width = gq.shape[0]
     heads = qkv.shape[1] // width - 2
-    vmem = pl.BlockSpec(memory_space=pltpu.VMEM)
+    block, dim = dy.shape
+    chips = count // 2
     return pl.pallas_call(
-        functools.partial(attend_kernel, heads, min(tile, span)),
+        functools.partial(attend_kernel, count, shards, cuts, heads, min(tile, span)),
         out_shape=(
+            jax.ShapeDtypeStruct((count * block, dim), BF16),
+            jax.ShapeDtypeStruct((count,) + routes.shape, BF16),
             jax.ShapeDtypeStruct((span, heads * width), BF16),
             jax.ShapeDtypeStruct((span, 2 * heads * width), BF16),
             jax.ShapeDtypeStruct((span, width), BF16),
+            whole_of(w_gate, 0, shards),
+            whole_of(w_down, 1, shards),
         ),
-        in_specs=[vmem] * 6,
-        out_specs=[vmem] * 3,
-        scratch_shapes=[pltpu.VMEM((span, 2 * width), BF16)],
-        compiler_params=pltpu.CompilerParams(vmem_limit_bytes=48 * MIB),
-    )(qkv, gq[None, :], gk[None, :], cos, sin, start[:, None])
+        in_specs=[VMEM] * 8 + [ANY] * 2,
+        out_specs=[ANY] + [VMEM] * 4 + [ANY] * 2,
+        scratch_shapes=gather_scratch(count, cuts + 1, block, dim)
+        + crossing_scratch(shards, 2)
+        + [
+            pltpu.VMEM((chips, 2) + routes.shape, BF16),
+            pltpu.VMEM((span, 2 * width), BF16),
+            pltpu.SemaphoreType.DMA((2,)),
+        ],
+        compiler_params=remote_params(call, 56),
+    )(dy, routes, qkv, gq[None, :], gk[None, :], cos, sin, start[:, None], w_gate, w_down)
 
 
 def attend_back_kernel(
+    count,
+    cuts,
+    capacity,
     heads,
     tile,
     qx_ref,
@@ -755,25 +1151,42 @@
     cos_ref,
     sin_ref,
     start_ref,
+    slot_ref,
+    ce_ref,
     dqkv_ref,
     gains_ref,
-    gx_ref,
-    dq_ref,
+    mixed_ref,
+    *rest,
 ):
+    bufs, sems = rest[:5], rest[5:9]
+    gx_ref, dq_ref, dk_ref, dv_ref, held, held_sem = rest[9:]
     span = qx_ref.shape[0]
     width = kn_ref.shape[1]
     scale = width**-0.5
-    ones = jnp.ones((tile, width), BF16)
-
-    def to_raw(d, h, rows, gain):
+    chips = count // 2
+    block = mixed_ref.shape[0]
+    load = pltpu.make_async_copy(ce_ref, held, held_sem)
+    load.start()
+
+    def produce(k, first, second):
+        @pl.when(k == 0)
+        def _():
+            load.wait()
+
+        pair = pl.multiple_of((k + 1) % chips * 2 * capacity, 16)
+        pick = one_hot_of(slot_ref, first, second, capacity)
+        both = mm(pick, held[pl.ds(pair, 2 * capacity), :], TN)
+        return both[:block], both[block:]
+
+    def to_raw(d, h, rows, gain, row):
         r, unit = unit_rows(qkv_ref[rows, pl.ds(h * width, width)].astype(F32))
         d = d * cos_ref[rows, :] + swap_halves(d * sin_ref[rows, :])
         dg = d * gain
         raw = r * (dg - unit * jnp.mean(dg * unit, axis=1, keepdims=True))
         dqkv_ref[rows, pl.ds(h * width, width)] = raw.astype(BF16)
-        return jnp.sum(d * unit, axis=0, keepdims=True)
-
-    for i in range(span // tile):
+        gains_ref[row : row + 1, :] += jnp.sum(d * unit, axis=0, keepdims=True)
+
+    def prepare(i):
         rows = pl.ds(i * tile, tile)
         for h in range(heads):
             cols = pl.ds(h * width, width)
@@ -783,74 +1196,92 @@
             gx_ref[rows, pl.ds((2 * h + 1) * width, width)] = in_lanes(
                 jnp.broadcast_to(-inner, (tile, width))
             )
-    dq_ref[...] = jnp.zeros_like(dq_ref)
-    key_gain = jnp.zeros((1, width), F32)
-    for j in range(span // tile):
+
+    def tile_back(j, i):
         keys = pl.ds(j * tile, tile)
+        rows = pl.ds(i * tile, tile)
+        ones = jnp.ones((tile, width), BF16)
         kn = kn_ref[keys, :]
         kx = jnp.concatenate([kn, ones], axis=1)
         vx = jnp.concatenate([qkv_ref[keys, pl.ds((heads + 1) * width, width)], ones], axis=1)
-        dk = jnp.zeros((tile, width), F32)
-        dv = jnp.zeros((tile, width), F32)
         key = j * tile + lax.broadcasted_iota(jnp.int32, (tile, tile), 0)
-        for i in range(j, span // tile):
-            rows = pl.ds(i * tile, tile)
-            keep = key >= start_ref[:, rows]
-            if i == j:
-                row = i * tile + lax.broadcasted_iota(jnp.int32, (tile, tile), 1)
-                keep = keep & (key <= row)
-            for h in range(heads):
-                qx = qx_ref[rows, pl.ds(2 * h * width, 2 * width)]
-                gx = gx_ref[rows, pl.ds(2 * h * width, 2 * width)]
-                s = lax.dot_general(kx, qx, NT, preferred_element_type=F32)
-                p = jnp.where(keep, jnp.exp2(s), 0.0)
-                dp = lax.dot_general(vx, gx, NT, preferred_element_type=F32)
-                ds = (p * dp).astype(BF16)
-                dv = dv + jnp.dot(p.astype(BF16), gx[:, :width], preferred_element_type=F32)
-                dk = dk + jnp.dot(ds, qx[:, :width], preferred_element_type=F32)
-                dq_ref[rows, pl.ds(h * width, width)] += lax.dot_general(
-                    ds, kn, TN, preferred_element_type=F32
-                )
-        dqkv_ref[keys, pl.ds((heads + 1) * width, width)] = dv.astype(BF16)
-        key_gain = key_gain + to_raw(dk * (1.0 / LOG2E), heads, keys, gk_ref[...])
-    query_gain = jnp.zeros((1, width), F32)
-    for i in range(span // tile):
+        keep = key >= start_ref[:, rows]
+        if i == j:
+            row = i * tile + lax.broadcasted_iota(jnp.int32, (tile, tile), 1)
+            keep = keep & (key <= row)
+        for h in range(heads):
+            qx = qx_ref[rows, pl.ds(2 * h * width, 2 * width)]
+            gx = gx_ref[rows, pl.ds(2 * h * width, 2 * width)]
+            p = jnp.where(keep, jnp.exp2(mm(kx, qx, NT)), 0.0)
+            ds = (p * mm(vx, gx, NT)).astype(BF16)
+            dv_ref[keys, :] += mm(p.astype(BF16), gx[:, :width])
+            dk_ref[keys, :] += mm(ds, qx[:, :width])
+            dq_ref[rows, pl.ds(h * width, width)] += mm(ds, kn, TN)
+
+    def finish_keys(j):
+        keys = pl.ds(j * tile, tile)
+        dqkv_ref[keys, pl.ds((heads + 1) * width, width)] = dv_ref[keys, :].astype(BF16)
+        to_raw(dk_ref[keys, :] * (1.0 / LOG2E), heads, keys, gk_ref[...], 1)
+
+    def finish_rows(i):
         rows = pl.ds(i * tile, tile)
         for h in range(heads):
-            dq = dq_ref[rows, pl.ds(h * width, width)] * scale
-            query_gain = query_gain + to_raw(dq, h, rows, gq_ref[...])
-    gains_ref[0:1, :] = query_gain
-    gains_ref[1:2, :] = key_gain
-
-
-def attend_back(qx, kn, qkv, o, do, gq, gk, cos, sin, start, tile=512):
+            to_raw(dq_ref[rows, pl.ds(h * width, width)] * scale, h, rows, gq_ref[...], 0)
+
+    tiles = span // tile
+    units = [(0.3, functools.partial(prepare, i)) for i in range(tiles)]
+    for j in range(tiles):
+        units += [(2.0, functools.partial(tile_back, j, i)) for i in range(j, tiles)]
+        units.append((0.3, functools.partial(finish_keys, j)))
+        units.append((0.6, functools.partial(finish_rows, j)))
+    plan = spread_units(units, chips - 1)
+    for ref in (dq_ref, dk_ref, dv_ref, gains_ref):
+        ref[...] = jnp.zeros_like(ref)
+
+    def extra(k):
+        run_units(plan, k)
+
+    scatter_steps(count, cuts, mixed_ref, bufs, sems, produce, extra)
+
+
+def attend_back(qx, kn, qkv, o, do, gq, gk, cos, sin, start, slot, ce, capacity, count, call, tile=512, cuts=2):
     span, width = kn.shape
     heads = o.shape[1] // width
-    vmem = pl.BlockSpec(memory_space=pltpu.VMEM)
+    block = slot.shape[1]
+    dim = ce.shape[1]
     return pl.pallas_call(
-        functools.partial(attend_back_kernel, heads, min(tile, span)),
+        functools.partial(attend_back_kernel, count, cuts, capacity, heads, min(tile, span)),
         out_shape=(
             jax.ShapeDtypeStruct(qkv.shape, BF16),
             jax.ShapeDtypeStruct((2, width), F32),
+            jax.ShapeDtypeStruct((block, dim), F32),
         ),
-        in_specs=[vmem] * 10,
-        out_specs=[vmem] * 2,
-        scratch_shapes=[
+        in_specs=[VMEM] * 11 + [ANY],
+        out_specs=[VMEM] * 3,
+        scratch_shapes=scatter_scratch(count, cuts, block, dim)
+        + [
             pltpu.VMEM((span, 2 * heads * width), BF16),
             pltpu.VMEM((span, heads * width), F32),
+            pltpu.VMEM((span, width), F32),
+            pltpu.VMEM((span, width), F32),
+            pltpu.VMEM(ce.shape, BF16),
+            pltpu.SemaphoreType.DMA,
         ],
-        compiler_params=pltpu.CompilerParams(vmem_limit_bytes=56 * MIB),
-    )(qx, kn, qkv, o, do, gq[None, :], gk[None, :], cos, sin, start[None, :])
+        compiler_params=remote_params(call, 60),
+    )(qx, kn, qkv, o, do, gq[None, :], gk[None, :], cos, sin, start[None, :], slot, ce)
 
 
 def last_gather_kernel(
-    count, members, cuts, q_ref, kv_ref, q_all, kv_all, heap, kv_sum, sems, own_sem, mo, mi, ro, ri, so, si
+    count, members, cuts, qkv_ref, q_all, kv_all, heap, kv_sum, sems, own_sem, mo, mi, ro, ri, so, si
 ):
     me, chips, lane, position, step, following, previous, sibling = places(count)
     chip = me // 2
     place = chip % members
     first = chip - place
     rows = kv_sum.shape[0]
+    gcols = q_all.shape[2]
+    q_ref = qkv_ref.at[:, pl.ds(0, gcols)]
+    kv_ref = qkv_ref.at[pl.ds(0, rows * members), pl.ds(gcols, kv_sum.shape[1])]
 
     def member(i):
         return (first + (place + i) % members) * 2 + lane
@@ -925,22 +1356,23 @@
     own_kv.wait()
 
 
-def last_gather(q, kv, count, members, call, cuts=4):
+def last_gather(qkv, gcols, local, count, members, call, cuts=4):
     chips = count // 2
-    rows = kv.shape[0] // members
+    rows = local // members
+    columns = qkv.shape[1] - gcols
     anywhere = pl.BlockSpec(memory_space=pl.ANY)
     dma = pltpu.SemaphoreType.DMA
     return pl.pallas_call(
         functools.partial(last_gather_kernel, count, members, cuts),
         out_shape=(
-            jax.ShapeDtypeStruct((count,) + q.shape, BF16),
-            jax.ShapeDtypeStruct((count, rows, kv.shape[1]), BF16),
+            jax.ShapeDtypeStruct((count, qkv.shape[0], gcols), BF16),
+            jax.ShapeDtypeStruct((count, rows, columns), BF16),
         ),
-        in_specs=[anywhere] * 2,
+        in_specs=[VMEM],
         out_specs=[anywhere] * 2,
         scratch_shapes=[
-            pltpu.VMEM((members - 1, rows, kv.shape[1]), BF16),
-            pltpu.VMEM((rows, kv.shape[1]), BF16),
+            pltpu.VMEM((members - 1, rows, columns), BF16),
+            pltpu.VMEM((rows, columns), BF16),
             dma,
             dma((3,)),
             dma((members - 1,)),
@@ -948,7 +1380,7 @@
         ]
         + [dma((chips, cuts + 1))] * 4,
         compiler_params=pltpu.CompilerParams(collective_id=call, has_side_effects=True),
-    )(q, kv)
+    )(qkv)
 
 
 def finish_kernel(
@@ -1062,55 +1494,66 @@
     experts = w_router.shape[1]
     local_rows = w_out.shape[0]
     capacity = tok * top * 9 // (8 * experts)
-    group = (me % 2) * chips + me // 2
     gcols = share * hd
-    kv_head = group * share // (heads // kv_heads)
 
     small = jnp.concatenate(
         [attn_gain, mlp_gain, query_gain, key_gain, w_router.reshape(-1)], axis=0
     )
-    small = lax.all_gather(small, "fsdp", axis=0, tiled=False)
     local_dim = attn_gain.shape[0]
     local_hd = query_gain.shape[0]
+    small = jnp.pad(small, (0, -small.shape[0] % (16 * 128))).reshape(-1, 128)
+    down_rows = w_down.shape[1] // 3 // 16 * 16
+    downs = (
+        w_down[0, :down_rows],
+        w_down[0, down_rows : 2 * down_rows],
+        w_down[0, 2 * down_rows :],
+    )
+    h1_all, qkv, w_qkv, w_o, small, wd1 = front(
+        activations[0],
+        small,
+        w_query,
+        key_weight,
+        value_weight,
+        w_out,
+        downs[0],
+        hd,
+        count,
+        shards,
+        1,
+    )
+    small = small.reshape(shards, -1)
     cut = [local_dim, 2 * local_dim, 2 * local_dim + local_hd, 2 * local_dim + 2 * local_hd]
     g_attn, g_mlp, g_query, g_key, router = jnp.split(small, cut, axis=1)
     g_attn = g_attn.reshape(-1).astype(F32)
     g_mlp = g_mlp.reshape(-1).astype(F32)
     g_query = g_query.reshape(-1).astype(F32)
     g_key = g_key.reshape(-1).astype(F32)
-    router = router.reshape(dim, experts)
-    qkv_local = jnp.concatenate(
-        [
-            lax.dynamic_slice_in_dim(w_query, group * gcols, gcols, 1),
-            lax.dynamic_slice_in_dim(key_weight, kv_head * hd, hd, 1),
-            lax.dynamic_slice_in_dim(value_weight, kv_head * hd, hd, 1),
-        ],
-        axis=1,
-    )
-    w_qkv = lax.all_gather(qkv_local, "fsdp", axis=0, tiled=True)
-    first_row = group * gcols
-    out_owner = first_row // local_rows
-    out_local = lax.dynamic_slice_in_dim(w_out, first_row % local_rows, gcols, 0)
-    w_o = lax.dynamic_index_in_dim(
-        lax.all_gather(out_local, "fsdp", axis=0, tiled=False), out_owner, 0, keepdims=False
-    )
-    wg = lax.all_gather(w_gate[0], "fsdp", axis=0, tiled=True)
-    wu = lax.all_gather(w_up[0], "fsdp", axis=0, tiled=True)
-    wd = lax.all_gather(w_down[0], "fsdp", axis=1, tiled=True)
-
+    router = router[:, : local_dim * experts].reshape(dim, experts)
     r1 = lax.rsqrt(jnp.mean(x * x, axis=-1, keepdims=True) + EPSILON)
-    h1 = (x * r1 * g_attn).astype(BF16)
-    dy_all, routes_all = gather_seq([dy, routes], count, 4, (4, 1))
-    h1, dy_all = lax.optimization_barrier((h1, dy_all))
-    h1_all, qkv = project_gathered(h1, w_qkv, count, 1)
     position, doc_start = run_starts(segment)
     cosine, sine = angles((position - doc_start).astype(F32), hd)
     start = jnp.where(segment > 0, doc_start, position)
 
     cos_full = jnp.concatenate([cosine, cosine], axis=1)
     sin_full = jnp.concatenate([-sine, sine], axis=1)
-    o, qx, kn = attend(qkv, g_query, g_key, cos_full, sin_full, start)
-    x2 = x + product_scattered(o, w_o, NN, count, 2)
+    routes_sent = jnp.pad(routes.T, ((0, -top % 16), (0, 0))).astype(BF16)
+    dy_all, routes_all, o, qx, kn, wg, wd2 = attend(
+        dy,
+        routes_sent,
+        qkv,
+        g_query,
+        g_key,
+        cos_full,
+        sin_full,
+        start,
+        w_gate[0],
+        downs[1],
+        count,
+        shards,
+        4,
+    )
+    x2, wu, wd3 = product_scattered(o, w_o, NN, [w_up[0], downs[2]], (0, 1), count, shards, 2)
+    x2 = x + x2
 
     r2 = lax.rsqrt(jnp.mean(x2 * x2, axis=-1, keepdims=True) + EPSILON)
     h2 = (x2 * r2 * g_mlp).astype(BF16)
@@ -1122,19 +1565,28 @@
         names = jnp.arange(experts, dtype=jnp.int32)
         return jnp.any(named[..., :, None] == names, axis=-2)
 
+    routes_all = jnp.swapaxes(routes_all[:, :top].astype(jnp.int32), 1, 2)
     hit = jnp.any(routes_all == me, axis=-1)
     rank = jnp.cumsum(hit.astype(jnp.int32), axis=1) - hit
     slot = jnp.where(hit & (rank < capacity), rank, -1)
     chosen_all = chosen_of(routes_all.reshape(span, top)).astype(BF16)
     chosen_all = jnp.pad(chosen_all, ((0, 0), (0, 128 - experts)))
     router_wide = jnp.pad(router, ((0, 0), (0, 128 - experts)))
-    xs, de, dxs, ce, hid, dgu = expert_gathered(
-        h2, slot, chosen_all, router_wide, dy_all, wg, wu, wd, capacity, count, 3
+    xs, de, dl, ce, hid, dgu = expert_gathered(
+        h2,
+        slot,
+        chosen_all,
+        router_wide,
+        dy_all,
+        (wg, wu, wd1, wd2, wd3, w_gate[0], w_up[0], w_down[0]),
+        capacity,
+        count,
+        shards,
+        3,
     )
-    dh2_wide, w_gate_up_part, w_down_part = slots_back(
-        slot, dxs, xs, de, hid, dgu, capacity, count, 6
+    dh2_wide, w_gate_up_part = slots_back(
+        slot, dl, xs, dgu, (wg, wu, w_gate[0], w_up[0]), capacity, count, shards, 6
     )
-    mixed = x2 + slots_scattered(ce, slot, capacity, count, 5)
     dgate = dh2_wide[:, dim : dim + experts] + dh2_wide[:, dim + 64 : dim + 64 + experts]
     gates = gates_of(h2, chosen_of(routes))
     dlogits = (gates * (dgate - jnp.sum(gates * dgate, axis=-1, keepdims=True))).astype(BF16)
@@ -1145,12 +1597,13 @@
     dn = dh2 * g_mlp
     dx2 = dy.astype(F32) + r2 * (dn - xh * jnp.mean(dn * xh, axis=-1, keepdims=True))
 
-    do, w_out_part = out_back(dx2.astype(BF16), w_o, o, count, 7)
-    dqkv, head_gains = attend_back(
-        qx, kn, qkv, o, do, g_query, g_key, cos_full, sin_full, start
+    do, w_out_part, w_down_part = out_back(dx2.astype(BF16), w_o, o, hid, de, count, 7)
+    dqkv, head_gains, mixed = attend_back(
+        qx, kn, qkv, o, do, g_query, g_key, cos_full, sin_full, start, slot, ce, capacity, count, 5
     )
+    mixed = x2 + mixed
     qkv_part = mm(h1_all, dqkv, TN).astype(BF16)
-    dh1 = product_scattered(dqkv, w_qkv, NT, count, 8)
+    dh1 = product_scattered(dqkv, w_qkv, NT, [], (), count, shards, 8)[0]
     xh1 = x * r1
     dn1 = dh1 * g_attn
     input_grad = dx2 + r1 * (dn1 - xh1 * jnp.mean(dn1 * xh1, axis=-1, keepdims=True))
@@ -1159,8 +1612,8 @@
         return lax.psum_scatter(part.astype(BF16), "fsdp", scatter_dimension=axis, tiled=True)
 
     w_gate_up_grad = sum_fsdp(w_gate_up_part, 0).astype(F32)
-    w_gate_grad = w_gate_up_grad[:, : wg.shape[1]]
-    w_up_grad = w_gate_up_grad[:, wg.shape[1] :]
+    w_gate_grad = w_gate_up_grad[:, : w_gate.shape[2]]
+    w_up_grad = w_gate_up_grad[:, w_gate.shape[2] :]
     w_down_grad = sum_fsdp(w_down_part, 1).astype(F32)
 
     small_part = jnp.concatenate(
@@ -1196,9 +1649,7 @@
         [qkv_part.reshape(shards, local_dim, -1), gains_part], axis=1
     ).reshape(shards * (local_dim + 16), -1)
     qkv_sum = sum_fsdp(qkv_part, 0)
-    q_all, kv_all = last_gather(
-        qkv_sum[:, :gcols], qkv_sum[:local_dim, gcols:], count, count // kv_heads, 10
-    )
+    q_all, kv_all = last_gather(qkv_sum, gcols, local_dim, count, count // kv_heads, 10)
     w_query_grad, w_key_grad, w_value_grad, attn_gain_grad = finish(
         q_all, kv_all, w_query, key_weight, value_weight, attn_gain, kv_heads
     )

time: 722 us -> 666 us (0.922)
  waiting for transfers between devices: 26.7 us -> 1.12 us
  Pallas kernels: 572 us -> 552 us
    pallas_call x2 -> x1, Pallas kernels: 102 us -> 51.6 us  [gather_seq(): pl.pallas_call(functools.partial(gather_kernel, count, cuts), out_shape=[...]
    pallas_call x8 -> x7, Pallas kernels: 347 us -> 374 us  [the longest x2 95.2 us: product_scattered(): pl.pallas_call(functools.partial(product_kernel, count, shards, cuts, dim...]
    all_gather x5 -> x0, waiting for transfers between devices: 18.7 us -> none  [the longest x1 18.7 us: per_device(): wd = lax.all_gather(w_down[0], 'fsdp', axis=1, tiled=True)]
    unnamed x89 -> x61, local copies, waits for them, and re-layouts: 15.5 us -> 14.1 us
  transfers between devices with their start and end apart: 11 -> 6, of which waited for: 2 -> 0; matrix products, arithmetic and copies ran while one was open for 9% -> 7% of each run, Pallas kernels for 56% -> 35%
where the time goes in v4:
time: 666 us; the launch traced here: 659 us
  Pallas kernels  552 us (83%)
  other arithmetic  45.6 us (7%)
  local copies, waits for them, and re-layouts  32.5 us (5%)
  between operations  15.1 us (2%)
  matrix products  12.1 us (2%)
    pallas_call x2, Pallas kernels, product_scattered(): pl.pallas_call(functools.partial(product_kernel, count, shards, cuts, dim...  95.2 us
    pallas_call x1, Pallas kernels, last_gather(): pl.pallas_call(functools.partial(last_gather_kernel, count, members, cuts...  62.8 us
    pallas_call x1, Pallas kernels, slots_back(): pl.pallas_call(functools.partial(slots_back_kernel, count, shards, cuts,...  61.8 us
    pallas_call x1, Pallas kernels, attend_back(): pl.pallas_call(functools.partial(attend_back_kernel, count, cuts, capacit...  56.5 us
    pallas_call x1, Pallas kernels, attend(): pl.pallas_call(functools.partial(attend_kernel, count, shards, cuts, head...  55.8 us
    pallas_call x1, Pallas kernels, front(): pl.pallas_call(functools.partial(front_kernel, count, shards, cuts, (gcol...  52.2 us
    pallas_call x1, Pallas kernels, expert_gathered(): pl.pallas_call(functools.partial(expert_kernel, count, shards, cuts, capa...  52.2 us
    pallas_call x1, Pallas kernels, gather_seq(): pl.pallas_call(functools.partial(gather_kernel, count, cuts), out_shape=[...  51.6 us
  transfers between devices with their start and end apart: 6, of which 0 were waited for; matrix products, arithmetic and copies ran while one was open for 7% of the time, Pallas kernels for 35%

profile of v4, /device:TPU:0, one launch (start us, length us, event | category | flops | bytes accessed | tf_op | source)
XLA Modules:
  0.0 659.0 jit_solution(13041610137965702744)
XLA Ops:
  10.0 2.8 concatenate.37
  12.8 2.4 slice_bitcast_fusion.2
  15.2 52.2 %shard_map.263 = (bf16[2048,2048]{1,0:T(8,128)(2,1)}, bf16[2048,512]{1,0:T(8,128)(2,1)}, bf16[2048,512]{1,0:T(8,128)(2,1)}, bf16[256,2048]{1,0:T(8,128)(2,1)S(1)...) custom-call(bf16[128,2048]{1,0:T(8,128)(2,1)S(1)} %bitcast.91, ...), custom_call_target="tpu_custom_call" | custom-call | tf_op jit(solution)/shard_map/pallas_call | solution.py:547
  71.9 3.7 fusion.12
  76.8 1.9 pad_maximum_fusion
  78.7 55.8 %shard_map.264 = (bf16[2048,2048]{1,0:T(8,128)(2,1)}, bf16[16,16,128]{2,1,0:T(8,128)(2,1)}, bf16[2048,256]{1,0:T(8,128)(2,1)}, bf16[2048,512]{1,0:T(8,128)(2,1)}...) custom-call(bf16[128,2048]{1,0:T(8,128)(2,1)} %bitcast.101, ...), custom_call_target="tpu_custom_call" | custom-call | tf_op jit(solution)/shard_map/pallas_call | solution.py:1114
  135.8 49.0 %shard_map.265 = (f32[128,2048]{1,0:T(8,128)S(1)}, bf16[2048,768]{1,0:T(8,128)(2,1)}, bf16[256,2048]{1,0:T(8,128)(2,1)S(1)}) custom-call(bf16[2048,256]{1,0:T(8,128)(2,1)S(1)} %copy-done, bf16[256,2048]{1,0:T(8,128)(2,1)S(1)} %get-tuple-element.55.w_ref, bf16[1024,768]{1,0:T(8,128)(2,1)} %bitcast.93, bf16[256,1024]{1,0:T(8,128)(2,1)S(1)} %get-tuple-element.142.refs_1_), custom_call_target="tpu_custom_call" | custom-call | tf_op jit(solution)/shard_map/pallas_call | solution.py:682
  192.0 52.2 %shard_map.266 = (bf16[1152,2048]{1,0:T(8,128)(2,1)}, bf16[1152,2048]{1,0:T(8,128)(2,1)}, bf16[1152,128]{1,0:T(8,128)(2,1)}, bf16[1152,2048]{1,0:T(8,128)(2,1)},...) custom-call(bf16[128,2048]{1,0:T(8,128)(2,1)} %copy-done.17, s32[16,128]{1,0:T(8,128)} %and_select_fusion.slot_ref, ...), custom_call_target="tpu_custom_call" | custom-call | tf_op jit(solution)/shard_map/pallas_call | solution.py:869
  244.3 61.8 %shard_map.267 = (f32[128,2176]{1,0:T(8,128)}, bf16[2048,1536]{1,0:T(8,128)(2,1)}) custom-call(s32[16,128]{1,0:T(8,128)} %and_select_fusion.slot_ref, bf16[1152,128]{1,0:T(8,128)(2,1)} %get-tuple-element.66.dl, bf16[1152,2048]{1,0:T(8,128)(2,1)} %get-tuple-element.67.xs_ref, bf16[1152,1536]{1,0:T(8,128)(2,1)} %get-tuple-element.68.dgu_ref, ...), custom_call_target="tpu_custom_call" | custom-call | tf_op jit(solution)/shard_map/pallas_call | solution.py:956
  311.1 48.5 %shard_map.268 = (bf16[2048,256]{1,0:T(8,128)(2,1)S(1)}, bf16[256,2048]{1,0:T(8,128)(2,1)}, bf16[768,2048]{1,0:T(8,128)(2,1)}) custom-call(bf16[128,2048]{1,0:T(8,128)(2,1)S(1)} %fusion.21.da_ref, bf16[256,2048]{1,0:T(8,128)(2,1)S(1)} %get-tuple-element.55.w_ref, bf16[2048,256]{1,0:T(8,128)(2,1)S(1)} %copy-done.1, ...), custom_call_target="tpu_custom_call" | custom-call | tf_op jit(solution)/shard_map/pallas_call | solution.py:627
  363.3 56.5 %shard_map.269 = (bf16[2048,512]{1,0:T(8,128)(2,1)}, f32[2,128]{1,0:T(2,128)}, f32[128,2048]{1,0:T(8,128)}) custom-call(bf16[2048,512]{1,0:T(8,128)(2,1)} %get-tuple-element.57.qx_ref, bf16[2048,128]{1,0:T(8,128)(2,1)} %get-tuple-element.58.kn_ref, bf16[2048,512]{1,0:T(8,128)(2,1)} %get-tuple-element.52.qkv_ref, ...), custom_call_target="tpu_custom_call" | custom-call | tf_op jit(solution)/shard_map/pallas_call | solution.py:1252
  420.8 3.3 reduce_sum.99
  424.3 8.4 %convolution_convert_fusion = bf16[2048,512]{1,0:T(8,128)(2,1)S(1)} fusion(bf16[2048,2048]{1,0:T(8,128)(2,1)} %get-tuple-element.77, bf16[2048,512]{1,0:T(8,128)(2,1)S(1)} %copy-done.8), kind=kOutput, calls=%fused_computation.5 | convolution fusion | flops 4296015872 | bytes 12582912 | tf_op jit(solution)/shard_map/dot_general | solution.py:196
  438.9 46.1 %shard_map.270 = f32[128,2048]{1,0:T(8,128)S(1)} custom-call(bf16[2048,512]{1,0:T(8,128)(2,1)S(1)} %copy-done.9, bf16[2048,512]{1,0:T(8,128)(2,1)S(1)} %copy-done.7), custom_call_target="tpu_custom_call" | custom-call | tf_op jit(solution)/shard_map/pallas_call | solution.py:682
  486.0 3.2 fusion.8
  489.2 1.9 dynamic-slice_reduce_fusion
  491.8 1.9 dynamic-slice_bitcast_fusion.refs_0_
  493.7 51.6 %shard_map.273 = (bf16[16,128,2048]{2,1,0:T(8,128)(2,1)}, bf16[16,16,2048]{2,1,0:T(8,128)(2,1)}) custom-call(bf16[128,2048]{1,0:T(8,128)(2,1)} %dynamic-slice_bitcast_fusion.refs_0_, bf16[16,2048]{1,0:T(8,128)(2,1)} %reshape.277.refs_1_), custom_call_target="tpu_custom_call" | custom-call | tf_op jit(solution)/shard_map/pallas_call | solution.py:179
  548.4 11.8 %bitcast_convert_fusion = f32[2048,2048]{1,0:T(8,128)} fusion(bf16[16,128,2048]{2,1,0:T(8,128)(2,1)} %get-tuple-element.87), kind=kLoop, calls=%fused_computation | loop fusion | flops 4194304 | bytes 25165824 | tf_op jit(solution)/shard_map/convert_element_type | solution.py:1686
  560.2 62.8 %shard_map.271 = (bf16[16,1040,256]{2,1,0:T(8,128)(2,1)}, bf16[16,256,256]{2,1,0:T(8,128)(2,1)}) custom-call(bf16[1040,512]{1,0:T(8,128)(2,1)} %reduce-scatter.4.cloned.1.call-done.qkv_ref), custom_call_target="tpu_custom_call" | custom-call | tf_op jit(solution)/shard_map/pallas_call | solution.py:1365
  624.7 15.5 %shard_map.272 = (f32[1024,4096]{1,0:T(8,128)}, f32[1024,512]{1,0:T(8,128)}, f32[1024,512]{1,0:T(8,128)}, f32[1024,1]{1,0:T(8,128)S(1)}) custom-call(bf16[16,1040,256]{2,1,0:T(8,128)(2,1)} %get-tuple-element.79.q_ref, bf16[16,256,256]{2,1,0:T(8,128)(2,1)S(1)} %copy-done.10, bf16[1024,4096]{1,0:T(8,128)(2,1)} %wq_ref.3, bf16[1024,512]{1,0:T(8,128)(2,1)S(1)} %copy-done.4, ...), custom_call_target="tpu_custom_call" | custom-call | tf_op jit(solution)/shard_map/pallas_call | solution.py:1425
  642.3 3.5 bitcast_convert_fusion.1
  645.8 2.8 convert_element_type.141
  648.6 3.2 slice_bitcast_fusion
  (146 shorter events, 40.9 us)
Async XLA Ops:
  7.2 8.0 %copy-start.2 = (bf16[1,128,2048]{2,1,0:T(8,128)(2,1)S(1)}, bf16[1,128,2048]{2,1,0:T(8,128)(2,1)}, u32[]{:S(2)}) copy-start(bf16[1,128,2048]{2,1,0:T(8,128)(2,1)} %param.16) | copy-start | bytes 1572868
  7.2 8.0 %copy-start.3 = (bf16[1024,512]{1,0:T(8,128)(2,1)S(1)}, bf16[1024,512]{1,0:T(8,128)(2,1)}, u32[]{:S(2)}) copy-start(bf16[1024,512]{1,0:T(8,128)(2,1)} %wk_ref.3) | copy-start | bytes 3145732
  7.2 413.6 %all-gather.5.cloned.1.call-start = ((), (), s32[]{:S(2)}) async-start(), calls=%async_computation.6 | async-start | bytes 3145728 | tf_op jit(solution)/shard_map/all_gather | solution.py:1627
  12.8 2.4 copy-start.5
  15.2 53.4 %copy-start.24 = (s32[1,128,8]{1,2,0:T(8,128)S(1)}, s32[1,128,8]{1,2,0:T(8,128)}, u32[]{:S(2)}) copy-start(s32[1,128,8]{1,2,0:T(8,128)} %param.19) | copy-start | bytes 12292
  135.8 50.3 %copy-start.23 = (bf16[16,16,128]{2,1,0:T(8,128)(2,1)S(1)}, bf16[16,16,128]{2,1,0:T(8,128)(2,1)}, u32[]{:S(2)}) copy-start(bf16[16,16,128]{2,1,0:T(8,128)(2,1)} %get-tuple-element.59) | copy-start | bytes 196612
  186.1 124.1 %copy-start.14 = (f32[128,2048]{1,0:T(8,128)}, f32[128,2048]{1,0:T(8,128)S(1)}, u32[]{:S(2)}) copy-start(f32[128,2048]{1,0:T(8,128)S(1)} %get-tuple-element.137) | copy-start | bytes 3145732
  190.2 1.8 copy-start.17
  244.3 64.1 %copy-start.20 = (bf16[2048,16]{1,0:T(8,128)(2,1)S(1)}, bf16[2048,16]{1,0:T(8,128)(2,1)}, u32[]{:S(2)}) copy-start(bf16[2048,16]{1,0:T(8,128)(2,1)} %copy-done.19) | copy-start | bytes 196612
  306.1 4.1 copy-start.21
  308.3 2.8 copy-start.1
  311.1 49.6 %copy-start.18 = (bf16[128,2048]{1,0:T(8,128)(2,1)S(1)}, bf16[128,2048]{1,0:T(8,128)(2,1)}, u32[]{:S(2)}) copy-start(bf16[128,2048]{1,0:T(8,128)(2,1)} %copy-done.17) | copy-start | bytes 1572868
  360.7 2.0 copy-start.22
  360.7 128.5 %all-reduce.9.cloned.1.call-start = ((), (), s32[]{:S(2)}) async-start(), calls=%async_computation.8 | async-start | bytes 262144
  362.6 129.2 %all-gather.7.cloned.1.call-start = ((), (), s32[]{:S(2)}) async-start(), calls=%async_computation.7 | async-start | bytes 3145728 | tf_op jit(solution)/shard_map/all_gather | solution.py:1629
  419.8 4.5 copy-start.8
  424.1 136.1 %reduce-scatter.4.cloned.1.call-start = ((), (), s32[]{:S(2)}) async-start(), calls=%async_computation.3 | async-start | bytes 3194880 | tf_op jit(solution)/shard_map/reduce_scatter | solution.py:1612
  434.2 208.1 %reduce-scatter.8.cloned.1.call-start = ((), (), s32[]{:S(2)}) async-start(), calls=%async_computation.5 | async-start | bytes 4718592 | tf_op jit(solution)/shard_map/reduce_scatter | solution.py:1612
  434.8 211.0 %reduce-scatter.6.cloned.1.call-start = ((), (), s32[]{:S(2)}) async-start(), calls=%async_computation.4 | async-start | bytes 9437184 | tf_op jit(solution)/shard_map/reduce_scatter | solution.py:1612
  435.5 49.6 %copy-start.26 = (u32[32]{0:T(128)S(1)}, u32[32]{0:T(128)}, u32[]{:S(2)}) copy-start(u32[32]{0:T(128)} %constant.89) | copy-start | bytes 388
  435.7 1.6 copy-start.7
  438.9 47.1 %copy-start.15 = (f32[128,2048]{1,0:T(8,128)S(1)}, f32[128,2048]{1,0:T(8,128)}, u32[]{:S(2)}) copy-start(f32[128,2048]{1,0:T(8,128)} %copy-done.14) | copy-start | bytes 3145732
  548.4 74.7 %copy-start.4 = (bf16[1024,512]{1,0:T(8,128)(2,1)S(1)}, bf16[1024,512]{1,0:T(8,128)(2,1)}, u32[]{:S(2)}) copy-start(bf16[1024,512]{1,0:T(8,128)(2,1)} %wk_ref.3) | copy-start | bytes 3145732
  548.4 74.7 %copy-start.6 = (bf16[1024,512]{1,0:T(8,128)(2,1)S(1)}, bf16[1024,512]{1,0:T(8,128)(2,1)}, u32[]{:S(2)}) copy-start(bf16[1024,512]{1,0:T(8,128)(2,1)} %wv_ref.3) | copy-start | bytes 3145732
  (9 other events, 10.1 us)
Sparse Core Ops, SparseCore 0:
  360.8 32.0 all-gather.4
  395.7 21.4 all-reduce.8
  424.2 10.5 all-gather.6
  437.5 33.3 reduce-scatter.3
  473.0 43.3 reduce-scatter.7
  518.6 77.0 reduce-scatter.5

commit v5 on v4

--- a/solution.py
+++ b/solution.py
@@ -38,14 +38,14 @@
     return me, chips, lane, position, step, following, previous, sibling
 
 
-def greet(places_over_seq, shards=1):
+def greet(places_over_seq, shards=1, more=0):
     barrier = pltpu.get_barrier_semaphore()
     for device in places_over_seq:
         pl.semaphore_signal(barrier, inc=1, device_id={"seq": device}, device_id_type=MESH)
     for i in range(1, shards):
         peer = (lax.axis_index("fsdp") + i) % shards
         pl.semaphore_signal(barrier, inc=1, device_id={"fsdp": peer}, device_id_type=MESH)
-    pl.semaphore_wait(barrier, len(places_over_seq) + shards - 1)
+    pl.semaphore_wait(barrier, len(places_over_seq) + shards - 1 + more)
 
 
 def crossing(shards, items, out_sems, in_sems, own_sems=None):
@@ -122,71 +122,6 @@
     ]
 
 
-def gather_kernel(count, cuts, *refs):
-    arrays = len(cuts)
-    x_refs, o_refs = refs[:arrays], refs[arrays : 2 * arrays]
-    own_sem, ring_out, ring_in, side_out, side_in = refs[2 * arrays :]
-    me, chips, lane, position, step, following, previous, sibling = places(count)
-    greet((previous, sibling))
-    pieces = []
-    for a in range(arrays):
-        pieces += [(x_refs[a], o_refs[a], part) for part in row_parts(x_refs[a].shape[0], cuts[a])]
-
-    def hop(c, owner, s, device, out_sem, in_sem, first):
-        x_ref, o_ref, part = pieces[c]
-        return pltpu.make_async_remote_copy(
-            src_ref=x_ref.at[part] if first else o_ref.at[owner, part],
-            dst_ref=o_ref.at[owner, part],
-            send_sem=out_sem.at[s, c],
-            recv_sem=in_sem.at[s, c],
-            device_id={"seq": device},
-            device_id_type=MESH,
-        )
-
-    def ring(c, owner, s, first=False):
-        return hop(c, owner, s, following, ring_out, ring_in, first)
-
-    def side(c, owner, s, first=False):
-        return hop(c, owner, s, sibling, side_out, side_in, first)
-
-    own = [
-        pltpu.make_async_copy(x_refs[a], o_refs[a].at[me], own_sem.at[a]) for a in range(arrays)
-    ]
-    for copy in own:
-        copy.start()
-    for c in range(len(pieces)):
-        ring(c, me, 0, True).start()
-        side(c, me, 0, True).start()
-    for s in range(1, chips):
-        owner = chip_of((position - s * step + chips) % chips, chips) * 2 + lane
-        for c in range(len(pieces)):
-            ring(c, owner, s - 1).wait_recv()
-            if s < chips - 1:
-                ring(c, owner, s).start()
-            side(c, owner, s).start()
-    for s in range(chips):
-        for c in range(len(pieces)):
-            side(c, me, s).wait()
-            if s < chips - 1:
-                ring(c, me, s).wait_send()
-    for copy in own:
-        copy.wait()
-
-
-def gather_seq(arrays, count, call, cuts):
-    chips = count // 2
-    anywhere = pl.BlockSpec(memory_space=pl.ANY)
-    return pl.pallas_call(
-        functools.partial(gather_kernel, count, cuts),
-        out_shape=[jax.ShapeDtypeStruct((count,) + x.shape, x.dtype) for x in arrays],
-        in_specs=[pl.BlockSpec(memory_space=pltpu.VMEM)] * len(arrays),
-        out_specs=[anywhere] * len(arrays),
-        scratch_shapes=[pltpu.SemaphoreType.DMA((len(arrays),))]
-        + [pltpu.SemaphoreType.DMA((chips, sum(cuts)))] * 4,
-        compiler_params=pltpu.CompilerParams(collective_id=call, has_side_effects=True),
-    )(*arrays)
-
-
 NT = (((1,), (1,)), ((), ()))
 TN = (((0,), (0,)), ((), ()))
 NN = (((1,), (0,)), ((), ()))
@@ -283,12 +218,16 @@
     ] * 4
 
 
-def scatter_steps(count, cuts, o_ref, bufs, sems, produce, extra=None, shards=1, begin=None):
+def scatter_steps(count, cuts, o_ref, bufs, sems, produce, extra=None, shards=1, begin=None, meeting=None):
     me, chips, lane, position, step, following, previous, sibling = places(count)
     own, sent, came, give, given = bufs
     ring_out, ring_in, side_out, side_in = sems
-    rows = own.shape[0] // cuts
-    greet((previous, sibling), shards)
+    rows = own.shape[1] // cuts
+    if meeting is None:
+        greet((previous, sibling), shards)
+    else:
+        meeting[0]()
+        greet((previous, sibling), shards, meeting[1])
     if begin is not None:
         begin()
 
@@ -317,7 +256,7 @@
         mine, theirs = produce(k, *pair_owners(count, (k + 1) % chips))
         give[k] = theirs.astype(BF16)
         side(k).start()
-        own[...] = mine
+        own[k % 2] = mine
 
     make(0)
 
@@ -329,9 +268,9 @@
             @pl.when(k > 0)
             def _():
                 ring(k - 1, c).wait_recv()
-                own[part] += came[k - 1, part].astype(F32)
-
-            total = own[part] + given[k, part].astype(F32)
+                own[k % 2, part] += came[k - 1, part].astype(F32)
+
+            total = own[k % 2, part] + given[k, part].astype(F32)
 
             @pl.when(k < chips - 1)
             def _():
@@ -342,9 +281,11 @@
             def _():
                 o_ref[part] = total
 
-        @pl.when(k < chips - 1)
-        def _():
-            make(k + 1)
+            if c == 0:
+
+                @pl.when(k < chips - 1)
+                def _():
+                    make(k + 1)
 
         if extra is not None:
             extra(k)
@@ -369,7 +310,7 @@
     chips = count // 2
     dma = pltpu.SemaphoreType.DMA
     return [
-        pltpu.VMEM((rows, columns), F32),
+        pltpu.VMEM((2, rows, columns), F32),
         pltpu.VMEM((chips - 1, rows, columns), BF16),
         pltpu.VMEM((chips - 1, rows, columns), BF16),
         pltpu.VMEM((chips, rows, columns), BF16),
@@ -398,6 +339,7 @@
     widths,
     x_ref,
     small_ref,
+    wr_ref,
     wq_ref,
     wk_ref,
     wv_ref,
@@ -408,6 +350,7 @@
     w_ref,
     wo_all,
     small_all,
+    wr_all,
     wd_all,
     land,
     ring_out,
@@ -440,9 +383,12 @@
         (wq_ref.at[:, q_cols], w_ref.at[:, pl.ds(0, gcols)], 0),
         (wk_ref.at[:, kv_cols], w_ref.at[:, pl.ds(gcols, hd)], 0),
         (wv_ref.at[:, kv_cols], w_ref.at[:, pl.ds(gcols + hd, hd)], 0),
+        (wr_ref, wr_all, 1),
     ]
     start, wait = crossing(shards, items, x_out, x_in, x_own)
-    start_down, wait_down = crossing(shards, [(wd_ref, wd_all, 1)], d_out, d_in)
+    start_down, wait_down = crossing(
+        shards, [(wd_ref.at[pl.ds(0, wd_all.shape[0])], wd_all, 1)], d_out, d_in
+    )
     owner = group * gcols // wo_ref.shape[0]
     wo_src = wo_ref.at[pl.ds(pl.multiple_of(group * gcols % wo_ref.shape[0], 16), gcols)]
     wo_own = pltpu.make_async_copy(wo_src, wo_all, o_own)
@@ -536,7 +482,20 @@
 
 
 def front(
-    x, small, w_query, key_weight, value_weight, w_out, w_down, hd, count, shards, call, cuts=4
+    x,
+    small,
+    w_router,
+    w_query,
+    key_weight,
+    value_weight,
+    w_out,
+    w_down,
+    down_rows,
+    hd,
+    count,
+    shards,
+    call,
+    cuts=4,
 ):
     block, dim = x.shape
     gcols = w_query.shape[1] // count
@@ -552,14 +511,15 @@
             jax.ShapeDtypeStruct((dim, columns), BF16),
             jax.ShapeDtypeStruct((gcols, w_out.shape[1]), BF16),
             jax.ShapeDtypeStruct((shards,) + small.shape, BF16),
-            whole_of(w_down, 1, shards),
+            whole_of(w_router, 1, shards),
+            jax.ShapeDtypeStruct((down_rows, dim), BF16),
         ),
-        in_specs=[VMEM, VMEM] + [ANY] * 5,
-        out_specs=[ANY, VMEM, VMEM, VMEM, VMEM, ANY],
+        in_specs=[VMEM, VMEM, VMEM] + [ANY] * 5,
+        out_specs=[ANY, VMEM, VMEM, VMEM, VMEM, VMEM, ANY],
         scratch_shapes=gather_scratch(count, cuts, block, dim)
-        + crossing_scratch(shards, 4)
+        + crossing_scratch(shards, 5)
         + [
-            dma((4,)),
+            dma((5,)),
         ]
         + crossing_scratch(shards, 1)
         + [
@@ -571,35 +531,58 @@
             dma,
         ],
         compiler_params=remote_params(call, 48),
-    )(x, small, w_query, key_weight, value_weight, w_out, w_down)
+    )(x, small, w_router, w_query, key_weight, value_weight, w_out, w_down)
 
 
 def out_back_kernel(
-    count, cuts, da_ref, w_ref, o_ref, hid_ref, de_ref, do_ref, part_ref, down_ref, land, *rest
+    count,
+    cuts,
+    da_ref,
+    w_ref,
+    o_ref,
+    hid_ref,
+    de_ref,
+    xs_ref,
+    dgu_ref,
+    do_ref,
+    part_ref,
+    down_ref,
+    up_ref,
+    land,
+    *rest,
 ):
     sems = rest[:4]
-    total, hid, de, hid_sem, de_sem = rest[4:]
+    total, hid, du, de, xs, sem, tile_sem = rest[4:]
     block = da_ref.shape[0]
     columns = de.shape[2]
+    ffe = hid.shape[1]
     total[...] = jnp.zeros_like(total)
-    load_hid = pltpu.make_async_copy(hid_ref, hid, hid_sem)
-
-    def load_de(s):
+    loads = [
+        pltpu.make_async_copy(hid_ref, hid, sem.at[0]),
+        pltpu.make_async_copy(dgu_ref.at[:, pl.ds(ffe, ffe)], du, sem.at[1]),
+    ]
+
+    def tiles(s):
         part = pl.ds(pl.multiple_of(s * columns, 128), columns)
-        return pltpu.make_async_copy(de_ref.at[:, part], de.at[s % 2], de_sem.at[s % 2])
+        return [
+            pltpu.make_async_copy(src.at[:, part], dst.at[s % 2], tile_sem.at[s % 2, n])
+            for n, (src, dst) in enumerate(((de_ref, de), (xs_ref, xs)))
+        ]
 
     def begin():
-        load_hid.start()
-        load_de(0).start()
+        for load in loads + tiles(0):
+            load.start()
 
     def use(s, first, second, pump):
         @pl.when(s == 0)
         def _():
-            load_hid.wait()
+            for load in loads:
+                load.wait()
 
         @pl.when(s < count // 2 - 1)
         def _():
-            load_de(s + 1).start()
+            for load in tiles(s + 1):
+                load.start()
 
         pair = land[s]
         a = at_block(first, block)
@@ -610,18 +593,23 @@
         pump(0)
         total[...] += mm(jnp.concatenate([o_ref[a, :], o_ref[b, :]], axis=0), pair, TN)
         pump(1)
-        load_de(s).wait()
+        for load in tiles(s):
+            load.wait()
         part = pl.ds(pl.multiple_of(s * columns, 128), columns)
         down_ref[:, part] = mm(hid[...], de[s % 2], TN).astype(BF16)
-        for c in range(2, cuts):
+        pump(2)
+        rows = pl.ds(pl.multiple_of(s * columns, 16), columns)
+        up_ref[rows, :] = mm(xs[s % 2], du[...], TN).astype(BF16)
+        for c in range(3, cuts):
             pump(c)
 
     gather_steps(count, cuts, da_ref, land, sems, use, 1, begin)
     part_ref[...] = total[...].astype(BF16)
 
 
-def out_back(da, w, o, hid, de, count, call, cuts=4):
+def out_back(da, w, o, hid, de, xs, dgu, count, call, cuts=4):
     block, dim = da.shape
+    ffe = hid.shape[1]
     chips = count // 2
     dma = pltpu.SemaphoreType.DMA
     return pl.pallas_call(
@@ -629,20 +617,23 @@
         out_shape=(
             jax.ShapeDtypeStruct(o.shape, BF16),
             jax.ShapeDtypeStruct(w.shape, BF16),
-            jax.ShapeDtypeStruct((hid.shape[1], dim), BF16),
+            jax.ShapeDtypeStruct((ffe, dim), BF16),
+            jax.ShapeDtypeStruct((dim, ffe), BF16),
         ),
-        in_specs=[VMEM] * 3 + [ANY] * 2,
-        out_specs=[VMEM] * 3,
+        in_specs=[VMEM] * 3 + [ANY] * 4,
+        out_specs=[VMEM] * 4,
         scratch_shapes=gather_scratch(count, cuts, block, dim)
         + [
             pltpu.VMEM(w.shape, F32),
             pltpu.VMEM(hid.shape, BF16),
+            pltpu.VMEM(hid.shape, BF16),
             pltpu.VMEM((2, de.shape[0], dim // chips), BF16),
-            dma,
+            pltpu.VMEM((2, xs.shape[0], dim // chips), BF16),
             dma((2,)),
+            dma((2, 2)),
         ],
-        compiler_params=remote_params(call, 48),
-    )(da, w, o, hid, de)
+        compiler_params=remote_params(call, 56),
+    )(da, w, o, hid, de, xs, dgu)
 
 
 def product_kernel(count, shards, cuts, dims, axes, y_ref, w_ref, *refs):
@@ -651,7 +642,11 @@
     rest = refs[2 * cargo + 1 :]
     block = o_ref.shape[0]
     if cargo:
-        start, wait = crossing(shards, list(zip(srcs, dsts, axes)), *rest[9:])
+        lasts = []
+        for src, dst, axis in zip(srcs, dsts, axes):
+            rows = dst.shape[0] if axis else src.shape[0]
+            lasts.append((src.at[pl.ds(src.shape[0] - rows, rows)], dst, axis))
+        start, wait = crossing(shards, lasts, *rest[9:])
 
     def begin():
         for n in range(cargo):
@@ -670,19 +665,156 @@
         wait(n)
 
 
+def token_back_kernel(
+    count,
+    shards,
+    cuts,
+    y_ref,
+    w_ref,
+    gains_ref,
+    h_ref,
+    o_ref,
+    sum_ref,
+    *rest,
+):
+    chips = count // 2
+    block = o_ref.shape[0]
+    hbuf, grad, came, gains, h_sem, w_out, w_in, g_out, g_in = rest[9:]
+    mine = lax.axis_index("fsdp")
+    dim, columns = grad.shape
+    local = dim // shards
+    part = dim // chips
+    per = local // part
+    width = gains_ref.shape[1]
+
+    def chunk(k):
+        return (k + (mine + 1) % shards * per) % chips
+
+    def load(k):
+        cols = pl.ds(pl.multiple_of(chunk(k) * part, 128), part)
+        return pltpu.make_async_copy(h_ref.at[:, cols], hbuf.at[k % 2], h_sem.at[k % 2])
+
+    def send(k):
+        n = chunk(k)
+        owner = n // per
+        slot = (owner - mine + shards) % shards - 1
+        return pltpu.make_async_remote_copy(
+            src_ref=grad.at[pl.ds(pl.multiple_of(n * part, 16), part)],
+            dst_ref=came.at[slot, pl.ds(pl.multiple_of(n % per * part, 16), part)],
+            send_sem=w_out.at[k],
+            recv_sem=w_in.at[slot, n % per],
+            device_id={"fsdp": owner},
+            device_id_type=MESH,
+        )
+
+    def send_gains(i):
+        return pltpu.make_async_remote_copy(
+            src_ref=gains_ref,
+            dst_ref=gains.at[i - 1],
+            send_sem=g_out.at[i - 1],
+            recv_sem=g_in.at[i - 1],
+            device_id={"fsdp": (mine + i) % shards},
+            device_id_type=MESH,
+        )
+
+    def begin():
+        load(0).start()
+        for i in range(1, shards):
+            send_gains(i).start()
+
+    def produce(k, first, second):
+        a = y_ref[at_block(first, block), :]
+        b = y_ref[at_block(second, block), :]
+        both = mm(jnp.concatenate([a, b], axis=0), w_ref[...], NT)
+        return both[:block], both[block:]
+
+    def extra(k):
+        load(k).wait()
+
+        @pl.when(k < chips - 1)
+        def _():
+            load(k + 1).start()
+
+        rows = pl.ds(pl.multiple_of(chunk(k) * part, 16), part)
+        grad[rows, :] = mm(hbuf[k % 2], y_ref[...], TN).astype(BF16)
+
+        @pl.when(k < chips - per)
+        def _():
+            send(k).start()
+
+    scatter_steps(count, cuts, o_ref, rest[:5], rest[5:9], produce, extra, shards, begin)
+    total = gains_ref[...]
+    for i in range(1, shards):
+        send_gains(i).wait()
+        total = total + gains[i - 1]
+    row = lax.broadcasted_iota(jnp.int32, (16, width), 0)
+    sum_ref[pl.ds(local, 16), :] = jnp.zeros((16, columns), BF16)
+    for n in range(2):
+        sum_ref[pl.ds(local, 16), pl.ds(n * width, width)] = jnp.where(
+            row == 0, jnp.broadcast_to(total[n : n + 1, :], (16, width)), 0.0
+        ).astype(BF16)
+    for k in range(chips - per):
+        send(k).wait_send()
+    for n in range(per):
+        part_rows = pl.ds(n * part, part)
+        own = grad[pl.ds(pl.multiple_of(mine * local + n * part, 16), part), :].astype(F32)
+        for i in range(1, shards):
+            pltpu.make_async_remote_copy(
+                src_ref=grad.at[part_rows],
+                dst_ref=came.at[i - 1, part_rows],
+                send_sem=w_out.at[0],
+                recv_sem=w_in.at[i - 1, n],
+                device_id={"fsdp": (mine + i) % shards},
+                device_id_type=MESH,
+            ).wait_recv()
+            own = own + came[i - 1, part_rows, :].astype(F32)
+        sum_ref[part_rows, :] = own.astype(BF16)
+
+
+def token_back(y, w, gains, h_all, count, shards, call, cuts=2):
+    block = y.shape[0] // count
+    dim, columns = w.shape
+    chips = count // 2
+    local = dim // shards
+    others = max(1, shards - 1)
+    dma = pltpu.SemaphoreType.DMA
+    return pl.pallas_call(
+        functools.partial(token_back_kernel, count, shards, cuts),
+        out_shape=(
+            jax.ShapeDtypeStruct((block, dim), F32),
+            jax.ShapeDtypeStruct((local + 16, columns), BF16),
+        ),
+        in_specs=[VMEM] * 3 + [ANY],
+        out_specs=[VMEM] * 2,
+        scratch_shapes=scatter_scratch(count, cuts, block, dim)
+        + [
+            pltpu.VMEM((2, h_all.shape[0], dim // chips), BF16),
+            pltpu.VMEM((dim, columns), BF16),
+            pltpu.VMEM((others, local, columns), BF16),
+            pltpu.VMEM((others,) + gains.shape, F32),
+            dma((2,)),
+            dma((chips,)),
+            dma((others, chips // shards)),
+            dma((others,)),
+            dma((others,)),
+        ],
+        compiler_params=remote_params(call, 48),
+    )(y, w, gains, h_all)
+
+
 def whole_of(part, axis, shards):
     shape = list(part.shape)
     shape[axis] *= shards
     return jax.ShapeDtypeStruct(tuple(shape), part.dtype)
 
 
-def product_scattered(y, w, dims, cargo, axes, count, shards, call, cuts=2):
+def product_scattered(y, w, dims, cargo, axes, wholes, count, shards, call, cuts=2):
     block = y.shape[0] // count
     columns = w.shape[1 - dims[0][1][0]]
     return pl.pallas_call(
         functools.partial(product_kernel, count, shards, cuts, dims, axes),
         out_shape=[jax.ShapeDtypeStruct((block, columns), F32)]
-        + [whole_of(part, axis, shards) for part, axis in zip(cargo, axes)],
+        + list(wholes),
         in_specs=[VMEM, VMEM] + [ANY] * len(cargo),
         out_specs=[VMEM] + [ANY] * len(cargo),
         scratch_shapes=scatter_scratch(count, cuts, block, columns)
@@ -743,6 +875,7 @@
     wd_own,
     xs_out,
     de_out,
+    dx_ref,
     dl_out,
     ce_out,
     hid_out,
@@ -778,7 +911,14 @@
             + down_parts(i, shards, wd_refs, wd_own, wd)
         )
     ]
-    staged = ((xs, xs_out), (de, de_out), (dl, dl_out), (ce, ce_out), (hid, hid_out), (dgu, dgu_out))
+    staged = (
+        (xs, xs_out),
+        (de, de_out),
+        (dl, dl_out),
+        (ce, ce_out),
+        (hid, hid_out),
+        (dgu, dgu_out),
+    )
 
     def dy_copies(s):
         first, second = pair_owners(count, s)
@@ -812,10 +952,11 @@
                 axis=0,
             ),
         )
-        logits = jnp.where(chosen > 0.5, mm(x, router_ref[...]), -1e30)
+        logits = jnp.where(chosen > 0.5, mm(x, router_ref[...], NT), -1e30)
         weight = jnp.exp(logits - jnp.max(logits, axis=1, keepdims=True)) * chosen
         mass = jnp.sum(weight, axis=1, keepdims=True)
         expert_lane = lax.broadcasted_iota(jnp.int32, weight.shape, 1)
+        wide_lane = lax.broadcasted_iota(jnp.int32, (2 * capacity, dl.shape[1]), 1)
         gate = jnp.sum(jnp.where(expert_lane == me, weight, 0.0), axis=1, keepdims=True)
         gate = gate / jnp.where(mass > 0.0, mass, 1.0)
 
@@ -848,9 +989,14 @@
         du = (dh * silu).astype(BF16)
         dgu[rows, :ffe] = dg
         dgu[rows, ffe:] = du
+
+        @pl.when(s == 1)
+        def _():
+            dx_ref[...] = mm(dgu[rows, :], wgu[...], NT).astype(BF16)
+
         high = dgate.astype(BF16).astype(F32)
         dl[rows, :] = jnp.where(
-            expert_lane == me, high, jnp.where(expert_lane == me + 64, dgate - high, 0.0)
+            wide_lane == me, high, jnp.where(wide_lane == me + 64, dgate - high, 0.0)
         ).astype(BF16)
         for i, (src, dst) in enumerate(staged):
             pltpu.make_async_copy(src.at[rows], dst.at[rows], out_sem.at[i]).start()
@@ -868,9 +1014,12 @@
     dma = pltpu.SemaphoreType.DMA
     return pl.pallas_call(
         functools.partial(expert_kernel, count, shards, cuts, capacity),
-        out_shape=[jax.ShapeDtypeStruct((total, n), BF16) for n in widths],
+        out_shape=[
+            jax.ShapeDtypeStruct((2 * capacity if i == 2 else total, n), BF16)
+            for i, n in enumerate(widths[:2] + (dim,) + widths[2:])
+        ],
         in_specs=[VMEM] * 4 + [ANY] * 9,
-        out_specs=[ANY] * 6,
+        out_specs=[ANY] * 2 + [VMEM] + [ANY] * 4,
         scratch_shapes=gather_scratch(count, cuts, block, dim)
         + [
             pltpu.VMEM((dim, 2 * ffe), BF16),
@@ -890,6 +1039,7 @@
     capacity,
     slot_ref,
     dl,
+    dx0_ref,
     xs_ref,
     dgu_ref,
     wg_ref,
@@ -897,18 +1047,16 @@
     wg_own,
     wu_own,
     o_ref,
-    gu_out,
+    gate_out,
     *rest,
 ):
     bufs, sems = rest[:5], rest[5:9]
-    xs, dgu, wgu, gu, sem, w_sem, gu_sem = rest[9:]
+    dx, xs, dgu, wgu, gate, sem, w_sem, gate_sem = rest[9:]
     chips = count // 2
     block = o_ref.shape[0]
-    dim = xs.shape[1]
-    loads = [
-        pltpu.make_async_copy(src, dst, sem.at[i])
-        for i, (src, dst) in enumerate(((dgu_ref, dgu), (xs_ref, xs)))
-    ]
+    ffe = gate.shape[1]
+    load_dgu = pltpu.make_async_copy(dgu_ref, dgu, sem.at[0])
+    load_xs = pltpu.make_async_copy(xs_ref, xs, sem.at[1])
     weights = [
         pltpu.make_async_copy(src, dst, w_sem.at[i, n])
         for i in range(shards)
@@ -916,39 +1064,47 @@
             gate_up_parts(i, shards, (wg_ref, wu_ref), (wg_own, wu_own), wgu)
         )
     ]
-    for load in loads[:1] + weights + loads[1:]:
-        load.start()
     part = xs.shape[1] // chips
 
+    def begin():
+        for load in [load_dgu] + weights + [load_xs]:
+            load.start()
+
     def produce(k, first, second):
+        rows = pl.ds(pl.multiple_of((k + 1) % chips * 2 * capacity, 16), 2 * capacity)
+
         @pl.when(k == 0)
         def _():
-            for load in loads[:1] + weights:
+            dx[...] = dx0_ref[...]
+
+        @pl.when(k == 1)
+        def _():
+            for load in [load_dgu] + weights:
                 load.wait()
 
-        pair = pl.multiple_of((k + 1) % chips * 2 * capacity, 16)
-        rows = pl.ds(pair, 2 * capacity)
+        @pl.when(k > 0)
+        def _():
+            dx[...] = mm(dgu[rows, :], wgu[...], NT).astype(BF16)
+
         pick = one_hot_of(slot_ref, first, second, capacity)
-        dx = mm(dgu[rows, :], wgu[...], NT).astype(BF16)
-        both = jnp.concatenate([mm(pick, dx, TN), mm(pick, dl[rows, :], TN)], axis=1)
+        both = jnp.concatenate([mm(pick, dx[...], TN), mm(pick, dl[rows, :], TN)], axis=1)
         return both[:block], both[block:]
 
     def extra(k):
         @pl.when(k == 0)
         def _():
-            for load in loads[1:]:
-                load.wait()
+            load_xs.wait()
 
         columns = pl.ds(pl.multiple_of(k * part, 128), part)
         rows = pl.ds(pl.multiple_of(k * part, 16), part)
-        gu[rows, :] = mm(xs[:, columns], dgu[...], TN).astype(BF16)
-        pltpu.make_async_copy(gu.at[rows], gu_out.at[rows], gu_sem).start()
-
-    scatter_steps(count, cuts, o_ref, bufs, sems, produce, extra)
-    pltpu.make_async_copy(gu, gu_out, gu_sem).wait()
-
-
-def slots_back(slot, dl, xs, dgu, weights, capacity, count, shards, call, cuts=2):
+        gate[rows, :] = mm(xs[:, columns], dgu[:, :ffe], TN).astype(BF16)
+        pltpu.make_async_copy(gate.at[rows], gate_out.at[rows], gate_sem).start()
+
+    scatter_steps(count, cuts, o_ref, bufs, sems, produce, extra, 1, begin)
+    pltpu.make_async_copy(gate, gate_out, gate_sem).wait()
+
+
+def slots_back(slot, dl, dx0, xs, dgu, weights, capacity, count, shards, call, cuts=2):
     block = slot.shape[1]
     dim, ffe = xs.shape[1], dgu.shape[1] // 2
     columns = dim + dl.shape[1]
@@ -957,16 +1113,16 @@
         functools.partial(slots_back_kernel, count, shards, cuts, capacity),
         out_shape=(
             jax.ShapeDtypeStruct((block, columns), F32),
-            jax.ShapeDtypeStruct((dim, 2 * ffe), BF16),
+            jax.ShapeDtypeStruct((dim, ffe), BF16),
         ),
-        in_specs=[VMEM] * 2 + [ANY] * 6,
+        in_specs=[VMEM] * 3 + [ANY] * 6,
         out_specs=[VMEM, ANY],
         scratch_shapes=scatter_scratch(count, cuts, block, columns)
-        + [pltpu.VMEM(a.shape, BF16) for a in (xs, dgu)]
-        + [pltpu.VMEM((dim, 2 * ffe), BF16)] * 2
+        + [pltpu.VMEM(a.shape, BF16) for a in (dx0, xs, dgu)]
+        + [pltpu.VMEM((dim, 2 * ffe), BF16), pltpu.VMEM((dim, ffe), BF16)]
         + [dma((2,)), dma((shards, 2)), dma],
         compiler_params=remote_params(call, 60),
-    )(slot, dl, xs, dgu, *weights)
+    )(slot, dl, dx0, xs, dgu, *weights)
 
 
 def split3(x):
@@ -1033,7 +1189,8 @@
     width = kn_ref.shape[1]
     block = dy_ref.shape[0]
     scale = width**-0.5 * LOG2E
-    items = [(wg_ref, wg_all, 0), (wd_ref, wd_all, 1)]
+    down = wd_all.shape[0]
+    items = [(wg_ref, wg_all, 0), (wd_ref.at[pl.ds(down, down)], wd_all, 1)]
     start_item, wait_item = crossing(shards, items, x_out, x_in)
 
     def prepare(i):
@@ -1105,7 +1262,7 @@
         ).wait()
 
 
-def attend(dy, routes, qkv, gq, gk, cos, sin, start, w_gate, w_down, count, shards, call, tile=512, cuts=4):
+def attend(dy, routes, qkv, gq, gk, cos, sin, start, w_gate, w_down, down_rows, count, shards, call, tile=512, cuts=4):
     span = qkv.shape[0]
     width = gq.shape[0]
     heads = qkv.shape[1] // width - 2
@@ -1120,7 +1277,7 @@
             jax.ShapeDtypeStruct((span, 2 * heads * width), BF16),
             jax.ShapeDtypeStruct((span, width), BF16),
             whole_of(w_gate, 0, shards),
-            whole_of(w_down, 1, shards),
+            jax.ShapeDtypeStruct((down_rows, dim), BF16),
         ),
         in_specs=[VMEM] * 8 + [ANY] * 2,
         out_specs=[ANY] + [VMEM] * 4 + [ANY] * 2,
@@ -1137,6 +1294,7 @@
 
 def attend_back_kernel(
     count,
+    shards,
     cuts,
     capacity,
     heads,
@@ -1152,14 +1310,16 @@
     sin_ref,
     start_ref,
     slot_ref,
+    part_ref,
     ce_ref,
     dqkv_ref,
     gains_ref,
     mixed_ref,
+    half_ref,
     *rest,
 ):
     bufs, sems = rest[:5], rest[5:9]
-    gx_ref, dq_ref, dk_ref, dv_ref, held, held_sem = rest[9:]
+    gx_ref, dq_ref, dk_ref, dv_ref, held, held_sem, pair, pair_own, pair_out, pair_in = rest[9:]
     span = qx_ref.shape[0]
     width = kn_ref.shape[1]
     scale = width**-0.5
@@ -1167,6 +1327,83 @@
     block = mixed_ref.shape[0]
     load = pltpu.make_async_copy(ce_ref, held, held_sem)
     load.start()
+
+    mine = lax.axis_index("fsdp")
+    me = lax.axis_index("seq")
+    lane = me % 2
+    chip_first = me - lane
+    half_rows = half_ref.shape[0]
+
+    def give_half(c):
+        return pltpu.make_async_remote_copy(
+            src_ref=part_ref.at[pl.ds(c * half_rows, half_rows)],
+            dst_ref=pair.at[(mine + lane) % 2],
+            send_sem=pair_out.at[c],
+            recv_sem=pair_in.at[(mine + lane) % 2],
+            device_id={"fsdp": lane, "seq": chip_first + c},
+            device_id_type=MESH,
+        )
+
+    def take_half(n):
+        return pltpu.make_async_remote_copy(
+            src_ref=part_ref.at[pl.ds(0, half_rows)],
+            dst_ref=pair.at[n],
+            send_sem=pair_out.at[0],
+            recv_sem=pair_in.at[n],
+            device_id={"fsdp": 1 - mine, "seq": chip_first + mine},
+            device_id_type=MESH,
+        )
+
+    keep_half = pltpu.make_async_copy(
+        part_ref.at[pl.ds(pl.multiple_of(lane * half_rows, 16), half_rows)], pair.at[0], pair_own
+    )
+
+    def meet():
+        barrier = pltpu.get_barrier_semaphore()
+        pl.semaphore_signal(
+            barrier,
+            inc=1,
+            device_id={"fsdp": 1 - mine, "seq": chip_first + mine},
+            device_id_type=MESH,
+        )
+
+        @pl.when(lane != mine)
+        def _():
+            pl.semaphore_signal(
+                barrier, inc=1, device_id={"seq": chip_first + mine}, device_id_type=MESH
+            )
+
+    def begin():
+        for c in range(2):
+
+            @pl.when((mine != lane) | (lane != c))
+            def _(c=c):
+                give_half(c).start()
+
+        @pl.when(mine == lane)
+        def _():
+            keep_half.start()
+
+    def end():
+        for c in range(2):
+
+            @pl.when((mine != lane) | (lane != c))
+            def _(c=c):
+                give_half(c).wait_send()
+
+        @pl.when(mine == lane)
+        def _():
+            keep_half.wait()
+
+        @pl.when(mine != lane)
+        def _():
+            take_half(0).wait_recv()
+
+        take_half(1).wait_recv()
+        half_ref[...] = (pair[0].astype(F32) + pair[1].astype(F32)).astype(BF16)
+
+    summing = shards == 2
+    partners = 1 + (mine != lane).astype(jnp.int32)
 
     def produce(k, first, second):
         @pl.when(k == 0)
@@ -1241,23 +1478,33 @@
     def extra(k):
         run_units(plan, k)
 
-    scatter_steps(count, cuts, mixed_ref, bufs, sems, produce, extra)
-
-
-def attend_back(qx, kn, qkv, o, do, gq, gk, cos, sin, start, slot, ce, capacity, count, call, tile=512, cuts=2):
+    if summing:
+        scatter_steps(
+            count, cuts, mixed_ref, bufs, sems, produce, extra, 1, begin, (meet, partners)
+        )
+        end()
+    else:
+        scatter_steps(count, cuts, mixed_ref, bufs, sems, produce, extra)
+        half_ref[...] = jnp.zeros_like(half_ref)
+
+
+def attend_back(qx, kn, qkv, o, do, gq, gk, cos, sin, start, slot, part, ce, capacity, count, shards, call, tile=512, cuts=2):
     span, width = kn.shape
     heads = o.shape[1] // width
     block = slot.shape[1]
     dim = ce.shape[1]
     return pl.pallas_call(
-        functools.partial(attend_back_kernel, count, cuts, capacity, heads, min(tile, span)),
+        functools.partial(
+            attend_back_kernel, count, shards, cuts, capacity, heads, min(tile, span)
+        ),
         out_shape=(
             jax.ShapeDtypeStruct(qkv.shape, BF16),
-            jax.ShapeDtypeStruct((2, width), F32),
+            jax.ShapeDtypeStruct((8, width), F32),
             jax.ShapeDtypeStruct((block, dim), F32),
+            jax.ShapeDtypeStruct((part.shape[0] // 2, dim), BF16),
         ),
-        in_specs=[VMEM] * 11 + [ANY],
-        out_specs=[VMEM] * 3,
+        in_specs=[VMEM] * 12 + [ANY],
+        out_specs=[VMEM] * 4,
         scratch_shapes=scatter_scratch(count, cuts, block, dim)
         + [
             pltpu.VMEM((span, 2 * heads * width), BF16),
@@ -1266,9 +1513,61 @@
             pltpu.VMEM((span, width), F32),
             pltpu.VMEM(ce.shape, BF16),
             pltpu.SemaphoreType.DMA,
+            pltpu.VMEM((2, part.shape[0] // 2, dim), BF16),
+            pltpu.SemaphoreType.DMA,
+            pltpu.SemaphoreType.DMA((2,)),
+            pltpu.SemaphoreType.DMA((2,)),
         ],
         compiler_params=remote_params(call, 60),
-    )(qx, kn, qkv, o, do, gq[None, :], gk[None, :], cos, sin, start[None, :], slot, ce)
+    )(qx, kn, qkv, o, do, gq[None, :], gk[None, :], cos, sin, start[None, :], slot, part, ce)
+
+
+def rows_kernel(count, cuts, x_ref, small_ref, all_ref, small_all, land, ro, ri, so, si, tag, sem):
+    block = x_ref.shape[0]
+    tag[0, 0] = small_ref[...]
+
+    def use(s, first, second, pump):
+        for c in range(cuts + 1):
+            pump(c)
+        for half, owner in ((0, first), (1, second)):
+            pltpu.make_async_copy(
+                land.at[s, pl.ds(half * block, block)],
+                all_ref.at[at_block(owner, block)],
+                sem.at[half],
+            ).start()
+            small_all[owner] = tag[s, half]
+
+    gather_steps(count, cuts, x_ref, land, (ro, ri, so, si), use, 1, None, tag)
+    half_rows = count * block // 2
+    for half in range(2):
+        pltpu.make_async_copy(
+            all_ref.at[pl.ds(0, half_rows)], all_ref.at[pl.ds(0, half_rows)], sem.at[half]
+        ).wait()
+
+
+def gather_rows(x, small, count, call, cuts=4):
+    block, dim = x.shape
+    return pl.pallas_call(
+        functools.partial(rows_kernel, count, cuts),
+        out_shape=(
+            jax.ShapeDtypeStruct((count * block, dim), BF16),
+            jax.ShapeDtypeStruct((count,) + small.shape, BF16),
+        ),
+        in_specs=[VMEM] * 2,
+        out_specs=[ANY, VMEM],
+        scratch_shapes=gather_scratch(count, cuts + 1, block, dim)
+        + [pltpu.VMEM((count // 2, 2) + small.shape, BF16), pltpu.SemaphoreType.DMA((2,))],
+        compiler_params=remote_params(call, 48),
+    )(x, small)
+
+
+def row_parts(rows, cuts):
+    if cuts == 1:
+        return [pl.ds(0, rows)]
+    size = rows // cuts // 16 * 16
+    return [pl.ds(c * size, size) for c in range(cuts - 1)] + [
+        pl.ds((cuts - 1) * size, rows - (cuts - 1) * size)
+    ]
 
 
 def last_gather_kernel(
@@ -1384,8 +1683,32 @@
 
 
 def finish_kernel(
-    count, kv_heads, tile, q_ref, kv_ref, wq_ref, wk_ref, wv_ref, gain_ref, dq_ref, dk_ref, dv_ref, dg_ref
+    count,
+    kv_heads,
+    tile,
+    q_ref,
+    kv_ref,
+    wq_ref,
+    wk_ref,
+    wv_ref,
+    gain_ref,
+    out_ref,
+    gate_ref,
+    up_ref,
+    down_ref,
+    dq_ref,
+    dk_ref,
+    dv_ref,
+    dg_ref,
+    dout_ref,
+    dgate_ref,
+    dup_ref,
+    ddown_ref,
 ):
+    dout_ref[...] = out_ref[...].astype(F32)
+    dgate_ref[...] = gate_ref[...].astype(F32)
+    dup_ref[...] = up_ref[...].astype(F32)
+    ddown_ref[...] = down_ref[...].astype(F32)
     chips = count // 2
     members = count // kv_heads
     width = q_ref.shape[2]
@@ -1411,7 +1734,7 @@
     dg_ref[...] = total / gain_ref[...].astype(F32)
 
 
-def finish(q_all, kv_all, w_query, key_weight, value_weight, gain, kv_heads):
+def finish(q_all, kv_all, w_query, key_weight, value_weight, gain, others, kv_heads):
     count = q_all.shape[0]
     local, columns = w_query.shape
     rows = kv_all.shape[1]
@@ -1419,8 +1742,12 @@
     per = rows // tile
     kv_columns = key_weight.shape[1]
 
-    def row_block(n):
-        return pl.BlockSpec((tile, n), lambda r: (r, 0))
+    steps = local // tile
+
+    def row_block(n, rows=tile):
+        return pl.BlockSpec((rows, n), lambda r: (r, 0))
+
+    other_blocks = [row_block(a.shape[1], a.shape[0] // steps) for a in others]
 
     return pl.pallas_call(
         functools.partial(finish_kernel, count, kv_heads, tile),
@@ -1430,7 +1757,8 @@
             jax.ShapeDtypeStruct((local, kv_columns), F32),
             jax.ShapeDtypeStruct((local, kv_columns), F32),
             jax.ShapeDtypeStruct((local, 1), F32),
-        ),
+        )
+        + tuple(jax.ShapeDtypeStruct(a.shape, F32) for a in others),
         in_specs=[
             pl.BlockSpec((count, tile, q_all.shape[2]), lambda r: (0, r, 0)),
             pl.BlockSpec((count, tile, kv_all.shape[2]), lambda r: (0, r % per, 0)),
@@ -1438,10 +1766,12 @@
             row_block(kv_columns),
             row_block(kv_columns),
             row_block(1),
-        ],
-        out_specs=[row_block(columns), row_block(kv_columns), row_block(kv_columns), row_block(1)],
+        ]
+        + other_blocks,
+        out_specs=[row_block(columns), row_block(kv_columns), row_block(kv_columns), row_block(1)]
+        + other_blocks,
         compiler_params=pltpu.CompilerParams(vmem_limit_bytes=48 * MIB),
-    )(q_all, kv_all, w_query, key_weight, value_weight, gain[:, None])
+    )(q_all, kv_all, w_query, key_weight, value_weight, gain[:, None], *others)
 
 
 def run_starts(segment):
@@ -1451,11 +1781,12 @@
 
 
 def angles(offset, head_size):
-    frequency = jnp.exp(
-        jnp.arange(head_size // 2, dtype=F32) * (-2.0 * math.log(THETA) / head_size)
-    )
+    half = head_size // 2
+    lane = jnp.arange(head_size, dtype=jnp.int32)
+    frequency = jnp.exp((lane % half).astype(F32) * (-2.0 * math.log(THETA) / head_size))
     phases = offset[:, None] * frequency[None, :]
-    return jnp.cos(phases), jnp.sin(phases)
+    sign = jnp.where(lane < half, -1.0, 1.0).astype(F32)
+    return jnp.cos(phases), jnp.sin(phases) * sign[None, :]
 
 
 def per_device(
@@ -1496,26 +1827,22 @@
     capacity = tok * top * 9 // (8 * experts)
     gcols = share * hd
 
-    small = jnp.concatenate(
-        [attn_gain, mlp_gain, query_gain, key_gain, w_router.reshape(-1)], axis=0
-    )
+    small = jnp.concatenate([attn_gain, mlp_gain, query_gain, key_gain], axis=0)
     local_dim = attn_gain.shape[0]
     local_hd = query_gain.shape[0]
     small = jnp.pad(small, (0, -small.shape[0] % (16 * 128))).reshape(-1, 128)
-    down_rows = w_down.shape[1] // 3 // 16 * 16
-    downs = (
-        w_down[0, :down_rows],
-        w_down[0, down_rows : 2 * down_rows],
-        w_down[0, 2 * down_rows :],
-    )
-    h1_all, qkv, w_qkv, w_o, small, wd1 = front(
+    ffe = w_down.shape[1]
+    down_rows = ffe // 3 // 16 * 16
+    h1_all, qkv, w_qkv, w_o, small, router, wd1 = front(
         activations[0],
         small,
+        w_router.T,
         w_query,
         key_weight,
         value_weight,
         w_out,
-        downs[0],
+        w_down[0],
+        down_rows,
         hd,
         count,
         shards,
@@ -1523,19 +1850,16 @@
     )
     small = small.reshape(shards, -1)
     cut = [local_dim, 2 * local_dim, 2 * local_dim + local_hd, 2 * local_dim + 2 * local_hd]
-    g_attn, g_mlp, g_query, g_key, router = jnp.split(small, cut, axis=1)
+    g_attn, g_mlp, g_query, g_key, _ = jnp.split(small, cut, axis=1)
     g_attn = g_attn.reshape(-1).astype(F32)
     g_mlp = g_mlp.reshape(-1).astype(F32)
     g_query = g_query.reshape(-1).astype(F32)
     g_key = g_key.reshape(-1).astype(F32)
-    router = router[:, : local_dim * experts].reshape(dim, experts)
     r1 = lax.rsqrt(jnp.mean(x * x, axis=-1, keepdims=True) + EPSILON)
     position, doc_start = run_starts(segment)
-    cosine, sine = angles((position - doc_start).astype(F32), hd)
+    cos_full, sin_full = angles((position - doc_start).astype(F32), hd)
     start = jnp.where(segment > 0, doc_start, position)
 
-    cos_full = jnp.concatenate([cosine, cosine], axis=1)
-    sin_full = jnp.concatenate([-sine, sine], axis=1)
     routes_sent = jnp.pad(routes.T, ((0, -top % 16), (0, 0))).astype(BF16)
     dy_all, routes_all, o, qx, kn, wg, wd2 = attend(
         dy,
@@ -1547,18 +1871,25 @@
         sin_full,
         start,
         w_gate[0],
-        downs[1],
+        w_down[0],
+        down_rows,
         count,
         shards,
         4,
     )
-    x2, wu, wd3 = product_scattered(o, w_o, NN, [w_up[0], downs[2]], (0, 1), count, shards, 2)
+    wholes = (
+        whole_of(w_up[0], 0, shards),
+        jax.ShapeDtypeStruct((ffe - 2 * down_rows, dim), BF16),
+    )
+    x2, wu, wd3 = product_scattered(
+        o, w_o, NN, [w_up[0], w_down[0]], (0, 1), wholes, count, shards, 2
+    )
     x2 = x + x2
 
     r2 = lax.rsqrt(jnp.mean(x2 * x2, axis=-1, keepdims=True) + EPSILON)
     h2 = (x2 * r2 * g_mlp).astype(BF16)
     def gates_of(hidden, chosen):
-        logits = mm(hidden, router)
+        logits = mm(hidden, router, NT)
         return jax.nn.softmax(jnp.where(chosen, logits, -1e30), axis=-1) * chosen
 
     def chosen_of(named):
@@ -1570,13 +1901,11 @@
     rank = jnp.cumsum(hit.astype(jnp.int32), axis=1) - hit
     slot = jnp.where(hit & (rank < capacity), rank, -1)
     chosen_all = chosen_of(routes_all.reshape(span, top)).astype(BF16)
-    chosen_all = jnp.pad(chosen_all, ((0, 0), (0, 128 - experts)))
-    router_wide = jnp.pad(router, ((0, 0), (0, 128 - experts)))
-    xs, de, dl, ce, hid, dgu = expert_gathered(
+    xs, de, dx0, dl, ce, hid, dgu = expert_gathered(
         h2,
         slot,
         chosen_all,
-        router_wide,
+        router,
         dy_all,
         (wg, wu, wd1, wd2, wd3, w_gate[0], w_up[0], w_down[0]),
         capacity,
@@ -1584,26 +1913,43 @@
         shards,
         3,
     )
-    dh2_wide, w_gate_up_part = slots_back(
-        slot, dl, xs, dgu, (wg, wu, w_gate[0], w_up[0]), capacity, count, shards, 6
+    dh2_wide, w_gate_part = slots_back(
+        slot, dl, dx0, xs, dgu, (wg, wu, w_gate[0], w_up[0]), capacity, count, shards, 6
     )
     dgate = dh2_wide[:, dim : dim + experts] + dh2_wide[:, dim + 64 : dim + 64 + experts]
     gates = gates_of(h2, chosen_of(routes))
     dlogits = (gates * (dgate - jnp.sum(gates * dgate, axis=-1, keepdims=True))).astype(BF16)
-    dh2 = dh2_wide[:, :dim] + mm(dlogits, router, NT)
-    router_part = mm(h2, dlogits, TN)
+    dh2 = dh2_wide[:, :dim] + mm(dlogits, router)
+    router_part = mm(dlogits, h2, TN)
     xh = x2 * r2
     mlp_gain_part = jnp.sum(dh2 * xh, axis=0)
     dn = dh2 * g_mlp
     dx2 = dy.astype(F32) + r2 * (dn - xh * jnp.mean(dn * xh, axis=-1, keepdims=True))
 
-    do, w_out_part, w_down_part = out_back(dx2.astype(BF16), w_o, o, hid, de, count, 7)
-    dqkv, head_gains, mixed = attend_back(
-        qx, kn, qkv, o, do, g_query, g_key, cos_full, sin_full, start, slot, ce, capacity, count, 5
+    do, w_out_part, w_down_part, w_up_part = out_back(
+        dx2.astype(BF16), w_o, o, hid, de, xs, dgu, count, 7
+    )
+    dqkv, head_gains, mixed, out_half = attend_back(
+        qx,
+        kn,
+        qkv,
+        o,
+        do,
+        g_query,
+        g_key,
+        cos_full,
+        sin_full,
+        start,
+        slot,
+        w_out_part,
+        ce,
+        capacity,
+        count,
+        shards,
+        5,
     )
     mixed = x2 + mixed
-    qkv_part = mm(h1_all, dqkv, TN).astype(BF16)
-    dh1 = product_scattered(dqkv, w_qkv, NT, [], (), count, shards, 8)[0]
+    dh1, qkv_sum = token_back(dqkv, w_qkv, head_gains, h1_all, count, shards, 8)
     xh1 = x * r1
     dn1 = dh1 * g_attn
     input_grad = dx2 + r1 * (dn1 - xh1 * jnp.mean(dn1 * xh1, axis=-1, keepdims=True))
@@ -1611,52 +1957,45 @@
     def sum_fsdp(part, axis):
         return lax.psum_scatter(part.astype(BF16), "fsdp", scatter_dimension=axis, tiled=True)
 
-    w_gate_up_grad = sum_fsdp(w_gate_up_part, 0).astype(F32)
-    w_gate_grad = w_gate_up_grad[:, : w_gate.shape[2]]
-    w_up_grad = w_gate_up_grad[:, w_gate.shape[2] :]
-    w_down_grad = sum_fsdp(w_down_part, 1).astype(F32)
-
-    small_part = jnp.concatenate(
-        [router_part.reshape(shards, -1), mlp_gain_part.reshape(shards, -1)], axis=1
-    )
-    small_rows = -(-small_part.shape[1] // dim // 16) * 16
-    small_part = jnp.pad(small_part, ((0, 0), (0, small_rows * dim - small_part.shape[1])))
-    small_sum = sum_fsdp(small_part, 0).reshape(small_rows, dim)
-
-    out_sum = jnp.sum(
-        lax.all_gather(w_out_part, "fsdp", axis=0, tiled=False).astype(F32), axis=0
-    ).astype(BF16)
-    pair = lax.all_gather(
-        out_sum,
-        "seq",
-        axis=0,
-        tiled=False,
-        axis_index_groups=[[2 * c, 2 * c + 1] for c in range(chips)],
-    )
-    w_out_grad, small_all = out_rows(pair, out_sum, small_sum, count, shards)
-    small_total = jnp.sum(small_all.astype(F32), axis=0).reshape(-1)
-    router_grad = small_total[: local_dim * experts].reshape(local_dim, experts)
-    mlp_gain_grad = small_total[local_dim * experts : local_dim * (experts + 1)]
-
-    gains_part = jnp.concatenate(
-        [head_gains[0].reshape(shards, 1, local_hd), head_gains[1].reshape(shards, 1, local_hd)],
-        axis=2,
-    ).astype(BF16)
-    gains_part = jnp.pad(
-        gains_part, ((0, 0), (0, 15), (0, qkv_part.shape[1] - 2 * local_hd))
-    )
-    qkv_part = jnp.concatenate(
-        [qkv_part.reshape(shards, local_dim, -1), gains_part], axis=1
-    ).reshape(shards * (local_dim + 16), -1)
-    qkv_sum = sum_fsdp(qkv_part, 0)
+    w_gate_sum = sum_fsdp(w_gate_part, 0)
+    w_up_sum = sum_fsdp(w_up_part, 0)
+    w_down_sum = sum_fsdp(w_down_part, 1)
+
+    small_part = jnp.concatenate([router_part, mlp_gain_part[None]], axis=0)
+    small_part = jnp.pad(small_part, ((0, -small_part.shape[0] % 16), (0, 0)))
+    small_sum = sum_fsdp(small_part, 1)
+    if shards == 2:
+        out_all, small_all = gather_rows(out_half, small_sum, count, 9)
+    else:
+        out_all, small_all = out_rows(w_out_part, small_sum, count, shards, local_rows)
+    small_total = jnp.sum(small_all.astype(F32), axis=0)
+    router_grad = small_total[:experts].T
+    mlp_gain_grad = small_total[experts]
     q_all, kv_all = last_gather(qkv_sum, gcols, local_dim, count, count // kv_heads, 10)
-    w_query_grad, w_key_grad, w_value_grad, attn_gain_grad = finish(
-        q_all, kv_all, w_query, key_weight, value_weight, attn_gain, kv_heads
+    (
+        w_query_grad,
+        w_key_grad,
+        w_value_grad,
+        attn_gain_grad,
+        w_out_grad,
+        w_gate_grad,
+        w_up_grad,
+        w_down_grad,
+    ) = finish(
+        q_all,
+        kv_all,
+        w_query,
+        key_weight,
+        value_weight,
+        attn_gain,
+        (out_all, w_gate_sum, w_up_sum, w_down_sum),
+        kv_heads,
     )
     attn_gain_grad = attn_gain_grad[:, 0]
-    head_gain_grads = jnp.sum(q_all[:, local_dim, : 2 * local_hd].astype(F32), axis=0)
-    query_gain_grad = head_gain_grads[:local_hd]
-    key_gain_grad = head_gain_grads[local_hd:]
+    head_gain_grads = jnp.sum(q_all[:, local_dim, : 2 * hd].astype(F32), axis=0)
+    own_half = lax.axis_index("fsdp") * local_hd
+    query_gain_grad = lax.dynamic_slice_in_dim(head_gain_grads[:hd], own_half, local_hd)
+    key_gain_grad = lax.dynamic_slice_in_dim(head_gain_grads[hd:], own_half, local_hd)
     return (
         mixed.astype(BF16)[None],
         input_grad[None],
@@ -1675,25 +2014,15 @@
     )
 
 
-def out_rows(pair, out_sum, small_sum, count, shards):
+def out_rows(part, small_sum, count, shards, local_rows):
     chips = count // 2
-    gcols, dim = out_sum.shape
+    gcols, dim = part.shape
     me = lax.axis_index("seq")
-    mine = lax.axis_index("fsdp")
-    if shards == 2:
-        half = lax.dynamic_slice(pair, (mine, (me % 2) * (gcols // 2), 0), (1, gcols // 2, dim))[0]
-        halves, small_all = gather_seq([half, small_sum], count, 9, (4, 1))
-        return halves.reshape(chips * gcols, dim).astype(F32), small_all
-    small_all = gather_seq([small_sum], count, 9, (1,))[0]
-    groups = count // shards
-    first = mine * groups
     group = (me % 2) * chips + me // 2
-    place = jnp.clip(group - first, 0, groups - 1)
-    keep = (group >= first) & (group < first + groups)
-    rows = jnp.where(keep, out_sum, jnp.zeros_like(out_sum))
-    blank = jnp.zeros((groups * gcols, dim), BF16)
-    total = lax.psum(lax.dynamic_update_slice(blank, rows, (place * gcols, 0)), "seq")
-    return total.astype(F32), small_all
+    blank = jnp.zeros((count * gcols, dim), BF16)
+    placed = lax.dynamic_update_slice(blank, part, (group * gcols, 0))
+    mine = lax.psum_scatter(placed, "fsdp", scatter_dimension=0, tiled=True)
+    return lax.psum(mine, "seq"), lax.all_gather(small_sum, "seq", axis=0, tiled=False)
 
 
 def solution(mesh):

time: 666 us -> 640 us (0.961)
  other arithmetic: 45.6 us -> 23 us
  Pallas kernels: 552 us -> 570 us
  matrix products: 12.1 us -> 2.32 us
  local copies, waits for them, and re-layouts: 32.5 us -> 23.9 us
    pallas_call x2 -> x3, Pallas kernels: 108 us -> 159 us  [the longest x1 55.1 us: attend_back(): pl.pallas_call(functools.partial(attend_back_kernel, count, shards, cuts,...]
    pallas_call x2 -> x1, Pallas kernels: 95.2 us -> 49 us  [product_scattered(): pl.pallas_call(functools.partial(product_kernel, count, shards, cuts, dim...]
    convert_element_type x3 -> x2, other arithmetic: 14.6 us -> 0.08 us  [the longest x1 0.08 us: per_device(): cos_full, sin_full = angles((position - doc_start).astype(F32), hd)]
    pallas_call x1, Pallas kernels: 15.5 us -> 27.7 us  [finish(): pl.pallas_call(functools.partial(finish_kernel, count, kv_heads, tile), g...]
    dot_general x4 -> x3, matrix products: 12.1 us -> 2.32 us  [mm(): return lax.dot_general(a, b, dims, preferred_element_type=F32)]
    pallas_call x1, Pallas kernels: 61.8 us -> 53.5 us  [slots_back(): pl.pallas_call(functools.partial(slots_back_kernel, count, shards, cuts,...]
  transfers between devices with their start and end apart: 6 -> 4, of which waited for: 0 -> 0; matrix products, arithmetic and copies ran while one was open for 7% -> 2% of each run, Pallas kernels for 35% -> 44%
where the time goes in v5:
time: 640 us; the launch traced here: 635 us
  Pallas kernels  570 us (89%)
  local copies, waits for them, and re-layouts  23.9 us (4%)
  other arithmetic  23 us (4%)
  between operations  14.4 us (2%)
    pallas_call x1, Pallas kernels, last_gather(): pl.pallas_call(functools.partial(last_gather_kernel, count, members, cuts...  64.1 us
    pallas_call x1, Pallas kernels, attend(): pl.pallas_call(functools.partial(attend_kernel, count, shards, cuts, head...  55.7 us
    pallas_call x1, Pallas kernels, attend_back(): pl.pallas_call(functools.partial(attend_back_kernel, count, shards, cuts,...  55.1 us
    pallas_call x1, Pallas kernels, expert_gathered(): pl.pallas_call(functools.partial(expert_kernel, count, shards, cuts, capa...  54.7 us
    pallas_call x1, Pallas kernels, out_back(): pl.pallas_call(functools.partial(out_back_kernel, count, cuts), out_shape...  53.7 us
    pallas_call x1, Pallas kernels, token_back(): pl.pallas_call(functools.partial(token_back_kernel, count, shards, cuts),...  53.6 us
    pallas_call x1, Pallas kernels, slots_back(): pl.pallas_call(functools.partial(slots_back_kernel, count, shards, cuts,...  53.5 us
    pallas_call x1, Pallas kernels, front(): pl.pallas_call(functools.partial(front_kernel, count, shards, cuts, (gcol...  52.4 us
  transfers between devices with their start and end apart: 4, of which 0 were waited for; matrix products, arithmetic and copies ran while one was open for 2% of the time, Pallas kernels for 44%

profile of v5, /device:TPU:0, one launch (start us, length us, event | category | flops | bytes accessed | tf_op | source)
XLA Modules:
  0.0 635.2 jit_solution(7340561641119292187)
XLA Ops:
  8.8 2.8 concatenate.12
  12.7 1.2 copy-done.4
  13.9 1.2 copy-done.6
  15.9 52.4 %shard_map.263 = (bf16[2048,2048]{1,0:T(8,128)(2,1)}, bf16[2048,512]{1,0:T(8,128)(2,1)}, bf16[2048,512]{1,0:T(8,128)(2,1)}, bf16[256,2048]{1,0:T(8,128)(2,1)S(1)...) custom-call(bf16[128,2048]{1,0:T(8,128)(2,1)S(1)} %bitcast.74, ...), custom_call_target="tpu_custom_call" | custom-call | tf_op jit(solution)/shard_map/pallas_call | solution.py:506
  72.9 1.1 iota_select_fusion.start_ref
  74.0 5.5 fusion.7
  79.5 55.7 %shard_map.264 = (bf16[2048,2048]{1,0:T(8,128)(2,1)}, bf16[16,16,128]{2,1,0:T(8,128)(2,1)}, bf16[2048,256]{1,0:T(8,128)(2,1)}, bf16[2048,512]{1,0:T(8,128)(2,1)}...) custom-call(bf16[128,2048]{1,0:T(8,128)(2,1)} %bitcast.84, ...), custom_call_target="tpu_custom_call" | custom-call | tf_op jit(solution)/shard_map/pallas_call | solution.py:1271
  138.9 1.2 copy-done.1
  140.1 49.0 %shard_map.265 = (f32[128,2048]{1,0:T(8,128)S(1)}, bf16[2048,768]{1,0:T(8,128)(2,1)}, bf16[256,2048]{1,0:T(8,128)(2,1)S(1)}) custom-call(bf16[2048,256]{1,0:T(8,128)(2,1)S(1)} %copy-done.1, bf16[256,2048]{1,0:T(8,128)(2,1)S(1)} %get-tuple-element.65.w_ref, bf16[1024,768]{1,0:T(8,128)(2,1)S(1)} %bitcast.73, bf16[768,1024]{1,0:T(8,128)(2,1)} %bitcast.79), custom_call_target="tpu_custom_call" | custom-call | tf_op jit(solution)/shard_map/pallas_call | solution.py:814
  191.2 54.7 %shard_map.266 = (bf16[1152,2048]{1,0:T(8,128)(2,1)}, bf16[1152,2048]{1,0:T(8,128)(2,1)}, bf16[144,2048]{1,0:T(8,128)(2,1)}, bf16[1152,128]{1,0:T(8,128)(2,1)}, ...) custom-call(bf16[128,2048]{1,0:T(8,128)(2,1)} %copy-done.25, ...), custom_call_target="tpu_custom_call" | custom-call | tf_op jit(solution)/shard_map/pallas_call | solution.py:1015
  245.9 53.5 %shard_map.267 = (f32[128,2176]{1,0:T(8,128)}, bf16[2048,768]{1,0:T(8,128)(2,1)}) custom-call(s32[16,128]{1,0:T(8,128)} %and_select_fusion.slot_ref, bf16[1152,128]{1,0:T(8,128)(2,1)} %get-tuple-element.77.dl, bf16[144,2048]{1,0:T(8,128)(2,1)} %get-tuple-element.78.dx0_ref, bf16[1152,2048]{1,0:T(8,128)(2,1)} %get-tuple-element.79.xs_ref, ...), custom_call_target="tpu_custom_call" | custom-call | tf_op jit(solution)/shard_map/pallas_call | solution.py:1112
  299.4 1.1 multiply_reduce_fusion.3
  301.9 1.8 multiply_reduce_fusion
  305.3 1.1 fusion.22.da_ref
  306.4 53.7 %shard_map.268 = (bf16[2048,256]{1,0:T(8,128)(2,1)}, bf16[256,2048]{1,0:T(8,128)(2,1)}, bf16[768,2048]{1,0:T(8,128)(2,1)}, bf16[2048,768]{1,0:T(8,128)(2,1)}) custom-call(bf16[128,2048]{1,0:T(8,128)(2,1)} %fusion.22.da_ref, bf16[256,2048]{1,0:T(8,128)(2,1)} %copy-done.8, bf16[2048,256]{1,0:T(8,128)(2,1)} %get-tuple-element.64.y_ref.o_ref, ...), custom_call_target="tpu_custom_call" | custom-call | tf_op jit(solution)/shard_map/pallas_call | solution.py:615
  361.6 55.1 %shard_map.269 = (bf16[2048,512]{1,0:T(8,128)(2,1)}, f32[8,128]{1,0:T(8,128)}, f32[128,2048]{1,0:T(8,128)}, bf16[128,2048]{1,0:T(8,128)(2,1)}) custom-call(bf16[2048,512]{1,0:T(8,128)(2,1)} %get-tuple-element.67.qx_ref, bf16[2048,128]{1,0:T(8,128)(2,1)} %get-tuple-element.68.kn_ref, bf16[2048,512]{1,0:T(8,128)(2,1)} %get-tuple-element.62.qkv_ref, ...), custom_call_target="tpu_custom_call" | custom-call | tf_op jit(solution)/shard_map/pallas_call | solution.py:1496
  416.7 1.6 copy-done.10
  418.9 53.6 %shard_map.270 = (f32[128,2048]{1,0:T(8,128)S(1)}, bf16[1040,512]{1,0:T(8,128)(2,1)S(1)}) custom-call(bf16[2048,512]{1,0:T(8,128)(2,1)S(1)} %copy-done.10, bf16[2048,512]{1,0:T(8,128)(2,1)} %get-tuple-element.89.w_ref, f32[8,128]{1,0:T(8,128)S(1)} %copy-done.21, bf16[2048,2048]{1,0:T(8,128)(2,1)} %get-tuple-element.91.h_ref), custom_call_target="tpu_custom_call" | custom-call | tf_op jit(solution)/shard_map/pallas_call | solution.py:781
  473.6 64.1 %shard_map.271 = (bf16[16,1040,256]{2,1,0:T(8,128)(2,1)}, bf16[16,256,256]{2,1,0:T(8,128)(2,1)}) custom-call(bf16[1040,512]{1,0:T(8,128)(2,1)} %copy-done.13), custom_call_target="tpu_custom_call" | custom-call | tf_op jit(solution)/shard_map/pallas_call | solution.py:1664
  540.1 4.1 fusion.6
  545.1 50.6 %shard_map.272 = (bf16[2048,2048]{1,0:T(8,128)(2,1)}, bf16[16,32,1024]{2,1,0:T(8,128)(2,1)S(1)}) custom-call(bf16[128,2048]{1,0:T(8,128)(2,1)S(1)} %copy-done.16, bf16[32,1024]{1,0:T(8,128)(2,1)S(1)} %copy-done.19), custom_call_target="tpu_custom_call" | custom-call | tf_op jit(solution)/shard_map/pallas_call | solution.py:1550
  597.1 1.4 copy-done.11
  598.5 1.4 copy-done.12
  599.9 27.7 %shard_map.273 = (f32[1024,4096]{1,0:T(8,128)}, f32[1024,512]{1,0:T(8,128)}, f32[1024,512]{1,0:T(8,128)}, f32[1024,1]{1,0:T(8,128)S(1)}, f32[2048,2048]{1,0:T(8,...) custom-call(bf16[16,1040,256]{2,1,0:T(8,128)(2,1)} %get-tuple-element.94.q_ref, ...), custom_call_target="tpu_custom_call" | custom-call | tf_op jit(solution)/shard_map/pallas_call | solution.py:1752
  (119 shorter events, 25.1 us)
Async XLA Ops:
  7.2 537.0 %reduce-scatter.5.cloned.1.call-start = ((), (), s32[]{:S(2)}) async-start(), calls=%async_computation.4 | async-start | bytes 196608 | tf_op jit(solution)/shard_map/reduce_scatter | solution.py:1958
  12.7 1.2 copy-start.4
  13.9 1.2 copy-start.6
  15.9 53.5 %copy-start.28 = (s32[1,128,8]{1,2,0:T(8,128)S(1)}, s32[1,128,8]{1,2,0:T(8,128)}, u32[]{:S(2)}) copy-start(s32[1,128,8]{1,2,0:T(8,128)} %param.19) | copy-start | bytes 12292
  69.3 69.6 %copy-start.8 = (bf16[256,2048]{1,0:T(8,128)(2,1)}, bf16[256,2048]{1,0:T(8,128)(2,1)S(1)}, u32[]{:S(2)}) copy-start(bf16[256,2048]{1,0:T(8,128)(2,1)S(1)} %get-tuple-element.65.w_ref) | copy-start | bytes 3145732
  69.3 121.0 %copy-start.17 = (bf16[16,2048]{1,0:T(8,128)(2,1)}, bf16[16,2048]{1,0:T(8,128)(2,1)S(1)}, u32[]{:S(2)}) copy-start(bf16[16,2048]{1,0:T(8,128)(2,1)S(1)} %get-tuple-element.70.router_ref) | copy-start | bytes 196612
  79.5 59.4 %copy-start = (bf16[1,1024,768]{2,1,0:T(8,128)(2,1)S(1)}, bf16[1,1024,768]{2,1,0:T(8,128)(2,1)}, u32[]{:S(2)}) copy-start(bf16[1,1024,768]{2,1,0:T(8,128)(2,1)} %param.30) | copy-start | bytes 4718596
  135.2 53.9 %copy-start.3 = (bf16[1,128,2048]{2,1,0:T(8,128)(2,1)S(1)}, bf16[1,128,2048]{2,1,0:T(8,128)(2,1)}, u32[]{:S(2)}) copy-start(bf16[1,128,2048]{2,1,0:T(8,128)(2,1)} %param.16) | copy-start | bytes 1572868
  138.9 1.2 copy-start.1
  190.1 115.2 %copy-start.22 = (f32[128,2048]{1,0:T(8,128)}, f32[128,2048]{1,0:T(8,128)S(1)}, u32[]{:S(2)}) copy-start(f32[128,2048]{1,0:T(8,128)S(1)} %get-tuple-element.113) | copy-start | bytes 3145732
  245.9 55.7 %copy-start.26 = (bf16[128,2048]{1,0:T(8,128)(2,1)S(1)}, bf16[128,2048]{1,0:T(8,128)(2,1)}, u32[]{:S(2)}) copy-start(bf16[128,2048]{1,0:T(8,128)(2,1)} %copy-done.25) | copy-start | bytes 1572868
  245.9 55.9 %copy-start.18 = (bf16[16,2048]{1,0:T(8,128)(2,1)S(1)}, bf16[16,2048]{1,0:T(8,128)(2,1)}, u32[]{:S(2)}) copy-start(bf16[16,2048]{1,0:T(8,128)(2,1)} %copy-done.17) | copy-start | bytes 196612
  301.9 3.4 copy-start.24
  303.6 2.8 copy-start.23
  304.4 292.7 %reduce-scatter.7.cloned.1.call-start = ((), (), s32[]{:S(2)}) async-start(), calls=%async_computation.5 | async-start | bytes 4718592 | tf_op jit(solution)/shard_map/reduce_scatter | solution.py:1958
  305.2 291.9 %reduce-scatter.9.cloned.1.call-start = ((), (), s32[]{:S(2)}) async-start(), calls=%async_computation.6 | async-start | bytes 4718592 | tf_op jit(solution)/shard_map/reduce_scatter | solution.py:1958
  360.1 237.0 %reduce-scatter.11.cloned.1.call-start = ((), (), s32[]{:S(2)}) async-start(), calls=%async_computation.7 | async-start | bytes 4718592 | tf_op jit(solution)/shard_map/reduce_scatter | solution.py:1958
  416.7 1.6 copy-start.10
  473.6 66.5 %copy-start.9 = (f32[128,2048]{1,0:T(8,128)}, f32[128,2048]{1,0:T(8,128)S(1)}, u32[]{:S(2)}) copy-start(f32[128,2048]{1,0:T(8,128)S(1)} %get-tuple-element.92) | copy-start | bytes 3145732
  540.1 4.1 copy-start.16
  540.1 57.0 %copy-start.5 = (bf16[1024,512]{1,0:T(8,128)(2,1)S(1)}, bf16[1024,512]{1,0:T(8,128)(2,1)}, u32[]{:S(2)}) copy-start(bf16[1024,512]{1,0:T(8,128)(2,1)} %wk_ref.3) | copy-start | bytes 3145732
  540.1 57.0 %copy-start.7 = (bf16[1024,512]{1,0:T(8,128)(2,1)S(1)}, bf16[1024,512]{1,0:T(8,128)(2,1)}, u32[]{:S(2)}) copy-start(bf16[1024,512]{1,0:T(8,128)(2,1)} %wv_ref.3) | copy-start | bytes 3145732
  597.1 1.4 copy-start.11
  598.5 1.4 copy-start.12
  (10 other events, 8.8 us)
Sparse Core Ops, SparseCore 0:
  304.6 8.4 reduce-scatter.4
  315.3 43.3 reduce-scatter.6
  361.0 54.5 reduce-scatter.8
  417.7 64.2 reduce-scatter.10

commit v6 on v5

--- a/solution.py
+++ b/solution.py
@@ -432,7 +432,7 @@
             wait(0)
             for f in range(shards):
                 for r in range(local // 128):
-                    gain[:, pl.ds(f * local + r * 128, 128)] = small_all[f, r : r + 1, :].astype(F32)
+                    gain[:, pl.ds(f * local + r * 128, 128)] = small_all[f, r : r + 1, :]
 
         x = land[s].astype(F32)
         r1 = lax.rsqrt(jnp.mean(x * x, axis=1, keepdims=True) + EPSILON)
@@ -510,7 +510,7 @@
             jax.ShapeDtypeStruct((count * block, columns), BF16),
             jax.ShapeDtypeStruct((dim, columns), BF16),
             jax.ShapeDtypeStruct((gcols, w_out.shape[1]), BF16),
-            jax.ShapeDtypeStruct((shards,) + small.shape, BF16),
+            jax.ShapeDtypeStruct((shards,) + small.shape, F32),
             whole_of(w_router, 1, shards),
             jax.ShapeDtypeStruct((down_rows, dim), BF16),
         ),
@@ -546,13 +546,13 @@
     dgu_ref,
     do_ref,
     part_ref,
-    down_ref,
-    up_ref,
+    down_out,
+    up_out,
     land,
     *rest,
 ):
     sems = rest[:4]
-    total, hid, du, de, xs, sem, tile_sem = rest[4:]
+    total, hid, du, de, xs, down_ref, up_ref, sem, tile_sem, store_sem = rest[4:]
     block = da_ref.shape[0]
     columns = de.shape[2]
     ffe = hid.shape[1]
@@ -600,11 +600,15 @@
         pump(2)
         rows = pl.ds(pl.multiple_of(s * columns, 16), columns)
         up_ref[rows, :] = mm(xs[s % 2], du[...], TN).astype(BF16)
+        pltpu.make_async_copy(down_ref.at[:, part], down_out.at[:, part], store_sem.at[0]).start()
+        pltpu.make_async_copy(up_ref.at[rows], up_out.at[rows], store_sem.at[1]).start()
         for c in range(3, cuts):
             pump(c)
 
     gather_steps(count, cuts, da_ref, land, sems, use, 1, begin)
     part_ref[...] = total[...].astype(BF16)
+    pltpu.make_async_copy(down_ref, down_out, store_sem.at[0]).wait()
+    pltpu.make_async_copy(up_ref, up_out, store_sem.at[1]).wait()
 
 
 def out_back(da, w, o, hid, de, xs, dgu, count, call, cuts=4):
@@ -621,7 +625,7 @@
             jax.ShapeDtypeStruct((dim, ffe), BF16),
         ),
         in_specs=[VMEM] * 3 + [ANY] * 4,
-        out_specs=[VMEM] * 4,
+        out_specs=[VMEM] * 2 + [ANY] * 2,
         scratch_shapes=gather_scratch(count, cuts, block, dim)
         + [
             pltpu.VMEM(w.shape, F32),
@@ -629,8 +633,11 @@
             pltpu.VMEM(hid.shape, BF16),
             pltpu.VMEM((2, de.shape[0], dim // chips), BF16),
             pltpu.VMEM((2, xs.shape[0], dim // chips), BF16),
+            pltpu.VMEM((ffe, dim), BF16),
+            pltpu.VMEM((dim, ffe), BF16),
             dma((2,)),
             dma((2, 2)),
+            dma((2,)),
         ],
         compiler_params=remote_params(call, 56),
     )(da, w, o, hid, de, xs, dgu)
@@ -1146,6 +1153,16 @@
     return jnp.concatenate([x[:, half:], x[:, :half]], axis=1)
 
 
+def rope_tables(cos_ref, sin_ref, i, tile):
+    rows, width = cos_ref.shape
+    late = i * tile // rows
+    part = pl.ds(i * tile - late * rows, tile)
+    lanes = slice(late * (width // 2), (late + 1) * (width // 2))
+    cos = cos_ref[part, :][:, lanes]
+    sin = sin_ref[part, :][:, lanes]
+    return jnp.concatenate([cos, cos], axis=1), jnp.concatenate([-sin, sin], axis=1)
+
+
 def unit_rows(u):
     r = lax.rsqrt(jnp.mean(u * u, axis=1, keepdims=True) + EPSILON)
     return r, u * r
@@ -1195,7 +1212,7 @@
 
     def prepare(i):
         rows = pl.ds(i * tile, tile)
-        cos, sin = cos_ref[rows, :], sin_ref[rows, :]
+        cos, sin = rope_tables(cos_ref, sin_ref, i, tile)
         for h in range(heads + 1):
             _, unit = unit_rows(qkv_ref[rows, pl.ds(h * width, width)].astype(F32))
             u = unit * (gk_ref[...] if h == heads else gq_ref[...])
@@ -1269,7 +1286,7 @@
     block, dim = dy.shape
     chips = count // 2
     return pl.pallas_call(
-        functools.partial(attend_kernel, count, shards, cuts, heads, min(tile, span)),
+        functools.partial(attend_kernel, count, shards, cuts, heads, min(tile, span // 2)),
         out_shape=(
             jax.ShapeDtypeStruct((count * block, dim), BF16),
             jax.ShapeDtypeStruct((count,) + routes.shape, BF16),
@@ -1415,9 +1432,11 @@
         both = mm(pick, held[pl.ds(pair, 2 * capacity), :], TN)
         return both[:block], both[block:]
 
-    def to_raw(d, h, rows, gain, row):
+    def to_raw(d, h, i, gain, row):
+        rows = pl.ds(i * tile, tile)
+        cos, sin = rope_tables(cos_ref, sin_ref, i, tile)
         r, unit = unit_rows(qkv_ref[rows, pl.ds(h * width, width)].astype(F32))
-        d = d * cos_ref[rows, :] + swap_halves(d * sin_ref[rows, :])
+        d = d * cos + swap_halves(d * sin)
         dg = d * gain
         raw = r * (dg - unit * jnp.mean(dg * unit, axis=1, keepdims=True))
         dqkv_ref[rows, pl.ds(h * width, width)] = raw.astype(BF16)
@@ -1458,12 +1477,12 @@
     def finish_keys(j):
         keys = pl.ds(j * tile, tile)
         dqkv_ref[keys, pl.ds((heads + 1) * width, width)] = dv_ref[keys, :].astype(BF16)
-        to_raw(dk_ref[keys, :] * (1.0 / LOG2E), heads, keys, gk_ref[...], 1)
+        to_raw(dk_ref[keys, :] * (1.0 / LOG2E), heads, j, gk_ref[...], 1)
 
     def finish_rows(i):
         rows = pl.ds(i * tile, tile)
         for h in range(heads):
-            to_raw(dq_ref[rows, pl.ds(h * width, width)] * scale, h, rows, gq_ref[...], 0)
+            to_raw(dq_ref[rows, pl.ds(h * width, width)] * scale, h, i, gq_ref[...], 0)
 
     tiles = span // tile
     units = [(0.3, functools.partial(prepare, i)) for i in range(tiles)]
@@ -1495,7 +1514,7 @@
     dim = ce.shape[1]
     return pl.pallas_call(
         functools.partial(
-            attend_back_kernel, count, shards, cuts, capacity, heads, min(tile, span)
+            attend_back_kernel, count, shards, cuts, capacity, heads, min(tile, span // 2)
         ),
         out_shape=(
             jax.ShapeDtypeStruct(qkv.shape, BF16),
@@ -1522,57 +1541,10 @@
     )(qx, kn, qkv, o, do, gq[None, :], gk[None, :], cos, sin, start[None, :], slot, part, ce)
 
 
-def rows_kernel(count, cuts, x_ref, small_ref, all_ref, small_all, land, ro, ri, so, si, tag, sem):
-    block = x_ref.shape[0]
-    tag[0, 0] = small_ref[...]
-
-    def use(s, first, second, pump):
-        for c in range(cuts + 1):
-            pump(c)
-        for half, owner in ((0, first), (1, second)):
-            pltpu.make_async_copy(
-                land.at[s, pl.ds(half * block, block)],
-                all_ref.at[at_block(owner, block)],
-                sem.at[half],
-            ).start()
-            small_all[owner] = tag[s, half]
-
-    gather_steps(count, cuts, x_ref, land, (ro, ri, so, si), use, 1, None, tag)
-    half_rows = count * block // 2
-    for half in range(2):
-        pltpu.make_async_copy(
-            all_ref.at[pl.ds(0, half_rows)], all_ref.at[pl.ds(0, half_rows)], sem.at[half]
-        ).wait()
-
-
-def gather_rows(x, small, count, call, cuts=4):
-    block, dim = x.shape
-    return pl.pallas_call(
-        functools.partial(rows_kernel, count, cuts),
-        out_shape=(
-            jax.ShapeDtypeStruct((count * block, dim), BF16),
-            jax.ShapeDtypeStruct((count,) + small.shape, BF16),
-        ),
-        in_specs=[VMEM] * 2,
-        out_specs=[ANY, VMEM],
-        scratch_shapes=gather_scratch(count, cuts + 1, block, dim)
-        + [pltpu.VMEM((count // 2, 2) + small.shape, BF16), pltpu.SemaphoreType.DMA((2,))],
-        compiler_params=remote_params(call, 48),
-    )(x, small)
-
-
-def row_parts(rows, cuts):
-    if cuts == 1:
-        return [pl.ds(0, rows)]
-    size = rows // cuts // 16 * 16
-    return [pl.ds(c * size, size) for c in range(cuts - 1)] + [
-        pl.ds((cuts - 1) * size, rows - (cuts - 1) * size)
-    ]
-
-
-def last_gather_kernel(
-    count, members, cuts, qkv_ref, q_all, kv_all, heap, kv_sum, sems, own_sem, mo, mi, ro, ri, so, si
-):
+def last_gather_kernel(count, members, cuts, extras, qkv_ref, *refs):
+    x_refs, (q_all, kv_all) = refs[:extras], refs[extras : extras + 2]
+    x_alls = refs[extras + 2 : 2 * extras + 2]
+    heap, kv_sum, own_sem, mo, mi, ro, ri, so, si = refs[2 * extras + 2 :]
     me, chips, lane, position, step, following, previous, sibling = places(count)
     chip = me // 2
     place = chip % members
@@ -1598,7 +1570,12 @@
             device_id_type=MESH,
         )
 
-    pieces = [(q_ref, q_all, part) for part in row_parts(q_ref.shape[0], cuts)]
+    pieces = []
+    for x_ref, x_all in zip(x_refs, x_alls):
+        parts = row_parts(x_ref.shape[0], cuts if x_ref.shape[0] >= 64 else 1)
+        pieces += [(x_ref, x_all, part) for part in parts]
+    pieces += [(q_ref, q_all, part) for part in row_parts(q_ref.shape[0], cuts)]
+    last = len(pieces)
     pieces.append((kv_sum, kv_all, pl.ds(0, rows)))
 
     def hop(c, owner, s, device, out_sem, in_sem, first_hop):
@@ -1622,24 +1599,28 @@
         give(i).start()
     mine = pltpu.make_async_copy(kv_ref.at[pl.ds(place * rows, rows)], kv_sum, own_sem.at[0])
     mine.start()
-    own_q = pltpu.make_async_copy(q_ref, q_all.at[me], own_sem.at[1])
-    own_q.start()
-    for c in range(cuts):
+    own = [
+        pltpu.make_async_copy(src, dst.at[me], own_sem.at[n + 2])
+        for n, (src, dst) in enumerate(zip((q_ref,) + x_refs, (q_all,) + x_alls))
+    ]
+    for c in range(last):
         ring(c, me, 0, True).start()
         side(c, me, 0, True).start()
+    for copy in own:
+        copy.start()
     mine.wait()
     total = kv_sum[...].astype(F32)
     for i in range(1, members):
         give(i).wait_recv()
         total = total + heap[i - 1].astype(F32)
     kv_sum[...] = total.astype(BF16)
-    own_kv = pltpu.make_async_copy(kv_sum, kv_all.at[me], own_sem.at[2])
+    own_kv = pltpu.make_async_copy(kv_sum, kv_all.at[me], own_sem.at[1])
     own_kv.start()
-    ring(cuts, me, 0, True).start()
-    side(cuts, me, 0, True).start()
+    ring(last, me, 0, True).start()
+    side(last, me, 0, True).start()
     for s in range(1, chips):
         owner = chip_of((position - s * step + chips) % chips, chips) * 2 + lane
-        for c in range(cuts + 1):
+        for c in range(last + 1):
             ring(c, owner, s - 1).wait_recv()
             if s < chips - 1:
                 ring(c, owner, s).start()
@@ -1647,39 +1628,39 @@
     for i in range(1, members):
         give(i).wait_send()
     for s in range(chips):
-        for c in range(cuts + 1):
+        for c in range(last + 1):
             side(c, me, s).wait()
             if s < chips - 1:
                 ring(c, me, s).wait_send()
-    own_q.wait()
-    own_kv.wait()
-
-
-def last_gather(qkv, gcols, local, count, members, call, cuts=4):
+    for copy in own + [own_kv]:
+        copy.wait()
+
+
+def last_gather(qkv, extras, gcols, local, count, members, call, cuts=4):
     chips = count // 2
     rows = local // members
     columns = qkv.shape[1] - gcols
-    anywhere = pl.BlockSpec(memory_space=pl.ANY)
+    pieces = cuts + 1 + sum(cuts if x.shape[0] >= 64 else 1 for x in extras)
     dma = pltpu.SemaphoreType.DMA
     return pl.pallas_call(
-        functools.partial(last_gather_kernel, count, members, cuts),
-        out_shape=(
+        functools.partial(last_gather_kernel, count, members, cuts, len(extras)),
+        out_shape=[
             jax.ShapeDtypeStruct((count, qkv.shape[0], gcols), BF16),
             jax.ShapeDtypeStruct((count, rows, columns), BF16),
-        ),
-        in_specs=[VMEM],
-        out_specs=[anywhere] * 2,
+        ]
+        + [jax.ShapeDtypeStruct((count,) + x.shape, BF16) for x in extras],
+        in_specs=[VMEM] * (1 + len(extras)),
+        out_specs=[ANY] * (2 + len(extras)),
         scratch_shapes=[
             pltpu.VMEM((members - 1, rows, columns), BF16),
             pltpu.VMEM((rows, columns), BF16),
-            dma,
-            dma((3,)),
+            dma((3 + len(extras),)),
             dma((members - 1,)),
             dma((members - 1,)),
         ]
-        + [dma((chips, cuts + 1))] * 4,
+        + [dma((chips, pieces))] * 4,
         compiler_params=pltpu.CompilerParams(collective_id=call, has_side_effects=True),
-    )(qkv)
+    )(qkv, *extras)
 
 
 def finish_kernel(
@@ -1784,9 +1765,9 @@
     half = head_size // 2
     lane = jnp.arange(head_size, dtype=jnp.int32)
     frequency = jnp.exp((lane % half).astype(F32) * (-2.0 * math.log(THETA) / head_size))
-    phases = offset[:, None] * frequency[None, :]
-    sign = jnp.where(lane < half, -1.0, 1.0).astype(F32)
-    return jnp.cos(phases), jnp.sin(phases) * sign[None, :]
+    early, late = offset.reshape(2, -1)
+    phases = jnp.where(lane[None, :] < half, early[:, None], late[:, None]) * frequency[None, :]
+    return jnp.cos(phases), jnp.sin(phases)
 
 
 def per_device(
@@ -1827,10 +1808,14 @@
     capacity = tok * top * 9 // (8 * experts)
     gcols = share * hd
 
-    small = jnp.concatenate([attn_gain, mlp_gain, query_gain, key_gain], axis=0)
     local_dim = attn_gain.shape[0]
     local_hd = query_gain.shape[0]
-    small = jnp.pad(small, (0, -small.shape[0] % (16 * 128))).reshape(-1, 128)
+    head_gains = jnp.concatenate([query_gain, key_gain], axis=0)
+    head_gains = jnp.pad(head_gains, (0, -head_gains.shape[0] % 128))
+    small = jnp.concatenate(
+        [v.astype(F32).reshape(-1, 128) for v in (attn_gain, mlp_gain, head_gains)], axis=0
+    )
+    small = jnp.pad(small, ((0, -small.shape[0] % 8), (0, 0)))
     ffe = w_down.shape[1]
     down_rows = ffe // 3 // 16 * 16
     h1_all, qkv, w_qkv, w_o, small, router, wd1 = front(
@@ -1848,13 +1833,11 @@
         shards,
         1,
     )
-    small = small.reshape(shards, -1)
-    cut = [local_dim, 2 * local_dim, 2 * local_dim + local_hd, 2 * local_dim + 2 * local_hd]
-    g_attn, g_mlp, g_query, g_key, _ = jnp.split(small, cut, axis=1)
-    g_attn = g_attn.reshape(-1).astype(F32)
-    g_mlp = g_mlp.reshape(-1).astype(F32)
-    g_query = g_query.reshape(-1).astype(F32)
-    g_key = g_key.reshape(-1).astype(F32)
+    gain_rows = local_dim // 128
+    g_attn = small[:, :gain_rows].reshape(-1)
+    g_mlp = small[:, gain_rows : 2 * gain_rows].reshape(-1)
+    g_query = small[:, 2 * gain_rows, :local_hd].reshape(-1)
+    g_key = small[:, 2 * gain_rows, local_hd : 2 * local_hd].reshape(-1)
     r1 = lax.rsqrt(jnp.mean(x * x, axis=-1, keepdims=True) + EPSILON)
     position, doc_start = run_starts(segment)
     cos_full, sin_full = angles((position - doc_start).astype(F32), hd)
@@ -1964,14 +1947,18 @@
     small_part = jnp.concatenate([router_part, mlp_gain_part[None]], axis=0)
     small_part = jnp.pad(small_part, ((0, -small_part.shape[0] % 16), (0, 0)))
     small_sum = sum_fsdp(small_part, 1)
+    extras = [out_half, small_sum] if shards == 2 else []
+    q_all, kv_all, *rows_all = last_gather(
+        qkv_sum, extras, gcols, local_dim, count, count // kv_heads, 10
+    )
     if shards == 2:
-        out_all, small_all = gather_rows(out_half, small_sum, count, 9)
+        out_all, small_all = rows_all
+        out_all = out_all.reshape(local_rows, dim)
     else:
-        out_all, small_all = out_rows(w_out_part, small_sum, count, shards, local_rows)
+        out_all, small_all = out_rows(w_out_part, small_sum, count)
     small_total = jnp.sum(small_all.astype(F32), axis=0)
     router_grad = small_total[:experts].T
     mlp_gain_grad = small_total[experts]
-    q_all, kv_all = last_gather(qkv_sum, gcols, local_dim, count, count // kv_heads, 10)
     (
         w_query_grad,
         w_key_grad,
@@ -2014,7 +2001,7 @@
     )
 
 
-def out_rows(part, small_sum, count, shards, local_rows):
+def out_rows(part, small_sum, count):
     chips = count // 2
     gcols, dim = part.shape
     me = lax.axis_index("seq")

time: 640 us -> 626 us (0.978)
  Pallas kernels: 570 us -> 563 us
    pallas_call x1 -> x0, Pallas kernels: 50.6 us -> none  [gather_rows(): pl.pallas_call(functools.partial(rows_kernel, count, cuts), out_shape=(ja...]
    pallas_call x1, Pallas kernels: 64.1 us -> 109 us  [last_gather(): pl.pallas_call(functools.partial(last_gather_kernel, count, members, cuts...]
    unnamed x61 -> x52, local copies, waits for them, and re-layouts: 14.5 us -> 13.2 us
  transfers between devices with their start and end apart: 4 -> 4, of which waited for: 0 -> 0; matrix products, arithmetic and copies ran while one was open for 2% -> 1% of each run, Pallas kernels for 44% -> 44%
where the time goes in v6:
time: 626 us; the launch traced here: 621 us
  Pallas kernels  563 us (90%)
  other arithmetic  19.9 us (3%)
  local copies, waits for them, and re-layouts  19.8 us (3%)
  between operations  14.4 us (2%)
    pallas_call x1, Pallas kernels, last_gather(): pl.pallas_call(functools.partial(last_gather_kernel, count, members, cuts...  109 us
    pallas_call x1, Pallas kernels, attend(): pl.pallas_call(functools.partial(attend_kernel, count, shards, cuts, head...  55.4 us
    pallas_call x1, Pallas kernels, expert_gathered(): pl.pallas_call(functools.partial(expert_kernel, count, shards, cuts, capa...  54.8 us
    pallas_call x1, Pallas kernels, token_back(): pl.pallas_call(functools.partial(token_back_kernel, count, shards, cuts),...  54.3 us
    pallas_call x1, Pallas kernels, attend_back(): pl.pallas_call(functools.partial(attend_back_kernel, count, shards, cuts,...  54.3 us
    pallas_call x1, Pallas kernels, slots_back(): pl.pallas_call(functools.partial(slots_back_kernel, count, shards, cuts,...  53.5 us
    pallas_call x1, Pallas kernels, front(): pl.pallas_call(functools.partial(front_kernel, count, shards, cuts, (gcol...  52.5 us
    pallas_call x1, Pallas kernels, out_back(): pl.pallas_call(functools.partial(out_back_kernel, count, cuts), out_shape...  52.3 us
  transfers between devices with their start and end apart: 4, of which 0 were waited for; matrix products, arithmetic and copies ran while one was open for 1% of the time, Pallas kernels for 44%

profile of v6, /device:TPU:0, one launch (start us, length us, event | category | flops | bytes accessed | tf_op | source)
XLA Modules:
  0.0 621.0 jit_solution(1393406029007189051)
XLA Ops:
  10.7 1.2 copy-done.5
  11.9 1.2 copy-done.7
  13.9 52.5 %shard_map.263 = (bf16[2048,2048]{1,0:T(8,128)(2,1)}, bf16[2048,512]{1,0:T(8,128)(2,1)}, bf16[2048,512]{1,0:T(8,128)(2,1)}, bf16[256,2048]{1,0:T(8,128)(2,1)S(1)...) custom-call(bf16[128,2048]{1,0:T(8,128)(2,1)S(1)} %bitcast.69, ...), custom_call_target="tpu_custom_call" | custom-call | tf_op jit(solution)/shard_map/pallas_call | solution.py:506
  70.9 1.1 iota_select_fusion.start_ref
  72.0 3.1 fusion.10
  75.1 55.4 %shard_map.264 = (bf16[2048,2048]{1,0:T(8,128)(2,1)}, bf16[16,16,128]{2,1,0:T(8,128)(2,1)}, bf16[2048,256]{1,0:T(8,128)(2,1)}, bf16[2048,512]{1,0:T(8,128)(2,1)}...) custom-call(bf16[128,2048]{1,0:T(8,128)(2,1)} %bitcast.79, ...), custom_call_target="tpu_custom_call" | custom-call | tf_op jit(solution)/shard_map/pallas_call | solution.py:1288
  134.2 1.2 copy-done.1
  135.4 48.9 %shard_map.265 = (f32[128,2048]{1,0:T(8,128)S(1)}, bf16[2048,768]{1,0:T(8,128)(2,1)}, bf16[256,2048]{1,0:T(8,128)(2,1)S(1)}) custom-call(bf16[2048,256]{1,0:T(8,128)(2,1)S(1)} %copy-done.1, bf16[256,2048]{1,0:T(8,128)(2,1)S(1)} %get-tuple-element.65.w_ref, bf16[1024,768]{1,0:T(8,128)(2,1)S(1)} %bitcast.68, bf16[768,1024]{1,0:T(8,128)(2,1)} %bitcast.73), custom_call_target="tpu_custom_call" | custom-call | tf_op jit(solution)/shard_map/pallas_call | solution.py:821
  186.3 54.8 %shard_map.266 = (bf16[1152,2048]{1,0:T(8,128)(2,1)}, bf16[1152,2048]{1,0:T(8,128)(2,1)}, bf16[144,2048]{1,0:T(8,128)(2,1)}, bf16[1152,128]{1,0:T(8,128)(2,1)}, ...) custom-call(bf16[128,2048]{1,0:T(8,128)(2,1)} %copy-done.19, ...), custom_call_target="tpu_custom_call" | custom-call | tf_op jit(solution)/shard_map/pallas_call | solution.py:1022
  241.2 53.5 %shard_map.267 = (f32[128,2176]{1,0:T(8,128)}, bf16[2048,768]{1,0:T(8,128)(2,1)}) custom-call(s32[16,128]{1,0:T(8,128)} %and_select_fusion.slot_ref, bf16[1152,128]{1,0:T(8,128)(2,1)} %get-tuple-element.77.dl, bf16[144,2048]{1,0:T(8,128)(2,1)} %get-tuple-element.78.dx0_ref, bf16[1152,2048]{1,0:T(8,128)(2,1)} %get-tuple-element.79.xs_ref, ...), custom_call_target="tpu_custom_call" | custom-call | tf_op jit(solution)/shard_map/pallas_call | solution.py:1119
  294.7 1.1 multiply_reduce_fusion.3
  295.8 1.1 multiply_convert_fusion.1
  297.1 1.8 multiply_reduce_fusion
  300.4 1.1 fusion.31.da_ref
  301.5 52.3 %shard_map.268 = (bf16[2048,256]{1,0:T(8,128)(2,1)}, bf16[256,2048]{1,0:T(8,128)(2,1)}, bf16[768,2048]{1,0:T(8,128)(2,1)}, bf16[2048,768]{1,0:T(8,128)(2,1)}) custom-call(bf16[128,2048]{1,0:T(8,128)(2,1)} %fusion.31.da_ref, bf16[256,2048]{1,0:T(8,128)(2,1)} %copy-done.4, bf16[2048,256]{1,0:T(8,128)(2,1)} %get-tuple-element.64.y_ref.o_ref, ...), custom_call_target="tpu_custom_call" | custom-call | tf_op jit(solution)/shard_map/pallas_call | solution.py:619
  355.3 54.3 %shard_map.269 = (bf16[2048,512]{1,0:T(8,128)(2,1)}, f32[8,128]{1,0:T(8,128)}, f32[128,2048]{1,0:T(8,128)}, bf16[128,2048]{1,0:T(8,128)(2,1)}) custom-call(bf16[2048,512]{1,0:T(8,128)(2,1)} %get-tuple-element.67.qx_ref, bf16[2048,128]{1,0:T(8,128)(2,1)} %get-tuple-element.68.kn_ref, bf16[2048,512]{1,0:T(8,128)(2,1)} %get-tuple-element.62.qkv_ref, ...), custom_call_target="tpu_custom_call" | custom-call | tf_op jit(solution)/shard_map/pallas_call | solution.py:1515
  409.6 1.6 copy-done.9
  411.9 54.3 %shard_map.270 = (f32[128,2048]{1,0:T(8,128)S(1)}, bf16[1040,512]{1,0:T(8,128)(2,1)S(1)}) custom-call(bf16[2048,512]{1,0:T(8,128)(2,1)S(1)} %copy-done.9, bf16[2048,512]{1,0:T(8,128)(2,1)} %get-tuple-element.89.w_ref, f32[8,128]{1,0:T(8,128)S(1)} %copy-done.18, bf16[2048,2048]{1,0:T(8,128)(2,1)} %get-tuple-element.91.h_ref), custom_call_target="tpu_custom_call" | custom-call | tf_op jit(solution)/shard_map/pallas_call | solution.py:788
  467.2 1.6 fusion.6
  468.8 109.4 %shard_map.271 = (bf16[16,1040,256]{2,1,0:T(8,128)(2,1)}, bf16[16,256,256]{2,1,0:T(8,128)(2,1)}, bf16[16,128,2048]{2,1,0:T(8,128)(2,1)}, bf16[16,32,1024]{2,1,0:T(8,128)(2,1)}) custom-call(bf16[1040,512]{1,0:T(8,128)(2,1)} %copy-done.12, bf16[128,2048]{1,0:T(8,128)(2,1)} %get-tuple-element.94.refs_0_, bf16[32,1024]{1,0:T(8,128)(2,1)} %reduce-scatter.5.cloned.1.call-done.refs_1_), custom_call_target="tpu_custom_call" | custom-call | tf_op jit(solution)/shard_map/pallas_call | solution.py:1645
  580.2 1.4 convert_reduce_fusion
  582.9 1.4 copy-done.10
  584.3 1.4 copy-done.11
  585.7 27.7 %shard_map.272 = (f32[1024,4096]{1,0:T(8,128)}, f32[1024,512]{1,0:T(8,128)}, f32[1024,512]{1,0:T(8,128)}, f32[1024,1]{1,0:T(8,128)S(1)}, f32[2048,2048]{1,0:T(8,...) custom-call(bf16[16,1040,256]{2,1,0:T(8,128)(2,1)} %get-tuple-element.95.q_ref, ...), custom_call_target="tpu_custom_call" | custom-call | tf_op jit(solution)/shard_map/pallas_call | solution.py:1733
  (108 shorter events, 23.2 us)
Async XLA Ops:
  7.2 461.6 %reduce-scatter.5.cloned.1.call-start = ((), (), s32[]{:S(2)}) async-start(), calls=%async_computation.4 | async-start | bytes 196608 | tf_op jit(solution)/shard_map/reduce_scatter | solution.py:1941
  9.7 1.0 copy-start.2
  10.7 1.2 copy-start.5
  11.9 1.2 copy-start.7
  13.9 53.6 %copy-start.24 = (s32[1,128,8]{1,2,0:T(8,128)S(1)}, s32[1,128,8]{1,2,0:T(8,128)}, u32[]{:S(2)}) copy-start(s32[1,128,8]{1,2,0:T(8,128)} %param.19) | copy-start | bytes 12292
  66.4 1.0 copy-start.13
  67.4 66.8 %copy-start.4 = (bf16[256,2048]{1,0:T(8,128)(2,1)}, bf16[256,2048]{1,0:T(8,128)(2,1)S(1)}, u32[]{:S(2)}) copy-start(bf16[256,2048]{1,0:T(8,128)(2,1)S(1)} %get-tuple-element.65.w_ref) | copy-start | bytes 3145732
  67.4 118.2 %copy-start.15 = (bf16[16,2048]{1,0:T(8,128)(2,1)}, bf16[16,2048]{1,0:T(8,128)(2,1)S(1)}, u32[]{:S(2)}) copy-start(bf16[16,2048]{1,0:T(8,128)(2,1)S(1)} %get-tuple-element.70.router_ref) | copy-start | bytes 196612
  75.1 59.1 %copy-start = (bf16[1,1024,768]{2,1,0:T(8,128)(2,1)S(1)}, bf16[1,1024,768]{2,1,0:T(8,128)(2,1)}, u32[]{:S(2)}) copy-start(bf16[1,1024,768]{2,1,0:T(8,128)(2,1)} %param.30) | copy-start | bytes 4718596
  130.5 53.9 %copy-start.3 = (bf16[1,128,2048]{2,1,0:T(8,128)(2,1)S(1)}, bf16[1,128,2048]{2,1,0:T(8,128)(2,1)}, u32[]{:S(2)}) copy-start(bf16[1,128,2048]{2,1,0:T(8,128)(2,1)} %param.16) | copy-start | bytes 1572868
  134.2 1.2 copy-start.1
  241.1 55.7 %copy-start.20 = (bf16[128,2048]{1,0:T(8,128)(2,1)S(1)}, bf16[128,2048]{1,0:T(8,128)(2,1)}, u32[]{:S(2)}) copy-start(bf16[128,2048]{1,0:T(8,128)(2,1)} %copy-done.19) | copy-start | bytes 1572868
  241.1 55.9 %copy-start.16 = (bf16[16,2048]{1,0:T(8,128)(2,1)S(1)}, bf16[16,2048]{1,0:T(8,128)(2,1)}, u32[]{:S(2)}) copy-start(bf16[16,2048]{1,0:T(8,128)(2,1)} %copy-done.15) | copy-start | bytes 196612
  297.1 3.3 copy-start.21
  299.5 283.3 %reduce-scatter.7.cloned.1.call-start = ((), (), s32[]{:S(2)}) async-start(), calls=%async_computation.5 | async-start | bytes 4718592 | tf_op jit(solution)/shard_map/reduce_scatter | solution.py:1941
  300.3 282.6 %reduce-scatter.9.cloned.1.call-start = ((), (), s32[]{:S(2)}) async-start(), calls=%async_computation.6 | async-start | bytes 4718592 | tf_op jit(solution)/shard_map/reduce_scatter | solution.py:1941
  353.9 229.0 %reduce-scatter.11.cloned.1.call-start = ((), (), s32[]{:S(2)}) async-start(), calls=%async_computation.7 | async-start | bytes 4718592 | tf_op jit(solution)/shard_map/reduce_scatter | solution.py:1941
  409.6 1.6 copy-start.9
  411.9 55.3 %copy-start.22 = (f32[128,2048]{1,0:T(8,128)S(1)}, f32[128,2048]{1,0:T(8,128)}, u32[]{:S(2)}) copy-start(f32[128,2048]{1,0:T(8,128)} %get-tuple-element.87) | copy-start | bytes 3145732
  466.2 1.0 copy-start.12
  468.8 114.1 %copy-start.6 = (bf16[1024,512]{1,0:T(8,128)(2,1)S(1)}, bf16[1024,512]{1,0:T(8,128)(2,1)}, u32[]{:S(2)}) copy-start(bf16[1024,512]{1,0:T(8,128)(2,1)} %wk_ref.3) | copy-start | bytes 3145732
  468.8 114.1 %copy-start.8 = (bf16[1024,512]{1,0:T(8,128)(2,1)S(1)}, bf16[1024,512]{1,0:T(8,128)(2,1)}, u32[]{:S(2)}) copy-start(bf16[1024,512]{1,0:T(8,128)(2,1)} %wv_ref.3) | copy-start | bytes 3145732
  582.9 1.4 copy-start.10
  584.3 1.4 copy-start.11
  (6 other events, 4.8 us)
Sparse Core Ops, SparseCore 0:
  299.7 8.4 reduce-scatter.4
  310.4 43.3 reduce-scatter.6
  356.1 53.8 reduce-scatter.8
  412.0 63.4 reduce-scatter.10

commit v7 on v6

--- a/solution.py
+++ b/solution.py
@@ -1942,7 +1942,8 @@
 
     w_gate_sum = sum_fsdp(w_gate_part, 0)
     w_up_sum = sum_fsdp(w_up_part, 0)
-    w_down_sum = sum_fsdp(w_down_part, 1)
+    w_down_later, _ = lax.optimization_barrier((w_down_part, qkv_sum))
+    w_down_sum = sum_fsdp(w_down_later, 1)
 
     small_part = jnp.concatenate([router_part, mlp_gain_part[None]], axis=0)
     small_part = jnp.pad(small_part, ((0, -small_part.shape[0] % 16), (0, 0)))

time: 626 us -> 622 us (level)
    unnamed x52 -> x56, local copies, waits for them, and re-layouts: 13.2 us -> 13.7 us
  transfers between devices with their start and end apart: 4 -> 4, of which waited for: 0 -> 0; matrix products, arithmetic and copies ran while one was open for 1% -> 2% of each run, Pallas kernels for 44% -> 43%
where the time goes in v7:
time: 622 us; the launch traced here: 617 us
  Pallas kernels  557 us (90%)
  other arithmetic  21.5 us (3%)
  local copies, waits for them, and re-layouts  20.3 us (3%)
  between operations  14.4 us (2%)
    pallas_call x1, Pallas kernels, last_gather(): pl.pallas_call(functools.partial(last_gather_kernel, count, members, cuts...  109 us
    pallas_call x1, Pallas kernels, attend(): pl.pallas_call(functools.partial(attend_kernel, count, shards, cuts, head...  55.5 us
    pallas_call x1, Pallas kernels, expert_gathered(): pl.pallas_call(functools.partial(expert_kernel, count, shards, cuts, capa...  54.7 us
    pallas_call x1, Pallas kernels, attend_back(): pl.pallas_call(functools.partial(attend_back_kernel, count, shards, cuts,...  54.2 us
    pallas_call x1, Pallas kernels, slots_back(): pl.pallas_call(functools.partial(slots_back_kernel, count, shards, cuts,...  53.5 us
    pallas_call x1, Pallas kernels, front(): pl.pallas_call(functools.partial(front_kernel, count, shards, cuts, (gcol...  52.5 us
    pallas_call x1, Pallas kernels, out_back(): pl.pallas_call(functools.partial(out_back_kernel, count, cuts), out_shape...  52.3 us
    pallas_call x1, Pallas kernels, product_scattered(): pl.pallas_call(functools.partial(product_kernel, count, shards, cuts, dim...  48.9 us
  transfers between devices with their start and end apart: 4, of which 0 were waited for; matrix products, arithmetic and copies ran while one was open for 2% of the time, Pallas kernels for 43%

profile of v7, /device:TPU:0, one launch (start us, length us, event | category | flops | bytes accessed | tf_op | source)
XLA Modules:
  0.0 616.9 jit_solution(3255817895703389131)
XLA Ops:
  10.7 1.2 copy-done.5
  11.9 1.2 copy-done.7
  13.9 52.5 %shard_map.263 = (bf16[2048,2048]{1,0:T(8,128)(2,1)}, bf16[2048,512]{1,0:T(8,128)(2,1)}, bf16[2048,512]{1,0:T(8,128)(2,1)}, bf16[256,2048]{1,0:T(8,128)(2,1)S(1)...) custom-call(bf16[128,2048]{1,0:T(8,128)(2,1)S(1)} %bitcast.69, ...), custom_call_target="tpu_custom_call" | custom-call | tf_op jit(solution)/shard_map/pallas_call | solution.py:506
  70.9 1.1 iota_select_fusion.start_ref
  72.0 3.1 fusion.10
  75.1 55.5 %shard_map.264 = (bf16[2048,2048]{1,0:T(8,128)(2,1)}, bf16[16,16,128]{2,1,0:T(8,128)(2,1)}, bf16[2048,256]{1,0:T(8,128)(2,1)}, bf16[2048,512]{1,0:T(8,128)(2,1)}...) custom-call(bf16[128,2048]{1,0:T(8,128)(2,1)} %bitcast.79, ...), custom_call_target="tpu_custom_call" | custom-call | tf_op jit(solution)/shard_map/pallas_call | solution.py:1288
  134.2 1.2 copy-done.1
  135.5 48.9 %shard_map.265 = (f32[128,2048]{1,0:T(8,128)S(1)}, bf16[2048,768]{1,0:T(8,128)(2,1)}, bf16[256,2048]{1,0:T(8,128)(2,1)S(1)}) custom-call(bf16[2048,256]{1,0:T(8,128)(2,1)S(1)} %copy-done.1, bf16[256,2048]{1,0:T(8,128)(2,1)S(1)} %get-tuple-element.66.w_ref, bf16[1024,768]{1,0:T(8,128)(2,1)S(1)} %bitcast.68, bf16[768,1024]{1,0:T(8,128)(2,1)} %bitcast.73), custom_call_target="tpu_custom_call" | custom-call | tf_op jit(solution)/shard_map/pallas_call | solution.py:821
  186.5 54.7 %shard_map.266 = (bf16[1152,2048]{1,0:T(8,128)(2,1)}, bf16[1152,2048]{1,0:T(8,128)(2,1)}, bf16[144,2048]{1,0:T(8,128)(2,1)}, bf16[1152,128]{1,0:T(8,128)(2,1)}, ...) custom-call(bf16[128,2048]{1,0:T(8,128)(2,1)} %copy-done.22, ...), custom_call_target="tpu_custom_call" | custom-call | tf_op jit(solution)/shard_map/pallas_call | solution.py:1022
  241.2 53.5 %shard_map.267 = (f32[128,2176]{1,0:T(8,128)}, bf16[2048,768]{1,0:T(8,128)(2,1)}) custom-call(s32[16,128]{1,0:T(8,128)} %and_select_fusion.slot_ref, bf16[1152,128]{1,0:T(8,128)(2,1)} %get-tuple-element.78.dl, bf16[144,2048]{1,0:T(8,128)(2,1)} %get-tuple-element.79.dx0_ref, bf16[1152,2048]{1,0:T(8,128)(2,1)} %get-tuple-element.80.xs_ref, ...), custom_call_target="tpu_custom_call" | custom-call | tf_op jit(solution)/shard_map/pallas_call | solution.py:1119
  294.8 1.1 multiply_reduce_fusion.3
  295.9 1.1 multiply_convert_fusion.1
  297.2 1.8 multiply_reduce_fusion
  300.6 1.1 fusion.31.da_ref
  301.7 52.3 %shard_map.268 = (bf16[2048,256]{1,0:T(8,128)(2,1)}, bf16[256,2048]{1,0:T(8,128)(2,1)}, bf16[768,2048]{1,0:T(8,128)(2,1)}, bf16[2048,768]{1,0:T(8,128)(2,1)}) custom-call(bf16[128,2048]{1,0:T(8,128)(2,1)} %fusion.31.da_ref, bf16[256,2048]{1,0:T(8,128)(2,1)} %copy-done.4, bf16[2048,256]{1,0:T(8,128)(2,1)} %get-tuple-element.65.y_ref.o_ref, ...), custom_call_target="tpu_custom_call" | custom-call | tf_op jit(solution)/shard_map/pallas_call | solution.py:619
  354.6 54.2 %shard_map.269 = (bf16[2048,512]{1,0:T(8,128)(2,1)}, f32[8,128]{1,0:T(8,128)}, f32[128,2048]{1,0:T(8,128)}, bf16[128,2048]{1,0:T(8,128)(2,1)}) custom-call(bf16[2048,512]{1,0:T(8,128)(2,1)} %get-tuple-element.68.qx_ref, bf16[2048,128]{1,0:T(8,128)(2,1)} %get-tuple-element.69.kn_ref, bf16[2048,512]{1,0:T(8,128)(2,1)} %get-tuple-element.63.qkv_ref, ...), custom_call_target="tpu_custom_call" | custom-call | tf_op jit(solution)/shard_map/pallas_call | solution.py:1515
  408.8 1.6 copy-done.9
  411.1 48.2 %shard_map.270 = (f32[128,2048]{1,0:T(8,128)S(1)}, bf16[1040,512]{1,0:T(8,128)(2,1)S(1)}) custom-call(bf16[2048,512]{1,0:T(8,128)(2,1)S(1)} %copy-done.9, bf16[2048,512]{1,0:T(8,128)(2,1)} %get-tuple-element.90.w_ref, f32[8,128]{1,0:T(8,128)S(1)} %copy-done.18, bf16[2048,2048]{1,0:T(8,128)(2,1)} %get-tuple-element.92.h_ref), custom_call_target="tpu_custom_call" | custom-call | tf_op jit(solution)/shard_map/pallas_call | solution.py:788
  461.5 3.1 fusion.6
  464.6 109.5 %shard_map.271 = (bf16[16,1040,256]{2,1,0:T(8,128)(2,1)}, bf16[16,256,256]{2,1,0:T(8,128)(2,1)}, bf16[16,128,2048]{2,1,0:T(8,128)(2,1)}, bf16[16,32,1024]{2,1,0:T(8,128)(2,1)}) custom-call(bf16[1040,512]{1,0:T(8,128)(2,1)} %copy-done.12, bf16[128,2048]{1,0:T(8,128)(2,1)} %get-tuple-element.95.refs_0_, bf16[32,1024]{1,0:T(8,128)(2,1)} %reduce-scatter.5.cloned.1.call-done.refs_1_), custom_call_target="tpu_custom_call" | custom-call | tf_op jit(solution)/shard_map/pallas_call | solution.py:1645
  576.2 1.4 convert_reduce_fusion
  578.9 1.4 copy-done.10
  580.3 1.4 copy-done.11
  581.7 27.7 %shard_map.272 = (f32[1024,4096]{1,0:T(8,128)}, f32[1024,512]{1,0:T(8,128)}, f32[1024,512]{1,0:T(8,128)}, f32[1024,1]{1,0:T(8,128)S(1)}, f32[2048,2048]{1,0:T(8,...) custom-call(bf16[16,1040,256]{2,1,0:T(8,128)(2,1)} %get-tuple-element.96.q_ref, ...), custom_call_target="tpu_custom_call" | custom-call | tf_op jit(solution)/shard_map/pallas_call | solution.py:1733
  (112 shorter events, 23.8 us)
Async XLA Ops:
  7.2 457.5 %reduce-scatter.5.cloned.1.call-start = ((), (), s32[]{:S(2)}) async-start(), calls=%async_computation.4 | async-start | bytes 196608 | tf_op jit(solution)/shard_map/reduce_scatter | solution.py:1941
  10.7 1.2 copy-start.5
  11.9 1.2 copy-start.7
  13.9 53.5 %copy-start.26 = (s32[1,128,8]{1,2,0:T(8,128)S(1)}, s32[1,128,8]{1,2,0:T(8,128)}, u32[]{:S(2)}) copy-start(s32[1,128,8]{1,2,0:T(8,128)} %param.19) | copy-start | bytes 12292
  67.4 66.9 %copy-start.4 = (bf16[256,2048]{1,0:T(8,128)(2,1)}, bf16[256,2048]{1,0:T(8,128)(2,1)S(1)}, u32[]{:S(2)}) copy-start(bf16[256,2048]{1,0:T(8,128)(2,1)S(1)} %get-tuple-element.66.w_ref) | copy-start | bytes 3145732
  67.4 118.2 %copy-start.15 = (bf16[16,2048]{1,0:T(8,128)(2,1)}, bf16[16,2048]{1,0:T(8,128)(2,1)S(1)}, u32[]{:S(2)}) copy-start(bf16[16,2048]{1,0:T(8,128)(2,1)S(1)} %get-tuple-element.71.router_ref) | copy-start | bytes 196612
  75.1 59.2 %copy-start = (bf16[1,1024,768]{2,1,0:T(8,128)(2,1)S(1)}, bf16[1,1024,768]{2,1,0:T(8,128)(2,1)}, u32[]{:S(2)}) copy-start(bf16[1,1024,768]{2,1,0:T(8,128)(2,1)} %param.30) | copy-start | bytes 4718596
  130.5 53.9 %copy-start.3 = (bf16[1,128,2048]{2,1,0:T(8,128)(2,1)S(1)}, bf16[1,128,2048]{2,1,0:T(8,128)(2,1)}, u32[]{:S(2)}) copy-start(bf16[1,128,2048]{2,1,0:T(8,128)(2,1)} %param.16) | copy-start | bytes 1572868
  134.2 1.2 copy-start.1
  185.4 115.2 %copy-start.19 = (f32[128,2048]{1,0:T(8,128)}, f32[128,2048]{1,0:T(8,128)S(1)}, u32[]{:S(2)}) copy-start(f32[128,2048]{1,0:T(8,128)S(1)} %get-tuple-element.117) | copy-start | bytes 3145732
  241.2 55.8 %copy-start.23 = (bf16[128,2048]{1,0:T(8,128)(2,1)S(1)}, bf16[128,2048]{1,0:T(8,128)(2,1)}, u32[]{:S(2)}) copy-start(bf16[128,2048]{1,0:T(8,128)(2,1)} %copy-done.22) | copy-start | bytes 1572868
  241.2 56.0 %copy-start.16 = (bf16[16,2048]{1,0:T(8,128)(2,1)S(1)}, bf16[16,2048]{1,0:T(8,128)(2,1)}, u32[]{:S(2)}) copy-start(bf16[16,2048]{1,0:T(8,128)(2,1)} %copy-done.15) | copy-start | bytes 196612
  297.2 3.4 copy-start.24
  298.9 2.7 copy-start.21
  299.7 279.1 %reduce-scatter.7.cloned.1.call-start = ((), (), s32[]{:S(2)}) async-start(), calls=%async_computation.5 | async-start | bytes 4718592 | tf_op jit(solution)/shard_map/reduce_scatter | solution.py:1941
  300.5 278.3 %reduce-scatter.11.cloned.1.call-start = ((), (), s32[]{:S(2)}) async-start(), calls=%async_computation.7 | async-start | bytes 4718592 | tf_op jit(solution)/shard_map/reduce_scatter | solution.py:1941
  301.7 52.3 %copy-start.25 = (s32[1,2048]{1,0:T(1,128)S(1)}, s32[1,2048]{1,0:T(1,128)}, u32[]{:S(2)}) copy-start(s32[1,2048]{1,0:T(1,128)} %param.18) | copy-start | bytes 24580
  408.8 1.6 copy-start.9
  460.2 1.2 copy-start.20
  460.2 118.6 %reduce-scatter.9.cloned.1.call-start = ((), (), s32[]{:S(2)}) async-start(), calls=%async_computation.6 | async-start | bytes 4718592 | tf_op jit(solution)/shard_map/reduce_scatter | solution.py:1941
  464.6 114.2 %copy-start.6 = (bf16[1024,512]{1,0:T(8,128)(2,1)S(1)}, bf16[1024,512]{1,0:T(8,128)(2,1)}, u32[]{:S(2)}) copy-start(bf16[1024,512]{1,0:T(8,128)(2,1)} %wk_ref.3) | copy-start | bytes 3145732
  464.6 114.2 %copy-start.8 = (bf16[1024,512]{1,0:T(8,128)(2,1)S(1)}, bf16[1024,512]{1,0:T(8,128)(2,1)}, u32[]{:S(2)}) copy-start(bf16[1024,512]{1,0:T(8,128)(2,1)} %wv_ref.3) | copy-start | bytes 3145732
  578.8 1.4 copy-start.10
  580.2 1.4 copy-start.11
  (8 other events, 7.0 us)
Sparse Core Ops, SparseCore 0:
  299.8 8.4 reduce-scatter.4
  310.5 43.3 reduce-scatter.6
  460.4 42.4 reduce-scatter.10
  504.9 43.3 reduce-scatter.8

commit v8 on v7

--- a/solution.py
+++ b/solution.py
@@ -1941,8 +1941,8 @@
         return lax.psum_scatter(part.astype(BF16), "fsdp", scatter_dimension=axis, tiled=True)
 
     w_gate_sum = sum_fsdp(w_gate_part, 0)
-    w_up_sum = sum_fsdp(w_up_part, 0)
-    w_down_later, _ = lax.optimization_barrier((w_down_part, qkv_sum))
+    w_up_later, w_down_later, _ = lax.optimization_barrier((w_up_part, w_down_part, qkv_sum))
+    w_up_sum = sum_fsdp(w_up_later, 0)
     w_down_sum = sum_fsdp(w_down_later, 1)
 
     small_part = jnp.concatenate([router_part, mlp_gain_part[None]], axis=0)

time: 622 us -> 622 us (level)
  no operation moved by 1% of the time
where the time goes in v8:
time: 622 us; the launch traced here: 617 us
  Pallas kernels  557 us (90%)
  other arithmetic  21.5 us (3%)
  local copies, waits for them, and re-layouts  20.3 us (3%)
  between operations  14.4 us (2%)
    pallas_call x1, Pallas kernels, last_gather(): pl.pallas_call(functools.partial(last_gather_kernel, count, members, cuts...  109 us
    pallas_call x1, Pallas kernels, attend(): pl.pallas_call(functools.partial(attend_kernel, count, shards, cuts, head...  55.5 us
    pallas_call x1, Pallas kernels, expert_gathered(): pl.pallas_call(functools.partial(expert_kernel, count, shards, cuts, capa...  54.7 us
    pallas_call x1, Pallas kernels, attend_back(): pl.pallas_call(functools.partial(attend_back_kernel, count, shards, cuts,...  54.2 us
    pallas_call x1, Pallas kernels, slots_back(): pl.pallas_call(functools.partial(slots_back_kernel, count, shards, cuts,...  53.5 us
    pallas_call x1, Pallas kernels, front(): pl.pallas_call(functools.partial(front_kernel, count, shards, cuts, (gcol...  52.5 us
    pallas_call x1, Pallas kernels, out_back(): pl.pallas_call(functools.partial(out_back_kernel, count, cuts), out_shape...  52.3 us
    pallas_call x1, Pallas kernels, product_scattered(): pl.pallas_call(functools.partial(product_kernel, count, shards, cuts, dim...  48.9 us
  transfers between devices with their start and end apart: 4, of which 0 were waited for; matrix products, arithmetic and copies ran while one was open for 2% of the time, Pallas kernels for 43%

profile of v8, /device:TPU:0, one launch (start us, length us, event | category | flops | bytes accessed | tf_op | source)
XLA Modules:
  0.0 616.9 jit_solution(2971661876005483548)
XLA Ops:
  10.7 1.2 copy-done.5
  11.9 1.2 copy-done.7
  13.9 52.5 %shard_map.263 = (bf16[2048,2048]{1,0:T(8,128)(2,1)}, bf16[2048,512]{1,0:T(8,128)(2,1)}, bf16[2048,512]{1,0:T(8,128)(2,1)}, bf16[256,2048]{1,0:T(8,128)(2,1)S(1)...) custom-call(bf16[128,2048]{1,0:T(8,128)(2,1)S(1)} %bitcast.69, ...), custom_call_target="tpu_custom_call" | custom-call | tf_op jit(solution)/shard_map/pallas_call | solution.py:506
  70.9 1.1 iota_select_fusion.start_ref
  72.0 3.1 fusion.10
  75.1 55.5 %shard_map.264 = (bf16[2048,2048]{1,0:T(8,128)(2,1)}, bf16[16,16,128]{2,1,0:T(8,128)(2,1)}, bf16[2048,256]{1,0:T(8,128)(2,1)}, bf16[2048,512]{1,0:T(8,128)(2,1)}...) custom-call(bf16[128,2048]{1,0:T(8,128)(2,1)} %bitcast.79, ...), custom_call_target="tpu_custom_call" | custom-call | tf_op jit(solution)/shard_map/pallas_call | solution.py:1288
  134.2 1.2 copy-done.1
  135.5 48.9 %shard_map.265 = (f32[128,2048]{1,0:T(8,128)S(1)}, bf16[2048,768]{1,0:T(8,128)(2,1)}, bf16[256,2048]{1,0:T(8,128)(2,1)S(1)}) custom-call(bf16[2048,256]{1,0:T(8,128)(2,1)S(1)} %copy-done.1, bf16[256,2048]{1,0:T(8,128)(2,1)S(1)} %get-tuple-element.67.w_ref, bf16[1024,768]{1,0:T(8,128)(2,1)S(1)} %bitcast.68, bf16[768,1024]{1,0:T(8,128)(2,1)} %bitcast.73), custom_call_target="tpu_custom_call" | custom-call | tf_op jit(solution)/shard_map/pallas_call | solution.py:821
  186.5 54.7 %shard_map.266 = (bf16[1152,2048]{1,0:T(8,128)(2,1)}, bf16[1152,2048]{1,0:T(8,128)(2,1)}, bf16[144,2048]{1,0:T(8,128)(2,1)}, bf16[1152,128]{1,0:T(8,128)(2,1)}, ...) custom-call(bf16[128,2048]{1,0:T(8,128)(2,1)} %copy-done.22, ...), custom_call_target="tpu_custom_call" | custom-call | tf_op jit(solution)/shard_map/pallas_call | solution.py:1022
  241.2 53.5 %shard_map.267 = (f32[128,2176]{1,0:T(8,128)}, bf16[2048,768]{1,0:T(8,128)(2,1)}) custom-call(s32[16,128]{1,0:T(8,128)} %and_select_fusion.slot_ref, bf16[1152,128]{1,0:T(8,128)(2,1)} %get-tuple-element.79.dl, bf16[144,2048]{1,0:T(8,128)(2,1)} %get-tuple-element.80.dx0_ref, bf16[1152,2048]{1,0:T(8,128)(2,1)} %get-tuple-element.81.xs_ref, ...), custom_call_target="tpu_custom_call" | custom-call | tf_op jit(solution)/shard_map/pallas_call | solution.py:1119
  294.8 1.1 multiply_reduce_fusion.3
  295.9 1.1 multiply_convert_fusion.1
  297.2 1.8 multiply_reduce_fusion
  300.6 1.1 fusion.31.da_ref
  301.7 52.3 %shard_map.268 = (bf16[2048,256]{1,0:T(8,128)(2,1)}, bf16[256,2048]{1,0:T(8,128)(2,1)}, bf16[768,2048]{1,0:T(8,128)(2,1)}, bf16[2048,768]{1,0:T(8,128)(2,1)}) custom-call(bf16[128,2048]{1,0:T(8,128)(2,1)} %fusion.31.da_ref, bf16[256,2048]{1,0:T(8,128)(2,1)} %copy-done.4, bf16[2048,256]{1,0:T(8,128)(2,1)} %get-tuple-element.66.y_ref.o_ref, ...), custom_call_target="tpu_custom_call" | custom-call | tf_op jit(solution)/shard_map/pallas_call | solution.py:619
  354.6 54.2 %shard_map.269 = (bf16[2048,512]{1,0:T(8,128)(2,1)}, f32[8,128]{1,0:T(8,128)}, f32[128,2048]{1,0:T(8,128)}, bf16[128,2048]{1,0:T(8,128)(2,1)}) custom-call(bf16[2048,512]{1,0:T(8,128)(2,1)} %get-tuple-element.69.qx_ref, bf16[2048,128]{1,0:T(8,128)(2,1)} %get-tuple-element.70.kn_ref, bf16[2048,512]{1,0:T(8,128)(2,1)} %get-tuple-element.64.qkv_ref, ...), custom_call_target="tpu_custom_call" | custom-call | tf_op jit(solution)/shard_map/pallas_call | solution.py:1515
  408.8 1.6 copy-done.9
  411.1 48.2 %shard_map.270 = (f32[128,2048]{1,0:T(8,128)S(1)}, bf16[1040,512]{1,0:T(8,128)(2,1)S(1)}) custom-call(bf16[2048,512]{1,0:T(8,128)(2,1)S(1)} %copy-done.9, bf16[2048,512]{1,0:T(8,128)(2,1)} %get-tuple-element.91.w_ref, f32[8,128]{1,0:T(8,128)S(1)} %copy-done.18, bf16[2048,2048]{1,0:T(8,128)(2,1)} %get-tuple-element.93.h_ref), custom_call_target="tpu_custom_call" | custom-call | tf_op jit(solution)/shard_map/pallas_call | solution.py:788
  461.5 3.1 fusion.6
  464.6 109.5 %shard_map.271 = (bf16[16,1040,256]{2,1,0:T(8,128)(2,1)}, bf16[16,256,256]{2,1,0:T(8,128)(2,1)}, bf16[16,128,2048]{2,1,0:T(8,128)(2,1)}, bf16[16,32,1024]{2,1,0:T(8,128)(2,1)}) custom-call(bf16[1040,512]{1,0:T(8,128)(2,1)} %copy-done.12, bf16[128,2048]{1,0:T(8,128)(2,1)} %get-tuple-element.96.refs_0_, bf16[32,1024]{1,0:T(8,128)(2,1)} %reduce-scatter.5.cloned.1.call-done.refs_1_), custom_call_target="tpu_custom_call" | custom-call | tf_op jit(solution)/shard_map/pallas_call | solution.py:1645
  576.2 1.4 convert_reduce_fusion
  578.8 1.4 copy-done.10
  580.2 1.4 copy-done.11
  581.7 27.7 %shard_map.272 = (f32[1024,4096]{1,0:T(8,128)}, f32[1024,512]{1,0:T(8,128)}, f32[1024,512]{1,0:T(8,128)}, f32[1024,1]{1,0:T(8,128)S(1)}, f32[2048,2048]{1,0:T(8,...) custom-call(bf16[16,1040,256]{2,1,0:T(8,128)(2,1)} %get-tuple-element.97.q_ref, ...), custom_call_target="tpu_custom_call" | custom-call | tf_op jit(solution)/shard_map/pallas_call | solution.py:1733
  (112 shorter events, 23.8 us)
Async XLA Ops:
  7.2 457.5 %reduce-scatter.5.cloned.1.call-start = ((), (), s32[]{:S(2)}) async-start(), calls=%async_computation.4 | async-start | bytes 196608 | tf_op jit(solution)/shard_map/reduce_scatter | solution.py:1941
  10.7 1.2 copy-start.5
  11.9 1.2 copy-start.7
  13.9 53.5 %copy-start.26 = (s32[1,128,8]{1,2,0:T(8,128)S(1)}, s32[1,128,8]{1,2,0:T(8,128)}, u32[]{:S(2)}) copy-start(s32[1,128,8]{1,2,0:T(8,128)} %param.19) | copy-start | bytes 12292
  67.4 66.9 %copy-start.4 = (bf16[256,2048]{1,0:T(8,128)(2,1)}, bf16[256,2048]{1,0:T(8,128)(2,1)S(1)}, u32[]{:S(2)}) copy-start(bf16[256,2048]{1,0:T(8,128)(2,1)S(1)} %get-tuple-element.67.w_ref) | copy-start | bytes 3145732
  67.4 118.2 %copy-start.15 = (bf16[16,2048]{1,0:T(8,128)(2,1)}, bf16[16,2048]{1,0:T(8,128)(2,1)S(1)}, u32[]{:S(2)}) copy-start(bf16[16,2048]{1,0:T(8,128)(2,1)S(1)} %get-tuple-element.72.router_ref) | copy-start | bytes 196612
  75.1 59.2 %copy-start = (bf16[1,1024,768]{2,1,0:T(8,128)(2,1)S(1)}, bf16[1,1024,768]{2,1,0:T(8,128)(2,1)}, u32[]{:S(2)}) copy-start(bf16[1,1024,768]{2,1,0:T(8,128)(2,1)} %param.30) | copy-start | bytes 4718596
  130.5 53.9 %copy-start.3 = (bf16[1,128,2048]{2,1,0:T(8,128)(2,1)S(1)}, bf16[1,128,2048]{2,1,0:T(8,128)(2,1)}, u32[]{:S(2)}) copy-start(bf16[1,128,2048]{2,1,0:T(8,128)(2,1)} %param.16) | copy-start | bytes 1572868
  134.2 1.2 copy-start.1
  185.4 115.2 %copy-start.19 = (f32[128,2048]{1,0:T(8,128)}, f32[128,2048]{1,0:T(8,128)S(1)}, u32[]{:S(2)}) copy-start(f32[128,2048]{1,0:T(8,128)S(1)} %get-tuple-element.119) | copy-start | bytes 3145732
  241.2 55.8 %copy-start.23 = (bf16[128,2048]{1,0:T(8,128)(2,1)S(1)}, bf16[128,2048]{1,0:T(8,128)(2,1)}, u32[]{:S(2)}) copy-start(bf16[128,2048]{1,0:T(8,128)(2,1)} %copy-done.22) | copy-start | bytes 1572868
  241.2 56.0 %copy-start.16 = (bf16[16,2048]{1,0:T(8,128)(2,1)S(1)}, bf16[16,2048]{1,0:T(8,128)(2,1)}, u32[]{:S(2)}) copy-start(bf16[16,2048]{1,0:T(8,128)(2,1)} %copy-done.15) | copy-start | bytes 196612
  297.2 3.4 copy-start.24
  298.9 2.7 copy-start.21
  299.7 279.1 %reduce-scatter.7.cloned.1.call-start = ((), (), s32[]{:S(2)}) async-start(), calls=%async_computation.5 | async-start | bytes 4718592 | tf_op jit(solution)/shard_map/reduce_scatter | solution.py:1941
  300.5 278.3 %reduce-scatter.9.cloned.1.call-start = ((), (), s32[]{:S(2)}) async-start(), calls=%async_computation.6 | async-start | bytes 4718592 | tf_op jit(solution)/shard_map/reduce_scatter | solution.py:1941
  301.7 52.3 %copy-start.25 = (s32[1,2048]{1,0:T(1,128)S(1)}, s32[1,2048]{1,0:T(1,128)}, u32[]{:S(2)}) copy-start(s32[1,2048]{1,0:T(1,128)} %param.18) | copy-start | bytes 24580
  408.8 1.6 copy-start.9
  460.2 1.2 copy-start.20
  460.2 118.6 %reduce-scatter.11.cloned.1.call-start = ((), (), s32[]{:S(2)}) async-start(), calls=%async_computation.7 | async-start | bytes 4718592 | tf_op jit(solution)/shard_map/reduce_scatter | solution.py:1941
  464.6 114.2 %copy-start.6 = (bf16[1024,512]{1,0:T(8,128)(2,1)S(1)}, bf16[1024,512]{1,0:T(8,128)(2,1)}, u32[]{:S(2)}) copy-start(bf16[1024,512]{1,0:T(8,128)(2,1)} %wk_ref.3) | copy-start | bytes 3145732
  464.6 114.2 %copy-start.8 = (bf16[1024,512]{1,0:T(8,128)(2,1)S(1)}, bf16[1024,512]{1,0:T(8,128)(2,1)}, u32[]{:S(2)}) copy-start(bf16[1024,512]{1,0:T(8,128)(2,1)} %wv_ref.3) | copy-start | bytes 3145732
  578.8 1.4 copy-start.10
  580.2 1.4 copy-start.11
  (8 other events, 7.0 us)
Sparse Core Ops, SparseCore 0:
  299.8 8.4 reduce-scatter.4
  310.5 43.3 reduce-scatter.6
  460.4 42.4 reduce-scatter.8
  504.9 43.3 reduce-scatter.10
